TPU v7x, 32 devices: a whole 2x2x4 slice. The times are simulated.
32 devices in a mesh: ctx: 8 (over y, x, core), head: 4 (over z).
Axes of the slice: x: 2, y: 2, z: 4, core: 2. Of those that a mesh axis runs over, the one named last changes fastest.
Arguments:
- hidden: bfloat16 [16384, 1024], P('ctx'), may hold values from -6 to 6
- norm_gain: float32 [1024], replicated, may hold values from 0.1 to 1.9
- w_zx: bfloat16 [1024, 2, 2048], P(None, None, 'head'), may hold values from -0.1875 to 0.1875
- w_bc: bfloat16 [1024, 256], replicated, may hold values from -0.1875 to 0.1875
- w_dt: bfloat16 [1024, 32], P(None, 'head'), may hold values from -0.1875 to 0.1875
- dt_bias: float32 [32], P('head'), may hold values from -2 to 1
- decay_rate: float32 [32], P('head'), may hold values from 1e-07 to 0.03
- skip_gain: float32 [32], P('head'), may hold values from 0.5 to 2
- conv_x: float32 [4, 2048], P(None, 'head'), may hold values from -3 to 3
- conv_bc: float32 [4, 256], replicated, may hold values from -3 to 3
- w_out: bfloat16 [2048, 1024], P('head'), may hold values from -0.125 to 0.125
Outputs:
- mixed: bfloat16 [16384, 1024], P(('ctx', 'head'))
All inputs are finite; a program needn't handle non-finite values.
Results may differ from a plain program's by a relative error of at most 0.013.
Values may be sent and summed in bfloat16 or wider, within the bound.
No kernel may reach another device: no remote copies, remote signals or barrier semaphores. Data moves between devices by JAX's collectives and lax.ppermute only.
A program may use at most 128 MiB of HBM per device.

v0:
```python
import functools

import jax
import jax.numpy as jnp
from jax import lax
from jax.experimental import pallas as pl
from jax.experimental.pallas import tpu as pltpu
from jax.sharding import PartitionSpec as P

STATE = 128
CHUNK = 128
TILE = 256
EPS = 1e-05
RIM = 16
TAIL = 16
F32 = jnp.float32
BF16 = jnp.bfloat16
MIB = 2**20


def params(limit=58):
    return pltpu.CompilerParams(
        dimension_semantics=("arbitrary",), vmem_limit_bytes=limit * MIB
    )


def cost(flops, bytes_accessed):
    return pl.CostEstimate(flops=int(flops), bytes_accessed=int(bytes_accessed), transcendentals=0)


def whole(shape):
    return pl.BlockSpec(shape, lambda *_: (0,) * len(shape))


def silu(x):
    half = 0.5 * x
    return half + half * jnp.tanh(half)


def tri(rows, reverse):
    r = lax.broadcasted_iota(jnp.int32, (rows, rows), 0)
    c = lax.broadcasted_iota(jnp.int32, (rows, rows), 1)
    return (r <= c) if reverse else (r >= c)


def spread_matrix(first, heads, width):
    r = lax.broadcasted_iota(jnp.int32, (2 * 128, heads * width), 0) % 128
    c = lax.broadcasted_iota(jnp.int32, (2 * 128, heads * width), 1) // width
    return (r == c + first).astype(BF16)


def spread(q, matrix):
    high = q.astype(BF16)
    low = (q - high.astype(F32)).astype(BF16)
    return jnp.dot(jnp.concatenate([high, low], axis=1), matrix, preferred_element_type=F32)


def prepare_kernel(inner, heads, zx_ref, bc_ref, dt_ref, gain_ref, wf_ref, wr_ref):
    rows = zx_ref.shape[0]
    gain = gain_ref[...]
    zx = zx_ref[...].astype(F32).reshape(rows, 2 * inner)
    r = lax.broadcasted_iota(jnp.int32, (rows, rows), 0)
    c = lax.broadcasted_iota(jnp.int32, (rows, rows), 1)
    turn = (r + c == rows - 1).astype(BF16)
    at = 0
    for part in (zx[:, inner:], bc_ref[...].astype(F32), zx[:, :inner], dt_ref[...].astype(F32)):
        scaled = (part * gain).astype(BF16)
        size = scaled.shape[1]
        wf_ref[:, at : at + size] = scaled
        wr_ref[:, at : at + size] = jnp.dot(turn, scaled, preferred_element_type=F32).astype(BF16)
        at += size


def prepare(w_zx, w_bc, w_dt, gain):
    depth, _, inner = w_zx.shape
    tile = min(256, depth)
    n = depth // tile
    wide = 2 * inner + w_bc.shape[1] + 128
    return pl.pallas_call(
        functools.partial(prepare_kernel, inner, None),
        grid=(n,),
        in_specs=[pl.BlockSpec((tile, 2, inner), lambda i: (i, 0, 0)),
                  pl.BlockSpec((tile, w_bc.shape[1]), lambda i: (i, 0)),
                  pl.BlockSpec((tile, 128), lambda i: (i, 0)),
                  pl.BlockSpec((tile, 1), lambda i: (i, 0))],
        out_specs=[pl.BlockSpec((tile, wide), lambda i: (i, 0)),
                   pl.BlockSpec((tile, wide), lambda i: (n - 1 - i, 0))],
        out_shape=[jax.ShapeDtypeStruct((depth, wide), BF16)] * 2,
        compiler_params=params(),
        cost_estimate=cost(1e9, 8e6),
        name="prepare",
    )(w_zx, w_bc, w_dt, gain)


def project_kernel(heads, inner, *refs):
    (hf_ref, hr_ref, rimf_ref, rimr_ref, wf_ref, wr_ref, conv_ref, bias_ref, rate_ref, copy_ref,
     actf_ref, zf_ref, smallf_ref, cumtf_ref, enterf_ref, priorf_ref,
     actr_ref, zr_ref, smallr_ref, cumtr_ref, enterr_ref, priorr_ref,
     msg_ref, buff, bufr, statef, stater, totalf, totalr) = refs
    step = pl.program_id(0)
    last = pl.num_programs(0) - 1
    stream = inner + 2 * STATE
    blocks = stream // 128
    wide = stream + inner
    rows = hf_ref.shape[0]
    sides = (
        (False, hf_ref, rimf_ref, wf_ref, actf_ref, zf_ref, smallf_ref, cumtf_ref, enterf_ref, priorf_ref,
         buff, statef, totalf),
        (True, hr_ref, rimr_ref, wr_ref, actr_ref, zr_ref, smallr_ref, cumtr_ref, enterr_ref, priorr_ref,
         bufr, stater, totalr),
    )

    def row_scale(h):
        hf = h.astype(F32)
        return lax.rsqrt(jnp.mean(hf * hf, axis=-1, keepdims=True) + EPS)

    @pl.when(step == 0)
    def _():
        for reverse, _, rim_ref, w_ref, _, _, _, _, _, _, buf, state, total in sides:
            edge = rows if reverse else 0
            state[...] = jnp.zeros_like(state)
            total[...] = jnp.zeros_like(total)
            rim = rim_ref[...]
            out = jnp.dot(rim, w_ref[:, :stream], preferred_element_type=F32) * row_scale(rim)
            for j in range(blocks):
                part = out[:, j * 128 : (j + 1) * 128]
                buf[j, edge : edge + 8, :] = part[:8] if reverse else part[RIM - 8 :]

    lane = lax.broadcasted_iota(jnp.int32, (CHUNK, 128), 1)
    copy = copy_ref[...]
    hs = [side[1][...] for side in sides]
    scales = [row_scale(h) for h in hs]
    small = []
    for k, (reverse, _, _, w_ref, _, _, small_ref, cumt_ref, _, _, _, _, _) in enumerate(sides):
        raw = jnp.dot(hs[k], w_ref[:, wide:], preferred_element_type=F32) * scales[k] + bias_ref[...]
        dt = jnp.maximum(raw, 0.0) + jnp.log1p(jnp.exp(-jnp.abs(raw)))
        steps = -rate_ref[...] * dt
        mask = tri(CHUNK, reverse).astype(F32)
        parts = []
        for c in range(0, rows, CHUNK):
            cum = jnp.dot(mask, steps[c : c + CHUNK], preferred_element_type=F32, precision=lax.Precision.HIGHEST)
            own = dt[c : c + CHUNK]
            small_ref[c : c + CHUNK, :] = jnp.where(lane < heads, own, pltpu.roll(cum, heads, 1))
            cumt_ref[:, c : c + CHUNK] = jnp.transpose(cum)[:heads]
            parts.append((own, cum))
        small.append(parts)

    for g in range(0, stream, 256):
        for k, (reverse, _, _, w_ref, act_ref, _, _, _, _, _, buf, _, _) in enumerate(sides):
            edge = rows if reverse else 0
            body = 0 if reverse else 8
            out = jnp.dot(hs[k], w_ref[:, g : g + 256], preferred_element_type=F32) * scales[k]
            for j in range(g // 128, g // 128 + 2):
                x = out[:, j * 128 - g : (j + 1) * 128 - g]
                buf[j, body : body + rows, :] = x
                cols = slice(j * 128, (j + 1) * 128)
                total = conv_ref[3:4, cols] * x
                for d in (1, 2, 3):
                    at = body + d if reverse else body - d
                    total = total + conv_ref[3 - d : 4 - d, cols] * buf[j, at : at + rows, :]
                act_ref[:, cols] = silu(total).astype(BF16)
                buf[j, edge : edge + 8, :] = x[:8] if reverse else x[rows - 8 :]

    for g in range(0, inner, 256):
        for k, (_, _, _, w_ref, _, z_ref, _, _, _, _, _, _, _) in enumerate(sides):
            out = jnp.dot(hs[k], w_ref[:, stream + g : stream + g + 256], preferred_element_type=F32) * scales[k]
            z_ref[:, g : g + 256] = out.astype(BF16)

    count = rows // CHUNK
    for i in range(count):
        for k, (reverse, _, _, _, act_ref, _, _, _, enter_ref, prior_ref, _, state, total) in enumerate(sides):
            c = count - 1 - i if reverse else i
            at = slice(c * CHUNK, (c + 1) * CHUNK)
            dt, cum = small[k][c]
            end = cum[:1] if reverse else cum[CHUNK - 1 :]
            weights = spread(jnp.where(lane < heads, dt * jnp.exp(end - cum), 0.0), copy)
            tails = (act_ref[at, :inner].astype(F32) * weights).astype(BF16)
            ends = lax.dot_general(act_ref[at, inner : inner + STATE], tails, (((0,), (0,)), ((), ())),
                                   preferred_element_type=F32)
            before = state[...]
            enter_ref[c] = before.astype(BF16)
            prior_ref[c] = spread(jnp.exp(total[...]), copy)
            decay = spread(jnp.exp(jnp.broadcast_to(end, (8, 128))), copy)[:1]
            state[...] = before * decay + ends
            total[...] = total[...] + end

    @pl.when(step == last)
    def _():
        for k, side in enumerate(sides):
            state, total = side[-2:]
            at = k * (STATE + TAIL)
            msg_ref[at : at + STATE, :] = state[...].astype(BF16)
            t = total[...]
            high = t.astype(BF16).astype(F32)
            mid = (t - high).astype(BF16).astype(F32)
            low = t - high - mid
            row = lax.broadcasted_iota(jnp.int32, (8, 128), 0)
            packed = jnp.where(row == 0, high, jnp.where(row == 1, mid, jnp.where(row == 2, low, 0.0)))
            rows3 = spread(packed, copy)
            msg_ref[at + STATE : at + STATE + TAIL, :] = jnp.concatenate(
                [rows3, jnp.zeros_like(rows3)], axis=0).astype(BF16)


def project(hidden, rim_f, rim_r, w_f, w_r, conv, bias, rate, copy, heads, inner):
    rows, depth = hidden.shape
    stream = inner + 2 * STATE
    n = rows // TILE
    per = TILE // CHUNK
    up, down = (lambda i: i), (lambda i: n - 1 - i)
    by_rows = lambda width, at: pl.BlockSpec((TILE, width), lambda i: (at(i), 0))
    out_specs, out_shape = [], []
    for at in (up, down):
        out_specs += [by_rows(stream, at), by_rows(inner, at), by_rows(128, at),
                      pl.BlockSpec((heads, TILE), lambda i, at=at: (0, at(i))),
                      pl.BlockSpec((per, STATE, inner), lambda i, at=at: (at(i), 0, 0)),
                      pl.BlockSpec((per, 8, inner), lambda i, at=at: (at(i), 0, 0))]
        out_shape += [jax.ShapeDtypeStruct((rows, stream), BF16), jax.ShapeDtypeStruct((rows, inner), BF16),
                      jax.ShapeDtypeStruct((rows, 128), F32), jax.ShapeDtypeStruct((heads, rows), F32),
                      jax.ShapeDtypeStruct((n * per, STATE, inner), BF16),
                      jax.ShapeDtypeStruct((n * per, 8, inner), F32)]
    message = (2 * (STATE + TAIL), inner)
    buf = pltpu.VMEM((stream // 128, TILE + 8, 128), F32)
    state, total = pltpu.VMEM((STATE, inner), F32), pltpu.VMEM((8, 128), F32)
    return pl.pallas_call(
        functools.partial(project_kernel, heads, inner),
        grid=(n,),
        in_specs=[by_rows(depth, up), by_rows(depth, down), whole(rim_f.shape), whole(rim_r.shape),
                  whole(w_f.shape), whole(w_r.shape), whole(conv.shape), whole((1, 128)), whole((1, 128)),
                  whole(copy.shape)],
        out_specs=out_specs + [whole(message)],
        out_shape=out_shape + [jax.ShapeDtypeStruct(message, BF16)],
        scratch_shapes=[buf, buf, state, state, total, total],
        compiler_params=params(),
        cost_estimate=cost(22e9, 40e6),
        name="project",
    )(hidden, hidden, rim_f, rim_r, w_f, w_r, conv, bias, rate, copy)


def inside_kernel(heads, inner, actf_ref, smallf_ref, cumtf_ref, actr_ref, smallr_ref, cumtr_ref, skip_ref, copy_ref,
                  basef_ref, baser_ref):
    width = inner // heads
    per = 128 // width
    copy = copy_ref[...]
    lane = lax.broadcasted_iota(jnp.int32, (CHUNK, 128), 1)
    group = lane // width
    sides = ((False, actf_ref, smallf_ref, cumtf_ref, basef_ref), (True, actr_ref, smallr_ref, cumtr_ref, baser_ref))
    for reverse, act_ref, small_ref, cumt_ref, base_ref in sides:
        small = small_ref[...]
        values = act_ref[:, :inner].astype(F32)
        weighted = (values * spread(jnp.where(lane < heads, small, 0.0), copy)).astype(BF16)
        scores = lax.dot_general(act_ref[:, inner + STATE :], act_ref[:, inner : inner + STATE],
                                 (((1,), (1,)), ((), ())), preferred_element_type=F32)
        scores = jnp.where(tri(CHUNK, reverse), scores, 0.0)
        for p in range(inner // 128):
            cols = slice(p * 128, (p + 1) * 128)
            pair = weighted[:, cols]
            mixing, stacked = [], []
            for q in range(per):
                h = p * per + q
                gap = jnp.minimum(small[:, heads + h : heads + h + 1] - cumt_ref[h : h + 1, :], 0.0)
                mixing.append((scores * jnp.exp(gap)).astype(BF16))
                stacked.append(jnp.where(group == q, pair, jnp.zeros_like(pair)))
            out = jnp.dot(jnp.concatenate(mixing, axis=1), jnp.concatenate(stacked, axis=0),
                          preferred_element_type=F32)
            base_ref[:, cols] = (out + skip_ref[:, cols] * values[:, cols]).astype(BF16)


def inside(strands, skip, copy, heads, inner):
    rows, columns = strands[0][0].shape
    by_rows = lambda width: pl.BlockSpec((CHUNK, width), lambda i: (i, 0))
    one = [by_rows(columns), by_rows(128), pl.BlockSpec((heads, CHUNK), lambda i: (0, i))]
    return pl.pallas_call(
        functools.partial(inside_kernel, heads, inner),
        grid=(rows // CHUNK,),
        in_specs=one + one + [whole((1, inner)), whole(copy.shape)],
        out_specs=[by_rows(inner)] * 2,
        out_shape=[jax.ShapeDtypeStruct((rows, inner), BF16)] * 2,
        compiler_params=params(),
        cost_estimate=cost(14e9, 16e6),
        name="inside",
    )(*strands[0], *strands[1], skip, copy)


def finish_kernel(heads, inner, *refs):
    (cf_ref, bf_ref, zf_ref, ef_ref, pf_ref, sf_ref, cr_ref, br_ref, zr_ref, er_ref, pr_ref, sr_ref,
     in_ref, copy_ref, out_ref) = refs
    width = inner // heads
    r = lax.broadcasted_iota(jnp.int32, (256, 256), 0) // width
    c = lax.broadcasted_iota(jnp.int32, (256, 256), 1) // width
    mean = jnp.where(r == c, 1.0 / width, 0.0).astype(BF16)
    copy = copy_ref[...]
    both = None
    for k, (c_ref, b_ref, z_ref, e_ref, p_ref, s_ref) in enumerate(
            ((cf_ref, bf_ref, zf_ref, ef_ref, pf_ref, sf_ref), (cr_ref, br_ref, zr_ref, er_ref, pr_ref, sr_ref))):
        entering = (e_ref[0].astype(F32) + p_ref[0, :1, :] * in_ref[k]).astype(BF16)
        reads = jnp.dot(c_ref[...], entering, preferred_element_type=F32)
        grown = spread(jnp.exp(jnp.minimum(s_ref[...], 0.0)), copy)
        out = b_ref[...].astype(F32) + reads * grown
        gated = out * silu(z_ref[...].astype(F32))
        squares = (gated * gated).astype(BF16)
        means = jnp.concatenate(
            [jnp.dot(squares[:, g : g + 256], mean, preferred_element_type=F32) for g in range(0, inner, 256)], axis=1)
        result = gated * lax.rsqrt(means + EPS)
        both = result if both is None else both + result
    out_ref[...] = both.astype(BF16)


def finish(chunks, strands, entering, copy, heads, inner):
    count, at = chunks
    last = strands[0][0].shape[1] // STATE - 1
    by_rows = lambda width: pl.BlockSpec((CHUNK, width), lambda i: (at(i), 0))
    one = [pl.BlockSpec((CHUNK, STATE), lambda i: (at(i), last)), by_rows(inner), by_rows(inner),
           pl.BlockSpec((1, STATE, inner), lambda i: (at(i), 0, 0)),
           pl.BlockSpec((1, 8, inner), lambda i: (at(i), 0, 0)), by_rows(128)]
    return pl.pallas_call(
        functools.partial(finish_kernel, heads, inner),
        grid=(count,),
        in_specs=one + one + [whole((2, STATE, inner)), whole(copy.shape)],
        out_specs=pl.BlockSpec((CHUNK, inner), lambda i: (i, 0)),
        out_shape=jax.ShapeDtypeStruct((count * CHUNK, inner), BF16),
        compiler_params=params(),
        cost_estimate=cost(8e9 * count / 16, 10e6),
        name="finish",
    )(*strands[0], *strands[1], entering, copy)


def hop_kernel(first, final, *refs):
    upper_ref, mine_ref, other_ref = refs[:3]
    into_ref = None if first else refs[3]
    outs = refs[3:] if first else refs[4:]
    upper = upper_ref[0].astype(F32)
    for k in (0, 1):
        later = upper if k == 0 else 1.0 - upper
        at = k * (STATE + TAIL)

        def read(ref):
            tail = ref[at + STATE : at + STATE + TAIL, :].astype(F32)
            return ref[at : at + STATE, :].astype(F32), tail[0:1] + tail[1:2] + tail[2:3]

        o_state, o_log = read(other_ref)
        if first:
            new_state, new_log = later * o_state, later * o_log
        else:
            into_log = into_ref[k, STATE : STATE + 1, :]
            new_state = into_ref[k, :STATE, :] + later * jnp.exp(into_log) * o_state
            new_log = into_log + later * o_log
        if final:
            outs[0][k] = new_state
            continue
        outs[0][k, :STATE, :] = new_state
        outs[0][k, STATE:, :] = jnp.broadcast_to(new_log, (8, new_log.shape[1]))
        state, log = read(mine_ref)
        of_other = later * jnp.exp(log) + (1.0 - later)
        of_mine = later + (1.0 - later) * jnp.exp(o_log)
        outs[1][at : at + STATE, :] = (of_other * o_state + of_mine * state).astype(BF16)
        t = log + o_log
        high = t.astype(BF16).astype(F32)
        mid = (t - high).astype(BF16).astype(F32)
        low = t - high - mid
        row = lax.broadcasted_iota(jnp.int32, (TAIL, t.shape[1]), 0)
        packed = jnp.where(row == 0, high, jnp.where(row == 1, mid, jnp.where(row == 2, low, 0.0)))
        outs[1][at + STATE : at + STATE + TAIL, :] = packed.astype(BF16)


def hop(upper, mine, other, into, final):
    inner = mine.shape[1]
    first = into is None
    smem = pl.BlockSpec(memory_space=pltpu.SMEM)
    if final:
        out_shape = [jax.ShapeDtypeStruct((2, STATE, inner), F32)]
    else:
        out_shape = [jax.ShapeDtypeStruct((2, STATE + 8, inner), F32), jax.ShapeDtypeStruct(mine.shape, BF16)]
    operands = [mine, other] + ([] if first else [into])
    return pl.pallas_call(
        functools.partial(hop_kernel, first, final),
        grid=(1,),
        in_specs=[smem] + [whole(x.shape) for x in operands],
        out_specs=[whole(x.shape) for x in out_shape],
        out_shape=out_shape,
        compiler_params=params(),
        cost_estimate=cost(1e6, 1.5e6),
        name="hop",
    )(upper, *operands)


def incoming(message, axis):
    count, index = lax.axis_size(axis), lax.axis_index(axis)
    into = None
    distance = 1
    while distance < count:
        other = lax.ppermute(message, axis, [(i, i ^ distance) for i in range(count)])
        upper = ((index // distance) % 2).astype(jnp.int32).reshape(1)
        final = 2 * distance >= count
        result = hop(upper, message, other, into, final)
        if final:
            return result[0]
        into, message = result
        distance *= 2


def shifted(block, axis, distance):
    devices = range(lax.axis_size(axis))
    return lax.ppermute(block, axis, [(i - distance, i) for i in devices if i - distance in devices])


def on_device(
    hidden, norm_gain, w_zx, w_bc, w_dt, dt_bias, decay_rate, skip_gain, conv_x, conv_bc, w_out
):
    rows, depth = hidden.shape
    inner = conv_x.shape[1]
    heads = dt_bias.shape[0]
    width = inner // heads
    n_ctx, n_head = lax.axis_size("ctx"), lax.axis_size("head")
    ctx, head = lax.axis_index("ctx"), lax.axis_index("head")

    rim_f = shifted(hidden[rows - RIM :], "ctx", 1)
    rim_r = shifted(hidden[:RIM], "ctx", -1)

    part = w_out.shape[0] // n_ctx
    own = lax.dynamic_slice_in_dim(w_out, ctx * part, part, 0)
    gathered = lax.all_gather(own, ("ctx", "head"), axis=0)
    gathered = gathered.reshape(n_ctx, n_head, part, depth)

    pad = lambda v: jnp.pad(v, [(0, 0)] * (v.ndim - 1) + [(0, 128 - heads)])
    w_f, w_r = prepare(w_zx, w_bc, pad(w_dt), norm_gain[:, None])
    conv = jnp.concatenate([conv_x, conv_bc], axis=1)
    skip = jnp.repeat(skip_gain, width)[None, :]
    copy_first = spread_matrix(0, heads, width)
    copy_second = spread_matrix(heads, heads, width)
    (act_f, z_f, small_f, cumt_f, enter_f, prior_f, act_r, z_r, small_r, cumt_r, enter_r, prior_r,
     message) = project(hidden, rim_f, rim_r, w_f, w_r, conv, pad(dt_bias)[None, :], pad(decay_rate)[None, :],
                        copy_first, heads, inner)
    entering = incoming(message, "ctx")
    base_f, base_r = inside(((act_f, small_f, cumt_f), (act_r, small_r, cumt_r)), skip, copy_first, heads, inner)

    share = rows // n_head
    per_share = share // CHUNK
    pieces = 2 if per_share % 2 == 0 else 1
    per_piece = per_share // pieces
    w_groups = gathered.transpose(1, 0, 2, 3).reshape(n_head, n_ctx * part, depth)
    own_rows = lax.dynamic_slice_in_dim(hidden, head * share, share, 0)
    outs = []
    for k in range(pieces):
        chunks = (n_head * per_piece, lambda i, k=k: (i // per_piece) * per_share + k * per_piece + i % per_piece)
        combined = finish(chunks, ((act_f, base_f, z_f, enter_f, prior_f, small_f),
                                   (act_r, base_r, z_r, enter_r, prior_r, small_r)),
                          entering, copy_second, heads, inner)
        size = per_piece * CHUNK
        total = own_rows[k * size : (k + 1) * size].astype(F32)
        for d in range(n_head):
            block = lax.dynamic_slice_in_dim(combined, ((head + d) % n_head) * size, size, 0)
            if d:
                block = lax.ppermute(block, "head", [(i, (i + d) % n_head) for i in range(n_head)])
            source = (head - d) % n_head
            weights = lax.dynamic_index_in_dim(w_groups, source, 0, keepdims=False)
            total = total + jnp.dot(block, weights, preferred_element_type=F32)
        outs.append(total.astype(BF16))
    return jnp.concatenate(outs, axis=0)


def solution(mesh):
    placed = (
        P("ctx", None),
        P(),
        P(None, None, "head"),
        P(),
        P(None, "head"),
        P("head"),
        P("head"),
        P("head"),
        P(None, "head"),
        P(),
        P("head", None),
    )
    return jax.shard_map(
        on_device, mesh=mesh, in_specs=placed, out_specs=P(("ctx", "head"), None), check_vma=False
    )
```

profile of v0, /device:TPU:0, one launch (start us, length us, event | category | flops | bytes accessed | tf_op | source)
XLA Modules:
  0.0 174.0 jit_solution(2635944155127764138)
XLA Ops:
  10.5 3.0 %collective-permute-start = (bf16[16,1024]{1,0:T(8,128)(2,1)S(1)}, bf16[16,1024]{1,0:T(8,128)(2,1)S(1)}, u32[]{:S(2)}, u32[]{:S(2)}) collective-permute-start(bf16[16,1024]{1,0:T(8,128)(2,1)S(1)} %get-tuple-element.48), channel_id=1, source_target_pairs={{0,4},{4,8},{8,12},{12,16},{16,20},{20,24},{24,28},{1,5},{5,9},{9,... | collective-permute-start | bytes 98312 | tf_op jit(solution)/shard_map/ppermute | solution.py:403
  14.5 1.7 copy.16.gain_ref
  20.5 5.8 %prepare.1 = (bf16[1024,1408]{1,0:T(8,128)(2,1)}, bf16[1024,1408]{1,0:T(8,128)(2,1)}) custom-call(bf16[1024,2,512]{2,1,0:T(2,128)(2,1)} %zx_ref.1, bf16[1024,256]{1,0:T(8,128)(2,1)} %bc_ref.1, bf16[1024,128]{1,0:T(8,128)(2,1)} %pad.11.dt_ref, f32[1024,1]{1,0:T(8,128)} %copy.16.gain_ref), custom_call_target="tpu_custom_call" | custom-call | flops 1000000000 | bytes 8000000 | tf_op jit(solution)/shard_map/prepare/pallas_call | solution.py:79
  26.9 36.1 %project.1 = (bf16[2048,768]{1,0:T(8,128)(2,1)}, bf16[2048,512]{1,0:T(8,128)(2,1)}, f32[2048,128]{1,0:T(8,128)}, f32[8,2048]{1,0:T(8,128)}, bf16[16,128,512]{2,1...) custom-call(bf16[2048,1024]{1,0:T(8,128)(2,1)} %refs_1_.1, ...), custom_call_target="tpu_custom_call" | custom-call | flops 22000001024 | bytes 40000000 | tf_op jit(solution)/shard_map/project/pallas_call | solution.py:224
  63.0 2.5 %collective-permute-start.2 = (bf16[288,512]{1,0:T(8,128)(2,1)}, bf16[288,512]{1,0:T(8,128)(2,1)S(1)}, u32[]{:S(2)}, u32[]{:S(2)}) collective-permute-start(bf16[288,512]{1,0:T(8,128)(2,1)} %get-tuple-element.42.refs_1_), channel_id=1, source_target_pairs={{0,4},{4,0},{8,12},{12,8},{16,20},{20,16},{24,28},{28,24},{1,5},{5... | collective-permute-start | bytes 884744 | tf_op jit(solution)/shard_map/ppermute | solution.py:391
  65.5 1.4 collective-permute-done.2.refs_2_
  67.7 2.1 %hop.3 = (f32[2,136,512]{2,1,0:T(8,128)}, bf16[288,512]{1,0:T(8,128)(2,1)}) custom-call(s32[1]{0:T(128)} %bitcast.5.refs_0_, bf16[288,512]{1,0:T(8,128)(2,1)} %get-tuple-element.42.refs_1_, bf16[288,512]{1,0:T(8,128)(2,1)} %copy-done.1), custom_call_target="tpu_custom_call" | custom-call | flops 1000000 | bytes 1500000 | tf_op jit(solution)/shard_map/hop/pallas_call | solution.py:374
  69.8 2.5 %collective-permute-start.3 = (bf16[288,512]{1,0:T(8,128)(2,1)}, bf16[288,512]{1,0:T(8,128)(2,1)S(1)}, u32[]{:S(2)}, u32[]{:S(2)}) collective-permute-start(bf16[288,512]{1,0:T(8,128)(2,1)} %get-tuple-element.43.refs_1_), channel_id=1, source_target_pairs={{0,8},{4,12},{8,0},{12,4},{16,24},{20,28},{24,16},{28,20},{1,9},{5... | collective-permute-start | bytes 884744 | tf_op jit(solution)/shard_map/ppermute | solution.py:391
  73.0 7.0 %collective-permute-done.3.refs_2_ = bf16[288,512]{1,0:T(8,128)(2,1)S(1)} collective-permute-done((bf16[288,512]{1,0:T(8,128)(2,1)}, bf16[288,512]{1,0:T(8,128)(2,1)S(1)}, u32[]{:S(2)}, u32[]{:S(2)}) %collective-permute-start.3) | collective-permute-done | bytes 294944 | tf_op jit(solution)/shard_map/ppermute | solution.py:391
  80.7 2.3 %hop.4 = (f32[2,136,512]{2,1,0:T(8,128)}, bf16[288,512]{1,0:T(8,128)(2,1)}) custom-call(s32[1]{0:T(128)} %bitcast.4.refs_0_, bf16[288,512]{1,0:T(8,128)(2,1)} %get-tuple-element.43.refs_1_, bf16[288,512]{1,0:T(8,128)(2,1)} %copy-done.2, f32[2,136,512]{2,1,0:T(8,128)} %get-tuple-element.44.refs_3_), custom_call_target="tpu_custom_call" | custom-call | flops 1000000 | bytes 1500000 | tf_op jit(solution)/shard_map/hop/pallas_call | solution.py:374
  83.8 16.0 %inside.1 = (bf16[2048,512]{1,0:T(8,128)(2,1)}, bf16[2048,512]{1,0:T(8,128)(2,1)}) custom-call(bf16[2048,768]{1,0:T(8,128)(2,1)} %get-tuple-element.28.actf_ref.refs_0_, f32[2048,128]{1,0:T(8,128)} %get-tuple-element.29.smallf_ref.refs_5_, f32[8,2048]{1,0:T(8,128)} %get-tuple-element.30.cumtf_ref, bf16[2048,768]{1,0:T(8,128)(2,1)} %get-tuple-element.31.actr_ref.refs_6_, ...), custom_call_target="tpu_custom_call" | custom-call | flops 14000000000 | bytes 16000000 | tf_op jit(solution)/shard_map/inside/pallas_call | solution.py:272
  100.6 2.1 %hop.5.refs_12_ = f32[2,128,512]{2,1,0:T(8,128)} custom-call(s32[1]{0:T(128)} %bitcast.3.refs_0_, bf16[288,512]{1,0:T(8,128)(2,1)} %get-tuple-element.45.refs_1_, bf16[288,512]{1,0:T(8,128)(2,1)} %copy-done.3, f32[2,136,512]{2,1,0:T(8,128)} %get-tuple-element.46.refs_3_), custom_call_target="tpu_custom_call" | custom-call | flops 1000000 | bytes 1500000 | tf_op jit(solution)/shard_map/hop/pallas_call | solution.py:374
  102.7 9.7 %finish.2 = bf16[1024,512]{1,0:T(8,128)(2,1)} custom-call(bf16[2048,768]{1,0:T(8,128)(2,1)} %get-tuple-element.28.actf_ref.refs_0_, bf16[2048,512]{1,0:T(8,128)(2,1)} %get-tuple-element.34.refs_1_, bf16[2048,512]{1,0:T(8,128)(2,1)} %get-tuple-element.35.refs_2_, bf16[16,128,512]{2,1,0:T(8,128)(2,1)} %get-tuple-element.36.refs_3_, ...), custom_call_target="tpu_custom_call" | custom-call | flops 4000000000 | bytes 10000000 | tf_op jit(solution)/shard_map/finish/pallas_call | solution.py:315
  113.5 2.7 %collective-permute-start.6 = (bf16[256,512]{1,0:T(8,128)(2,1)S(1)}, bf16[256,512]{1,0:T(8,128)(2,1)S(1)}, u32[]{:S(2)}, u32[]{:S(2)}) collective-permute-start(bf16[256,512]{1,0:T(8,128)(2,1)S(1)} %get-tuple-element.51), channel_id=1, source_target_pairs={{0,2},{1,3},{2,0},{3,1},{4,6},{5,7},{6,4},{7,5},{8,10},{9,11},{10,... | collective-permute-start | bytes 786440 | tf_op jit(solution)/shard_map/ppermute | solution.py:453
  116.2 9.5 %finish.3 = bf16[1024,512]{1,0:T(8,128)(2,1)} custom-call(bf16[2048,768]{1,0:T(8,128)(2,1)} %get-tuple-element.28.actf_ref.refs_0_, bf16[2048,512]{1,0:T(8,128)(2,1)} %get-tuple-element.34.refs_1_, bf16[2048,512]{1,0:T(8,128)(2,1)} %get-tuple-element.35.refs_2_, bf16[16,128,512]{2,1,0:T(8,128)(2,1)} %get-tuple-element.36.refs_3_, ...), custom_call_target="tpu_custom_call" | custom-call | flops 4000000000 | bytes 10000000 | tf_op jit(solution)/shard_map/finish/pallas_call | solution.py:315
  125.7 1.6 collective-permute-start.5
  127.3 2.3 %collective-permute-start.7 = (bf16[256,512]{1,0:T(8,128)(2,1)S(1)}, bf16[256,512]{1,0:T(8,128)(2,1)}, u32[]{:S(2)}, u32[]{:S(2)}) collective-permute-start(bf16[256,512]{1,0:T(8,128)(2,1)S(1)} %get-tuple-element.50), channel_id=1, source_target_pairs={{0,3},{1,0},{2,1},{3,2},{4,7},{5,4},{6,5},{7,6},{8,11},{9,8},{10,9... | collective-permute-start | bytes 786440 | tf_op jit(solution)/shard_map/ppermute | solution.py:453
  130.8 3.8 %collective-permute-start.10 = (bf16[256,512]{1,0:T(8,128)(2,1)S(1)}, bf16[256,512]{1,0:T(8,128)(2,1)}, u32[]{:S(2)}, u32[]{:S(2)}) collective-permute-start(bf16[256,512]{1,0:T(8,128)(2,1)S(1)} %get-tuple-element.53), channel_id=1, source_target_pairs={{0,3},{1,0},{2,1},{3,2},{4,7},{5,4},{6,5},{7,6},{8,11},{9,8},{10,9... | collective-permute-start | bytes 786440 | tf_op jit(solution)/shard_map/ppermute | solution.py:453
  134.6 2.6 %copy.17 = bf16[4,8,64,1024]{3,2,1,0:T(8,128)(2,1)S(1)} copy(bf16[4,8,64,1024]{3,2,0,1:T(8,128)(2,1)} %bitcast.46) | data formatting | bytes 8388608 | tf_op jit(solution)/shard_map/transpose | solution.py:440
  137.8 6.6 %collective-permute-done.7 = bf16[256,512]{1,0:T(8,128)(2,1)} collective-permute-done((bf16[256,512]{1,0:T(8,128)(2,1)S(1)}, bf16[256,512]{1,0:T(8,128)(2,1)}, u32[]{:S(2)}, u32[]{:S(2)}) %collective-permute-start.7) | collective-permute-done | bytes 262176 | tf_op jit(solution)/shard_map/ppermute | solution.py:453
  146.3 1.6 fusion.6
  147.9 14.2 %collective-permute-done.9 = bf16[256,512]{1,0:T(8,128)(2,1)S(1)} collective-permute-done((bf16[256,512]{1,0:T(8,128)(2,1)S(1)}, bf16[256,512]{1,0:T(8,128)(2,1)S(1)}, u32[]{:S(2)}, u32[]{:S(2)}) %collective-permute-start.9) | collective-permute-done | bytes 262176 | tf_op jit(solution)/shard_map/ppermute | solution.py:453
  162.6 1.4 fusion.8
  164.4 1.6 fusion.7
  (49 shorter events, 20.1 us)
Async XLA Ops:
  6.5 1.2 copy-start
  6.5 128.1 %all-gather.3.cloned.1.call-start = ((), (), s32[]{:S(2)}) async-start(), calls=%async_computation | async-start | bytes 4325376 | tf_op jit(solution)/shard_map/all_gather | solution.py:421
  9.2 17.1 %collective-permute-start.1 = (bf16[16,1024]{1,0:T(8,128)(2,1)S(1)}, bf16[16,1024]{1,0:T(8,128)(2,1)S(1)}, u32[]{:S(2)}, u32[]{:S(2)}) collective-permute-start(bf16[16,1024]{1,0:T(8,128)(2,1)S(1)} %get-tuple-element.47), channel_id=1, source_target_pairs={{4,0},{8,4},{12,8},{16,12},{20,16},{24,20},{28,24},{5,1},{9,5},{13... | collective-permute-start | bytes 98312 | tf_op jit(solution)/shard_map/ppermute | solution.py:403
  10.5 15.8 %collective-permute-start = (bf16[16,1024]{1,0:T(8,128)(2,1)S(1)}, bf16[16,1024]{1,0:T(8,128)(2,1)S(1)}, u32[]{:S(2)}, u32[]{:S(2)}) collective-permute-start(bf16[16,1024]{1,0:T(8,128)(2,1)S(1)} %get-tuple-element.48), channel_id=1, source_target_pairs={{0,4},{4,8},{8,12},{12,16},{16,20},{20,24},{24,28},{1,5},{5,9},{9,... | collective-permute-start | bytes 98312 | tf_op jit(solution)/shard_map/ppermute | solution.py:403
  26.3 0.6 copy-start.5
  26.3 0.6 copy-start.6
  26.9 45.3 %copy-start.4 = (f32[8]{0:T(128)S(1)}, f32[8]{0:T(128)}, u32[]{:S(2)}) copy-start(f32[8]{0:T(128)} %param.18) | copy-start | bytes 100
  63.0 4.0 %collective-permute-start.2 = (bf16[288,512]{1,0:T(8,128)(2,1)}, bf16[288,512]{1,0:T(8,128)(2,1)S(1)}, u32[]{:S(2)}, u32[]{:S(2)}) collective-permute-start(bf16[288,512]{1,0:T(8,128)(2,1)} %get-tuple-element.42.refs_1_), channel_id=1, source_target_pairs={{0,4},{4,0},{8,12},{12,8},{16,20},{20,16},{24,28},{28,24},{1,5},{5... | collective-permute-start | bytes 884744 | tf_op jit(solution)/shard_map/ppermute | solution.py:391
  67.0 0.7 copy-start.1
  69.8 10.2 %collective-permute-start.3 = (bf16[288,512]{1,0:T(8,128)(2,1)}, bf16[288,512]{1,0:T(8,128)(2,1)S(1)}, u32[]{:S(2)}, u32[]{:S(2)}) collective-permute-start(bf16[288,512]{1,0:T(8,128)(2,1)} %get-tuple-element.43.refs_1_), channel_id=1, source_target_pairs={{0,8},{4,12},{8,0},{12,4},{16,24},{20,28},{24,16},{28,20},{1,9},{5... | collective-permute-start | bytes 884744 | tf_op jit(solution)/shard_map/ppermute | solution.py:391
  80.0 0.7 copy-start.2
  83.0 16.8 %collective-permute-start.4 = (bf16[288,512]{1,0:T(8,128)(2,1)}, bf16[288,512]{1,0:T(8,128)(2,1)S(1)}, u32[]{:S(2)}, u32[]{:S(2)}) collective-permute-start(bf16[288,512]{1,0:T(8,128)(2,1)} %get-tuple-element.45.refs_1_), channel_id=1, source_target_pairs={{0,16},{4,20},{8,24},{12,28},{16,0},{20,4},{24,8},{28,12},{1,17},{... | collective-permute-start | bytes 884744 | tf_op jit(solution)/shard_map/ppermute | solution.py:391
  99.8 0.7 copy-start.3
  113.5 23.8 %collective-permute-start.6 = (bf16[256,512]{1,0:T(8,128)(2,1)S(1)}, bf16[256,512]{1,0:T(8,128)(2,1)S(1)}, u32[]{:S(2)}, u32[]{:S(2)}) collective-permute-start(bf16[256,512]{1,0:T(8,128)(2,1)S(1)} %get-tuple-element.51), channel_id=1, source_target_pairs={{0,2},{1,3},{2,0},{3,1},{4,6},{5,7},{6,4},{7,5},{8,10},{9,11},{10,... | collective-permute-start | bytes 786440 | tf_op jit(solution)/shard_map/ppermute | solution.py:453
  125.7 20.1 %collective-permute-start.5 = (bf16[256,512]{1,0:T(8,128)(2,1)S(1)}, bf16[256,512]{1,0:T(8,128)(2,1)S(1)}, u32[]{:S(2)}, u32[]{:S(2)}) collective-permute-start(bf16[256,512]{1,0:T(8,128)(2,1)S(1)} %get-tuple-element.49), channel_id=1, source_target_pairs={{0,1},{1,2},{2,3},{3,0},{4,5},{5,6},{6,7},{7,4},{8,9},{9,10},{10,1... | collective-permute-start | bytes 786440 | tf_op jit(solution)/shard_map/ppermute | solution.py:453
  127.3 17.1 %collective-permute-start.7 = (bf16[256,512]{1,0:T(8,128)(2,1)S(1)}, bf16[256,512]{1,0:T(8,128)(2,1)}, u32[]{:S(2)}, u32[]{:S(2)}) collective-permute-start(bf16[256,512]{1,0:T(8,128)(2,1)S(1)} %get-tuple-element.50), channel_id=1, source_target_pairs={{0,3},{1,0},{2,1},{3,2},{4,7},{5,4},{6,5},{7,6},{8,11},{9,8},{10,9... | collective-permute-start | bytes 786440 | tf_op jit(solution)/shard_map/ppermute | solution.py:453
  130.8 33.2 %collective-permute-start.8 = (bf16[256,512]{1,0:T(8,128)(2,1)S(1)}, bf16[256,512]{1,0:T(8,128)(2,1)S(1)}, u32[]{:S(2)}, u32[]{:S(2)}) collective-permute-start(bf16[256,512]{1,0:T(8,128)(2,1)S(1)} %get-tuple-element.52), channel_id=1, source_target_pairs={{0,1},{1,2},{2,3},{3,0},{4,5},{5,6},{6,7},{7,4},{8,9},{9,10},{10,1... | collective-permute-start | bytes 786440 | tf_op jit(solution)/shard_map/ppermute | solution.py:453
  130.8 31.7 %collective-permute-start.10 = (bf16[256,512]{1,0:T(8,128)(2,1)S(1)}, bf16[256,512]{1,0:T(8,128)(2,1)}, u32[]{:S(2)}, u32[]{:S(2)}) collective-permute-start(bf16[256,512]{1,0:T(8,128)(2,1)S(1)} %get-tuple-element.53), channel_id=1, source_target_pairs={{0,3},{1,0},{2,1},{3,2},{4,7},{5,4},{6,5},{7,6},{8,11},{9,8},{10,9... | collective-permute-start | bytes 786440 | tf_op jit(solution)/shard_map/ppermute | solution.py:453
  137.3 24.8 %collective-permute-start.9 = (bf16[256,512]{1,0:T(8,128)(2,1)S(1)}, bf16[256,512]{1,0:T(8,128)(2,1)S(1)}, u32[]{:S(2)}, u32[]{:S(2)}) collective-permute-start(bf16[256,512]{1,0:T(8,128)(2,1)S(1)} %get-tuple-element.54), channel_id=1, source_target_pairs={{0,2},{1,3},{2,0},{3,1},{4,6},{5,7},{6,4},{7,5},{8,10},{9,11},{10,... | collective-permute-start | bytes 786440 | tf_op jit(solution)/shard_map/ppermute | solution.py:453
Sparse Core Ops, SparseCore 0:
  10.4 64.8 all-gather.2
where the time goes:
time: 175 us; the launch traced here: 174 us
  Pallas kernels  83.6 us (48%)
  waiting for transfers between devices  29.2 us (17%)
  starting transfers between devices  20.6 us (12%)
  local copies, waits for them, and re-layouts  15.7 us (9%)
  between operations  13.6 us (8%)
  matrix products  7.82 us (4%)
  other arithmetic  3.38 us (2%)
    pallas_call x1, Pallas kernels, project(): pl.pallas_call(functools.partial(project_kernel, heads, inner), grid=(n,)...  36.1 us
    ppermute x6, waiting for transfers between devices, on_device(): lax.ppermute(block, 'head', [(i, (i + d) % n_head) for i in range(n_head)])  20.8 us
    pallas_call x2, Pallas kernels, finish(): pl.pallas_call(functools.partial(finish_kernel, heads, inner), grid=(coun...  19.2 us
    pallas_call x1, Pallas kernels, inside(): pl.pallas_call(functools.partial(inside_kernel, heads, inner), grid=(rows...  16 us
    ppermute x6, starting transfers between devices, on_device(): lax.ppermute(block, 'head', [(i, (i + d) % n_head) for i in range(n_head)])  10.5 us
    ppermute x3, waiting for transfers between devices, incoming(): lax.ppermute(message, axis, [(i, i ^ distance) for i in range(count)])  8.41 us
    dot_general x8, matrix products, on_device(): total = total + jnp.dot(block, weights, preferred_element_type=F32)  7.82 us
    pallas_call x3, Pallas kernels, hop(): pl.pallas_call(functools.partial(hop_kernel, first, final), grid=(1,), in...  6.47 us
  transfers between devices with their start and end apart: 12, of which 4 were waited for; matrix products, arithmetic and copies ran while one was open for 11% of the time, Pallas kernels for 48%

commit v1 on v0

v1 whole, which is shorter than its diff:
```python
import functools

import jax
import jax.numpy as jnp
import numpy as np
from jax import lax
from jax.experimental import pallas as pl
from jax.experimental.pallas import tpu as pltpu
from jax.sharding import PartitionSpec as P

STATE = 128
CHUNK = 128
TILE = 256
EPS = 1e-05
RIM = 16
TAIL = 16
F32 = jnp.float32
BF16 = jnp.bfloat16
MIB = 2**20


def params(limit):
    return pltpu.CompilerParams(
        dimension_semantics=("arbitrary",), vmem_limit_bytes=limit * MIB
    )


def cost(flops, bytes_accessed):
    return pl.CostEstimate(flops=int(flops), bytes_accessed=int(bytes_accessed), transcendentals=0)


def whole(shape):
    return pl.BlockSpec(shape, lambda *_: (0,) * len(shape), pipeline_mode=pl.Buffered(1))


def silu(x):
    half = 0.5 * x
    return half + half * jnp.tanh(half)


def tri(rows, reverse):
    r = lax.broadcasted_iota(jnp.int32, (rows, rows), 0)
    c = lax.broadcasted_iota(jnp.int32, (rows, rows), 1)
    return (r <= c) if reverse else (r >= c)


def spread_matrix(first, heads, width):
    r = np.arange(2 * 128)[:, None] % 128
    c = np.arange(heads * width)[None, :] // width
    return jnp.asarray((r == c + first).astype(BF16))


def spread(q, matrix):
    high = q.astype(BF16)
    low = (q - high.astype(F32)).astype(BF16)
    return jnp.dot(jnp.concatenate([high, low], axis=1), matrix, preferred_element_type=F32)


def prepare_kernel(inner, zx_ref, bc_ref, dt_ref, gain_ref, wf_ref, wr_ref, gf_ref, gr_ref):
    rows = zx_ref.shape[0]
    gain = jnp.transpose(jnp.broadcast_to(gain_ref[...], (128, rows)))
    zx = zx_ref[...].astype(F32).reshape(rows, 2 * inner)
    steps = dt_ref[...].astype(F32)
    steps = jnp.transpose(jnp.concatenate([steps, jnp.zeros((128 - steps.shape[0], rows), F32)], axis=0))
    r = lax.broadcasted_iota(jnp.int32, (rows, rows), 0)
    c = lax.broadcasted_iota(jnp.int32, (rows, rows), 1)
    turn = (r + c == rows - 1).astype(BF16)

    def put(part, at, forward_ref, turned_ref):
        size = part.shape[1]
        scaled = jnp.concatenate([part[:, g : g + 128] * gain for g in range(0, size, 128)], axis=1).astype(BF16)
        forward_ref[:, at : at + size] = scaled
        turned_ref[:, at : at + size] = jnp.dot(turn, scaled, preferred_element_type=F32).astype(BF16)

    put(zx[:, inner:], 0, wf_ref, wr_ref)
    put(bc_ref[...].astype(F32), inner, wf_ref, wr_ref)
    put(steps, inner + bc_ref.shape[1], wf_ref, wr_ref)
    put(zx[:, :inner], 0, gf_ref, gr_ref)


def prepare(w_zx, w_bc, w_dt, gain):
    depth, _, inner = w_zx.shape
    tile = min(256, depth)
    n = depth // tile
    wide = inner + w_bc.shape[1] + 128
    forward, turned = (lambda i: (i, 0)), (lambda i: (n - 1 - i, 0))
    return pl.pallas_call(
        functools.partial(prepare_kernel, inner),
        grid=(n,),
        in_specs=[pl.BlockSpec((tile, 2, inner), lambda i: (i, 0, 0)),
                  pl.BlockSpec((tile, w_bc.shape[1]), forward),
                  pl.BlockSpec((w_dt.shape[1], tile), lambda i: (0, i)),
                  pl.BlockSpec((1, tile), lambda i: (0, i))],
        out_specs=[pl.BlockSpec((tile, wide), forward), pl.BlockSpec((tile, wide), turned),
                   pl.BlockSpec((tile, inner), forward), pl.BlockSpec((tile, inner), turned)],
        out_shape=[jax.ShapeDtypeStruct((depth, wide), BF16)] * 2 + [jax.ShapeDtypeStruct((depth, inner), BF16)] * 2,
        compiler_params=params(58),
        cost_estimate=cost(4e9, 8e6),
        name="prepare",
    )(w_zx, w_bc, w_dt.T, gain[None, :])


def row_scale(h):
    hf = h.astype(F32)
    return lax.rsqrt(jnp.mean(hf * hf, axis=-1, keepdims=True) + EPS)


def project_kernel(heads, inner, *refs):
    (hf_ref, hr_ref, rimf_ref, rimr_ref, wf_ref, wr_ref, convx_ref, convbc_ref, lanes_ref, copy_ref,
     actf_ref, smallf_ref, cumtf_ref, enterf_ref, priorf_ref,
     actr_ref, smallr_ref, cumtr_ref, enterr_ref, priorr_ref,
     msg_ref, buff, bufr, statef, stater, totalf, totalr) = refs
    step = pl.program_id(0)
    last = pl.num_programs(0) - 1
    stream = inner + 2 * STATE
    blocks = stream // 128
    rows = hf_ref.shape[0]
    count = rows // CHUNK
    sides = (
        (False, hf_ref, rimf_ref, wf_ref, actf_ref, smallf_ref, cumtf_ref, enterf_ref, priorf_ref, buff, statef, totalf),
        (True, hr_ref, rimr_ref, wr_ref, actr_ref, smallr_ref, cumtr_ref, enterr_ref, priorr_ref, bufr, stater, totalr),
    )

    @pl.when(step == 0)
    def _():
        for reverse, _, rim_ref, w_ref, _, _, _, _, _, buf, state, total in sides:
            edge = rows if reverse else 0
            state[...] = jnp.zeros_like(state)
            total[...] = jnp.zeros_like(total)
            rim = rim_ref[...]
            out = jnp.dot(rim, w_ref[:, :stream], preferred_element_type=F32) * row_scale(rim)
            for j in range(blocks):
                part = out[:, j * 128 : (j + 1) * 128]
                buf[j, edge : edge + 8, :] = part[:8] if reverse else part[RIM - 8 :]

    lane = lax.broadcasted_iota(jnp.int32, (rows, 128), 1)
    row8 = lax.broadcasted_iota(jnp.int32, (8, 128), 0)
    r = lax.broadcasted_iota(jnp.int32, (rows, rows), 0)
    c = lax.broadcasted_iota(jnp.int32, (rows, rows), 1)
    same = r // CHUNK == c // CHUNK
    hs = [side[1][...] for side in sides]
    scales = [row_scale(h) for h in hs]
    tail_rows, aux_rows = [], []
    for k, (reverse, _, _, w_ref, _, small_ref, cumt_ref, _, _, _, _, total_ref) in enumerate(sides):
        raw = jnp.dot(hs[k], w_ref[:, stream:], preferred_element_type=F32) * scales[k] + lanes_ref[0:1, :]
        dt = jnp.maximum(raw, 0.0) + jnp.log1p(jnp.exp(-jnp.abs(raw)))
        dt = jnp.where(lane < heads, dt, 0.0)
        steps = -lanes_ref[1:2, :] * dt
        high = steps.astype(BF16).astype(F32)
        mid = (steps - high).astype(BF16).astype(F32)
        low = steps - high - mid
        packed = (high + pltpu.roll(mid, heads, 1) + pltpu.roll(low, 2 * heads, 1)).astype(BF16)
        mask = jnp.where(jnp.logical_and(same, (r <= c) if reverse else (r >= c)), 1.0, 0.0).astype(BF16)
        sums = jnp.dot(mask, packed, preferred_element_type=F32)
        sums = sums + pltpu.roll(sums, 128 - heads, 1) + pltpu.roll(sums, 128 - 2 * heads, 1)
        cum = jnp.where(lane < heads, sums, 0.0)
        small_ref[...] = dt + pltpu.roll(cum, heads, 1)
        running = total_ref[...]
        tails = [None] * count
        aux = [None] * count
        for i in range(count):
            n = count - 1 - i if reverse else i
            at = slice(n * CHUNK, (n + 1) * CHUNK)
            cumt_ref[:, at] = jnp.transpose(cum[at])[:heads]
            end = cum[n * CHUNK : n * CHUNK + 1] if reverse else cum[(n + 1) * CHUNK - 1 : (n + 1) * CHUNK]
            tails[n] = dt[at] * jnp.exp(end - cum[at])
            aux[n] = jnp.where(row8 == 0, jnp.exp(end), jnp.exp(running))
            running = running + end
        total_ref[...] = running
        tail_rows += tails
        aux_rows += aux
    weights = spread(jnp.concatenate(tail_rows + aux_rows, axis=0), copy_ref[...])

    for g in range(0, stream, 256):
        for k, (reverse, _, _, w_ref, act_ref, _, _, _, _, buf, _, _) in enumerate(sides):
            edge = rows if reverse else 0
            body = 0 if reverse else 8
            out = jnp.dot(hs[k], w_ref[:, g : g + 256], preferred_element_type=F32) * scales[k]
            for j in range(g // 128, g // 128 + 2):
                x = out[:, j * 128 - g : (j + 1) * 128 - g]
                buf[j, body : body + rows, :] = x
                own = j * 128 - (0 if j * 128 < inner else inner)
                taps = (convx_ref if j * 128 < inner else convbc_ref)[:, own : own + 128]
                total = taps[3:4] * x
                for d in (1, 2, 3):
                    at = body + d if reverse else body - d
                    total = total + taps[3 - d : 4 - d] * buf[j, at : at + rows, :]
                act_ref[:, j * 128 : (j + 1) * 128] = silu(total).astype(BF16)
                buf[j, edge : edge + 8, :] = x[:8] if reverse else x[rows - 8 :]

    for i in range(count):
        for k, (reverse, _, _, _, act_ref, _, _, enter_ref, prior_ref, _, state, _) in enumerate(sides):
            n = count - 1 - i if reverse else i
            at = slice(n * CHUNK, (n + 1) * CHUNK)
            own = weights[(k * count + n) * CHUNK : (k * count + n + 1) * CHUNK]
            aux = weights[2 * rows + (k * count + n) * 8 : 2 * rows + (k * count + n + 1) * 8]
            tails = (act_ref[at, :inner].astype(F32) * own).astype(BF16)
            ends = lax.dot_general(act_ref[at, inner : inner + STATE], tails, (((0,), (0,)), ((), ())),
                                   preferred_element_type=F32)
            before = state[...]
            enter_ref[n] = before.astype(BF16)
            prior_ref[n] = aux
            state[...] = before * aux[:1] + ends

    @pl.when(step == last)
    def _():
        for k, side in enumerate(sides):
            state, total = side[-2:]
            at = k * (STATE + TAIL)
            msg_ref[at : at + STATE, :] = state[...].astype(BF16)
            t = total[...]
            high = t.astype(BF16).astype(F32)
            mid = (t - high).astype(BF16).astype(F32)
            low = t - high - mid
            packed = jnp.where(row8 == 0, high, jnp.where(row8 == 1, mid, jnp.where(row8 == 2, low, 0.0)))
            rows3 = spread(packed, copy_ref[...])
            msg_ref[at + STATE : at + STATE + TAIL, :] = jnp.concatenate(
                [rows3, jnp.zeros_like(rows3)], axis=0).astype(BF16)


def project(hidden, rim_f, rim_r, w_f, w_r, conv_x, conv_bc, lanes, copy, heads, inner):
    rows, depth = hidden.shape
    stream = inner + 2 * STATE
    n = rows // TILE
    per = TILE // CHUNK
    up, down = (lambda i: i), (lambda i: n - 1 - i)
    by_rows = lambda width, at: pl.BlockSpec((TILE, width), lambda i: (at(i), 0))
    out_specs, out_shape = [], []
    for at in (up, down):
        out_specs += [by_rows(stream, at), by_rows(128, at),
                      pl.BlockSpec((heads, TILE), lambda i, at=at: (0, at(i))),
                      pl.BlockSpec((per, STATE, inner), lambda i, at=at: (at(i), 0, 0)),
                      pl.BlockSpec((per, 8, inner), lambda i, at=at: (at(i), 0, 0))]
        out_shape += [jax.ShapeDtypeStruct((rows, stream), BF16),
                      jax.ShapeDtypeStruct((rows, 128), F32), jax.ShapeDtypeStruct((heads, rows), F32),
                      jax.ShapeDtypeStruct((n * per, STATE, inner), BF16),
                      jax.ShapeDtypeStruct((n * per, 8, inner), F32)]
    message = (2 * (STATE + TAIL), inner)
    buf = pltpu.VMEM((stream // 128, TILE + 8, 128), F32)
    state, total = pltpu.VMEM((STATE, inner), F32), pltpu.VMEM((8, 128), F32)
    return pl.pallas_call(
        functools.partial(project_kernel, heads, inner),
        grid=(n,),
        in_specs=[by_rows(depth, up), by_rows(depth, down), whole(rim_f.shape), whole(rim_r.shape),
                  whole(w_f.shape), whole(w_r.shape), whole(conv_x.shape), whole(conv_bc.shape), whole(lanes.shape),
                  whole(copy.shape)],
        out_specs=out_specs + [whole(message)],
        out_shape=out_shape + [jax.ShapeDtypeStruct(message, BF16)],
        scratch_shapes=[buf, buf, state, state, total, total],
        compiler_params=params(58),
        cost_estimate=cost(22e9, 40e6),
        name="project",
    )(hidden, hidden, rim_f, rim_r, w_f, w_r, conv_x, conv_bc, lanes, copy)


def gates_kernel(h_ref, wf_ref, wr_ref, zf_ref, zr_ref):
    h = h_ref[...]
    scale = row_scale(h)
    for w_ref, z_ref in ((wf_ref, zf_ref), (wr_ref, zr_ref)):
        z_ref[...] = (jnp.dot(h, w_ref[...], preferred_element_type=F32) * scale).astype(BF16)


def gates(hidden, w_f, w_r):
    rows, depth = hidden.shape
    inner = w_f.shape[1]
    by_rows = lambda width: pl.BlockSpec((TILE, width), lambda i: (i, 0))
    return pl.pallas_call(
        gates_kernel,
        grid=(rows // TILE,),
        in_specs=[by_rows(depth), whole(w_f.shape), whole(w_r.shape)],
        out_specs=[by_rows(inner)] * 2,
        out_shape=[jax.ShapeDtypeStruct((rows, inner), BF16)] * 2,
        compiler_params=params(58),
        cost_estimate=cost(10e9, 10e6),
        name="gates",
    )(hidden, w_f, w_r)


def inside_kernel(heads, inner, actf_ref, smallf_ref, cumtf_ref, actr_ref, smallr_ref, cumtr_ref, lanes_ref, copy_ref,
                  basef_ref, baser_ref):
    width = inner // heads
    per = 128 // width
    size = actf_ref.shape[0]
    lane = lax.broadcasted_iota(jnp.int32, (size, 128), 1)
    group = lax.broadcasted_iota(jnp.int32, (CHUNK, 128), 1) // width
    dts = [jnp.where(lane < heads, ref[...], 0.0) for ref in (smallf_ref, smallr_ref)]
    wide = spread(jnp.concatenate(dts + [jnp.broadcast_to(lanes_ref[2:3, :], (8, 128))], axis=0), copy_ref[...])
    skip = wide[2 * size : 2 * size + 1]
    sides = ((False, actf_ref, smallf_ref, cumtf_ref, basef_ref), (True, actr_ref, smallr_ref, cumtr_ref, baser_ref))
    for c in range(0, size, CHUNK):
        rows = slice(c, c + CHUNK)
        for k, (reverse, act_ref, small_ref, cumt_ref, base_ref) in enumerate(sides):
            small = small_ref[rows, :]
            values = act_ref[rows, :inner].astype(F32)
            weighted = (values * wide[k * size + c : k * size + c + CHUNK]).astype(BF16)
            scores = lax.dot_general(act_ref[rows, inner + STATE :], act_ref[rows, inner : inner + STATE],
                                     (((1,), (1,)), ((), ())), preferred_element_type=F32)
            scores = jnp.where(tri(CHUNK, reverse), scores, 0.0)
            for p in range(inner // 128):
                cols = slice(p * 128, (p + 1) * 128)
                pair = weighted[:, cols]
                mixing, stacked = [], []
                for q in range(per):
                    h = p * per + q
                    gap = jnp.minimum(small[:, heads + h : heads + h + 1] - cumt_ref[h : h + 1, rows], 0.0)
                    mixing.append((scores * jnp.exp(gap)).astype(BF16))
                    stacked.append(jnp.where(group == q, pair, jnp.zeros_like(pair)))
                out = jnp.dot(jnp.concatenate(mixing, axis=1), jnp.concatenate(stacked, axis=0),
                              preferred_element_type=F32)
                base_ref[rows, cols] = (out + skip[:, cols] * values[:, cols]).astype(BF16)


def inside(tile, blocks, strands, lanes, copy, heads, inner, work):
    count, at = blocks
    columns = strands[0][0].shape[1]
    by_rows = lambda width: pl.BlockSpec((tile, width), lambda i: (at(i), 0))
    one = [by_rows(columns), by_rows(128), pl.BlockSpec((heads, tile), lambda i: (0, at(i)))]
    return pl.pallas_call(
        functools.partial(inside_kernel, heads, inner),
        grid=(count,),
        in_specs=one + one + [whole(lanes.shape), whole(copy.shape)],
        out_specs=[pl.BlockSpec((tile, inner), lambda i: (i, 0))] * 2,
        out_shape=[jax.ShapeDtypeStruct((count * tile, inner), BF16)] * 2,
        compiler_params=params(58),
        cost_estimate=cost(work, 1e6),
        name="inside",
    )(*strands[0], *strands[1], lanes, copy)


def finish_kernel(heads, inner, *refs):
    (cf_ref, zf_ref, ef_ref, pf_ref, sf_ref, cr_ref, zr_ref, er_ref, pr_ref, sr_ref, bf_ref, br_ref,
     in_ref, copy_ref, out_ref) = refs
    width = inner // heads
    size = cf_ref.shape[0]
    row = lax.broadcasted_iota(jnp.int32, (256, 256), 0) // width
    column = lax.broadcasted_iota(jnp.int32, (256, 256), 1) // width
    mean = jnp.where(row == column, 1.0 / width, 0.0).astype(BF16)
    grown = spread(jnp.exp(jnp.minimum(jnp.concatenate([sf_ref[...], sr_ref[...]], axis=0), 0.0)), copy_ref[...])
    both = None
    for k, (c_ref, b_ref, z_ref, e_ref, p_ref) in enumerate(
            ((cf_ref, bf_ref, zf_ref, ef_ref, pf_ref), (cr_ref, br_ref, zr_ref, er_ref, pr_ref))):
        parts = []
        for c in range(e_ref.shape[0]):
            entering = (e_ref[c].astype(F32) + p_ref[c, 1:2, :] * in_ref[k]).astype(BF16)
            parts.append(jnp.dot(c_ref[c * CHUNK : (c + 1) * CHUNK, :], entering, preferred_element_type=F32))
        reads = jnp.concatenate(parts, axis=0)
        out = b_ref[...].astype(F32) + reads * grown[k * size : (k + 1) * size]
        gated = out * silu(z_ref[...].astype(F32))
        squares = (gated * gated).astype(BF16)
        means = jnp.concatenate(
            [jnp.dot(squares[:, g : g + 256], mean, preferred_element_type=F32) for g in range(0, inner, 256)], axis=1)
        result = gated * lax.rsqrt(means + EPS)
        both = result if both is None else both + result
    out_ref[...] = both.astype(BF16)


def finish(tile, blocks, strands, bases, entering, copy, heads, inner):
    count, at = blocks
    per = tile // CHUNK
    last = strands[0][0].shape[1] // STATE - 1
    by_rows = lambda width: pl.BlockSpec((tile, width), lambda i: (at(i), 0))
    in_order = pl.BlockSpec((tile, inner), lambda i: (i, 0))
    one = [pl.BlockSpec((tile, STATE), lambda i: (at(i), last)), by_rows(inner),
           pl.BlockSpec((per, STATE, inner), lambda i: (at(i), 0, 0)),
           pl.BlockSpec((per, 8, inner), lambda i: (at(i), 0, 0)), by_rows(128)]
    return pl.pallas_call(
        functools.partial(finish_kernel, heads, inner),
        grid=(count,),
        in_specs=one + one + [in_order, in_order, whole((2, STATE, inner)), whole(copy.shape)],
        out_specs=in_order,
        out_shape=jax.ShapeDtypeStruct((count * tile, inner), BF16),
        compiler_params=params(58),
        cost_estimate=cost(1e8, 1e6),
        name="finish",
    )(*strands[0], *strands[1], *bases, entering, copy)


def read_message(ref, at):
    tail = ref[at + STATE : at + STATE + TAIL, :].astype(F32)
    return ref[at : at + STATE, :].astype(F32), tail[0:1] + tail[1:2] + tail[2:3]


def hop_kernel(first, *refs):
    upper_ref, mine_ref, other_ref = refs[:3]
    into_ref = None if first else refs[3]
    new_ref, msg_ref = refs[-2:]
    upper = upper_ref[0].astype(F32)
    for k in (0, 1):
        later = upper if k == 0 else 1.0 - upper
        at = k * (STATE + TAIL)
        o_state, o_log = read_message(other_ref, at)
        if first:
            new_state, new_log = later * o_state, later * o_log
        else:
            into_log = into_ref[k, STATE : STATE + 1, :]
            new_state = into_ref[k, :STATE, :] + later * jnp.exp(into_log) * o_state
            new_log = into_log + later * o_log
        new_ref[k, :STATE, :] = new_state
        new_ref[k, STATE:, :] = jnp.broadcast_to(new_log, (8, new_log.shape[1]))
        state, log = read_message(mine_ref, at)
        of_other = later * jnp.exp(log) + (1.0 - later)
        of_mine = later + (1.0 - later) * jnp.exp(o_log)
        msg_ref[at : at + STATE, :] = (of_other * o_state + of_mine * state).astype(BF16)
        t = log + o_log
        high = t.astype(BF16).astype(F32)
        mid = (t - high).astype(BF16).astype(F32)
        low = t - high - mid
        row = lax.broadcasted_iota(jnp.int32, (TAIL, t.shape[1]), 0)
        packed = jnp.where(row == 0, high, jnp.where(row == 1, mid, jnp.where(row == 2, low, 0.0)))
        msg_ref[at + STATE : at + STATE + TAIL, :] = packed.astype(BF16)


def local_call(kernel, name, smem, operands, out_shape):
    return pl.pallas_call(
        kernel,
        grid=(1,),
        in_specs=[pl.BlockSpec(memory_space=pltpu.SMEM)] + [whole(x.shape) for x in operands],
        out_specs=[whole(x.shape) for x in out_shape],
        out_shape=out_shape,
        compiler_params=params(10),
        cost_estimate=cost(1e6, 1.5e6),
        name=name,
    )(smem, *operands)


def join_kernel(count, *refs):
    place_ref, into_ref = refs[:2]
    slots, out_ref = refs[2:-1], refs[-1]
    place = place_ref[0]
    groups = [place ^ d for d in range(1, count)]
    read = [read_message(ref, 0) for ref in slots]
    ones = lambda condition: jnp.where(condition, 1.0, 0.0)
    sums = [None, None]
    for j, (state, _) in zip(groups, read):
        lower = ones(j < place)
        log = None
        for i, (_, other) in zip(groups, read):
            between = jnp.logical_or(jnp.logical_and(j < i, i < place), jnp.logical_and(place < i, i < j))
            term = ones(between) * other
            log = term if log is None else log + term
        part = jnp.exp(log) * state
        for k, share in enumerate((lower, 1.0 - lower)):
            sums[k] = share * part if sums[k] is None else sums[k] + share * part
    for k in (0, 1):
        out_ref[k] = into_ref[k, :STATE, :] + jnp.exp(into_ref[k, STATE : STATE + 1, :]) * sums[k]


def incoming(message, axis):
    count, index = lax.axis_size(axis), lax.axis_index(axis)
    inner = message.shape[1]
    into = None
    distance = 1
    while count // distance > 4:
        other = lax.ppermute(message, axis, [(i, i ^ distance) for i in range(count)])
        upper = ((index // distance) % 2).astype(jnp.int32).reshape(1)
        operands = [message, other] + ([] if into is None else [into])
        out_shape = [jax.ShapeDtypeStruct((2, STATE + 8, inner), F32), jax.ShapeDtypeStruct(message.shape, BF16)]
        into, message = local_call(functools.partial(hop_kernel, into is None), "hop", upper, operands, out_shape)
        distance *= 2
    if into is None:
        into = jnp.zeros((2, STATE + 8, inner), F32)
    groups = count // distance
    place = index // distance
    half = STATE + TAIL
    slots = []
    for d in range(1, groups):
        highest = 1 << (d.bit_length() - 1)
        above = (place // highest) % 2
        block = lax.dynamic_slice_in_dim(message, above * half, half, 0)
        slots.append(lax.ppermute(block, axis, [(i, i ^ (d * distance)) for i in range(count)]))
    return local_call(functools.partial(join_kernel, groups), "join", place.astype(jnp.int32).reshape(1), [into] + slots,
                      [jax.ShapeDtypeStruct((2, STATE, inner), F32)])[0]


def shifted(block, axis, distance):
    devices = range(lax.axis_size(axis))
    return lax.ppermute(block, axis, [(i - distance, i) for i in devices if i - distance in devices])


def on_device(
    hidden, norm_gain, w_zx, w_bc, w_dt, dt_bias, decay_rate, skip_gain, conv_x, conv_bc, w_out
):
    rows, depth = hidden.shape
    inner = conv_x.shape[1]
    heads = dt_bias.shape[0]
    width = inner // heads
    n_ctx, n_head = lax.axis_size("ctx"), lax.axis_size("head")
    ctx, head = lax.axis_index("ctx"), lax.axis_index("head")

    rim_f = shifted(hidden[rows - RIM :], "ctx", 1)
    rim_r = shifted(hidden[:RIM], "ctx", -1)

    part = w_out.shape[0] // n_ctx
    own = lax.dynamic_slice_in_dim(w_out, ctx * part, part, 0)
    gathered = lax.all_gather(own, ("ctx", "head"), axis=0)
    gathered = gathered.reshape(n_ctx, n_head, part, depth)

    w_f, w_r, g_f, g_r = prepare(w_zx, w_bc, w_dt, norm_gain)
    lanes = jnp.pad(jnp.stack([dt_bias, decay_rate, skip_gain]), [(0, 0), (0, 128 - heads)])
    copy_first = spread_matrix(0, heads, width)
    copy_second = spread_matrix(heads, heads, width)
    (act_f, small_f, cumt_f, enter_f, prior_f, act_r, small_r, cumt_r, enter_r, prior_r,
     message) = project(hidden, rim_f, rim_r, w_f, w_r, conv_x, conv_bc, lanes, copy_first, heads, inner)
    entering = incoming(message, "ctx")
    z_f, z_r = gates(hidden, g_f, g_r)

    share = rows // n_head
    pieces = 2 if share % (2 * CHUNK) == 0 else 1
    size = share // pieces
    tile = min(TILE, size)
    inner_blocks, share_blocks = size // tile, share // tile
    w_groups = gathered.transpose(1, 0, 2, 3).reshape(n_head, n_ctx * part, depth)
    own_rows = lax.dynamic_slice_in_dim(hidden, head * share, share, 0)
    arrived = [[None] * n_head for _ in range(pieces)]

    def rotated(blocks, d):
        return lax.ppermute(blocks, "head", [(i, (i + d) % n_head) for i in range(n_head)])

    combined = None
    for k in range(pieces):
        blocks = (n_head * inner_blocks,
                  lambda i, k=k: (i // inner_blocks) * share_blocks + k * inner_blocks + i % inner_blocks)
        if combined is not None:
            act_f, act_r, combined = lax.optimization_barrier((act_f, act_r, combined))
        bases = inside(tile, blocks, ((act_f, small_f, cumt_f), (act_r, small_r, cumt_r)), lanes, copy_first, heads, inner,
                       1e8 if k else 8e9)
        combined = finish(tile, blocks, ((act_f, z_f, enter_f, prior_f, small_f), (act_r, z_r, enter_r, prior_r, small_r)),
                          bases, entering, copy_second, heads, inner)
        if k:
            combined, *arrived[k - 1] = lax.optimization_barrier((combined, *arrived[k - 1]))
        for d in range(n_head):
            block = lax.dynamic_slice_in_dim(combined, ((head + d) % n_head) * size, size, 0)
            arrived[k][d] = rotated(block, d) if d else block
    outs = []
    for k in range(pieces):
        total = own_rows[k * size : (k + 1) * size].astype(F32)
        for d in range(n_head):
            weights = lax.dynamic_index_in_dim(w_groups, (head - d) % n_head, 0, keepdims=False)
            total = total + jnp.dot(arrived[k][d], weights, preferred_element_type=F32)
        outs.append(total.astype(BF16))
    return jnp.concatenate(outs, axis=0)


def solution(mesh):
    placed = (
        P("ctx", None),
        P(),
        P(None, None, "head"),
        P(),
        P(None, "head"),
        P("head"),
        P("head"),
        P("head"),
        P(None, "head"),
        P(),
        P("head", None),
    )
    return jax.shard_map(
        on_device, mesh=mesh, in_specs=placed, out_specs=P(("ctx", "head"), None), check_vma=False
    )
```

time: 175 us -> 147 us (0.84)
  waiting for transfers between devices: 29.2 us -> 16.1 us
  Pallas kernels: 83.6 us -> 74.2 us
  local copies, waits for them, and re-layouts: 15.7 us -> 9.19 us
  starting transfers between devices: 20.6 us -> 24.4 us
  other arithmetic: 3.38 us -> 1.63 us
    ppermute x3 -> x1, waiting for transfers between devices: 8.41 us -> 0.01 us  [incoming(): lax.ppermute(message, axis, [(i, i ^ distance) for i in range(count)])]
    ppermute x6 -> x9, starting transfers between devices: 10.5 us -> 17.6 us  [the longest x6 13.4 us: rotated(): lax.ppermute(blocks, 'head', [(i, (i + d) % n_head) for i in range(n_head)])]
    pallas_call x1, Pallas kernels: 36.1 us -> 29.9 us  [project(): pl.pallas_call(functools.partial(project_kernel, heads, inner), grid=(n,)...]
    pallas_call x2, Pallas kernels: 19.2 us -> 14.3 us  [finish(): pl.pallas_call(functools.partial(finish_kernel, heads, inner), grid=(coun...]
    ppermute x6 -> x9, waiting for transfers between devices: 20.8 us -> 16 us  [the longest x6 15.8 us: rotated(): lax.ppermute(blocks, 'head', [(i, (i + d) % n_head) for i in range(n_head)])]
    broadcast_in_dim x3 -> x0, local copies, waits for them, and re-layouts: 2.97 us -> none  [the longest x1 1.71 us: on_device(): w_f, w_r = prepare(w_zx, w_bc, pad(w_dt), norm_gain[:, None])]
    ppermute x3 -> x1, starting transfers between devices: 5.83 us -> 3.19 us  [incoming(): lax.ppermute(message, axis, [(i, i ^ distance) for i in range(count)])]
    unnamed x15 -> x16, local copies, waits for them, and re-layouts: 4.89 us -> 2.67 us
  transfers between devices with their start and end apart: 12 -> 13, of which waited for: 4 -> 4; matrix products, arithmetic and copies ran while one was open for 11% -> 9% of each run, Pallas kernels for 48% -> 51%
where the time goes in v1:
time: 147 us; the launch traced here: 146 us
  Pallas kernels  74.2 us (50%)
  starting transfers between devices  24.4 us (17%)
  waiting for transfers between devices  16.1 us (11%)
  between operations  13.6 us (9%)
  local copies, waits for them, and re-layouts  9.19 us (6%)
  matrix products  6.75 us (5%)
  other arithmetic  1.63 us (1%)
    pallas_call x1, Pallas kernels, project(): pl.pallas_call(functools.partial(project_kernel, heads, inner), grid=(n,)...  29.9 us
    ppermute x6, waiting for transfers between devices, rotated(): lax.ppermute(blocks, 'head', [(i, (i + d) % n_head) for i in range(n_head)])  15.8 us
    pallas_call x2, Pallas kernels, finish(): pl.pallas_call(functools.partial(finish_kernel, heads, inner), grid=(coun...  14.3 us
    pallas_call x2, Pallas kernels, inside(): pl.pallas_call(functools.partial(inside_kernel, heads, inner), grid=(coun...  14.2 us
    ppermute x6, starting transfers between devices, rotated(): lax.ppermute(blocks, 'head', [(i, (i + d) % n_head) for i in range(n_head)])  13.4 us
    pallas_call x1, Pallas kernels, gates(): pl.pallas_call(gates_kernel, grid=(rows // TILE,), in_specs=[by_rows(dept...  9.8 us
    dot_general x8, matrix products, on_device(): total = total + jnp.dot(arrived[k][d], weights, preferred_element_type=F32)  6.75 us
    pallas_call x1, Pallas kernels, prepare(): pl.pallas_call(functools.partial(prepare_kernel, inner), grid=(n,), in_sp...  5.69 us
  transfers between devices with their start and end apart: 13, of which 4 were waited for; matrix products, arithmetic and copies ran while one was open for 9% of the time, Pallas kernels for 51%

profile of v1, /device:TPU:0, one launch (start us, length us, event | category | flops | bytes accessed | tf_op | source)
XLA Modules:
  0.0 145.9 jit_solution(9183651020101335658)
XLA Ops:
  6.5 1.2 copy-done
  9.2 2.3 %collective-permute-start = (bf16[16,1024]{1,0:T(8,128)(2,1)S(1)}, bf16[16,1024]{1,0:T(8,128)(2,1)S(1)}, u32[]{:S(2)}, u32[]{:S(2)}) collective-permute-start(bf16[16,1024]{1,0:T(8,128)(2,1)S(1)} %get-tuple-element.66), channel_id=1, source_target_pairs={{0,4},{4,8},{8,12},{12,16},{16,20},{20,24},{24,28},{1,5},{5,9},{9,... | collective-permute-start | bytes 98312 | tf_op jit(solution)/shard_map/ppermute | solution.py:477
  11.6 1.3 collective-permute-start.1
  12.9 5.7 %prepare.1 = (bf16[1024,896]{1,0:T(8,128)(2,1)}, bf16[1024,896]{1,0:T(8,128)(2,1)}, bf16[1024,512]{1,0:T(8,128)(2,1)}, bf16[1024,512]{1,0:T(8,128)(2,1)}) custom-call(bf16[1024,2,512]{2,1,0:T(2,128)(2,1)} %zx_ref.1, bf16[1024,256]{1,0:T(8,128)(2,1)} %bc_ref.1, bf16[8,1024]{1,0:T(8,128)(2,1)} %bitcast.50, f32[1,1024]{1,0:T(1,128)} %bitcast.51), custom_call_target="tpu_custom_call" | custom-call | flops 4000000000 | bytes 8000000 | tf_op jit(solution)/shard_map/prepare/pallas_call | solution.py:87
  19.9 29.9 %project.1 = (bf16[2048,768]{1,0:T(8,128)(2,1)}, f32[2048,128]{1,0:T(8,128)}, f32[8,2048]{1,0:T(8,128)}, bf16[16,128,512]{2,1,0:T(8,128)(2,1)}, f32[16,8,512]{2,...) custom-call(bf16[2048,1024]{1,0:T(8,128)(2,1)} %h_ref.1, ...), custom_call_target="tpu_custom_call" | custom-call | flops 22000001024 | bytes 40000000 | tf_op jit(solution)/shard_map/project/pallas_call | solution.py:241
  49.7 3.2 %collective-permute-start.2 = (bf16[288,512]{1,0:T(8,128)(2,1)}, bf16[288,512]{1,0:T(8,128)(2,1)S(1)}, u32[]{:S(2)}, u32[]{:S(2)}) collective-permute-start(bf16[288,512]{1,0:T(8,128)(2,1)} %get-tuple-element.53.refs_1_), channel_id=1, source_target_pairs={{0,4},{4,0},{8,12},{12,8},{16,20},{20,16},{24,28},{28,24},{1,5},{5... | collective-permute-start | bytes 884744 | tf_op jit(solution)/shard_map/ppermute | solution.py:454
  52.9 9.8 %gates.1 = (bf16[2048,512]{1,0:T(8,128)(2,1)}, bf16[2048,512]{1,0:T(8,128)(2,1)}) custom-call(bf16[2048,1024]{1,0:T(8,128)(2,1)} %h_ref.1, bf16[1024,512]{1,0:T(8,128)(2,1)} %get-tuple-element.39.wf_ref, bf16[1024,512]{1,0:T(8,128)(2,1)} %get-tuple-element.40.wr_ref), custom_call_target="tpu_custom_call" | custom-call | flops 10000000000 | bytes 10000000 | tf_op jit(solution)/shard_map/gates/pallas_call | solution.py:267
  62.9 2.7 %collective-permute-start.4 = (bf16[144,512]{1,0:T(8,128)(2,1)S(1)}, bf16[144,512]{1,0:T(8,128)(2,1)S(1)}, u32[]{:S(2)}, u32[]{:S(2)}) collective-permute-start(bf16[144,512]{1,0:T(8,128)(2,1)S(1)} %get-tuple-element.74), channel_id=1, source_target_pairs={{0,16},{4,20},{8,24},{12,28},{16,0},{20,4},{24,8},{28,12},{1,17},{... | collective-permute-start | bytes 442376 | tf_op jit(solution)/shard_map/ppermute | solution.py:470
  67.1 7.1 %inside.2 = (bf16[1024,512]{1,0:T(8,128)(2,1)}, bf16[1024,512]{1,0:T(8,128)(2,1)}) custom-call(bf16[2048,768]{1,0:T(8,128)(2,1)} %get-tuple-element.56.actf_ref.refs_0_, f32[2048,128]{1,0:T(8,128)} %get-tuple-element.44.smallf_ref.refs_4_, f32[8,2048]{1,0:T(8,128)} %get-tuple-element.49.cumtf_ref, bf16[2048,768]{1,0:T(8,128)(2,1)} %get-tuple-element.57.actr_ref.refs_5_, ...), custom_call_target="tpu_custom_call" | custom-call | flops 8000000000 | bytes 1000000 | tf_op jit(solution)/shard_map/inside/pallas_call | solution.py:318
  75.5 7.3 %finish.2 = bf16[1024,512]{1,0:T(8,128)(2,1)} custom-call(bf16[2048,768]{1,0:T(8,128)(2,1)} %get-tuple-element.56.actf_ref.refs_0_, bf16[2048,512]{1,0:T(8,128)(2,1)} %get-tuple-element.41.refs_1_, bf16[16,128,512]{2,1,0:T(8,128)(2,1)} %get-tuple-element.42.refs_2_, f32[16,8,512]{2,1,0:T(8,128)} %get-tuple-element.43.refs_3_, ...), custom_call_target="tpu_custom_call" | custom-call | flops 100000000 | bytes 1000000 | tf_op jit(solution)/shard_map/finish/pallas_call | solution.py:366
  82.7 1.3 constant_dynamic-slice_fusion.4
  84.0 1.6 %collective-permute-start.6 = (bf16[256,512]{1,0:T(8,128)(2,1)S(1)}, bf16[256,512]{1,0:T(8,128)(2,1)S(1)}, u32[]{:S(2)}, u32[]{:S(2)}) collective-permute-start(bf16[256,512]{1,0:T(8,128)(2,1)S(1)} %get-tuple-element.72), channel_id=1, source_target_pairs={{0,1},{1,2},{2,3},{3,0},{4,5},{5,6},{6,7},{7,4},{8,9},{9,10},{10,1... | collective-permute-start | bytes 786440 | tf_op jit(solution)/shard_map/ppermute | solution.py:517
  85.6 2.6 %collective-permute-start.7 = (bf16[256,512]{1,0:T(8,128)(2,1)S(1)}, bf16[256,512]{1,0:T(8,128)(2,1)S(1)}, u32[]{:S(2)}, u32[]{:S(2)}) collective-permute-start(bf16[256,512]{1,0:T(8,128)(2,1)S(1)} %get-tuple-element.71), channel_id=1, source_target_pairs={{0,2},{1,3},{2,0},{3,1},{4,6},{5,7},{6,4},{7,5},{8,10},{9,11},{10,... | collective-permute-start | bytes 786440 | tf_op jit(solution)/shard_map/ppermute | solution.py:517
  88.2 1.3 collective-permute-start.8
  89.6 7.1 %inside.3 = (bf16[1024,512]{1,0:T(8,128)(2,1)}, bf16[1024,512]{1,0:T(8,128)(2,1)}) custom-call(bf16[2048,768]{1,0:T(8,128)(2,1)} %get-tuple-element.56.actf_ref.refs_0_, f32[2048,128]{1,0:T(8,128)} %get-tuple-element.44.smallf_ref.refs_4_, f32[8,2048]{1,0:T(8,128)} %get-tuple-element.49.cumtf_ref, bf16[2048,768]{1,0:T(8,128)(2,1)} %get-tuple-element.57.actr_ref.refs_5_, ...), custom_call_target="tpu_custom_call" | custom-call | flops 100000000 | bytes 1000000 | tf_op jit(solution)/shard_map/inside/pallas_call | solution.py:318
  96.7 7.0 %finish.3 = bf16[1024,512]{1,0:T(8,128)(2,1)} custom-call(bf16[2048,768]{1,0:T(8,128)(2,1)} %get-tuple-element.56.actf_ref.refs_0_, bf16[2048,512]{1,0:T(8,128)(2,1)} %get-tuple-element.41.refs_1_, bf16[16,128,512]{2,1,0:T(8,128)(2,1)} %get-tuple-element.42.refs_2_, f32[16,8,512]{2,1,0:T(8,128)} %get-tuple-element.43.refs_3_, ...), custom_call_target="tpu_custom_call" | custom-call | flops 100000000 | bytes 1000000 | tf_op jit(solution)/shard_map/finish/pallas_call | solution.py:366
  103.7 1.5 %collective-permute-done.7 = bf16[256,512]{1,0:T(8,128)(2,1)S(1)} collective-permute-done((bf16[256,512]{1,0:T(8,128)(2,1)S(1)}, bf16[256,512]{1,0:T(8,128)(2,1)S(1)}, u32[]{:S(2)}, u32[]{:S(2)}) %collective-permute-start.7) | collective-permute-done | bytes 262176 | tf_op jit(solution)/shard_map/ppermute | solution.py:517
  105.2 1.2 constant_dynamic-slice_fusion.2
  106.4 7.2 %collective-permute-start.11 = (bf16[256,512]{1,0:T(8,128)(2,1)S(1)}, bf16[256,512]{1,0:T(8,128)(2,1)}, u32[]{:S(2)}, u32[]{:S(2)}) collective-permute-start(bf16[256,512]{1,0:T(8,128)(2,1)S(1)} %get-tuple-element.68), channel_id=1, source_target_pairs={{0,3},{1,0},{2,1},{3,2},{4,7},{5,4},{6,5},{7,6},{8,11},{9,8},{10,9... | collective-permute-start | bytes 786440 | tf_op jit(solution)/shard_map/ppermute | solution.py:517
  114.2 2.6 %copy.14 = bf16[4,8,64,1024]{3,2,1,0:T(8,128)(2,1)S(1)} copy(bf16[4,8,64,1024]{3,2,0,1:T(8,128)(2,1)} %bitcast.46) | data formatting | bytes 8388608 | tf_op jit(solution)/shard_map/transpose | solution.py:512
  118.2 1.6 %fusion.5 = bf16[256,1024]{1,0:T(8,128)(2,1)S(1)} fusion(f32[256,1024]{1,0:T(8,128)S(1)} %fusion.9, f32[256,1024]{1,0:T(8,128)S(1)} %fusion.13, f32[256,1024]{1,0:T(8,128)S(1)} %fusion.16, bf16[256,512]{1,0:T(8,128)(2,1)S(1)} %get-tuple-element.60, bf16[4,512,1024]{2,1,0:T(8,128)(2,1)S(1)} %bitcast.41, s32[]{:T(128)S(6)} %select_n.136, ...), kind=kOutput, calls=%fused_computation.8 | convolution fusion | flops 270008320 | bytes 5505032 | tf_op jit(solution)/shard_map/dot_general | solution.py:539
  120.3 1.4 fusion.7
  121.7 1.6 %convolution_add_fusion.1 = f32[256,1024]{1,0:T(8,128)S(1)} fusion(bf16[4,512,1024]{2,1,0:T(8,128)(2,1)S(1)} %bitcast.43, s32[]{:T(128)S(6)} %select_n.136, bf16[2048,1024]{1,0:T(8,128)(2,1)} %h_ref.1, s32[]{:T(128)S(6)} %add.165, bf16[1024,512]{1,0:T(8,128)(2,1)} %finish.3, s32[]{:T(128)S(6)} %select_n.128), kind=kOutput, calls=%fused_computation.3 | convolution fusion | flops 268959744 | bytes 2883596 | tf_op jit(solution)/shard_map/dot_general | solution.py:539
  123.3 13.7 %collective-permute-done.10 = bf16[256,512]{1,0:T(8,128)(2,1)S(1)} collective-permute-done((bf16[256,512]{1,0:T(8,128)(2,1)S(1)}, bf16[256,512]{1,0:T(8,128)(2,1)S(1)}, u32[]{:S(2)}, u32[]{:S(2)}) %collective-permute-start.10) | collective-permute-done | bytes 262176 | tf_op jit(solution)/shard_map/ppermute | solution.py:517
  (44 shorter events, 10.2 us)
Async XLA Ops:
  6.5 1.2 copy-start
  6.5 107.7 %all-gather.3.cloned.1.call-start = ((), (), s32[]{:S(2)}) async-start(), calls=%async_computation | async-start | bytes 4325376 | tf_op jit(solution)/shard_map/all_gather | solution.py:495
  9.2 10.0 %collective-permute-start = (bf16[16,1024]{1,0:T(8,128)(2,1)S(1)}, bf16[16,1024]{1,0:T(8,128)(2,1)S(1)}, u32[]{:S(2)}, u32[]{:S(2)}) collective-permute-start(bf16[16,1024]{1,0:T(8,128)(2,1)S(1)} %get-tuple-element.66), channel_id=1, source_target_pairs={{0,4},{4,8},{8,12},{12,16},{16,20},{20,24},{24,28},{1,5},{5,9},{9,... | collective-permute-start | bytes 98312 | tf_op jit(solution)/shard_map/ppermute | solution.py:477
  11.6 7.7 %collective-permute-start.1 = (bf16[16,1024]{1,0:T(8,128)(2,1)S(1)}, bf16[16,1024]{1,0:T(8,128)(2,1)S(1)}, u32[]{:S(2)}, u32[]{:S(2)}) collective-permute-start(bf16[16,1024]{1,0:T(8,128)(2,1)S(1)} %get-tuple-element.65), channel_id=1, source_target_pairs={{4,0},{8,4},{12,8},{16,12},{20,16},{24,20},{28,24},{5,1},{9,5},{13... | collective-permute-start | bytes 98312 | tf_op jit(solution)/shard_map/ppermute | solution.py:477
  12.9 5.7 %copy-start.3 = (f32[8]{0:T(128)S(1)}, f32[8]{0:T(128)}, u32[]{:S(2)}) copy-start(f32[8]{0:T(128)} %param.20) | copy-start | bytes 100
  12.9 5.7 %copy-start.4 = (f32[8]{0:T(128)S(1)}, f32[8]{0:T(128)}, u32[]{:S(2)}) copy-start(f32[8]{0:T(128)} %param.19) | copy-start | bytes 100
  12.9 5.7 %copy-start.5 = (f32[8]{0:T(128)S(1)}, f32[8]{0:T(128)}, u32[]{:S(2)}) copy-start(f32[8]{0:T(128)} %param.18) | copy-start | bytes 100
  19.2 0.6 copy-start.6
  19.2 0.6 copy-start.7
  49.7 13.0 %collective-permute-start.2 = (bf16[288,512]{1,0:T(8,128)(2,1)}, bf16[288,512]{1,0:T(8,128)(2,1)S(1)}, u32[]{:S(2)}, u32[]{:S(2)}) collective-permute-start(bf16[288,512]{1,0:T(8,128)(2,1)} %get-tuple-element.53.refs_1_), channel_id=1, source_target_pairs={{0,4},{4,0},{8,12},{12,8},{16,20},{20,16},{24,28},{28,24},{1,5},{5... | collective-permute-start | bytes 884744 | tf_op jit(solution)/shard_map/ppermute | solution.py:454
  52.9 9.8 %copy-start.2 = (bf16[288,512]{1,0:T(8,128)(2,1)S(1)}, bf16[288,512]{1,0:T(8,128)(2,1)}, u32[]{:S(2)}) copy-start(bf16[288,512]{1,0:T(8,128)(2,1)} %get-tuple-element.53.refs_1_) | copy-start | bytes 884740
  62.9 11.5 %collective-permute-start.4 = (bf16[144,512]{1,0:T(8,128)(2,1)S(1)}, bf16[144,512]{1,0:T(8,128)(2,1)S(1)}, u32[]{:S(2)}, u32[]{:S(2)}) collective-permute-start(bf16[144,512]{1,0:T(8,128)(2,1)S(1)} %get-tuple-element.74), channel_id=1, source_target_pairs={{0,16},{4,20},{8,24},{12,28},{16,0},{20,4},{24,8},{28,12},{1,17},{... | collective-permute-start | bytes 442376 | tf_op jit(solution)/shard_map/ppermute | solution.py:470
  65.6 8.8 %collective-permute-start.5 = (bf16[144,512]{1,0:T(8,128)(2,1)S(1)}, bf16[144,512]{1,0:T(8,128)(2,1)S(1)}, u32[]{:S(2)}, u32[]{:S(2)}) collective-permute-start(bf16[144,512]{1,0:T(8,128)(2,1)S(1)} %get-tuple-element.74), channel_id=1, source_target_pairs={{0,24},{4,28},{8,16},{12,20},{16,8},{20,12},{24,0},{28,4},{1,25},{... | collective-permute-start | bytes 442376 | tf_op jit(solution)/shard_map/ppermute | solution.py:470
  66.1 8.3 %collective-permute-start.3 = (bf16[144,512]{1,0:T(8,128)(2,1)S(1)}, bf16[144,512]{1,0:T(8,128)(2,1)S(1)}, u32[]{:S(2)}, u32[]{:S(2)}) collective-permute-start(bf16[144,512]{1,0:T(8,128)(2,1)S(1)} %get-tuple-element.75), channel_id=1, source_target_pairs={{0,8},{4,12},{8,0},{12,4},{16,24},{20,28},{24,16},{28,20},{1,9},{5... | collective-permute-start | bytes 442376 | tf_op jit(solution)/shard_map/ppermute | solution.py:470
  74.6 0.8 copy-start.1
  84.0 19.7 %collective-permute-start.6 = (bf16[256,512]{1,0:T(8,128)(2,1)S(1)}, bf16[256,512]{1,0:T(8,128)(2,1)S(1)}, u32[]{:S(2)}, u32[]{:S(2)}) collective-permute-start(bf16[256,512]{1,0:T(8,128)(2,1)S(1)} %get-tuple-element.72), channel_id=1, source_target_pairs={{0,1},{1,2},{2,3},{3,0},{4,5},{5,6},{6,7},{7,4},{8,9},{9,10},{10,1... | collective-permute-start | bytes 786440 | tf_op jit(solution)/shard_map/ppermute | solution.py:517
  85.6 19.6 %collective-permute-start.7 = (bf16[256,512]{1,0:T(8,128)(2,1)S(1)}, bf16[256,512]{1,0:T(8,128)(2,1)S(1)}, u32[]{:S(2)}, u32[]{:S(2)}) collective-permute-start(bf16[256,512]{1,0:T(8,128)(2,1)S(1)} %get-tuple-element.71), channel_id=1, source_target_pairs={{0,2},{1,3},{2,0},{3,1},{4,6},{5,7},{6,4},{7,5},{8,10},{9,11},{10,... | collective-permute-start | bytes 786440 | tf_op jit(solution)/shard_map/ppermute | solution.py:517
  88.2 17.0 %collective-permute-start.8 = (bf16[256,512]{1,0:T(8,128)(2,1)S(1)}, bf16[256,512]{1,0:T(8,128)(2,1)S(1)}, u32[]{:S(2)}, u32[]{:S(2)}) collective-permute-start(bf16[256,512]{1,0:T(8,128)(2,1)S(1)} %get-tuple-element.70), channel_id=1, source_target_pairs={{0,3},{1,0},{2,1},{3,2},{4,7},{5,4},{6,5},{7,6},{8,11},{9,8},{10,9... | collective-permute-start | bytes 786440 | tf_op jit(solution)/shard_map/ppermute | solution.py:517
  106.4 14.0 %collective-permute-start.11 = (bf16[256,512]{1,0:T(8,128)(2,1)S(1)}, bf16[256,512]{1,0:T(8,128)(2,1)}, u32[]{:S(2)}, u32[]{:S(2)}) collective-permute-start(bf16[256,512]{1,0:T(8,128)(2,1)S(1)} %get-tuple-element.68), channel_id=1, source_target_pairs={{0,3},{1,0},{2,1},{3,2},{4,7},{5,4},{6,5},{7,6},{8,11},{9,8},{10,9... | collective-permute-start | bytes 786440 | tf_op jit(solution)/shard_map/ppermute | solution.py:517
  113.5 23.5 %collective-permute-start.10 = (bf16[256,512]{1,0:T(8,128)(2,1)S(1)}, bf16[256,512]{1,0:T(8,128)(2,1)S(1)}, u32[]{:S(2)}, u32[]{:S(2)}) collective-permute-start(bf16[256,512]{1,0:T(8,128)(2,1)S(1)} %get-tuple-element.69), channel_id=1, source_target_pairs={{0,2},{1,3},{2,0},{3,1},{4,6},{5,7},{6,4},{7,5},{8,10},{9,11},{10,... | collective-permute-start | bytes 786440 | tf_op jit(solution)/shard_map/ppermute | solution.py:517
  114.0 23.5 %collective-permute-start.9 = (bf16[256,512]{1,0:T(8,128)(2,1)S(1)}, bf16[256,512]{1,0:T(8,128)(2,1)S(1)}, u32[]{:S(2)}, u32[]{:S(2)}) collective-permute-start(bf16[256,512]{1,0:T(8,128)(2,1)S(1)} %get-tuple-element.67), channel_id=1, source_target_pairs={{0,1},{1,2},{2,3},{3,0},{4,5},{5,6},{6,7},{7,4},{8,9},{9,10},{10,1... | collective-permute-start | bytes 786440 | tf_op jit(solution)/shard_map/ppermute | solution.py:517
Sparse Core Ops, SparseCore 0:
  10.4 64.8 all-gather.2

commit v2 on v1

--- a/solution.py
+++ b/solution.py
@@ -445,13 +445,15 @@
         out_ref[k] = into_ref[k, :STATE, :] + jnp.exp(into_ref[k, STATE : STATE + 1, :]) * sums[k]
 
 
-def incoming(message, axis):
+def incoming(message, axis, beside, before):
     count, index = lax.axis_size(axis), lax.axis_index(axis)
     inner = message.shape[1]
     into = None
     distance = 1
     while count // distance > 4:
         other = lax.ppermute(message, axis, [(i, i ^ distance) for i in range(count)])
+        if into is None:
+            other, *beside = lax.optimization_barrier((other, *beside))
         upper = ((index // distance) % 2).astype(jnp.int32).reshape(1)
         operands = [message, other] + ([] if into is None else [into])
         out_shape = [jax.ShapeDtypeStruct((2, STATE + 8, inner), F32), jax.ShapeDtypeStruct(message.shape, BF16)]
@@ -459,6 +461,7 @@
         distance *= 2
     if into is None:
         into = jnp.zeros((2, STATE + 8, inner), F32)
+    message, *before = lax.optimization_barrier((message, *before))
     groups = count // distance
     place = index // distance
     half = STATE + TAIL
@@ -468,13 +471,18 @@
         above = (place // highest) % 2
         block = lax.dynamic_slice_in_dim(message, above * half, half, 0)
         slots.append(lax.ppermute(block, axis, [(i, i ^ (d * distance)) for i in range(count)]))
-    return local_call(functools.partial(join_kernel, groups), "join", place.astype(jnp.int32).reshape(1), [into] + slots,
-                      [jax.ShapeDtypeStruct((2, STATE, inner), F32)])[0]
+    joined = local_call(functools.partial(join_kernel, groups), "join", place.astype(jnp.int32).reshape(1), [into] + slots,
+                        [jax.ShapeDtypeStruct((2, STATE, inner), F32)])[0]
+    return joined, beside, before
 
 
 def shifted(block, axis, distance):
     devices = range(lax.axis_size(axis))
     return lax.ppermute(block, axis, [(i - distance, i) for i in devices if i - distance in devices])
+
+
+def rotated(block, d, count):
+    return lax.ppermute(block, "head", [(i, (i + d) % count) for i in range(count)])
 
 
 def on_device(
@@ -490,10 +498,10 @@
     rim_f = shifted(hidden[rows - RIM :], "ctx", 1)
     rim_r = shifted(hidden[:RIM], "ctx", -1)
 
-    part = w_out.shape[0] // n_ctx
-    own = lax.dynamic_slice_in_dim(w_out, ctx * part, part, 0)
-    gathered = lax.all_gather(own, ("ctx", "head"), axis=0)
-    gathered = gathered.reshape(n_ctx, n_head, part, depth)
+    half = w_out.shape[0] // 2
+    parity = ctx % 2
+    own_half = lax.dynamic_slice_in_dim(w_out, parity * half, half, 0)
+    same = [rotated(own_half, d, n_head) for d in range(1, n_head)]
 
     w_f, w_r, g_f, g_r = prepare(w_zx, w_bc, w_dt, norm_gain)
     lanes = jnp.pad(jnp.stack([dt_bias, decay_rate, skip_gain]), [(0, 0), (0, 128 - heads)])
@@ -501,20 +509,19 @@
     copy_second = spread_matrix(heads, heads, width)
     (act_f, small_f, cumt_f, enter_f, prior_f, act_r, small_r, cumt_r, enter_r, prior_r,
      message) = project(hidden, rim_f, rim_r, w_f, w_r, conv_x, conv_bc, lanes, copy_first, heads, inner)
-    entering = incoming(message, "ctx")
-    z_f, z_r = gates(hidden, g_f, g_r)
+    entering, (z_f, z_r), same = incoming(message, "ctx", gates(hidden, g_f, g_r), same)
 
     share = rows // n_head
     pieces = 2 if share % (2 * CHUNK) == 0 else 1
     size = share // pieces
     tile = min(TILE, size)
     inner_blocks, share_blocks = size // tile, share // tile
-    w_groups = gathered.transpose(1, 0, 2, 3).reshape(n_head, n_ctx * part, depth)
+    other = lax.ppermute(jnp.concatenate(same, axis=0), "ctx", [(i, i ^ 1) for i in range(n_ctx)])
+    entering, other = lax.optimization_barrier((entering, other))
+    other = [other[i * half : (i + 1) * half] for i in range(n_head - 1)]
+    groups = [w_out]
     own_rows = lax.dynamic_slice_in_dim(hidden, head * share, share, 0)
     arrived = [[None] * n_head for _ in range(pieces)]
-
-    def rotated(blocks, d):
-        return lax.ppermute(blocks, "head", [(i, (i + d) % n_head) for i in range(n_head)])
 
     combined = None
     for k in range(pieces):
@@ -528,17 +535,21 @@
                           bases, entering, copy_second, heads, inner)
         if k:
             combined, *arrived[k - 1] = lax.optimization_barrier((combined, *arrived[k - 1]))
-        for d in range(n_head):
-            block = lax.dynamic_slice_in_dim(combined, ((head + d) % n_head) * size, size, 0)
-            arrived[k][d] = rotated(block, d) if d else block
-    outs = []
+        parts = [lax.dynamic_slice_in_dim(combined, ((head + d) % n_head) * size, size, 0) for d in range(n_head)]
+        arrived[k] = [rotated(block, d, n_head) if d else block for d, block in enumerate(parts)]
+    for one, two in zip(same, other):
+        groups.append(jnp.concatenate([jnp.where(parity == 0, one, two), jnp.where(parity == 0, two, one)], axis=0))
+    result = None
     for k in range(pieces):
         total = own_rows[k * size : (k + 1) * size].astype(F32)
-        for d in range(n_head):
-            weights = lax.dynamic_index_in_dim(w_groups, (head - d) % n_head, 0, keepdims=False)
-            total = total + jnp.dot(arrived[k][d], weights, preferred_element_type=F32)
-        outs.append(total.astype(BF16))
-    return jnp.concatenate(outs, axis=0)
+        for block, weights in zip(arrived[k], groups):
+            total = total + jnp.dot(block, weights, preferred_element_type=F32)
+        total = total.astype(BF16)
+        if result is None:
+            result = jnp.pad(total, ((0, share - size), (0, 0)))
+        else:
+            result = lax.dynamic_update_slice(result, total, (k * size, 0))
+    return result
 
 
 def solution(mesh):

time: 147 us -> 133 us (0.905)
  the two profiles are of different devices: /device:TPU:0 before, /device:TPU:10 now
where the time goes in v2:
time: 133 us; the launch traced here: 131 us
  Pallas kernels  73.9 us (56%)
  waiting for transfers between devices  21.3 us (16%)
  starting transfers between devices  20.2 us (15%)
  matrix products  5.78 us (4%)
  local copies, waits for them, and re-layouts  4.82 us (4%)
  other arithmetic  4.62 us (3%)
    pallas_call x1, Pallas kernels, project(): pl.pallas_call(functools.partial(project_kernel, heads, inner), grid=(n,)...  29.8 us
    ppermute x9, waiting for transfers between devices, rotated(): lax.ppermute(block, 'head', [(i, (i + d) % count) for i in range(count)])  21.3 us
    pallas_call x2, Pallas kernels, finish(): pl.pallas_call(functools.partial(finish_kernel, heads, inner), grid=(coun...  14.3 us
    pallas_call x2, Pallas kernels, inside(): pl.pallas_call(functools.partial(inside_kernel, heads, inner), grid=(coun...  14.1 us
    ppermute x9, starting transfers between devices, rotated(): lax.ppermute(block, 'head', [(i, (i + d) % count) for i in range(count)])  10.6 us
    pallas_call x1, Pallas kernels, gates(): pl.pallas_call(gates_kernel, grid=(rows // TILE,), in_specs=[by_rows(dept...  9.66 us
    dot_general x8, matrix products, on_device(): total = total + jnp.dot(block, weights, preferred_element_type=F32)  5.78 us
    pallas_call x1, Pallas kernels, prepare(): pl.pallas_call(functools.partial(prepare_kernel, inner), grid=(n,), in_sp...  5.69 us
  transfers between devices with their start and end apart: 16, of which 4 were waited for; matrix products, arithmetic and copies ran while one was open for 6% of the time, Pallas kernels for 51%

profile of v2, /device:TPU:10, one launch (start us, length us, event | category | flops | bytes accessed | tf_op | source)
XLA Modules:
  0.0 131.0 jit_solution(256861930353892429)
XLA Ops:
  0.0 1.2 copy-done
  1.3 1.6 %collective-permute-start.3 = (bf16[256,1024]{1,0:T(8,128)(2,1)S(1)}, bf16[256,1024]{1,0:T(8,128)(2,1)S(1)}, u32[]{:S(2)}, u32[]{:S(2)}) collective-permute-start(bf16[256,1024]{1,0:T(8,128)(2,1)S(1)} %constant_dynamic-slice_fusion.9), channel_id=1, source_target_pairs={{0,1},{1,2},{2,3},{3,0},{4,5},{5,6},{6,7},{7,4},{8,9},{9,10},{10,1... | collective-permute-start | bytes 1572872 | tf_op jit(solution)/shard_map/ppermute | solution.py:485
  2.9 1.2 collective-permute-start.4
  4.1 1.8 %collective-permute-start.5 = (bf16[256,1024]{1,0:T(8,128)(2,1)S(1)}, bf16[256,1024]{1,0:T(8,128)(2,1)S(1)}, u32[]{:S(2)}, u32[]{:S(2)}) collective-permute-start(bf16[256,1024]{1,0:T(8,128)(2,1)S(1)} %constant_dynamic-slice_fusion.9), channel_id=1, source_target_pairs={{0,3},{1,0},{2,1},{3,2},{4,7},{5,4},{6,5},{7,6},{8,11},{9,8},{10,9... | collective-permute-start | bytes 1572872 | tf_op jit(solution)/shard_map/ppermute | solution.py:485
  6.7 1.9 %collective-permute-start = (bf16[16,1024]{1,0:T(8,128)(2,1)S(1)}, bf16[16,1024]{1,0:T(8,128)(2,1)S(1)}, u32[]{:S(2)}, u32[]{:S(2)}) collective-permute-start(bf16[16,1024]{1,0:T(8,128)(2,1)S(1)} %get-tuple-element.84), channel_id=1, source_target_pairs={{0,4},{4,8},{8,12},{12,16},{16,20},{20,24},{24,28},{1,5},{5,9},{9,... | collective-permute-start | bytes 98312 | tf_op jit(solution)/shard_map/ppermute | solution.py:481
  8.6 3.6 %collective-permute-start.1 = (bf16[16,1024]{1,0:T(8,128)(2,1)S(1)}, bf16[16,1024]{1,0:T(8,128)(2,1)S(1)}, u32[]{:S(2)}, u32[]{:S(2)}) collective-permute-start(bf16[16,1024]{1,0:T(8,128)(2,1)S(1)} %get-tuple-element.83), channel_id=1, source_target_pairs={{4,0},{8,4},{12,8},{16,12},{20,16},{24,20},{28,24},{5,1},{9,5},{13... | collective-permute-start | bytes 98312 | tf_op jit(solution)/shard_map/ppermute | solution.py:481
  12.3 5.7 %prepare.1 = (bf16[1024,896]{1,0:T(8,128)(2,1)}, bf16[1024,896]{1,0:T(8,128)(2,1)}, bf16[1024,512]{1,0:T(8,128)(2,1)}, bf16[1024,512]{1,0:T(8,128)(2,1)}) custom-call(bf16[1024,2,512]{2,1,0:T(2,128)(2,1)} %zx_ref.1, bf16[1024,256]{1,0:T(8,128)(2,1)} %bc_ref.1, bf16[8,1024]{1,0:T(8,128)(2,1)} %bitcast.19, f32[1,1024]{1,0:T(1,128)} %bitcast.20), custom_call_target="tpu_custom_call" | custom-call | flops 4000000000 | bytes 8000000 | tf_op jit(solution)/shard_map/prepare/pallas_call | solution.py:87
  19.3 29.8 %project.1 = (bf16[2048,768]{1,0:T(8,128)(2,1)}, f32[2048,128]{1,0:T(8,128)}, f32[8,2048]{1,0:T(8,128)}, bf16[16,128,512]{2,1,0:T(8,128)(2,1)}, f32[16,8,512]{2,...) custom-call(bf16[2048,1024]{1,0:T(8,128)(2,1)} %h_ref.1, ...), custom_call_target="tpu_custom_call" | custom-call | flops 22000001024 | bytes 40000000 | tf_op jit(solution)/shard_map/project/pallas_call | solution.py:241
  49.1 9.7 %gates.1 = (bf16[2048,512]{1,0:T(8,128)(2,1)}, bf16[2048,512]{1,0:T(8,128)(2,1)}) custom-call(bf16[2048,1024]{1,0:T(8,128)(2,1)} %h_ref.1, bf16[1024,512]{1,0:T(8,128)(2,1)} %get-tuple-element.49.wf_ref, bf16[1024,512]{1,0:T(8,128)(2,1)} %get-tuple-element.50.wr_ref), custom_call_target="tpu_custom_call" | custom-call | flops 10000000000 | bytes 10000000 | tf_op jit(solution)/shard_map/gates/pallas_call | solution.py:267
  59.0 1.3 pad_maximum_fusion
  60.8 1.6 %collective-permute-start.7 = (bf16[144,512]{1,0:T(8,128)(2,1)S(1)}, bf16[144,512]{1,0:T(8,128)(2,1)S(1)}, u32[]{:S(2)}, u32[]{:S(2)}) collective-permute-start(bf16[144,512]{1,0:T(8,128)(2,1)S(1)} %get-tuple-element.102), channel_id=1, source_target_pairs={{0,16},{4,20},{8,24},{12,28},{16,0},{20,4},{24,8},{28,12},{1,17},{... | collective-permute-start | bytes 442376 | tf_op jit(solution)/shard_map/ppermute | solution.py:473
  64.3 7.1 %inside.2 = (bf16[1024,512]{1,0:T(8,128)(2,1)}, bf16[1024,512]{1,0:T(8,128)(2,1)}) custom-call(bf16[2048,768]{1,0:T(8,128)(2,1)} %get-tuple-element.73.actf_ref.refs_0_, f32[2048,128]{1,0:T(8,128)} %get-tuple-element.56.smallf_ref.refs_4_, f32[8,2048]{1,0:T(8,128)} %get-tuple-element.61.cumtf_ref, bf16[2048,768]{1,0:T(8,128)(2,1)} %get-tuple-element.74.actr_ref.refs_5_, ...), custom_call_target="tpu_custom_call" | custom-call | flops 8000000000 | bytes 1000000 | tf_op jit(solution)/shard_map/inside/pallas_call | solution.py:318
  72.5 7.3 %finish.2 = bf16[1024,512]{1,0:T(8,128)(2,1)} custom-call(bf16[2048,768]{1,0:T(8,128)(2,1)} %get-tuple-element.73.actf_ref.refs_0_, bf16[2048,512]{1,0:T(8,128)(2,1)} %get-tuple-element.53.refs_1_, bf16[16,128,512]{2,1,0:T(8,128)(2,1)} %get-tuple-element.54.refs_2_, f32[16,8,512]{2,1,0:T(8,128)} %get-tuple-element.55.refs_3_, ...), custom_call_target="tpu_custom_call" | custom-call | flops 100000000 | bytes 1000000 | tf_op jit(solution)/shard_map/finish/pallas_call | solution.py:366
  79.7 1.3 constant_dynamic-slice_fusion.3
  81.3 3.5 %collective-permute-start.11 = (bf16[256,512]{1,0:T(8,128)(2,1)S(1)}, bf16[256,512]{1,0:T(8,128)(2,1)S(1)}, u32[]{:S(2)}, u32[]{:S(2)}) collective-permute-start(bf16[256,512]{1,0:T(8,128)(2,1)S(1)} %get-tuple-element.99), channel_id=1, source_target_pairs={{0,2},{1,3},{2,0},{3,1},{4,6},{5,7},{6,4},{7,5},{8,10},{9,11},{10,... | collective-permute-start | bytes 786440 | tf_op jit(solution)/shard_map/ppermute | solution.py:485
  84.8 7.1 %inside.3 = (bf16[1024,512]{1,0:T(8,128)(2,1)}, bf16[1024,512]{1,0:T(8,128)(2,1)}) custom-call(bf16[2048,768]{1,0:T(8,128)(2,1)} %get-tuple-element.73.actf_ref.refs_0_, f32[2048,128]{1,0:T(8,128)} %get-tuple-element.56.smallf_ref.refs_4_, f32[8,2048]{1,0:T(8,128)} %get-tuple-element.61.cumtf_ref, bf16[2048,768]{1,0:T(8,128)(2,1)} %get-tuple-element.74.actr_ref.refs_5_, ...), custom_call_target="tpu_custom_call" | custom-call | flops 100000000 | bytes 1000000 | tf_op jit(solution)/shard_map/inside/pallas_call | solution.py:318
  91.8 7.0 %finish.3 = bf16[1024,512]{1,0:T(8,128)(2,1)} custom-call(bf16[2048,768]{1,0:T(8,128)(2,1)} %get-tuple-element.73.actf_ref.refs_0_, bf16[2048,512]{1,0:T(8,128)(2,1)} %get-tuple-element.53.refs_1_, bf16[16,128,512]{2,1,0:T(8,128)(2,1)} %get-tuple-element.54.refs_2_, f32[16,8,512]{2,1,0:T(8,128)} %get-tuple-element.55.refs_3_, ...), custom_call_target="tpu_custom_call" | custom-call | flops 100000000 | bytes 1000000 | tf_op jit(solution)/shard_map/finish/pallas_call | solution.py:366
  98.9 1.7 %broadcast_select_fusion.5 = (bf16[256,1024]{1,0:T(8,128)(2,1)S(1)}, bf16[256,1024]{1,0:T(8,128)(2,1)S(1)}, bf16[256,1024]{1,0:T(8,128)(2,1)S(1)}, bf16[256,1024...) fusion(bf16[256,1024]{1,0:T(8,128)(2,1)S(1)} %collective-permute-done.3, ...), kind=kLoop, calls=%fused_computation.25 | loop fusion | flops 1572864 | bytes 6291457 | tf_op jit(solution)/shard_map/jit(_where)/select_n | solution.py:541
  100.6 2.5 %collective-permute-done.11 = bf16[256,512]{1,0:T(8,128)(2,1)S(1)} collective-permute-done((bf16[256,512]{1,0:T(8,128)(2,1)S(1)}, bf16[256,512]{1,0:T(8,128)(2,1)S(1)}, u32[]{:S(2)}, u32[]{:S(2)}) %collective-permute-start.11) | collective-permute-done | bytes 262176 | tf_op jit(solution)/shard_map/ppermute | solution.py:485
  103.1 3.4 %collective-permute-done.12 = bf16[256,512]{1,0:T(8,128)(2,1)S(1)} collective-permute-done((bf16[256,512]{1,0:T(8,128)(2,1)S(1)}, bf16[256,512]{1,0:T(8,128)(2,1)S(1)}, u32[]{:S(2)}, u32[]{:S(2)}) %collective-permute-start.12) | collective-permute-done | bytes 262176 | tf_op jit(solution)/shard_map/ppermute | solution.py:485
  110.1 1.6 %fusion.5 = bf16[256,1024]{1,0:T(8,128)(2,1)S(1)} fusion(f32[256,1024]{1,0:T(8,128)S(1)} %fusion.8, f32[256,1024]{1,0:T(8,128)S(1)} %fusion.10, f32[256,1024]{1,0:T(8,128)S(1)} %fusion.11, bf16[256,512]{1,0:T(8,128)(2,1)S(1)} %get-tuple-element.77, bf16[512,1024]{1,0:T(8,128)(2,1)S(1)} %copy-done, bf16[2048,1024]{1,0:T(8,128)(2,1)} %h_ref.1, s32[]{:T(128)S(6)} %select_n.110), kind=kOutput, calls=%fused_computation.9 | convolution fusion | flops 270008320 | bytes 5505028 | tf_op jit(solution)/shard_map/dot_general | solution.py:546
  111.7 1.5 %convolution_add_fusion.1 = f32[256,1024]{1,0:T(8,128)S(1)} fusion(bf16[512,1024]{1,0:T(8,128)(2,1)S(1)} %copy-done, bf16[2048,1024]{1,0:T(8,128)(2,1)} %h_ref.1, s32[]{:T(128)S(6)} %add.125, bf16[1024,512]{1,0:T(8,128)(2,1)S(1)} %copy-done.3, s32[]{:T(128)S(6)} %select_n.120), kind=kOutput, calls=%fused_computation.4 | convolution fusion | flops 268959744 | bytes 2883592 | tf_op jit(solution)/shard_map/dot_general | solution.py:546
  113.2 10.4 %collective-permute-done.14 = bf16[256,512]{1,0:T(8,128)(2,1)S(1)} collective-permute-done((bf16[256,512]{1,0:T(8,128)(2,1)S(1)}, bf16[256,512]{1,0:T(8,128)(2,1)S(1)}, u32[]{:S(2)}, u32[]{:S(2)}) %collective-permute-start.14) | collective-permute-done | bytes 262176 | tf_op jit(solution)/shard_map/ppermute | solution.py:485
  124.1 4.9 %collective-permute-done.15 = bf16[256,512]{1,0:T(8,128)(2,1)S(1)} collective-permute-done((bf16[256,512]{1,0:T(8,128)(2,1)S(1)}, bf16[256,512]{1,0:T(8,128)(2,1)S(1)}, u32[]{:S(2)}, u32[]{:S(2)}) %collective-permute-start.15) | collective-permute-done | bytes 262176 | tf_op jit(solution)/shard_map/ppermute | solution.py:485
  (52 shorter events, 12.1 us)
Async XLA Ops:
  0.0 1.2 copy-start
  1.3 57.7 %collective-permute-start.3 = (bf16[256,1024]{1,0:T(8,128)(2,1)S(1)}, bf16[256,1024]{1,0:T(8,128)(2,1)S(1)}, u32[]{:S(2)}, u32[]{:S(2)}) collective-permute-start(bf16[256,1024]{1,0:T(8,128)(2,1)S(1)} %constant_dynamic-slice_fusion.9), channel_id=1, source_target_pairs={{0,1},{1,2},{2,3},{3,0},{4,5},{5,6},{6,7},{7,4},{8,9},{9,10},{10,1... | collective-permute-start | bytes 1572872 | tf_op jit(solution)/shard_map/ppermute | solution.py:485
  2.9 56.1 %collective-permute-start.4 = (bf16[256,1024]{1,0:T(8,128)(2,1)S(1)}, bf16[256,1024]{1,0:T(8,128)(2,1)S(1)}, u32[]{:S(2)}, u32[]{:S(2)}) collective-permute-start(bf16[256,1024]{1,0:T(8,128)(2,1)S(1)} %constant_dynamic-slice_fusion.9), channel_id=1, source_target_pairs={{0,2},{1,3},{2,0},{3,1},{4,6},{5,7},{6,4},{7,5},{8,10},{9,11},{10,... | collective-permute-start | bytes 1572872 | tf_op jit(solution)/shard_map/ppermute | solution.py:485
  4.1 54.9 %collective-permute-start.5 = (bf16[256,1024]{1,0:T(8,128)(2,1)S(1)}, bf16[256,1024]{1,0:T(8,128)(2,1)S(1)}, u32[]{:S(2)}, u32[]{:S(2)}) collective-permute-start(bf16[256,1024]{1,0:T(8,128)(2,1)S(1)} %constant_dynamic-slice_fusion.9), channel_id=1, source_target_pairs={{0,3},{1,0},{2,1},{3,2},{4,7},{5,4},{6,5},{7,6},{8,11},{9,8},{10,9... | collective-permute-start | bytes 1572872 | tf_op jit(solution)/shard_map/ppermute | solution.py:485
  6.7 11.9 %collective-permute-start = (bf16[16,1024]{1,0:T(8,128)(2,1)S(1)}, bf16[16,1024]{1,0:T(8,128)(2,1)S(1)}, u32[]{:S(2)}, u32[]{:S(2)}) collective-permute-start(bf16[16,1024]{1,0:T(8,128)(2,1)S(1)} %get-tuple-element.84), channel_id=1, source_target_pairs={{0,4},{4,8},{8,12},{12,16},{16,20},{20,24},{24,28},{1,5},{5,9},{9,... | collective-permute-start | bytes 98312 | tf_op jit(solution)/shard_map/ppermute | solution.py:481
  8.6 10.0 %collective-permute-start.1 = (bf16[16,1024]{1,0:T(8,128)(2,1)S(1)}, bf16[16,1024]{1,0:T(8,128)(2,1)S(1)}, u32[]{:S(2)}, u32[]{:S(2)}) collective-permute-start(bf16[16,1024]{1,0:T(8,128)(2,1)S(1)} %get-tuple-element.83), channel_id=1, source_target_pairs={{4,0},{8,4},{12,8},{16,12},{20,16},{24,20},{28,24},{5,1},{9,5},{13... | collective-permute-start | bytes 98312 | tf_op jit(solution)/shard_map/ppermute | solution.py:481
  12.3 5.7 %copy-start.4 = (f32[8]{0:T(128)S(1)}, f32[8]{0:T(128)}, u32[]{:S(2)}) copy-start(f32[8]{0:T(128)} %param.20) | copy-start | bytes 100
  12.3 5.7 %copy-start.5 = (f32[8]{0:T(128)S(1)}, f32[8]{0:T(128)}, u32[]{:S(2)}) copy-start(f32[8]{0:T(128)} %param.19) | copy-start | bytes 100
  12.3 5.7 %copy-start.6 = (f32[8]{0:T(128)S(1)}, f32[8]{0:T(128)}, u32[]{:S(2)}) copy-start(f32[8]{0:T(128)} %param.18) | copy-start | bytes 100
  18.6 0.6 copy-start.8
  49.0 9.8 %collective-permute-start.2 = (bf16[288,512]{1,0:T(8,128)(2,1)}, bf16[288,512]{1,0:T(8,128)(2,1)S(1)}, u32[]{:S(2)}, u32[]{:S(2)}) collective-permute-start(bf16[288,512]{1,0:T(8,128)(2,1)} %get-tuple-element.48.refs_1_), channel_id=1, source_target_pairs={{0,4},{4,0},{8,12},{12,8},{16,20},{20,16},{24,28},{28,24},{1,5},{5... | collective-permute-start | bytes 884744 | tf_op jit(solution)/shard_map/ppermute | solution.py:454
  49.1 9.7 %copy-start.2 = (bf16[288,512]{1,0:T(8,128)(2,1)S(1)}, bf16[288,512]{1,0:T(8,128)(2,1)}, u32[]{:S(2)}) copy-start(bf16[288,512]{1,0:T(8,128)(2,1)} %get-tuple-element.48.refs_1_) | copy-start | bytes 884740
  60.3 12.2 %collective-permute-start.9 = (bf16[768,1024]{1,0:T(8,128)(2,1)}, bf16[768,1024]{1,0:T(8,128)(2,1)}, u32[]{:S(2)}, u32[]{:S(2)}) collective-permute-start(bf16[768,1024]{1,0:T(8,128)(2,1)} %pad_maximum_fusion), channel_id=1, source_target_pairs={{0,4},{4,0},{8,12},{12,8},{16,20},{20,16},{24,28},{28,24},{1,5},{5... | collective-permute-start | bytes 4718600 | tf_op jit(solution)/shard_map/ppermute | solution.py:519
  60.8 10.6 %collective-permute-start.7 = (bf16[144,512]{1,0:T(8,128)(2,1)S(1)}, bf16[144,512]{1,0:T(8,128)(2,1)S(1)}, u32[]{:S(2)}, u32[]{:S(2)}) collective-permute-start(bf16[144,512]{1,0:T(8,128)(2,1)S(1)} %get-tuple-element.102), channel_id=1, source_target_pairs={{0,16},{4,20},{8,24},{12,28},{16,0},{20,4},{24,8},{28,12},{1,17},{... | collective-permute-start | bytes 442376 | tf_op jit(solution)/shard_map/ppermute | solution.py:473
  62.4 9.1 %collective-permute-start.8 = (bf16[144,512]{1,0:T(8,128)(2,1)S(1)}, bf16[144,512]{1,0:T(8,128)(2,1)S(1)}, u32[]{:S(2)}, u32[]{:S(2)}) collective-permute-start(bf16[144,512]{1,0:T(8,128)(2,1)S(1)} %get-tuple-element.102), channel_id=1, source_target_pairs={{0,24},{4,28},{8,16},{12,20},{16,8},{20,12},{24,0},{28,4},{1,25},{... | collective-permute-start | bytes 442376 | tf_op jit(solution)/shard_map/ppermute | solution.py:473
  63.3 8.1 %collective-permute-start.6 = (bf16[144,512]{1,0:T(8,128)(2,1)S(1)}, bf16[144,512]{1,0:T(8,128)(2,1)S(1)}, u32[]{:S(2)}, u32[]{:S(2)}) collective-permute-start(bf16[144,512]{1,0:T(8,128)(2,1)S(1)} %get-tuple-element.103), channel_id=1, source_target_pairs={{0,8},{4,12},{8,0},{12,4},{16,24},{20,28},{24,16},{28,20},{1,9},{5... | collective-permute-start | bytes 442376 | tf_op jit(solution)/shard_map/ppermute | solution.py:473
  71.7 0.8 copy-start.1
  81.0 19.6 %collective-permute-start.10 = (bf16[256,512]{1,0:T(8,128)(2,1)S(1)}, bf16[256,512]{1,0:T(8,128)(2,1)S(1)}, u32[]{:S(2)}, u32[]{:S(2)}) collective-permute-start(bf16[256,512]{1,0:T(8,128)(2,1)S(1)} %get-tuple-element.100), channel_id=1, source_target_pairs={{0,1},{1,2},{2,3},{3,0},{4,5},{5,6},{6,7},{7,4},{8,9},{9,10},{10,1... | collective-permute-start | bytes 786440 | tf_op jit(solution)/shard_map/ppermute | solution.py:485
  81.3 21.8 %collective-permute-start.11 = (bf16[256,512]{1,0:T(8,128)(2,1)S(1)}, bf16[256,512]{1,0:T(8,128)(2,1)S(1)}, u32[]{:S(2)}, u32[]{:S(2)}) collective-permute-start(bf16[256,512]{1,0:T(8,128)(2,1)S(1)} %get-tuple-element.99), channel_id=1, source_target_pairs={{0,2},{1,3},{2,0},{3,1},{4,6},{5,7},{6,4},{7,5},{8,10},{9,11},{10,... | collective-permute-start | bytes 786440 | tf_op jit(solution)/shard_map/ppermute | solution.py:485
  84.8 21.8 %collective-permute-start.12 = (bf16[256,512]{1,0:T(8,128)(2,1)S(1)}, bf16[256,512]{1,0:T(8,128)(2,1)S(1)}, u32[]{:S(2)}, u32[]{:S(2)}) collective-permute-start(bf16[256,512]{1,0:T(8,128)(2,1)S(1)} %get-tuple-element.98), channel_id=1, source_target_pairs={{0,3},{1,0},{2,1},{3,2},{4,7},{5,4},{6,5},{7,6},{8,11},{9,8},{10,9... | collective-permute-start | bytes 786440 | tf_op jit(solution)/shard_map/ppermute | solution.py:485
  98.9 7.7 %copy-start.3 = (bf16[1024,512]{1,0:T(8,128)(2,1)S(1)}, bf16[1024,512]{1,0:T(8,128)(2,1)}, u32[]{:S(2)}) copy-start(bf16[1024,512]{1,0:T(8,128)(2,1)} %finish.3) | copy-start | bytes 3145732
  106.6 17.1 %collective-permute-start.14 = (bf16[256,512]{1,0:T(8,128)(2,1)S(1)}, bf16[256,512]{1,0:T(8,128)(2,1)S(1)}, u32[]{:S(2)}, u32[]{:S(2)}) collective-permute-start(bf16[256,512]{1,0:T(8,128)(2,1)S(1)} %get-tuple-element.97), channel_id=1, source_target_pairs={{0,2},{1,3},{2,0},{3,1},{4,6},{5,7},{6,4},{7,5},{8,10},{9,11},{10,... | collective-permute-start | bytes 786440 | tf_op jit(solution)/shard_map/ppermute | solution.py:485
  106.7 22.3 %collective-permute-start.15 = (bf16[256,512]{1,0:T(8,128)(2,1)S(1)}, bf16[256,512]{1,0:T(8,128)(2,1)S(1)}, u32[]{:S(2)}, u32[]{:S(2)}) collective-permute-start(bf16[256,512]{1,0:T(8,128)(2,1)S(1)} %get-tuple-element.96), channel_id=1, source_target_pairs={{0,3},{1,0},{2,1},{3,2},{4,7},{5,4},{6,5},{7,6},{8,11},{9,8},{10,9... | collective-permute-start | bytes 786440 | tf_op jit(solution)/shard_map/ppermute | solution.py:485
  107.7 21.8 %collective-permute-start.13 = (bf16[256,512]{1,0:T(8,128)(2,1)S(1)}, bf16[256,512]{1,0:T(8,128)(2,1)S(1)}, u32[]{:S(2)}, u32[]{:S(2)}) collective-permute-start(bf16[256,512]{1,0:T(8,128)(2,1)S(1)} %get-tuple-element.95), channel_id=1, source_target_pairs={{0,1},{1,2},{2,3},{3,0},{4,5},{5,6},{6,7},{7,4},{8,9},{9,10},{10,1... | collective-permute-start | bytes 786440 | tf_op jit(solution)/shard_map/ppermute | solution.py:485
  (1 other events, 0.6 us)

commit v3 on v2

--- a/solution.py
+++ b/solution.py
@@ -260,18 +260,17 @@
         z_ref[...] = (jnp.dot(h, w_ref[...], preferred_element_type=F32) * scale).astype(BF16)
 
 
-def gates(hidden, w_f, w_r):
-    rows, depth = hidden.shape
+def gates(tile, blocks, hidden, w_f, w_r, work):
+    count, at = blocks
     inner = w_f.shape[1]
-    by_rows = lambda width: pl.BlockSpec((TILE, width), lambda i: (i, 0))
     return pl.pallas_call(
         gates_kernel,
-        grid=(rows // TILE,),
-        in_specs=[by_rows(depth), whole(w_f.shape), whole(w_r.shape)],
-        out_specs=[by_rows(inner)] * 2,
-        out_shape=[jax.ShapeDtypeStruct((rows, inner), BF16)] * 2,
+        grid=(count,),
+        in_specs=[pl.BlockSpec((tile, hidden.shape[1]), lambda i: (at(i), 0)), whole(w_f.shape), whole(w_r.shape)],
+        out_specs=[pl.BlockSpec((tile, inner), lambda i: (i, 0))] * 2,
+        out_shape=[jax.ShapeDtypeStruct((count * tile, inner), BF16)] * 2,
         compiler_params=params(58),
-        cost_estimate=cost(10e9, 10e6),
+        cost_estimate=cost(work, 1e6),
         name="gates",
     )(hidden, w_f, w_r)
 
@@ -360,7 +359,7 @@
     last = strands[0][0].shape[1] // STATE - 1
     by_rows = lambda width: pl.BlockSpec((tile, width), lambda i: (at(i), 0))
     in_order = pl.BlockSpec((tile, inner), lambda i: (i, 0))
-    one = [pl.BlockSpec((tile, STATE), lambda i: (at(i), last)), by_rows(inner),
+    one = [pl.BlockSpec((tile, STATE), lambda i: (at(i), last)), in_order,
            pl.BlockSpec((per, STATE, inner), lambda i: (at(i), 0, 0)),
            pl.BlockSpec((per, 8, inner), lambda i: (at(i), 0, 0)), by_rows(128)]
     return pl.pallas_call(
@@ -373,6 +372,39 @@
         cost_estimate=cost(1e8, 1e6),
         name="finish",
     )(*strands[0], *strands[1], *bases, entering, copy)
+
+
+def settle_kernel(heads, inner, *refs):
+    (actf_ref, smallf_ref, cumtf_ref, actr_ref, smallr_ref, cumtr_ref, lanes_ref, first_ref,
+     zf_ref, ef_ref, pf_ref, zr_ref, er_ref, pr_ref, in_ref, second_ref, out_ref, basef, baser) = refs
+    inside_kernel(heads, inner, actf_ref, smallf_ref, cumtf_ref, actr_ref, smallr_ref, cumtr_ref, lanes_ref, first_ref,
+                  basef, baser)
+    maps = [ref.at[:, pl.ds(inner + STATE, STATE)] for ref in (actf_ref, actr_ref)]
+    finish_kernel(heads, inner, maps[0], zf_ref, ef_ref, pf_ref, smallf_ref, maps[1], zr_ref, er_ref, pr_ref, smallr_ref,
+                  basef, baser, in_ref, second_ref, out_ref)
+
+
+def settle(tile, blocks, strands, ends, lanes, first, entering, second, heads, inner):
+    count, at = blocks
+    per = tile // CHUNK
+    columns = strands[0][0].shape[1]
+    by_rows = lambda width: pl.BlockSpec((tile, width), lambda i: (at(i), 0))
+    in_order = pl.BlockSpec((tile, inner), lambda i: (i, 0))
+    one = [by_rows(columns), by_rows(128), pl.BlockSpec((heads, tile), lambda i: (0, at(i)))]
+    two = [in_order, pl.BlockSpec((per, STATE, inner), lambda i: (at(i), 0, 0)),
+           pl.BlockSpec((per, 8, inner), lambda i: (at(i), 0, 0))]
+    return pl.pallas_call(
+        functools.partial(settle_kernel, heads, inner),
+        grid=(count,),
+        in_specs=one + one + [whole(lanes.shape), whole(first.shape)] + two + two
+        + [whole((2, STATE, inner)), whole(second.shape)],
+        out_specs=in_order,
+        out_shape=jax.ShapeDtypeStruct((count * tile, inner), BF16),
+        scratch_shapes=[pltpu.VMEM((tile, inner), BF16)] * 2,
+        compiler_params=params(58),
+        cost_estimate=cost(1e8, 1e6),
+        name="settle",
+    )(*strands[0], *strands[1], lanes, first, *ends[0], *ends[1], entering, second)
 
 
 def read_message(ref, at):
@@ -509,13 +541,17 @@
     copy_second = spread_matrix(heads, heads, width)
     (act_f, small_f, cumt_f, enter_f, prior_f, act_r, small_r, cumt_r, enter_r, prior_r,
      message) = project(hidden, rim_f, rim_r, w_f, w_r, conv_x, conv_bc, lanes, copy_first, heads, inner)
-    entering, (z_f, z_r), same = incoming(message, "ctx", gates(hidden, g_f, g_r), same)
-
     share = rows // n_head
     pieces = 2 if share % (2 * CHUNK) == 0 else 1
     size = share // pieces
     tile = min(TILE, size)
     inner_blocks, share_blocks = size // tile, share // tile
+
+    def piece(k):
+        return (n_head * inner_blocks,
+                lambda i: (i // inner_blocks) * share_blocks + k * inner_blocks + i % inner_blocks)
+
+    entering, (z_f, z_r), same = incoming(message, "ctx", gates(tile, piece(0), hidden, g_f, g_r, 5e9), same)
     other = lax.ppermute(jnp.concatenate(same, axis=0), "ctx", [(i, i ^ 1) for i in range(n_ctx)])
     entering, other = lax.optimization_barrier((entering, other))
     other = [other[i * half : (i + 1) * half] for i in range(n_head - 1)]
@@ -525,14 +561,18 @@
 
     combined = None
     for k in range(pieces):
-        blocks = (n_head * inner_blocks,
-                  lambda i, k=k: (i // inner_blocks) * share_blocks + k * inner_blocks + i % inner_blocks)
-        if combined is not None:
-            act_f, act_r, combined = lax.optimization_barrier((act_f, act_r, combined))
-        bases = inside(tile, blocks, ((act_f, small_f, cumt_f), (act_r, small_r, cumt_r)), lanes, copy_first, heads, inner,
-                       1e8 if k else 8e9)
-        combined = finish(tile, blocks, ((act_f, z_f, enter_f, prior_f, small_f), (act_r, z_r, enter_r, prior_r, small_r)),
-                          bases, entering, copy_second, heads, inner)
+        if k == 0:
+            bases = inside(tile, piece(k), ((act_f, small_f, cumt_f), (act_r, small_r, cumt_r)), lanes, copy_first,
+                           heads, inner, 8e9)
+            combined = finish(tile, piece(k), ((act_f, z_f, enter_f, prior_f, small_f),
+                                               (act_r, z_r, enter_r, prior_r, small_r)),
+                              bases, entering, copy_second, heads, inner)
+        else:
+            g_f, g_r, combined = lax.optimization_barrier((g_f, g_r, combined))
+            z_f, z_r = gates(tile, piece(k), hidden, g_f, g_r, 1e8)
+            combined = settle(tile, piece(k), ((act_f, small_f, cumt_f), (act_r, small_r, cumt_r)),
+                              ((z_f, enter_f, prior_f), (z_r, enter_r, prior_r)), lanes, copy_first, entering, copy_second,
+                              heads, inner)
         if k:
             combined, *arrived[k - 1] = lax.optimization_barrier((combined, *arrived[k - 1]))
         parts = [lax.dynamic_slice_in_dim(combined, ((head + d) % n_head) * size, size, 0) for d in range(n_head)]

time: 133 us -> 130 us (0.977)
  waiting for transfers between devices: 21.3 us -> 16.4 us
  matrix products: 5.78 us -> 8.57 us
  Pallas kernels: 73.9 us -> 72.3 us
    pallas_call x1 -> x3, Pallas kernels: 9.66 us -> 22.2 us  [the longest x2 11.7 us: gates(): pl.pallas_call(gates_kernel, grid=(count,), in_specs=[pl.BlockSpec((tile,...]
    pallas_call x2 -> x1, Pallas kernels: 14.1 us -> 7.1 us  [inside(): pl.pallas_call(functools.partial(inside_kernel, heads, inner), grid=(coun...]
    pallas_call x2 -> x1, Pallas kernels: 14.3 us -> 7.27 us  [finish(): pl.pallas_call(functools.partial(finish_kernel, heads, inner), grid=(coun...]
    ppermute x9, waiting for transfers between devices: 21.3 us -> 16.3 us  [rotated(): lax.ppermute(block, 'head', [(i, (i + d) % count) for i in range(count)])]
    dot_general x8, matrix products: 5.78 us -> 8.57 us  [on_device(): total = total + jnp.dot(block, weights, preferred_element_type=F32)]
  transfers between devices with their start and end apart: 16 -> 16, of which waited for: 4 -> 4; matrix products, arithmetic and copies ran while one was open for 6% -> 9% of each run, Pallas kernels for 51% -> 51%
where the time goes in v3:
time: 130 us; the launch traced here: 128 us
  Pallas kernels  72.3 us (56%)
  starting transfers between devices  20.2 us (16%)
  waiting for transfers between devices  16.4 us (13%)
  matrix products  8.57 us (7%)
  local copies, waits for them, and re-layouts  5.55 us (4%)
  other arithmetic  4.58 us (4%)
    pallas_call x1, Pallas kernels, project(): pl.pallas_call(functools.partial(project_kernel, heads, inner), grid=(n,)...  29.7 us
    ppermute x9, waiting for transfers between devices, rotated(): lax.ppermute(block, 'head', [(i, (i + d) % count) for i in range(count)])  16.3 us
    pallas_call x2, Pallas kernels, gates(): pl.pallas_call(gates_kernel, grid=(count,), in_specs=[pl.BlockSpec((tile,...  11.7 us
    ppermute x9, starting transfers between devices, rotated(): lax.ppermute(block, 'head', [(i, (i + d) % count) for i in range(count)])  10.5 us
    pallas_call x1, Pallas kernels, settle(): pl.pallas_call(functools.partial(settle_kernel, heads, inner), grid=(coun...  10.5 us
    dot_general x8, matrix products, on_device(): total = total + jnp.dot(block, weights, preferred_element_type=F32)  8.57 us
    pallas_call x1, Pallas kernels, finish(): pl.pallas_call(functools.partial(finish_kernel, heads, inner), grid=(coun...  7.27 us
    pallas_call x1, Pallas kernels, inside(): pl.pallas_call(functools.partial(inside_kernel, heads, inner), grid=(coun...  7.1 us
  transfers between devices with their start and end apart: 16, of which 4 were waited for; matrix products, arithmetic and copies ran while one was open for 9% of the time, Pallas kernels for 51%

profile of v3, /device:TPU:10, one launch (start us, length us, event | category | flops | bytes accessed | tf_op | source)
XLA Modules:
  0.0 127.8 jit_solution(7903947257510247539)
XLA Ops:
  1.3 1.6 %collective-permute-start.3 = (bf16[256,1024]{1,0:T(8,128)(2,1)S(1)}, bf16[256,1024]{1,0:T(8,128)(2,1)S(1)}, u32[]{:S(2)}, u32[]{:S(2)}) collective-permute-start(bf16[256,1024]{1,0:T(8,128)(2,1)S(1)} %constant_dynamic-slice_fusion.9), channel_id=1, source_target_pairs={{0,1},{1,2},{2,3},{3,0},{4,5},{5,6},{6,7},{7,4},{8,9},{9,10},{10,1... | collective-permute-start | bytes 1572872 | tf_op jit(solution)/shard_map/ppermute | solution.py:517
  4.1 1.8 %collective-permute-start.5 = (bf16[256,1024]{1,0:T(8,128)(2,1)S(1)}, bf16[256,1024]{1,0:T(8,128)(2,1)S(1)}, u32[]{:S(2)}, u32[]{:S(2)}) collective-permute-start(bf16[256,1024]{1,0:T(8,128)(2,1)S(1)} %constant_dynamic-slice_fusion.9), channel_id=1, source_target_pairs={{0,3},{1,0},{2,1},{3,2},{4,7},{5,4},{6,5},{7,6},{8,11},{9,8},{10,9... | collective-permute-start | bytes 1572872 | tf_op jit(solution)/shard_map/ppermute | solution.py:517
  6.7 1.9 %collective-permute-start = (bf16[16,1024]{1,0:T(8,128)(2,1)S(1)}, bf16[16,1024]{1,0:T(8,128)(2,1)S(1)}, u32[]{:S(2)}, u32[]{:S(2)}) collective-permute-start(bf16[16,1024]{1,0:T(8,128)(2,1)S(1)} %get-tuple-element.84), channel_id=1, source_target_pairs={{0,4},{4,8},{8,12},{12,16},{16,20},{20,24},{24,28},{1,5},{5,9},{9,... | collective-permute-start | bytes 98312 | tf_op jit(solution)/shard_map/ppermute | solution.py:513
  8.6 3.6 %collective-permute-start.1 = (bf16[16,1024]{1,0:T(8,128)(2,1)S(1)}, bf16[16,1024]{1,0:T(8,128)(2,1)S(1)}, u32[]{:S(2)}, u32[]{:S(2)}) collective-permute-start(bf16[16,1024]{1,0:T(8,128)(2,1)S(1)} %get-tuple-element.83), channel_id=1, source_target_pairs={{4,0},{8,4},{12,8},{16,12},{20,16},{24,20},{28,24},{5,1},{9,5},{13... | collective-permute-start | bytes 98312 | tf_op jit(solution)/shard_map/ppermute | solution.py:513
  12.3 5.7 %prepare.1 = (bf16[1024,896]{1,0:T(8,128)(2,1)}, bf16[1024,896]{1,0:T(8,128)(2,1)}, bf16[1024,512]{1,0:T(8,128)(2,1)}, bf16[1024,512]{1,0:T(8,128)(2,1)}) custom-call(bf16[1024,2,512]{2,1,0:T(2,128)(2,1)} %zx_ref.1, bf16[1024,256]{1,0:T(8,128)(2,1)} %bc_ref.1, bf16[8,1024]{1,0:T(8,128)(2,1)} %bitcast.19, f32[1,1024]{1,0:T(1,128)} %bitcast.20), custom_call_target="tpu_custom_call" | custom-call | flops 4000000000 | bytes 8000000 | tf_op jit(solution)/shard_map/prepare/pallas_call | solution.py:87
  19.2 29.7 %project.1 = (bf16[2048,768]{1,0:T(8,128)(2,1)}, f32[2048,128]{1,0:T(8,128)}, f32[8,2048]{1,0:T(8,128)}, bf16[16,128,512]{2,1,0:T(8,128)(2,1)}, f32[16,8,512]{2,...) custom-call(bf16[2048,1024]{1,0:T(8,128)(2,1)} %h_ref.3, ...), custom_call_target="tpu_custom_call" | custom-call | flops 22000001024 | bytes 40000000 | tf_op jit(solution)/shard_map/project/pallas_call | solution.py:241
  49.0 5.9 %gates.2 = (bf16[1024,512]{1,0:T(8,128)(2,1)}, bf16[1024,512]{1,0:T(8,128)(2,1)}) custom-call(bf16[2048,1024]{1,0:T(8,128)(2,1)} %h_ref.3, bf16[1024,512]{1,0:T(8,128)(2,1)} %get-tuple-element.73.wf_ref, bf16[1024,512]{1,0:T(8,128)(2,1)} %get-tuple-element.74.wr_ref), custom_call_target="tpu_custom_call" | custom-call | flops 5000000000 | bytes 1000000 | tf_op jit(solution)/shard_map/gates/pallas_call | solution.py:266
  55.1 1.3 %pad_maximum_fusion = bf16[768,1024]{1,0:T(8,128)(2,1)} fusion(bf16[256,1024]{1,0:T(8,128)(2,1)S(1)} %collective-permute-done.5, bf16[256,1024]{1,0:T(8,128)(2,1)S(1)} %collective-permute-done.4, bf16[256,1024]{1,0:T(8,128)(2,1)S(1)} %collective-permute-done.3), kind=kLoop, calls=%fused_computation | loop fusion | flops 4718592 | bytes 3145728 | tf_op jit(solution)/shard_map/concatenate | solution.py:555
  56.9 1.6 %collective-permute-start.7 = (bf16[144,512]{1,0:T(8,128)(2,1)S(1)}, bf16[144,512]{1,0:T(8,128)(2,1)S(1)}, u32[]{:S(2)}, u32[]{:S(2)}) collective-permute-start(bf16[144,512]{1,0:T(8,128)(2,1)S(1)} %get-tuple-element.102), channel_id=1, source_target_pairs={{0,16},{4,20},{8,24},{12,28},{16,0},{20,4},{24,8},{28,12},{1,17},{... | collective-permute-start | bytes 442376 | tf_op jit(solution)/shard_map/ppermute | solution.py:505
  60.4 7.1 %inside.1 = (bf16[1024,512]{1,0:T(8,128)(2,1)}, bf16[1024,512]{1,0:T(8,128)(2,1)}) custom-call(bf16[2048,768]{1,0:T(8,128)(2,1)} %get-tuple-element.46.actf_ref.refs_0_, f32[2048,128]{1,0:T(8,128)} %get-tuple-element.47.smallf_ref.refs_4_.refs_1_, f32[8,2048]{1,0:T(8,128)} %get-tuple-element.48.cumtf_ref.refs_2_, ...), custom_call_target="tpu_custom_call" | custom-call | flops 8000000000 | bytes 1000000 | tf_op jit(solution)/shard_map/inside/pallas_call | solution.py:317
  68.6 7.3 %finish.1 = bf16[1024,512]{1,0:T(8,128)(2,1)} custom-call(bf16[2048,768]{1,0:T(8,128)(2,1)} %get-tuple-element.46.actf_ref.refs_0_, bf16[1024,512]{1,0:T(8,128)(2,1)} %get-tuple-element.57.refs_1_, bf16[16,128,512]{2,1,0:T(8,128)(2,1)} %get-tuple-element.58.refs_2_.refs_9_, f32[16,8,512]{2,1,0:T(8,128)} %get-tuple-element.59.refs_3_.refs_10_, ...), custom_call_target="tpu_custom_call" | custom-call | flops 100000000 | bytes 1000000 | tf_op jit(solution)/shard_map/finish/pallas_call | solution.py:365
  75.9 2.0 %constant_dynamic-slice_fusion.3 = (bf16[256,512]{1,0:T(8,128)(2,1)S(1)}, bf16[256,512]{1,0:T(8,128)(2,1)S(1)}, bf16[256,512]{1,0:T(8,128)(2,1)}, bf16[256,512]{1,0:T(8,128)(2,1)S(1)}) fusion(bf16[1024,512]{1,0:T(8,128)(2,1)} %finish.1, s32[]{:T(128)S(6)} %select_n.126, s32[]{:T(128)S(6)} %select_n.124, s32[]{:T(128)S(6)} %select_n.122, s32[]{:T(128)S(6)} %select_n.120), kind=kLoop, calls=%fused_computation.30 | loop fusion | bytes 2097168 | tf_op jit(solution)/shard_map/dynamic_slice | solution.py:578
  78.1 3.5 %collective-permute-start.11 = (bf16[256,512]{1,0:T(8,128)(2,1)S(1)}, bf16[256,512]{1,0:T(8,128)(2,1)}, u32[]{:S(2)}, u32[]{:S(2)}) collective-permute-start(bf16[256,512]{1,0:T(8,128)(2,1)S(1)} %get-tuple-element.99), channel_id=1, source_target_pairs={{0,2},{1,3},{2,0},{3,1},{4,6},{5,7},{6,4},{7,5},{8,10},{9,11},{10,... | collective-permute-start | bytes 786440 | tf_op jit(solution)/shard_map/ppermute | solution.py:517
  81.5 5.8 %gates.3 = (bf16[1024,512]{1,0:T(8,128)(2,1)}, bf16[1024,512]{1,0:T(8,128)(2,1)}) custom-call(bf16[2048,1024]{1,0:T(8,128)(2,1)} %h_ref.3, bf16[1024,512]{1,0:T(8,128)(2,1)} %get-tuple-element.73.wf_ref, bf16[1024,512]{1,0:T(8,128)(2,1)} %get-tuple-element.74.wr_ref), custom_call_target="tpu_custom_call" | custom-call | flops 100000000 | bytes 1000000 | tf_op jit(solution)/shard_map/gates/pallas_call | solution.py:266
  87.4 10.5 %settle.1 = bf16[1024,512]{1,0:T(8,128)(2,1)} custom-call(bf16[2048,768]{1,0:T(8,128)(2,1)} %get-tuple-element.46.actf_ref.refs_0_, f32[2048,128]{1,0:T(8,128)} %get-tuple-element.47.smallf_ref.refs_4_.refs_1_, f32[8,2048]{1,0:T(8,128)} %get-tuple-element.48.cumtf_ref.refs_2_, bf16[2048,768]{1,0:T(8,128)(2,1)} %get-tuple-element.49.actr_ref.refs_5_.refs_3_, ...), custom_call_target="tpu_custom_call" | custom-call | flops 100000000 | bytes 1000000 | tf_op jit(solution)/shard_map/settle/pallas_call | solution.py:396
  97.9 1.7 %broadcast_select_fusion.5 = (bf16[256,1024]{1,0:T(8,128)(2,1)S(1)}, bf16[256,1024]{1,0:T(8,128)(2,1)S(1)}, bf16[256,1024]{1,0:T(8,128)(2,1)S(1)}, bf16[256,1024...) fusion(bf16[256,1024]{1,0:T(8,128)(2,1)S(1)} %collective-permute-done.3, ...), kind=kLoop, calls=%fused_computation.25 | loop fusion | flops 1572864 | bytes 6291457 | tf_op jit(solution)/shard_map/jit(_where)/select_n | solution.py:581
  100.1 3.5 %collective-permute-done.12 = bf16[256,512]{1,0:T(8,128)(2,1)} collective-permute-done((bf16[256,512]{1,0:T(8,128)(2,1)S(1)}, bf16[256,512]{1,0:T(8,128)(2,1)}, u32[]{:S(2)}, u32[]{:S(2)}) %collective-permute-start.12) | collective-permute-done | bytes 262176 | tf_op jit(solution)/shard_map/ppermute | solution.py:517
  105.8 1.4 %fusion.11 = f32[256,1024]{1,0:T(8,128)S(1)} fusion(bf16[256,512]{1,0:T(8,128)(2,1)} %collective-permute-done.10, bf16[256,1024]{1,0:T(8,128)(2,1)S(1)} %get-tuple-element.86, bf16[256,1024]{1,0:T(8,128)(2,1)S(1)} %get-tuple-element.85), kind=kOutput, calls=%fused_computation.19 | convolution fusion | flops 270532608 | bytes 2359296 | tf_op jit(solution)/shard_map/dot_general | solution.py:586
  107.2 1.4 %fusion.10 = f32[256,1024]{1,0:T(8,128)S(1)} fusion(bf16[256,512]{1,0:T(8,128)(2,1)} %collective-permute-done.11, bf16[256,1024]{1,0:T(8,128)(2,1)S(1)} %get-tuple-element.91, bf16[256,1024]{1,0:T(8,128)(2,1)S(1)} %get-tuple-element.92), kind=kOutput, calls=%fused_computation.18 | convolution fusion | flops 270532608 | bytes 2359296 | tf_op jit(solution)/shard_map/dot_general | solution.py:586
  108.6 1.4 %fusion.8 = f32[256,1024]{1,0:T(8,128)S(1)} fusion(bf16[256,512]{1,0:T(8,128)(2,1)} %collective-permute-done.12, bf16[256,1024]{1,0:T(8,128)(2,1)S(1)} %get-tuple-element.93, bf16[256,1024]{1,0:T(8,128)(2,1)S(1)} %get-tuple-element.94), kind=kOutput, calls=%fused_computation.16 | convolution fusion | flops 270532608 | bytes 2359296 | tf_op jit(solution)/shard_map/dot_general | solution.py:586
  110.0 1.6 %fusion.5 = bf16[256,1024]{1,0:T(8,128)(2,1)S(1)} fusion(f32[256,1024]{1,0:T(8,128)S(1)} %fusion.8, f32[256,1024]{1,0:T(8,128)S(1)} %fusion.10, f32[256,1024]{1,0:T(8,128)S(1)} %fusion.11, bf16[256,512]{1,0:T(8,128)(2,1)S(1)} %get-tuple-element.77, bf16[512,1024]{1,0:T(8,128)(2,1)S(1)} %copy-done, bf16[2048,1024]{1,0:T(8,128)(2,1)} %h_ref.3, s32[]{:T(128)S(6)} %select_n.110), kind=kOutput, calls=%fused_computation.9 | convolution fusion | flops 270008320 | bytes 5505028 | tf_op jit(solution)/shard_map/dot_general | solution.py:586
  111.5 1.5 %convolution_add_fusion.1 = f32[256,1024]{1,0:T(8,128)S(1)} fusion(bf16[512,1024]{1,0:T(8,128)(2,1)S(1)} %copy-done, bf16[2048,1024]{1,0:T(8,128)(2,1)} %h_ref.3, s32[]{:T(128)S(6)} %add.125, bf16[1024,512]{1,0:T(8,128)(2,1)S(1)} %copy-done.3, s32[]{:T(128)S(6)} %select_n.120), kind=kOutput, calls=%fused_computation.4 | convolution fusion | flops 268959744 | bytes 2883592 | tf_op jit(solution)/shard_map/dot_general | solution.py:586
  113.1 7.2 %collective-permute-done.14 = bf16[256,512]{1,0:T(8,128)(2,1)S(1)} collective-permute-done((bf16[256,512]{1,0:T(8,128)(2,1)S(1)}, bf16[256,512]{1,0:T(8,128)(2,1)S(1)}, u32[]{:S(2)}, u32[]{:S(2)}) %collective-permute-start.14) | collective-permute-done | bytes 262176 | tf_op jit(solution)/shard_map/ppermute | solution.py:517
  120.7 5.1 %collective-permute-done.15 = bf16[256,512]{1,0:T(8,128)(2,1)S(1)} collective-permute-done((bf16[256,512]{1,0:T(8,128)(2,1)S(1)}, bf16[256,512]{1,0:T(8,128)(2,1)S(1)}, u32[]{:S(2)}, u32[]{:S(2)}) %collective-permute-start.15) | collective-permute-done | bytes 262176 | tf_op jit(solution)/shard_map/ppermute | solution.py:517
  (52 shorter events, 13.7 us)
Async XLA Ops:
  0.0 1.2 copy-start
  1.3 53.8 %collective-permute-start.3 = (bf16[256,1024]{1,0:T(8,128)(2,1)S(1)}, bf16[256,1024]{1,0:T(8,128)(2,1)S(1)}, u32[]{:S(2)}, u32[]{:S(2)}) collective-permute-start(bf16[256,1024]{1,0:T(8,128)(2,1)S(1)} %constant_dynamic-slice_fusion.9), channel_id=1, source_target_pairs={{0,1},{1,2},{2,3},{3,0},{4,5},{5,6},{6,7},{7,4},{8,9},{9,10},{10,1... | collective-permute-start | bytes 1572872 | tf_op jit(solution)/shard_map/ppermute | solution.py:517
  2.9 52.2 %collective-permute-start.4 = (bf16[256,1024]{1,0:T(8,128)(2,1)S(1)}, bf16[256,1024]{1,0:T(8,128)(2,1)S(1)}, u32[]{:S(2)}, u32[]{:S(2)}) collective-permute-start(bf16[256,1024]{1,0:T(8,128)(2,1)S(1)} %constant_dynamic-slice_fusion.9), channel_id=1, source_target_pairs={{0,2},{1,3},{2,0},{3,1},{4,6},{5,7},{6,4},{7,5},{8,10},{9,11},{10,... | collective-permute-start | bytes 1572872 | tf_op jit(solution)/shard_map/ppermute | solution.py:517
  4.1 50.9 %collective-permute-start.5 = (bf16[256,1024]{1,0:T(8,128)(2,1)S(1)}, bf16[256,1024]{1,0:T(8,128)(2,1)S(1)}, u32[]{:S(2)}, u32[]{:S(2)}) collective-permute-start(bf16[256,1024]{1,0:T(8,128)(2,1)S(1)} %constant_dynamic-slice_fusion.9), channel_id=1, source_target_pairs={{0,3},{1,0},{2,1},{3,2},{4,7},{5,4},{6,5},{7,6},{8,11},{9,8},{10,9... | collective-permute-start | bytes 1572872 | tf_op jit(solution)/shard_map/ppermute | solution.py:517
  6.7 11.9 %collective-permute-start = (bf16[16,1024]{1,0:T(8,128)(2,1)S(1)}, bf16[16,1024]{1,0:T(8,128)(2,1)S(1)}, u32[]{:S(2)}, u32[]{:S(2)}) collective-permute-start(bf16[16,1024]{1,0:T(8,128)(2,1)S(1)} %get-tuple-element.84), channel_id=1, source_target_pairs={{0,4},{4,8},{8,12},{12,16},{16,20},{20,24},{24,28},{1,5},{5,9},{9,... | collective-permute-start | bytes 98312 | tf_op jit(solution)/shard_map/ppermute | solution.py:513
  8.6 10.0 %collective-permute-start.1 = (bf16[16,1024]{1,0:T(8,128)(2,1)S(1)}, bf16[16,1024]{1,0:T(8,128)(2,1)S(1)}, u32[]{:S(2)}, u32[]{:S(2)}) collective-permute-start(bf16[16,1024]{1,0:T(8,128)(2,1)S(1)} %get-tuple-element.83), channel_id=1, source_target_pairs={{4,0},{8,4},{12,8},{16,12},{20,16},{24,20},{28,24},{5,1},{9,5},{13... | collective-permute-start | bytes 98312 | tf_op jit(solution)/shard_map/ppermute | solution.py:513
  12.3 5.7 %copy-start.4 = (f32[8]{0:T(128)S(1)}, f32[8]{0:T(128)}, u32[]{:S(2)}) copy-start(f32[8]{0:T(128)} %param.20) | copy-start | bytes 100
  12.3 5.7 %copy-start.5 = (f32[8]{0:T(128)S(1)}, f32[8]{0:T(128)}, u32[]{:S(2)}) copy-start(f32[8]{0:T(128)} %param.19) | copy-start | bytes 100
  12.3 5.7 %copy-start.6 = (f32[8]{0:T(128)S(1)}, f32[8]{0:T(128)}, u32[]{:S(2)}) copy-start(f32[8]{0:T(128)} %param.18) | copy-start | bytes 100
  18.6 0.6 copy-start.8
  48.9 5.9 %collective-permute-start.2 = (bf16[288,512]{1,0:T(8,128)(2,1)}, bf16[288,512]{1,0:T(8,128)(2,1)S(1)}, u32[]{:S(2)}, u32[]{:S(2)}) collective-permute-start(bf16[288,512]{1,0:T(8,128)(2,1)} %get-tuple-element.54.refs_1_), channel_id=1, source_target_pairs={{0,4},{4,0},{8,12},{12,8},{16,20},{20,16},{24,28},{28,24},{1,5},{5... | collective-permute-start | bytes 884744 | tf_op jit(solution)/shard_map/ppermute | solution.py:486
  49.0 5.9 %copy-start.2 = (bf16[288,512]{1,0:T(8,128)(2,1)S(1)}, bf16[288,512]{1,0:T(8,128)(2,1)}, u32[]{:S(2)}) copy-start(bf16[288,512]{1,0:T(8,128)(2,1)} %get-tuple-element.54.refs_1_) | copy-start | bytes 884740
  56.4 12.2 %collective-permute-start.9 = (bf16[768,1024]{1,0:T(8,128)(2,1)}, bf16[768,1024]{1,0:T(8,128)(2,1)}, u32[]{:S(2)}, u32[]{:S(2)}) collective-permute-start(bf16[768,1024]{1,0:T(8,128)(2,1)} %pad_maximum_fusion), channel_id=1, source_target_pairs={{0,4},{4,0},{8,12},{12,8},{16,20},{20,16},{24,28},{28,24},{1,5},{5... | collective-permute-start | bytes 4718600 | tf_op jit(solution)/shard_map/ppermute | solution.py:555
  56.9 10.7 %collective-permute-start.7 = (bf16[144,512]{1,0:T(8,128)(2,1)S(1)}, bf16[144,512]{1,0:T(8,128)(2,1)S(1)}, u32[]{:S(2)}, u32[]{:S(2)}) collective-permute-start(bf16[144,512]{1,0:T(8,128)(2,1)S(1)} %get-tuple-element.102), channel_id=1, source_target_pairs={{0,16},{4,20},{8,24},{12,28},{16,0},{20,4},{24,8},{28,12},{1,17},{... | collective-permute-start | bytes 442376 | tf_op jit(solution)/shard_map/ppermute | solution.py:505
  58.4 9.1 %collective-permute-start.8 = (bf16[144,512]{1,0:T(8,128)(2,1)S(1)}, bf16[144,512]{1,0:T(8,128)(2,1)S(1)}, u32[]{:S(2)}, u32[]{:S(2)}) collective-permute-start(bf16[144,512]{1,0:T(8,128)(2,1)S(1)} %get-tuple-element.102), channel_id=1, source_target_pairs={{0,24},{4,28},{8,16},{12,20},{16,8},{20,12},{24,0},{28,4},{1,25},{... | collective-permute-start | bytes 442376 | tf_op jit(solution)/shard_map/ppermute | solution.py:505
  59.4 8.1 %collective-permute-start.6 = (bf16[144,512]{1,0:T(8,128)(2,1)S(1)}, bf16[144,512]{1,0:T(8,128)(2,1)S(1)}, u32[]{:S(2)}, u32[]{:S(2)}) collective-permute-start(bf16[144,512]{1,0:T(8,128)(2,1)S(1)} %get-tuple-element.103), channel_id=1, source_target_pairs={{0,8},{4,12},{8,0},{12,4},{16,24},{20,28},{24,16},{28,20},{1,9},{5... | collective-permute-start | bytes 442376 | tf_op jit(solution)/shard_map/ppermute | solution.py:505
  67.8 0.8 copy-start.1
  77.8 21.7 %collective-permute-start.10 = (bf16[256,512]{1,0:T(8,128)(2,1)}, bf16[256,512]{1,0:T(8,128)(2,1)}, u32[]{:S(2)}, u32[]{:S(2)}) collective-permute-start(bf16[256,512]{1,0:T(8,128)(2,1)} %get-tuple-element.100), channel_id=1, source_target_pairs={{0,1},{1,2},{2,3},{3,0},{4,5},{5,6},{6,7},{7,4},{8,9},{9,10},{10,1... | collective-permute-start | bytes 786440 | tf_op jit(solution)/shard_map/ppermute | solution.py:517
  78.1 22.1 %collective-permute-start.11 = (bf16[256,512]{1,0:T(8,128)(2,1)S(1)}, bf16[256,512]{1,0:T(8,128)(2,1)}, u32[]{:S(2)}, u32[]{:S(2)}) collective-permute-start(bf16[256,512]{1,0:T(8,128)(2,1)S(1)} %get-tuple-element.99), channel_id=1, source_target_pairs={{0,2},{1,3},{2,0},{3,1},{4,6},{5,7},{6,4},{7,5},{8,10},{9,11},{10,... | collective-permute-start | bytes 786440 | tf_op jit(solution)/shard_map/ppermute | solution.py:517
  81.5 22.0 %collective-permute-start.12 = (bf16[256,512]{1,0:T(8,128)(2,1)S(1)}, bf16[256,512]{1,0:T(8,128)(2,1)}, u32[]{:S(2)}, u32[]{:S(2)}) collective-permute-start(bf16[256,512]{1,0:T(8,128)(2,1)S(1)} %get-tuple-element.98), channel_id=1, source_target_pairs={{0,3},{1,0},{2,1},{3,2},{4,7},{5,4},{6,5},{7,6},{8,11},{9,8},{10,9... | collective-permute-start | bytes 786440 | tf_op jit(solution)/shard_map/ppermute | solution.py:517
  97.9 5.7 %copy-start.3 = (bf16[1024,512]{1,0:T(8,128)(2,1)S(1)}, bf16[1024,512]{1,0:T(8,128)(2,1)}, u32[]{:S(2)}) copy-start(bf16[1024,512]{1,0:T(8,128)(2,1)} %settle.1) | copy-start | bytes 3145732
  103.6 16.6 %collective-permute-start.14 = (bf16[256,512]{1,0:T(8,128)(2,1)S(1)}, bf16[256,512]{1,0:T(8,128)(2,1)S(1)}, u32[]{:S(2)}, u32[]{:S(2)}) collective-permute-start(bf16[256,512]{1,0:T(8,128)(2,1)S(1)} %get-tuple-element.97), channel_id=1, source_target_pairs={{0,2},{1,3},{2,0},{3,1},{4,6},{5,7},{6,4},{7,5},{8,10},{9,11},{10,... | collective-permute-start | bytes 786440 | tf_op jit(solution)/shard_map/ppermute | solution.py:517
  103.7 22.1 %collective-permute-start.15 = (bf16[256,512]{1,0:T(8,128)(2,1)S(1)}, bf16[256,512]{1,0:T(8,128)(2,1)S(1)}, u32[]{:S(2)}, u32[]{:S(2)}) collective-permute-start(bf16[256,512]{1,0:T(8,128)(2,1)S(1)} %get-tuple-element.96), channel_id=1, source_target_pairs={{0,3},{1,0},{2,1},{3,2},{4,7},{5,4},{6,5},{7,6},{8,11},{9,8},{10,9... | collective-permute-start | bytes 786440 | tf_op jit(solution)/shard_map/ppermute | solution.py:517
  104.6 21.7 %collective-permute-start.13 = (bf16[256,512]{1,0:T(8,128)(2,1)S(1)}, bf16[256,512]{1,0:T(8,128)(2,1)S(1)}, u32[]{:S(2)}, u32[]{:S(2)}) collective-permute-start(bf16[256,512]{1,0:T(8,128)(2,1)S(1)} %get-tuple-element.95), channel_id=1, source_target_pairs={{0,1},{1,2},{2,3},{3,0},{4,5},{5,6},{6,7},{7,4},{8,9},{9,10},{10,1... | collective-permute-start | bytes 786440 | tf_op jit(solution)/shard_map/ppermute | solution.py:517
  (1 other events, 0.6 us)

commit v4 on v2

--- a/solution.py
+++ b/solution.py
@@ -56,48 +56,29 @@
     return jnp.dot(jnp.concatenate([high, low], axis=1), matrix, preferred_element_type=F32)
 
 
-def prepare_kernel(inner, zx_ref, bc_ref, dt_ref, gain_ref, wf_ref, wr_ref, gf_ref, gr_ref):
-    rows = zx_ref.shape[0]
-    gain = jnp.transpose(jnp.broadcast_to(gain_ref[...], (128, rows)))
-    zx = zx_ref[...].astype(F32).reshape(rows, 2 * inner)
-    steps = dt_ref[...].astype(F32)
-    steps = jnp.transpose(jnp.concatenate([steps, jnp.zeros((128 - steps.shape[0], rows), F32)], axis=0))
+def prepare(inner, zx_ref, bc_ref, dt_ref, gain_ref, wf_ref, wr_ref, gf_ref, gr_ref):
+    depth = zx_ref.shape[0]
+    rows = min(256, depth)
     r = lax.broadcasted_iota(jnp.int32, (rows, rows), 0)
     c = lax.broadcasted_iota(jnp.int32, (rows, rows), 1)
     turn = (r + c == rows - 1).astype(BF16)
-
-    def put(part, at, forward_ref, turned_ref):
-        size = part.shape[1]
-        scaled = jnp.concatenate([part[:, g : g + 128] * gain for g in range(0, size, 128)], axis=1).astype(BF16)
-        forward_ref[:, at : at + size] = scaled
-        turned_ref[:, at : at + size] = jnp.dot(turn, scaled, preferred_element_type=F32).astype(BF16)
-
-    put(zx[:, inner:], 0, wf_ref, wr_ref)
-    put(bc_ref[...].astype(F32), inner, wf_ref, wr_ref)
-    put(steps, inner + bc_ref.shape[1], wf_ref, wr_ref)
-    put(zx[:, :inner], 0, gf_ref, gr_ref)
-
-
-def prepare(w_zx, w_bc, w_dt, gain):
-    depth, _, inner = w_zx.shape
-    tile = min(256, depth)
-    n = depth // tile
-    wide = inner + w_bc.shape[1] + 128
-    forward, turned = (lambda i: (i, 0)), (lambda i: (n - 1 - i, 0))
-    return pl.pallas_call(
-        functools.partial(prepare_kernel, inner),
-        grid=(n,),
-        in_specs=[pl.BlockSpec((tile, 2, inner), lambda i: (i, 0, 0)),
-                  pl.BlockSpec((tile, w_bc.shape[1]), forward),
-                  pl.BlockSpec((w_dt.shape[1], tile), lambda i: (0, i)),
-                  pl.BlockSpec((1, tile), lambda i: (0, i))],
-        out_specs=[pl.BlockSpec((tile, wide), forward), pl.BlockSpec((tile, wide), turned),
-                   pl.BlockSpec((tile, inner), forward), pl.BlockSpec((tile, inner), turned)],
-        out_shape=[jax.ShapeDtypeStruct((depth, wide), BF16)] * 2 + [jax.ShapeDtypeStruct((depth, inner), BF16)] * 2,
-        compiler_params=params(58),
-        cost_estimate=cost(4e9, 8e6),
-        name="prepare",
-    )(w_zx, w_bc, w_dt.T, gain[None, :])
+    for b in range(0, depth, rows):
+        here, there = slice(b, b + rows), slice(depth - rows - b, depth - b)
+        gain = jnp.transpose(jnp.broadcast_to(gain_ref[:, here], (128, rows)))
+        zx = zx_ref[here].astype(F32).reshape(rows, 2 * inner)
+        steps = dt_ref[:, here].astype(F32)
+        steps = jnp.transpose(jnp.concatenate([steps, jnp.zeros((128 - steps.shape[0], rows), F32)], axis=0))
+
+        def put(part, at, forward_ref, turned_ref):
+            size = part.shape[1]
+            scaled = jnp.concatenate([part[:, g : g + 128] * gain for g in range(0, size, 128)], axis=1).astype(BF16)
+            forward_ref[here, at : at + size] = scaled
+            turned_ref[there, at : at + size] = jnp.dot(turn, scaled, preferred_element_type=F32).astype(BF16)
+
+        put(zx[:, inner:], 0, wf_ref, wr_ref)
+        put(bc_ref[here].astype(F32), inner, wf_ref, wr_ref)
+        put(steps, inner + bc_ref.shape[1], wf_ref, wr_ref)
+        put(zx[:, :inner], 0, gf_ref, gr_ref)
 
 
 def row_scale(h):
@@ -106,10 +87,10 @@
 
 
 def project_kernel(heads, inner, *refs):
-    (hf_ref, hr_ref, rimf_ref, rimr_ref, wf_ref, wr_ref, convx_ref, convbc_ref, lanes_ref, copy_ref,
+    (hf_ref, hr_ref, rimf_ref, rimr_ref, zx_ref, bc_ref, wdt_ref, gain_ref, convx_ref, convbc_ref, lanes_ref, copy_ref,
      actf_ref, smallf_ref, cumtf_ref, enterf_ref, priorf_ref,
      actr_ref, smallr_ref, cumtr_ref, enterr_ref, priorr_ref,
-     msg_ref, buff, bufr, statef, stater, totalf, totalr) = refs
+     msg_ref, gf_ref, gr_ref, wf_ref, wr_ref, buff, bufr, statef, stater, totalf, totalr) = refs
     step = pl.program_id(0)
     last = pl.num_programs(0) - 1
     stream = inner + 2 * STATE
@@ -123,6 +104,7 @@
 
     @pl.when(step == 0)
     def _():
+        prepare(inner, zx_ref, bc_ref, wdt_ref, gain_ref, wf_ref, wr_ref, gf_ref, gr_ref)
         for reverse, _, rim_ref, w_ref, _, _, _, _, _, buf, state, total in sides:
             edge = rows if reverse else 0
             state[...] = jnp.zeros_like(state)
@@ -218,7 +200,7 @@
                 [rows3, jnp.zeros_like(rows3)], axis=0).astype(BF16)
 
 
-def project(hidden, rim_f, rim_r, w_f, w_r, conv_x, conv_bc, lanes, copy, heads, inner):
+def project(hidden, rim_f, rim_r, weights, conv_x, conv_bc, lanes, copy, heads, inner):
     rows, depth = hidden.shape
     stream = inner + 2 * STATE
     n = rows // TILE
@@ -242,15 +224,15 @@
         functools.partial(project_kernel, heads, inner),
         grid=(n,),
         in_specs=[by_rows(depth, up), by_rows(depth, down), whole(rim_f.shape), whole(rim_r.shape),
-                  whole(w_f.shape), whole(w_r.shape), whole(conv_x.shape), whole(conv_bc.shape), whole(lanes.shape),
+                  *[whole(x.shape) for x in weights], whole(conv_x.shape), whole(conv_bc.shape), whole(lanes.shape),
                   whole(copy.shape)],
-        out_specs=out_specs + [whole(message)],
-        out_shape=out_shape + [jax.ShapeDtypeStruct(message, BF16)],
-        scratch_shapes=[buf, buf, state, state, total, total],
+        out_specs=out_specs + [whole(message), whole((depth, inner)), whole((depth, inner))],
+        out_shape=out_shape + [jax.ShapeDtypeStruct(message, BF16)] + [jax.ShapeDtypeStruct((depth, inner), BF16)] * 2,
+        scratch_shapes=[pltpu.VMEM((depth, stream + 128), BF16)] * 2 + [buf, buf, state, state, total, total],
         compiler_params=params(58),
         cost_estimate=cost(22e9, 40e6),
         name="project",
-    )(hidden, hidden, rim_f, rim_r, w_f, w_r, conv_x, conv_bc, lanes, copy)
+    )(hidden, hidden, rim_f, rim_r, *weights, conv_x, conv_bc, lanes, copy)
 
 
 def gates_kernel(h_ref, wf_ref, wr_ref, zf_ref, zr_ref):
@@ -260,20 +242,56 @@
         z_ref[...] = (jnp.dot(h, w_ref[...], preferred_element_type=F32) * scale).astype(BF16)
 
 
-def gates(hidden, w_f, w_r):
-    rows, depth = hidden.shape
-    inner = w_f.shape[1]
-    by_rows = lambda width: pl.BlockSpec((TILE, width), lambda i: (i, 0))
+def by_destination(kernel, name, place, rows_in, fixed, by_order, out_shape, out_specs, work, scratch=()):
+    k, pieces, tile, rows, head, n_head = place
+    share = rows // n_head
+    per_piece, per_share = share // pieces // tile, share // tile
+
+    def at(i, head_ref):
+        return lax.rem(head_ref[0] + i // per_piece, n_head) * per_share + k * per_piece + lax.rem(i, per_piece)
+
+    def spec(shape, dim, last):
+        def index(i, head_ref):
+            where = [0] * len(shape)
+            where[-1] = last
+            where[dim] = at(i, head_ref)
+            return tuple(where)
+
+        return pl.BlockSpec(shape, index)
+
+    in_specs = [spec(*one[1:]) for one in rows_in] + [whole(x.shape) for x in fixed]
+    in_specs += [pl.BlockSpec((tile, x.shape[1]), lambda i, _: (i, 0)) for x in by_order]
     return pl.pallas_call(
-        gates_kernel,
-        grid=(rows // TILE,),
-        in_specs=[by_rows(depth), whole(w_f.shape), whole(w_r.shape)],
-        out_specs=[by_rows(inner)] * 2,
-        out_shape=[jax.ShapeDtypeStruct((rows, inner), BF16)] * 2,
+        lambda _, *refs: kernel(*refs),
+        grid_spec=pltpu.PrefetchScalarGridSpec(
+            num_scalar_prefetch=1,
+            grid=(n_head * per_piece,),
+            in_specs=in_specs,
+            out_specs=out_specs,
+            scratch_shapes=scratch,
+        ),
+        out_shape=out_shape,
         compiler_params=params(58),
-        cost_estimate=cost(10e9, 10e6),
-        name="gates",
-    )(hidden, w_f, w_r)
+        cost_estimate=cost(work, 1e6),
+        name=name,
+    )(head, *[one[0] for one in rows_in], *fixed, *by_order)
+
+
+def ordered(place, inner):
+    _, pieces, tile, rows, _, _ = place
+    return jax.ShapeDtypeStruct((rows // pieces, inner), BF16), pl.BlockSpec((tile, inner), lambda i, _: (i, 0))
+
+
+def sent(place, inner):
+    _, pieces, _, rows, _, n_head = place
+    size = rows // n_head // pieces
+    return [jax.ShapeDtypeStruct((size, inner), BF16)] * n_head, [whole((size, inner))] * n_head
+
+
+def gates(place, hidden, w_f, w_r, work):
+    shape, spec = ordered(place, w_f.shape[1])
+    return by_destination(gates_kernel, "gates", place, [(hidden, (place[2], hidden.shape[1]), 0, 0)], [w_f, w_r], [],
+                          [shape] * 2, [spec] * 2, work)
 
 
 def inside_kernel(heads, inner, actf_ref, smallf_ref, cumtf_ref, actr_ref, smallr_ref, cumtr_ref, lanes_ref, copy_ref,
@@ -310,26 +328,22 @@
                 base_ref[rows, cols] = (out + skip[:, cols] * values[:, cols]).astype(BF16)
 
 
-def inside(tile, blocks, strands, lanes, copy, heads, inner, work):
-    count, at = blocks
-    columns = strands[0][0].shape[1]
-    by_rows = lambda width: pl.BlockSpec((tile, width), lambda i: (at(i), 0))
-    one = [by_rows(columns), by_rows(128), pl.BlockSpec((heads, tile), lambda i: (0, at(i)))]
-    return pl.pallas_call(
-        functools.partial(inside_kernel, heads, inner),
-        grid=(count,),
-        in_specs=one + one + [whole(lanes.shape), whole(copy.shape)],
-        out_specs=[pl.BlockSpec((tile, inner), lambda i: (i, 0))] * 2,
-        out_shape=[jax.ShapeDtypeStruct((count * tile, inner), BF16)] * 2,
-        compiler_params=params(58),
-        cost_estimate=cost(work, 1e6),
-        name="inside",
-    )(*strands[0], *strands[1], lanes, copy)
+def inside_rows(strands, tile, heads):
+    rows_in = []
+    for act, small, cumt in strands:
+        rows_in += [(act, (tile, act.shape[1]), 0, 0), (small, (tile, 128), 0, 0), (cumt, (heads, tile), 1, 0)]
+    return rows_in
+
+
+def inside(place, strands, lanes, copy, heads, inner, work):
+    shape, spec = ordered(place, inner)
+    return by_destination(functools.partial(inside_kernel, heads, inner), "inside", place,
+                          inside_rows(strands, place[2], heads), [lanes, copy], [], [shape] * 2, [spec] * 2, work)
 
 
 def finish_kernel(heads, inner, *refs):
-    (cf_ref, zf_ref, ef_ref, pf_ref, sf_ref, cr_ref, zr_ref, er_ref, pr_ref, sr_ref, bf_ref, br_ref,
-     in_ref, copy_ref, out_ref) = refs
+    (cf_ref, ef_ref, pf_ref, sf_ref, cr_ref, er_ref, pr_ref, sr_ref, in_ref, copy_ref,
+     zf_ref, zr_ref, bf_ref, br_ref, *out_refs) = refs
     width = inner // heads
     size = cf_ref.shape[0]
     row = lax.broadcasted_iota(jnp.int32, (256, 256), 0) // width
@@ -351,28 +365,49 @@
             [jnp.dot(squares[:, g : g + 256], mean, preferred_element_type=F32) for g in range(0, inner, 256)], axis=1)
         result = gated * lax.rsqrt(means + EPS)
         both = result if both is None else both + result
-    out_ref[...] = both.astype(BF16)
-
-
-def finish(tile, blocks, strands, bases, entering, copy, heads, inner):
-    count, at = blocks
+    both = both.astype(BF16)
+    step = pl.program_id(0)
+    per_piece = out_refs[0].shape[0] // size
+    for d, ref in enumerate(out_refs):
+        @pl.when(step // per_piece == d)
+        def _():
+            ref[pl.ds(pl.multiple_of(lax.rem(step, per_piece) * size, size), size), :] = both
+
+
+def finish_rows(strand, tile, inner):
+    enter, prior = strand
     per = tile // CHUNK
-    last = strands[0][0].shape[1] // STATE - 1
-    by_rows = lambda width: pl.BlockSpec((tile, width), lambda i: (at(i), 0))
-    in_order = pl.BlockSpec((tile, inner), lambda i: (i, 0))
-    one = [pl.BlockSpec((tile, STATE), lambda i: (at(i), last)), by_rows(inner),
-           pl.BlockSpec((per, STATE, inner), lambda i: (at(i), 0, 0)),
-           pl.BlockSpec((per, 8, inner), lambda i: (at(i), 0, 0)), by_rows(128)]
-    return pl.pallas_call(
-        functools.partial(finish_kernel, heads, inner),
-        grid=(count,),
-        in_specs=one + one + [in_order, in_order, whole((2, STATE, inner)), whole(copy.shape)],
-        out_specs=in_order,
-        out_shape=jax.ShapeDtypeStruct((count * tile, inner), BF16),
-        compiler_params=params(58),
-        cost_estimate=cost(1e8, 1e6),
-        name="finish",
-    )(*strands[0], *strands[1], *bases, entering, copy)
+    return [(enter, (per, STATE, inner), 0, 0), (prior, (per, 8, inner), 0, 0)]
+
+
+def finish(place, strands, ends, bases, gated, entering, copy, heads, inner):
+    tile = place[2]
+    shapes, specs = sent(place, inner)
+    rows_in = []
+    for (act, small, _), end in zip(strands, ends):
+        rows_in += [(act, (tile, STATE), 0, act.shape[1] // STATE - 1)] + finish_rows(end, tile, inner)
+        rows_in += [(small, (tile, 128), 0, 0)]
+    return by_destination(functools.partial(finish_kernel, heads, inner), "finish", place, rows_in, [entering, copy],
+                          [*gated, *bases], shapes, specs, 1e8)
+
+
+def settle_kernel(heads, inner, *refs):
+    (actf_ref, smallf_ref, cumtf_ref, actr_ref, smallr_ref, cumtr_ref, ef_ref, pf_ref, er_ref, pr_ref,
+     lanes_ref, first_ref, in_ref, second_ref, zf_ref, zr_ref, *out_refs, basef, baser) = refs
+    inside_kernel(heads, inner, actf_ref, smallf_ref, cumtf_ref, actr_ref, smallr_ref, cumtr_ref, lanes_ref, first_ref,
+                  basef, baser)
+    maps = [ref.at[:, pl.ds(inner + STATE, STATE)] for ref in (actf_ref, actr_ref)]
+    finish_kernel(heads, inner, maps[0], ef_ref, pf_ref, smallf_ref, maps[1], er_ref, pr_ref, smallr_ref,
+                  in_ref, second_ref, zf_ref, zr_ref, basef, baser, *out_refs)
+
+
+def settle(place, strands, ends, gated, lanes, first, entering, second, heads, inner):
+    tile = place[2]
+    shapes, specs = sent(place, inner)
+    rows_in = inside_rows(strands, tile, heads) + finish_rows(ends[0], tile, inner) + finish_rows(ends[1], tile, inner)
+    return by_destination(functools.partial(settle_kernel, heads, inner), "settle", place, rows_in,
+                          [lanes, first, entering, second], list(gated), shapes, specs, 1e8,
+                          [pltpu.VMEM((tile, inner), BF16)] * 2)
 
 
 def read_message(ref, at):
@@ -472,7 +507,7 @@
         block = lax.dynamic_slice_in_dim(message, above * half, half, 0)
         slots.append(lax.ppermute(block, axis, [(i, i ^ (d * distance)) for i in range(count)]))
     joined = local_call(functools.partial(join_kernel, groups), "join", place.astype(jnp.int32).reshape(1), [into] + slots,
-                        [jax.ShapeDtypeStruct((2, STATE, inner), F32)])[0]
+                        [pltpu.HBM((2, STATE, inner), F32)])[0]
     return joined, beside, before
 
 
@@ -503,41 +538,37 @@
     own_half = lax.dynamic_slice_in_dim(w_out, parity * half, half, 0)
     same = [rotated(own_half, d, n_head) for d in range(1, n_head)]
 
-    w_f, w_r, g_f, g_r = prepare(w_zx, w_bc, w_dt, norm_gain)
     lanes = jnp.pad(jnp.stack([dt_bias, decay_rate, skip_gain]), [(0, 0), (0, 128 - heads)])
     copy_first = spread_matrix(0, heads, width)
     copy_second = spread_matrix(heads, heads, width)
     (act_f, small_f, cumt_f, enter_f, prior_f, act_r, small_r, cumt_r, enter_r, prior_r,
-     message) = project(hidden, rim_f, rim_r, w_f, w_r, conv_x, conv_bc, lanes, copy_first, heads, inner)
-    entering, (z_f, z_r), same = incoming(message, "ctx", gates(hidden, g_f, g_r), same)
-
+     message, g_f, g_r) = project(hidden, rim_f, rim_r, (w_zx, w_bc, w_dt.T, norm_gain[None, :]), conv_x, conv_bc, lanes, copy_first, heads, inner)
     share = rows // n_head
     pieces = 2 if share % (2 * CHUNK) == 0 else 1
     size = share // pieces
     tile = min(TILE, size)
-    inner_blocks, share_blocks = size // tile, share // tile
-    other = lax.ppermute(jnp.concatenate(same, axis=0), "ctx", [(i, i ^ 1) for i in range(n_ctx)])
-    entering, other = lax.optimization_barrier((entering, other))
-    other = [other[i * half : (i + 1) * half] for i in range(n_head - 1)]
+    place = lambda k: (k, pieces, tile, rows, head.astype(jnp.int32).reshape(1), n_head)
+    strands = ((act_f, small_f, cumt_f), (act_r, small_r, cumt_r))
+    ends = ((enter_f, prior_f), (enter_r, prior_r))
+    entering, gated, same = incoming(message, "ctx", gates(place(0), hidden, g_f, g_r, 5e9), same)
+    bases = inside(place(0), strands, lanes, copy_first, heads, inner, 8e9)
+    parts = finish(place(0), strands, ends, bases, gated, entering, copy_second, heads, inner)
+    (g_f, g_r), same, parts = lax.optimization_barrier(((g_f, g_r), same, parts))
+    swapped = lambda blocks: lax.ppermute(jnp.concatenate(blocks, axis=0), "ctx", [(i, i ^ 1) for i in range(n_ctx)])
+    other = None if pieces > 1 else swapped(same)
+    arrived = [[rotated(block, d, n_head) if d else block for d, block in enumerate(parts)]]
+    for k in range(1, pieces):
+        gated = gates(place(k), hidden, g_f, g_r, 1e8)
+        if other is None:
+            gated, same = lax.optimization_barrier((gated, same))
+            other = swapped(same)
+        parts = settle(place(k), strands, ends, gated, lanes, copy_first, entering, copy_second, heads, inner)
+        parts, arrived[k - 1], other, same = lax.optimization_barrier((parts, arrived[k - 1], other, same))
+        arrived.append([rotated(block, d, n_head) if d else block for d, block in enumerate(parts)])
+    own_rows = lax.dynamic_slice_in_dim(hidden, head * share, share, 0)
     groups = [w_out]
-    own_rows = lax.dynamic_slice_in_dim(hidden, head * share, share, 0)
-    arrived = [[None] * n_head for _ in range(pieces)]
-
-    combined = None
-    for k in range(pieces):
-        blocks = (n_head * inner_blocks,
-                  lambda i, k=k: (i // inner_blocks) * share_blocks + k * inner_blocks + i % inner_blocks)
-        if combined is not None:
-            act_f, act_r, combined = lax.optimization_barrier((act_f, act_r, combined))
-        bases = inside(tile, blocks, ((act_f, small_f, cumt_f), (act_r, small_r, cumt_r)), lanes, copy_first, heads, inner,
-                       1e8 if k else 8e9)
-        combined = finish(tile, blocks, ((act_f, z_f, enter_f, prior_f, small_f), (act_r, z_r, enter_r, prior_r, small_r)),
-                          bases, entering, copy_second, heads, inner)
-        if k:
-            combined, *arrived[k - 1] = lax.optimization_barrier((combined, *arrived[k - 1]))
-        parts = [lax.dynamic_slice_in_dim(combined, ((head + d) % n_head) * size, size, 0) for d in range(n_head)]
-        arrived[k] = [rotated(block, d, n_head) if d else block for d, block in enumerate(parts)]
-    for one, two in zip(same, other):
+    for d, one in enumerate(same):
+        two = other[d * half : (d + 1) * half]
         groups.append(jnp.concatenate([jnp.where(parity == 0, one, two), jnp.where(parity == 0, two, one)], axis=0))
     result = None
     for k in range(pieces):

time: 133 us -> 139 us (1.045)
  the two profiles are of different devices: /device:TPU:10 before, /device:TPU:0 now
where the time goes in v4:
time: 139 us
  Pallas kernels  70.8 us (51%)
  starting transfers between devices  27.3 us (20%)
  waiting for transfers between devices  26.6 us (19%)
  matrix products  5.77 us (4%)
  other arithmetic  5.14 us (4%)
  local copies, waits for them, and re-layouts  2.71 us (2%)
    pallas_call x5, Pallas kernels, by_destination(): pl.pallas_call(lambda _, *refs: kernel(*refs), grid_spec=pltpu.PrefetchSc...  37.7 us
    pallas_call x1, Pallas kernels, project(): pl.pallas_call(functools.partial(project_kernel, heads, inner), grid=(n,)...  31.9 us
    ppermute x9, waiting for transfers between devices, rotated(): lax.ppermute(block, 'head', [(i, (i + d) % count) for i in range(count)])  24.4 us
    ppermute x9, starting transfers between devices, rotated(): lax.ppermute(block, 'head', [(i, (i + d) % count) for i in range(count)])  17.8 us
    dot_general x8, matrix products, on_device(): total = total + jnp.dot(block, weights, preferred_element_type=F32)  5.77 us
    ppermute x3, starting transfers between devices, incoming(): lax.ppermute(block, axis, [(i, i ^ d * distance) for i in range(count)])  3.92 us
    ppermute x1, starting transfers between devices, incoming(): lax.ppermute(message, axis, [(i, i ^ distance) for i in range(count)])  2.98 us
  transfers between devices with their start and end apart: 16, of which 4 were waited for; matrix products, arithmetic and copies ran while one was open for 5% of the time, Pallas kernels for 41%

profile of v4, /device:TPU:0, one launch (start us, length us, event | category | flops | bytes accessed | tf_op | source)
XLA Modules:
  0.0 138.6 jit_solution(9605994290647985677)
XLA Ops:
  1.3 3.1 %collective-permute-start.3 = (bf16[256,1024]{1,0:T(8,128)(2,1)S(1)}, bf16[256,1024]{1,0:T(8,128)(2,1)S(1)}, u32[]{:S(2)}, u32[]{:S(2)}) collective-permute-start(bf16[256,1024]{1,0:T(8,128)(2,1)S(1)} %constant_dynamic-slice_fusion.2), channel_id=1, source_target_pairs={{0,1},{1,2},{2,3},{3,0},{4,5},{5,6},{6,7},{7,4},{8,9},{9,10},{10,1... | collective-permute-start | bytes 1572872 | tf_op jit(solution)/shard_map/ppermute | solution.py:520
  4.3 2.6 %collective-permute-start.4 = (bf16[256,1024]{1,0:T(8,128)(2,1)S(1)}, bf16[256,1024]{1,0:T(8,128)(2,1)S(1)}, u32[]{:S(2)}, u32[]{:S(2)}) collective-permute-start(bf16[256,1024]{1,0:T(8,128)(2,1)S(1)} %constant_dynamic-slice_fusion.2), channel_id=1, source_target_pairs={{0,2},{1,3},{2,0},{3,1},{4,6},{5,7},{6,4},{7,5},{8,10},{9,11},{10,... | collective-permute-start | bytes 1572872 | tf_op jit(solution)/shard_map/ppermute | solution.py:520
  6.9 1.3 collective-permute-start.5
  9.1 1.3 collective-permute-start
  10.3 1.3 collective-permute-start.1
  11.6 1.3 select_maximum_fusion.refs_10_.refs_6_
  12.9 2.2 %collective-permute-done.1.refs_3_ = bf16[16,1024]{1,0:T(8,128)(2,1)S(1)} collective-permute-done((bf16[16,1024]{1,0:T(8,128)(2,1)S(1)}, bf16[16,1024]{1,0:T(8,128)(2,1)S(1)}, u32[]{:S(2)}, u32[]{:S(2)}) %collective-permute-start.1) | collective-permute-done | bytes 32800 | tf_op jit(solution)/shard_map/ppermute | solution.py:516
  15.8 31.9 %project.1 = (bf16[2048,768]{1,0:T(8,128)(2,1)}, f32[2048,128]{1,0:T(8,128)}, f32[8,2048]{1,0:T(8,128)}, bf16[16,128,512]{2,1,0:T(8,128)(2,1)}, f32[16,8,512]{2,...) custom-call(bf16[2048,1024]{1,0:T(8,128)(2,1)} %refs_0_.5, ...), custom_call_target="tpu_custom_call" | custom-call | flops 22000001024 | bytes 40000000 | tf_op jit(solution)/shard_map/project/pallas_call | solution.py:223
  47.7 3.0 %collective-permute-start.2 = (bf16[288,512]{1,0:T(8,128)(2,1)}, bf16[288,512]{1,0:T(8,128)(2,1)S(1)}, u32[]{:S(2)}, u32[]{:S(2)}) collective-permute-start(bf16[288,512]{1,0:T(8,128)(2,1)} %get-tuple-element.77.refs_1_), channel_id=1, source_target_pairs={{0,4},{4,0},{8,12},{12,8},{16,20},{20,16},{24,28},{28,24},{1,5},{5... | collective-permute-start | bytes 884744 | tf_op jit(solution)/shard_map/ppermute | solution.py:489
  50.7 5.8 %gates.2 = (bf16[1024,512]{1,0:T(8,128)(2,1)}, bf16[1024,512]{1,0:T(8,128)(2,1)}) custom-call(s32[1]{0:T(128)} %bitcast._, bf16[2048,1024]{1,0:T(8,128)(2,1)} %refs_0_.5, bf16[1024,512]{1,0:T(8,128)(2,1)} %get-tuple-element.97.refs_1_, bf16[1024,512]{1,0:T(8,128)(2,1)} %get-tuple-element.98.refs_2_), custom_call_target="tpu_custom_call" | custom-call | flops 5000000000 | bytes 1000000 | tf_op jit(solution)/shard_map/gates/pallas_call | solution.py:264
  56.8 1.6 %collective-permute-start.7 = (bf16[144,512]{1,0:T(8,128)(2,1)S(1)}, bf16[144,512]{1,0:T(8,128)(2,1)S(1)}, u32[]{:S(2)}, u32[]{:S(2)}) collective-permute-start(bf16[144,512]{1,0:T(8,128)(2,1)S(1)} %get-tuple-element.141), channel_id=1, source_target_pairs={{0,16},{4,20},{8,24},{12,28},{16,0},{20,4},{24,8},{28,12},{1,17},{... | collective-permute-start | bytes 442376 | tf_op jit(solution)/shard_map/ppermute | solution.py:508
  58.4 2.3 %collective-permute-start.8 = (bf16[144,512]{1,0:T(8,128)(2,1)S(1)}, bf16[144,512]{1,0:T(8,128)(2,1)S(1)}, u32[]{:S(2)}, u32[]{:S(2)}) collective-permute-start(bf16[144,512]{1,0:T(8,128)(2,1)S(1)} %get-tuple-element.141), channel_id=1, source_target_pairs={{0,24},{4,28},{8,16},{12,20},{16,8},{20,12},{24,0},{28,4},{1,25},{... | collective-permute-start | bytes 442376 | tf_op jit(solution)/shard_map/ppermute | solution.py:508
  60.7 7.2 %inside.1 = (bf16[1024,512]{1,0:T(8,128)(2,1)}, bf16[1024,512]{1,0:T(8,128)(2,1)}) custom-call(s32[1]{0:T(128)} %bitcast._, bf16[2048,768]{1,0:T(8,128)(2,1)} %get-tuple-element.67.refs_0_, f32[2048,128]{1,0:T(8,128)} %get-tuple-element.68.refs_1_.refs_3_, f32[8,2048]{1,0:T(8,128)} %get-tuple-element.69.refs_2_, ...), custom_call_target="tpu_custom_call" | custom-call | flops 8000000000 | bytes 1000000 | tf_op jit(solution)/shard_map/inside/pallas_call | solution.py:264
  69.0 7.5 %finish.1 = (bf16[256,512]{1,0:T(8,128)(2,1)}, bf16[256,512]{1,0:T(8,128)(2,1)}, bf16[256,512]{1,0:T(8,128)(2,1)}, bf16[256,512]{1,0:T(8,128)(2,1)}) custom-call(s32[1]{0:T(128)} %bitcast._, bf16[2048,768]{1,0:T(8,128)(2,1)} %get-tuple-element.67.refs_0_, bf16[16,128,512]{2,1,0:T(8,128)(2,1)} %get-tuple-element.73.refs_1_.refs_6_, ...), custom_call_target="tpu_custom_call" | custom-call | flops 100000000 | bytes 1000000 | tf_op jit(solution)/shard_map/finish/pallas_call | solution.py:264
  76.5 5.8 %gates.3 = (bf16[1024,512]{1,0:T(8,128)(2,1)}, bf16[1024,512]{1,0:T(8,128)(2,1)}) custom-call(s32[1]{0:T(128)} %bitcast._, bf16[2048,1024]{1,0:T(8,128)(2,1)} %refs_0_.5, bf16[1024,512]{1,0:T(8,128)(2,1)} %get-tuple-element.97.refs_1_, bf16[1024,512]{1,0:T(8,128)(2,1)} %get-tuple-element.98.refs_2_), custom_call_target="tpu_custom_call" | custom-call | flops 100000000 | bytes 1000000 | tf_op jit(solution)/shard_map/gates/pallas_call | solution.py:264
  84.3 3.1 %collective-permute-start.11 = (bf16[256,512]{1,0:T(8,128)(2,1)}, bf16[256,512]{1,0:T(8,128)(2,1)S(1)}, u32[]{:S(2)}, u32[]{:S(2)}) collective-permute-start(bf16[256,512]{1,0:T(8,128)(2,1)} %get-tuple-element.113), channel_id=1, source_target_pairs={{0,3},{1,0},{2,1},{3,2},{4,7},{5,4},{6,5},{7,6},{8,11},{9,8},{10,9... | collective-permute-start | bytes 786440 | tf_op jit(solution)/shard_map/ppermute | solution.py:520
  87.4 11.4 %settle.1 = (bf16[256,512]{1,0:T(8,128)(2,1)}, bf16[256,512]{1,0:T(8,128)(2,1)}, bf16[256,512]{1,0:T(8,128)(2,1)}, bf16[256,512]{1,0:T(8,128)(2,1)}) custom-call(s32[1]{0:T(128)} %bitcast._, bf16[2048,768]{1,0:T(8,128)(2,1)} %get-tuple-element.67.refs_0_, f32[2048,128]{1,0:T(8,128)} %get-tuple-element.68.refs_1_.refs_3_, ...), custom_call_target="tpu_custom_call" | custom-call | flops 100000000 | bytes 1000000 | tf_op jit(solution)/shard_map/settle/pallas_call | solution.py:264
  98.7 6.7 %collective-permute-done.10 = bf16[256,512]{1,0:T(8,128)(2,1)S(1)} collective-permute-done((bf16[256,512]{1,0:T(8,128)(2,1)}, bf16[256,512]{1,0:T(8,128)(2,1)S(1)}, u32[]{:S(2)}, u32[]{:S(2)}) %collective-permute-start.10) | collective-permute-done | bytes 262176 | tf_op jit(solution)/shard_map/ppermute | solution.py:520
  105.5 4.9 %collective-permute-start.15 = (bf16[256,512]{1,0:T(8,128)(2,1)}, bf16[256,512]{1,0:T(8,128)(2,1)S(1)}, u32[]{:S(2)}, u32[]{:S(2)}) collective-permute-start(bf16[256,512]{1,0:T(8,128)(2,1)} %get-tuple-element.128), channel_id=1, source_target_pairs={{0,3},{1,0},{2,1},{3,2},{4,7},{5,4},{6,5},{7,6},{8,11},{9,8},{10,9... | collective-permute-start | bytes 786440 | tf_op jit(solution)/shard_map/ppermute | solution.py:520
  110.3 2.1 %collective-permute-start.14 = (bf16[256,512]{1,0:T(8,128)(2,1)}, bf16[256,512]{1,0:T(8,128)(2,1)S(1)}, u32[]{:S(2)}, u32[]{:S(2)}) collective-permute-start(bf16[256,512]{1,0:T(8,128)(2,1)} %get-tuple-element.127), channel_id=1, source_target_pairs={{0,2},{1,3},{2,0},{3,1},{4,6},{5,7},{6,4},{7,5},{8,10},{9,11},{10,... | collective-permute-start | bytes 786440 | tf_op jit(solution)/shard_map/ppermute | solution.py:520
  112.4 1.6 %broadcast_select_fusion.5 = (bf16[256,1024]{1,0:T(8,128)(2,1)S(1)}, bf16[256,1024]{1,0:T(8,128)(2,1)S(1)}, bf16[256,1024]{1,0:T(8,128)(2,1)S(1)}, bf16[256,1024...) fusion(bf16[256,1024]{1,0:T(8,128)(2,1)S(1)} %collective-permute-done.3, ...), kind=kLoop, calls=%fused_computation.26 | loop fusion | flops 1572864 | bytes 6291457 | tf_op jit(solution)/shard_map/jit(_where)/select_n | solution.py:572
  115.4 1.6 %fusion.6 = bf16[256,1024]{1,0:T(8,128)(2,1)S(1)} fusion(f32[256,1024]{1,0:T(8,128)S(1)} %fusion.9, f32[256,1024]{1,0:T(8,128)S(1)} %fusion.11, f32[256,1024]{1,0:T(8,128)S(1)} %fusion.13, bf16[256,512]{1,0:T(8,128)(2,1)S(1)} %copy-done.2, bf16[512,1024]{1,0:T(8,128)(2,1)S(1)} %copy-done, bf16[2048,1024]{1,0:T(8,128)(2,1)} %refs_0_.5, s32[]{:T(128)S(6)} %select_n.70), kind=kOutput, calls=%fused_computation.9 | convolution fusion | flops 270008320 | bytes 5505028 | tf_op jit(solution)/shard_map/dot_general | solution.py:577
  117.9 17.2 %collective-permute-done.14 = bf16[256,512]{1,0:T(8,128)(2,1)S(1)} collective-permute-done((bf16[256,512]{1,0:T(8,128)(2,1)}, bf16[256,512]{1,0:T(8,128)(2,1)S(1)}, u32[]{:S(2)}, u32[]{:S(2)}) %collective-permute-start.14) | collective-permute-done | bytes 262176 | tf_op jit(solution)/shard_map/ppermute | solution.py:520
  136.0 1.6 %fusion.7 = bf16[256,1024]{1,0:T(8,128)(2,1)S(1)} fusion(f32[256,1024]{1,0:T(8,128)S(1)} %fusion.8, f32[256,1024]{1,0:T(8,128)S(1)} %fusion.10, f32[256,1024]{1,0:T(8,128)S(1)} %fusion.12, bf16[256,512]{1,0:T(8,128)(2,1)S(1)} %copy-done.3, bf16[512,1024]{1,0:T(8,128)(2,1)S(1)} %copy-done, bf16[2048,1024]{1,0:T(8,128)(2,1)} %refs_0_.5, s32[]{:T(128)S(6)} %add.70), kind=kOutput, calls=%fused_computation.10 | convolution fusion | flops 270008320 | bytes 5505028 | tf_op jit(solution)/shard_map/dot_general | solution.py:577
  (43 shorter events, 10.1 us)
Async XLA Ops:
  0.0 1.2 copy-start
  1.3 55.5 %collective-permute-start.3 = (bf16[256,1024]{1,0:T(8,128)(2,1)S(1)}, bf16[256,1024]{1,0:T(8,128)(2,1)S(1)}, u32[]{:S(2)}, u32[]{:S(2)}) collective-permute-start(bf16[256,1024]{1,0:T(8,128)(2,1)S(1)} %constant_dynamic-slice_fusion.2), channel_id=1, source_target_pairs={{0,1},{1,2},{2,3},{3,0},{4,5},{5,6},{6,7},{7,4},{8,9},{9,10},{10,1... | collective-permute-start | bytes 1572872 | tf_op jit(solution)/shard_map/ppermute | solution.py:520
  4.3 52.4 %collective-permute-start.4 = (bf16[256,1024]{1,0:T(8,128)(2,1)S(1)}, bf16[256,1024]{1,0:T(8,128)(2,1)S(1)}, u32[]{:S(2)}, u32[]{:S(2)}) collective-permute-start(bf16[256,1024]{1,0:T(8,128)(2,1)S(1)} %constant_dynamic-slice_fusion.2), channel_id=1, source_target_pairs={{0,2},{1,3},{2,0},{3,1},{4,6},{5,7},{6,4},{7,5},{8,10},{9,11},{10,... | collective-permute-start | bytes 1572872 | tf_op jit(solution)/shard_map/ppermute | solution.py:520
  6.9 49.8 %collective-permute-start.5 = (bf16[256,1024]{1,0:T(8,128)(2,1)S(1)}, bf16[256,1024]{1,0:T(8,128)(2,1)S(1)}, u32[]{:S(2)}, u32[]{:S(2)}) collective-permute-start(bf16[256,1024]{1,0:T(8,128)(2,1)S(1)} %constant_dynamic-slice_fusion.2), channel_id=1, source_target_pairs={{0,3},{1,0},{2,1},{3,2},{4,7},{5,4},{6,5},{7,6},{8,11},{9,8},{10,9... | collective-permute-start | bytes 1572872 | tf_op jit(solution)/shard_map/ppermute | solution.py:520
  9.1 3.9 %collective-permute-start = (bf16[16,1024]{1,0:T(8,128)(2,1)S(1)}, bf16[16,1024]{1,0:T(8,128)(2,1)S(1)}, u32[]{:S(2)}, u32[]{:S(2)}) collective-permute-start(bf16[16,1024]{1,0:T(8,128)(2,1)S(1)} %get-tuple-element.130), channel_id=1, source_target_pairs={{0,4},{4,8},{8,12},{12,16},{16,20},{20,24},{24,28},{1,5},{5,9},{9,... | collective-permute-start | bytes 98312 | tf_op jit(solution)/shard_map/ppermute | solution.py:516
  10.3 4.8 %collective-permute-start.1 = (bf16[16,1024]{1,0:T(8,128)(2,1)S(1)}, bf16[16,1024]{1,0:T(8,128)(2,1)S(1)}, u32[]{:S(2)}, u32[]{:S(2)}) collective-permute-start(bf16[16,1024]{1,0:T(8,128)(2,1)S(1)} %get-tuple-element.129), channel_id=1, source_target_pairs={{4,0},{8,4},{12,8},{16,12},{20,16},{24,20},{28,24},{5,1},{9,5},{13... | collective-permute-start | bytes 98312 | tf_op jit(solution)/shard_map/ppermute | solution.py:516
  12.9 2.2 %copy-start.4 = (bf16[16,1024]{1,0:T(8,128)(2,1)}, bf16[16,1024]{1,0:T(8,128)(2,1)S(1)}, u32[]{:S(2)}) copy-start(bf16[16,1024]{1,0:T(8,128)(2,1)S(1)} %collective-permute-done.refs_2_) | copy-start | bytes 98308
  15.2 0.6 copy-start.5
  47.7 8.8 %collective-permute-start.2 = (bf16[288,512]{1,0:T(8,128)(2,1)}, bf16[288,512]{1,0:T(8,128)(2,1)S(1)}, u32[]{:S(2)}, u32[]{:S(2)}) collective-permute-start(bf16[288,512]{1,0:T(8,128)(2,1)} %get-tuple-element.77.refs_1_), channel_id=1, source_target_pairs={{0,4},{4,0},{8,12},{12,8},{16,20},{20,16},{24,28},{28,24},{1,5},{5... | collective-permute-start | bytes 884744 | tf_op jit(solution)/shard_map/ppermute | solution.py:489
  50.7 5.8 %copy-start.1 = (bf16[288,512]{1,0:T(8,128)(2,1)S(1)}, bf16[288,512]{1,0:T(8,128)(2,1)}, u32[]{:S(2)}) copy-start(bf16[288,512]{1,0:T(8,128)(2,1)} %get-tuple-element.77.refs_1_) | copy-start | bytes 884740
  56.8 11.1 %collective-permute-start.7 = (bf16[144,512]{1,0:T(8,128)(2,1)S(1)}, bf16[144,512]{1,0:T(8,128)(2,1)S(1)}, u32[]{:S(2)}, u32[]{:S(2)}) collective-permute-start(bf16[144,512]{1,0:T(8,128)(2,1)S(1)} %get-tuple-element.141), channel_id=1, source_target_pairs={{0,16},{4,20},{8,24},{12,28},{16,0},{20,4},{24,8},{28,12},{1,17},{... | collective-permute-start | bytes 442376 | tf_op jit(solution)/shard_map/ppermute | solution.py:508
  58.4 9.5 %collective-permute-start.8 = (bf16[144,512]{1,0:T(8,128)(2,1)S(1)}, bf16[144,512]{1,0:T(8,128)(2,1)S(1)}, u32[]{:S(2)}, u32[]{:S(2)}) collective-permute-start(bf16[144,512]{1,0:T(8,128)(2,1)S(1)} %get-tuple-element.141), channel_id=1, source_target_pairs={{0,24},{4,28},{8,16},{12,20},{16,8},{20,12},{24,0},{28,4},{1,25},{... | collective-permute-start | bytes 442376 | tf_op jit(solution)/shard_map/ppermute | solution.py:508
  60.7 7.2 %collective-permute-start.6 = (bf16[144,512]{1,0:T(8,128)(2,1)S(1)}, bf16[144,512]{1,0:T(8,128)(2,1)S(1)}, u32[]{:S(2)}, u32[]{:S(2)}) collective-permute-start(bf16[144,512]{1,0:T(8,128)(2,1)S(1)} %get-tuple-element.142), channel_id=1, source_target_pairs={{0,8},{4,12},{8,0},{12,4},{16,24},{20,28},{24,16},{28,20},{1,9},{5... | collective-permute-start | bytes 442376 | tf_op jit(solution)/shard_map/ppermute | solution.py:508
  83.5 21.9 %collective-permute-start.12 = (bf16[768,1024]{1,0:T(8,128)(2,1)}, bf16[768,1024]{1,0:T(8,128)(2,1)}, u32[]{:S(2)}, u32[]{:S(2)}) collective-permute-start(bf16[768,1024]{1,0:T(8,128)(2,1)} %pad_maximum_fusion), channel_id=1, source_target_pairs={{0,4},{4,0},{8,12},{12,8},{16,20},{20,16},{24,28},{28,24},{1,5},{5... | collective-permute-start | bytes 4718600 | tf_op jit(solution)/shard_map/ppermute | solution.py:557
  83.5 15.2 %collective-permute-start.9 = (bf16[256,512]{1,0:T(8,128)(2,1)}, bf16[256,512]{1,0:T(8,128)(2,1)S(1)}, u32[]{:S(2)}, u32[]{:S(2)}) collective-permute-start(bf16[256,512]{1,0:T(8,128)(2,1)} %get-tuple-element.111), channel_id=1, source_target_pairs={{0,1},{1,2},{2,3},{3,0},{4,5},{5,6},{6,7},{7,4},{8,9},{9,10},{10,1... | collective-permute-start | bytes 786440 | tf_op jit(solution)/shard_map/ppermute | solution.py:520
  83.9 21.5 %collective-permute-start.10 = (bf16[256,512]{1,0:T(8,128)(2,1)}, bf16[256,512]{1,0:T(8,128)(2,1)S(1)}, u32[]{:S(2)}, u32[]{:S(2)}) collective-permute-start(bf16[256,512]{1,0:T(8,128)(2,1)} %get-tuple-element.112), channel_id=1, source_target_pairs={{0,2},{1,3},{2,0},{3,1},{4,6},{5,7},{6,4},{7,5},{8,10},{9,11},{10,... | collective-permute-start | bytes 786440 | tf_op jit(solution)/shard_map/ppermute | solution.py:520
  84.3 21.2 %collective-permute-start.11 = (bf16[256,512]{1,0:T(8,128)(2,1)}, bf16[256,512]{1,0:T(8,128)(2,1)S(1)}, u32[]{:S(2)}, u32[]{:S(2)}) collective-permute-start(bf16[256,512]{1,0:T(8,128)(2,1)} %get-tuple-element.113), channel_id=1, source_target_pairs={{0,3},{1,0},{2,1},{3,2},{4,7},{5,4},{6,5},{7,6},{8,11},{9,8},{10,9... | collective-permute-start | bytes 786440 | tf_op jit(solution)/shard_map/ppermute | solution.py:520
  105.5 12.0 %collective-permute-start.15 = (bf16[256,512]{1,0:T(8,128)(2,1)}, bf16[256,512]{1,0:T(8,128)(2,1)S(1)}, u32[]{:S(2)}, u32[]{:S(2)}) collective-permute-start(bf16[256,512]{1,0:T(8,128)(2,1)} %get-tuple-element.128), channel_id=1, source_target_pairs={{0,3},{1,0},{2,1},{3,2},{4,7},{5,4},{6,5},{7,6},{8,11},{9,8},{10,9... | collective-permute-start | bytes 786440 | tf_op jit(solution)/shard_map/ppermute | solution.py:520
  110.3 24.7 %collective-permute-start.14 = (bf16[256,512]{1,0:T(8,128)(2,1)}, bf16[256,512]{1,0:T(8,128)(2,1)S(1)}, u32[]{:S(2)}, u32[]{:S(2)}) collective-permute-start(bf16[256,512]{1,0:T(8,128)(2,1)} %get-tuple-element.127), channel_id=1, source_target_pairs={{0,2},{1,3},{2,0},{3,1},{4,6},{5,7},{6,4},{7,5},{8,10},{9,11},{10,... | collective-permute-start | bytes 786440 | tf_op jit(solution)/shard_map/ppermute | solution.py:520
  112.4 23.1 %collective-permute-start.13 = (bf16[256,512]{1,0:T(8,128)(2,1)}, bf16[256,512]{1,0:T(8,128)(2,1)S(1)}, u32[]{:S(2)}, u32[]{:S(2)}) collective-permute-start(bf16[256,512]{1,0:T(8,128)(2,1)} %get-tuple-element.126), channel_id=1, source_target_pairs={{0,1},{1,2},{2,3},{3,0},{4,5},{5,6},{6,7},{7,4},{8,9},{9,10},{10,1... | collective-permute-start | bytes 786440 | tf_op jit(solution)/shard_map/ppermute | solution.py:520
  114.4 1.0 copy-start.2
  117.9 18.1 %copy-start.3 = (bf16[256,512]{1,0:T(8,128)(2,1)S(1)}, bf16[256,512]{1,0:T(8,128)(2,1)}, u32[]{:S(2)}) copy-start(bf16[256,512]{1,0:T(8,128)(2,1)} %get-tuple-element.125) | copy-start | bytes 786436

commit v5 on v4

--- a/solution.py
+++ b/solution.py
@@ -551,19 +551,16 @@
     strands = ((act_f, small_f, cumt_f), (act_r, small_r, cumt_r))
     ends = ((enter_f, prior_f), (enter_r, prior_r))
     entering, gated, same = incoming(message, "ctx", gates(place(0), hidden, g_f, g_r, 5e9), same)
+    other = lax.ppermute(jnp.concatenate(same, axis=0), "ctx", [(i, i ^ 1) for i in range(n_ctx)])
+    entering, other = lax.optimization_barrier((entering, other))
     bases = inside(place(0), strands, lanes, copy_first, heads, inner, 8e9)
     parts = finish(place(0), strands, ends, bases, gated, entering, copy_second, heads, inner)
-    (g_f, g_r), same, parts = lax.optimization_barrier(((g_f, g_r), same, parts))
-    swapped = lambda blocks: lax.ppermute(jnp.concatenate(blocks, axis=0), "ctx", [(i, i ^ 1) for i in range(n_ctx)])
-    other = None if pieces > 1 else swapped(same)
+    (g_f, g_r), parts = lax.optimization_barrier(((g_f, g_r), parts))
     arrived = [[rotated(block, d, n_head) if d else block for d, block in enumerate(parts)]]
     for k in range(1, pieces):
         gated = gates(place(k), hidden, g_f, g_r, 1e8)
-        if other is None:
-            gated, same = lax.optimization_barrier((gated, same))
-            other = swapped(same)
         parts = settle(place(k), strands, ends, gated, lanes, copy_first, entering, copy_second, heads, inner)
-        parts, arrived[k - 1], other, same = lax.optimization_barrier((parts, arrived[k - 1], other, same))
+        parts, arrived[k - 1] = lax.optimization_barrier((parts, arrived[k - 1]))
         arrived.append([rotated(block, d, n_head) if d else block for d, block in enumerate(parts)])
     own_rows = lax.dynamic_slice_in_dim(hidden, head * share, share, 0)
     groups = [w_out]

time: 139 us -> 133 us (0.957)
  waiting for transfers between devices: 26.6 us -> 21.1 us
  starting transfers between devices: 27.3 us -> 25.9 us
    ppermute x9, waiting for transfers between devices: 24.4 us -> 18.8 us  [rotated(): lax.ppermute(block, 'head', [(i, (i + d) % count) for i in range(count)])]
    ppermute x9, starting transfers between devices: 17.8 us -> 16.4 us  [rotated(): lax.ppermute(block, 'head', [(i, (i + d) % count) for i in range(count)])]
  transfers between devices with their start and end apart: 16 -> 16, of which waited for: 4 -> 3; matrix products, arithmetic and copies ran while one was open for 5% -> 6% of each run, Pallas kernels for 41% -> 48%
where the time goes in v5:
time: 133 us
  Pallas kernels  70.8 us (53%)
  starting transfers between devices  25.9 us (19%)
  waiting for transfers between devices  21.1 us (16%)
  matrix products  5.78 us (4%)
  other arithmetic  5.27 us (4%)
  local copies, waits for them, and re-layouts  3.51 us (3%)
    pallas_call x5, Pallas kernels, by_destination(): pl.pallas_call(lambda _, *refs: kernel(*refs), grid_spec=pltpu.PrefetchSc...  37.7 us
    pallas_call x1, Pallas kernels, project(): pl.pallas_call(functools.partial(project_kernel, heads, inner), grid=(n,)...  31.9 us
    ppermute x9, waiting for transfers between devices, rotated(): lax.ppermute(block, 'head', [(i, (i + d) % count) for i in range(count)])  18.8 us
    ppermute x9, starting transfers between devices, rotated(): lax.ppermute(block, 'head', [(i, (i + d) % count) for i in range(count)])  16.4 us
    dot_general x8, matrix products, on_device(): total = total + jnp.dot(block, weights, preferred_element_type=F32)  5.78 us
    ppermute x3, starting transfers between devices, incoming(): lax.ppermute(block, axis, [(i, i ^ d * distance) for i in range(count)])  3.92 us
    ppermute x1, starting transfers between devices, incoming(): lax.ppermute(message, axis, [(i, i ^ distance) for i in range(count)])  3 us
  transfers between devices with their start and end apart: 16, of which 3 were waited for; matrix products, arithmetic and copies ran while one was open for 6% of the time, Pallas kernels for 48%

profile of v5, /device:TPU:0, one launch (start us, length us, event | category | flops | bytes accessed | tf_op | source)
XLA Modules:
  0.0 132.6 jit_solution(3969424789099494431)
XLA Ops:
  2.1 3.0 %collective-permute-start.3 = (bf16[256,1024]{1,0:T(8,128)(2,1)}, bf16[256,1024]{1,0:T(8,128)(2,1)S(1)}, u32[]{:S(2)}, u32[]{:S(2)}) collective-permute-start(bf16[256,1024]{1,0:T(8,128)(2,1)} %constant_dynamic-slice_fusion.2), channel_id=1, source_target_pairs={{0,1},{1,2},{2,3},{3,0},{4,5},{5,6},{6,7},{7,4},{8,9},{9,10},{10,1... | collective-permute-start | bytes 1572872 | tf_op jit(solution)/shard_map/ppermute | solution.py:520
  5.1 2.6 %collective-permute-start.4 = (bf16[256,1024]{1,0:T(8,128)(2,1)}, bf16[256,1024]{1,0:T(8,128)(2,1)S(1)}, u32[]{:S(2)}, u32[]{:S(2)}) collective-permute-start(bf16[256,1024]{1,0:T(8,128)(2,1)} %constant_dynamic-slice_fusion.2), channel_id=1, source_target_pairs={{0,2},{1,3},{2,0},{3,1},{4,6},{5,7},{6,4},{7,5},{8,10},{9,11},{10,... | collective-permute-start | bytes 1572872 | tf_op jit(solution)/shard_map/ppermute | solution.py:520
  7.7 1.3 %collective-permute-start.5 = (bf16[256,1024]{1,0:T(8,128)(2,1)}, bf16[256,1024]{1,0:T(8,128)(2,1)S(1)}, u32[]{:S(2)}, u32[]{:S(2)}) collective-permute-start(bf16[256,1024]{1,0:T(8,128)(2,1)} %constant_dynamic-slice_fusion.2), channel_id=1, source_target_pairs={{0,3},{1,0},{2,1},{3,2},{4,7},{5,4},{6,5},{7,6},{8,11},{9,8},{10,9... | collective-permute-start | bytes 1572872 | tf_op jit(solution)/shard_map/ppermute | solution.py:520
  9.8 1.3 collective-permute-start
  11.1 1.3 collective-permute-start.1
  13.7 2.3 %collective-permute-done.1.refs_3_ = bf16[16,1024]{1,0:T(8,128)(2,1)S(1)} collective-permute-done((bf16[16,1024]{1,0:T(8,128)(2,1)S(1)}, bf16[16,1024]{1,0:T(8,128)(2,1)S(1)}, u32[]{:S(2)}, u32[]{:S(2)}) %collective-permute-start.1) | collective-permute-done | bytes 32800 | tf_op jit(solution)/shard_map/ppermute | solution.py:516
  16.5 31.9 %project.1 = (bf16[2048,768]{1,0:T(8,128)(2,1)}, f32[2048,128]{1,0:T(8,128)}, f32[8,2048]{1,0:T(8,128)}, bf16[16,128,512]{2,1,0:T(8,128)(2,1)}, f32[16,8,512]{2,...) custom-call(bf16[2048,1024]{1,0:T(8,128)(2,1)} %refs_0_.5, ...), custom_call_target="tpu_custom_call" | custom-call | flops 22000001024 | bytes 40000000 | tf_op jit(solution)/shard_map/project/pallas_call | solution.py:223
  48.4 3.0 %collective-permute-start.2 = (bf16[288,512]{1,0:T(8,128)(2,1)}, bf16[288,512]{1,0:T(8,128)(2,1)S(1)}, u32[]{:S(2)}, u32[]{:S(2)}) collective-permute-start(bf16[288,512]{1,0:T(8,128)(2,1)} %get-tuple-element.67.refs_1_), channel_id=1, source_target_pairs={{0,4},{4,0},{8,12},{12,8},{16,20},{20,16},{24,28},{28,24},{1,5},{5... | collective-permute-start | bytes 884744 | tf_op jit(solution)/shard_map/ppermute | solution.py:489
  51.4 5.8 %gates.2 = (bf16[1024,512]{1,0:T(8,128)(2,1)}, bf16[1024,512]{1,0:T(8,128)(2,1)}) custom-call(s32[1]{0:T(128)} %bitcast._, bf16[2048,1024]{1,0:T(8,128)(2,1)} %refs_0_.5, bf16[1024,512]{1,0:T(8,128)(2,1)} %get-tuple-element.88.refs_1_, bf16[1024,512]{1,0:T(8,128)(2,1)} %get-tuple-element.89.refs_2_), custom_call_target="tpu_custom_call" | custom-call | flops 5000000000 | bytes 1000000 | tf_op jit(solution)/shard_map/gates/pallas_call | solution.py:264
  57.5 1.3 pad_maximum_fusion
  58.9 1.6 %collective-permute-start.7 = (bf16[144,512]{1,0:T(8,128)(2,1)S(1)}, bf16[144,512]{1,0:T(8,128)(2,1)S(1)}, u32[]{:S(2)}, u32[]{:S(2)}) collective-permute-start(bf16[144,512]{1,0:T(8,128)(2,1)S(1)} %get-tuple-element.121), channel_id=1, source_target_pairs={{0,16},{4,20},{8,24},{12,28},{16,0},{20,4},{24,8},{28,12},{1,17},{... | collective-permute-start | bytes 442376 | tf_op jit(solution)/shard_map/ppermute | solution.py:508
  60.5 2.3 %collective-permute-start.8 = (bf16[144,512]{1,0:T(8,128)(2,1)S(1)}, bf16[144,512]{1,0:T(8,128)(2,1)S(1)}, u32[]{:S(2)}, u32[]{:S(2)}) collective-permute-start(bf16[144,512]{1,0:T(8,128)(2,1)S(1)} %get-tuple-element.121), channel_id=1, source_target_pairs={{0,24},{4,28},{8,16},{12,20},{16,8},{20,12},{24,0},{28,4},{1,25},{... | collective-permute-start | bytes 442376 | tf_op jit(solution)/shard_map/ppermute | solution.py:508
  62.8 7.2 %inside.1 = (bf16[1024,512]{1,0:T(8,128)(2,1)}, bf16[1024,512]{1,0:T(8,128)(2,1)}) custom-call(s32[1]{0:T(128)} %bitcast._, bf16[2048,768]{1,0:T(8,128)(2,1)} %get-tuple-element.57.refs_0_, f32[2048,128]{1,0:T(8,128)} %get-tuple-element.58.refs_1_.refs_3_, f32[8,2048]{1,0:T(8,128)} %get-tuple-element.59.refs_2_, ...), custom_call_target="tpu_custom_call" | custom-call | flops 8000000000 | bytes 1000000 | tf_op jit(solution)/shard_map/inside/pallas_call | solution.py:264
  71.1 7.5 %finish.1 = (bf16[256,512]{1,0:T(8,128)(2,1)}, bf16[256,512]{1,0:T(8,128)(2,1)}, bf16[256,512]{1,0:T(8,128)(2,1)}, bf16[256,512]{1,0:T(8,128)(2,1)}) custom-call(s32[1]{0:T(128)} %bitcast._, bf16[2048,768]{1,0:T(8,128)(2,1)} %get-tuple-element.57.refs_0_, bf16[16,128,512]{2,1,0:T(8,128)(2,1)} %get-tuple-element.63.refs_1_.refs_6_, ...), custom_call_target="tpu_custom_call" | custom-call | flops 100000000 | bytes 1000000 | tf_op jit(solution)/shard_map/finish/pallas_call | solution.py:264
  79.3 3.1 %collective-permute-start.12 = (bf16[256,512]{1,0:T(8,128)(2,1)}, bf16[256,512]{1,0:T(8,128)(2,1)S(1)}, u32[]{:S(2)}, u32[]{:S(2)}) collective-permute-start(bf16[256,512]{1,0:T(8,128)(2,1)} %get-tuple-element.99), channel_id=1, source_target_pairs={{0,3},{1,0},{2,1},{3,2},{4,7},{5,4},{6,5},{7,6},{8,11},{9,8},{10,9... | collective-permute-start | bytes 786440 | tf_op jit(solution)/shard_map/ppermute | solution.py:520
  82.5 5.8 %gates.3 = (bf16[1024,512]{1,0:T(8,128)(2,1)}, bf16[1024,512]{1,0:T(8,128)(2,1)}) custom-call(s32[1]{0:T(128)} %bitcast._, bf16[2048,1024]{1,0:T(8,128)(2,1)} %refs_0_.5, bf16[1024,512]{1,0:T(8,128)(2,1)} %get-tuple-element.88.refs_1_, bf16[1024,512]{1,0:T(8,128)(2,1)} %get-tuple-element.89.refs_2_), custom_call_target="tpu_custom_call" | custom-call | flops 100000000 | bytes 1000000 | tf_op jit(solution)/shard_map/gates/pallas_call | solution.py:264
  88.3 11.4 %settle.1 = (bf16[256,512]{1,0:T(8,128)(2,1)}, bf16[256,512]{1,0:T(8,128)(2,1)}, bf16[256,512]{1,0:T(8,128)(2,1)}, bf16[256,512]{1,0:T(8,128)(2,1)}) custom-call(s32[1]{0:T(128)} %bitcast._, bf16[2048,768]{1,0:T(8,128)(2,1)} %get-tuple-element.57.refs_0_, f32[2048,128]{1,0:T(8,128)} %get-tuple-element.58.refs_1_.refs_3_, ...), custom_call_target="tpu_custom_call" | custom-call | flops 100000000 | bytes 1000000 | tf_op jit(solution)/shard_map/settle/pallas_call | solution.py:264
  99.7 1.6 %broadcast_select_fusion.5 = (bf16[256,1024]{1,0:T(8,128)(2,1)S(1)}, bf16[256,1024]{1,0:T(8,128)(2,1)S(1)}, bf16[256,1024]{1,0:T(8,128)(2,1)S(1)}, bf16[256,1024...) fusion(bf16[256,1024]{1,0:T(8,128)(2,1)S(1)} %collective-permute-done.3, ...), kind=kLoop, calls=%fused_computation.26 | loop fusion | flops 1572864 | bytes 6291457 | tf_op jit(solution)/shard_map/jit(_where)/select_n | solution.py:569
  101.4 3.5 %collective-permute-start.15 = (bf16[256,512]{1,0:T(8,128)(2,1)S(1)}, bf16[256,512]{1,0:T(8,128)(2,1)S(1)}, u32[]{:S(2)}, u32[]{:S(2)}) collective-permute-start(bf16[256,512]{1,0:T(8,128)(2,1)S(1)} %copy-done.6), channel_id=1, source_target_pairs={{0,3},{1,0},{2,1},{3,2},{4,7},{5,4},{6,5},{7,6},{8,11},{9,8},{10,9... | collective-permute-start | bytes 786440 | tf_op jit(solution)/shard_map/ppermute | solution.py:520
  104.8 2.1 %collective-permute-start.14 = (bf16[256,512]{1,0:T(8,128)(2,1)S(1)}, bf16[256,512]{1,0:T(8,128)(2,1)S(1)}, u32[]{:S(2)}, u32[]{:S(2)}) collective-permute-start(bf16[256,512]{1,0:T(8,128)(2,1)S(1)} %copy-done.5), channel_id=1, source_target_pairs={{0,2},{1,3},{2,0},{3,1},{4,6},{5,7},{6,4},{7,5},{8,10},{9,11},{10,... | collective-permute-start | bytes 786440 | tf_op jit(solution)/shard_map/ppermute | solution.py:520
  108.3 1.6 %fusion.6 = bf16[256,1024]{1,0:T(8,128)(2,1)S(1)} fusion(f32[256,1024]{1,0:T(8,128)S(1)} %fusion.9, f32[256,1024]{1,0:T(8,128)S(1)} %fusion.11, f32[256,1024]{1,0:T(8,128)S(1)} %fusion.13, bf16[256,512]{1,0:T(8,128)(2,1)S(1)} %copy-done.3, bf16[512,1024]{1,0:T(8,128)(2,1)S(1)} %copy-done, bf16[2048,1024]{1,0:T(8,128)(2,1)} %refs_0_.5, s32[]{:T(128)S(6)} %select_n.70), kind=kOutput, calls=%fused_computation.9 | convolution fusion | flops 270008320 | bytes 5505028 | tf_op jit(solution)/shard_map/dot_general | solution.py:574
  109.9 1.8 %collective-permute-done.15 = bf16[256,512]{1,0:T(8,128)(2,1)S(1)} collective-permute-done((bf16[256,512]{1,0:T(8,128)(2,1)S(1)}, bf16[256,512]{1,0:T(8,128)(2,1)S(1)}, u32[]{:S(2)}, u32[]{:S(2)}) %collective-permute-start.15) | collective-permute-done | bytes 262176 | tf_op jit(solution)/shard_map/ppermute | solution.py:520
  112.1 17.0 %collective-permute-done.14 = bf16[256,512]{1,0:T(8,128)(2,1)S(1)} collective-permute-done((bf16[256,512]{1,0:T(8,128)(2,1)S(1)}, bf16[256,512]{1,0:T(8,128)(2,1)S(1)}, u32[]{:S(2)}, u32[]{:S(2)}) %collective-permute-start.14) | collective-permute-done | bytes 262176 | tf_op jit(solution)/shard_map/ppermute | solution.py:520
  130.0 1.6 %fusion.7 = bf16[256,1024]{1,0:T(8,128)(2,1)S(1)} fusion(f32[256,1024]{1,0:T(8,128)S(1)} %fusion.8, f32[256,1024]{1,0:T(8,128)S(1)} %fusion.10, f32[256,1024]{1,0:T(8,128)S(1)} %fusion.12, bf16[256,512]{1,0:T(8,128)(2,1)S(1)} %copy-done.2, bf16[512,1024]{1,0:T(8,128)(2,1)S(1)} %copy-done, bf16[2048,1024]{1,0:T(8,128)(2,1)} %refs_0_.5, s32[]{:T(128)S(6)} %add.70), kind=kOutput, calls=%fused_computation.10 | convolution fusion | flops 270008320 | bytes 5505028 | tf_op jit(solution)/shard_map/dot_general | solution.py:574
  (49 shorter events, 10.5 us)
Async XLA Ops:
  0.0 1.2 copy-start
  2.1 55.4 %collective-permute-start.3 = (bf16[256,1024]{1,0:T(8,128)(2,1)}, bf16[256,1024]{1,0:T(8,128)(2,1)S(1)}, u32[]{:S(2)}, u32[]{:S(2)}) collective-permute-start(bf16[256,1024]{1,0:T(8,128)(2,1)} %constant_dynamic-slice_fusion.2), channel_id=1, source_target_pairs={{0,1},{1,2},{2,3},{3,0},{4,5},{5,6},{6,7},{7,4},{8,9},{9,10},{10,1... | collective-permute-start | bytes 1572872 | tf_op jit(solution)/shard_map/ppermute | solution.py:520
  5.1 52.4 %collective-permute-start.4 = (bf16[256,1024]{1,0:T(8,128)(2,1)}, bf16[256,1024]{1,0:T(8,128)(2,1)S(1)}, u32[]{:S(2)}, u32[]{:S(2)}) collective-permute-start(bf16[256,1024]{1,0:T(8,128)(2,1)} %constant_dynamic-slice_fusion.2), channel_id=1, source_target_pairs={{0,2},{1,3},{2,0},{3,1},{4,6},{5,7},{6,4},{7,5},{8,10},{9,11},{10,... | collective-permute-start | bytes 1572872 | tf_op jit(solution)/shard_map/ppermute | solution.py:520
  7.7 49.8 %collective-permute-start.5 = (bf16[256,1024]{1,0:T(8,128)(2,1)}, bf16[256,1024]{1,0:T(8,128)(2,1)S(1)}, u32[]{:S(2)}, u32[]{:S(2)}) collective-permute-start(bf16[256,1024]{1,0:T(8,128)(2,1)} %constant_dynamic-slice_fusion.2), channel_id=1, source_target_pairs={{0,3},{1,0},{2,1},{3,2},{4,7},{5,4},{6,5},{7,6},{8,11},{9,8},{10,9... | collective-permute-start | bytes 1572872 | tf_op jit(solution)/shard_map/ppermute | solution.py:520
  9.8 3.9 %collective-permute-start = (bf16[16,1024]{1,0:T(8,128)(2,1)S(1)}, bf16[16,1024]{1,0:T(8,128)(2,1)S(1)}, u32[]{:S(2)}, u32[]{:S(2)}) collective-permute-start(bf16[16,1024]{1,0:T(8,128)(2,1)S(1)} %get-tuple-element.110), channel_id=1, source_target_pairs={{0,4},{4,8},{8,12},{12,16},{16,20},{20,24},{24,28},{1,5},{5,9},{9,... | collective-permute-start | bytes 98312 | tf_op jit(solution)/shard_map/ppermute | solution.py:516
  11.1 4.8 %collective-permute-start.1 = (bf16[16,1024]{1,0:T(8,128)(2,1)S(1)}, bf16[16,1024]{1,0:T(8,128)(2,1)S(1)}, u32[]{:S(2)}, u32[]{:S(2)}) collective-permute-start(bf16[16,1024]{1,0:T(8,128)(2,1)S(1)} %get-tuple-element.109), channel_id=1, source_target_pairs={{4,0},{8,4},{12,8},{16,12},{20,16},{24,20},{28,24},{5,1},{9,5},{13... | collective-permute-start | bytes 98312 | tf_op jit(solution)/shard_map/ppermute | solution.py:516
  13.7 2.3 %copy-start.7 = (bf16[16,1024]{1,0:T(8,128)(2,1)}, bf16[16,1024]{1,0:T(8,128)(2,1)S(1)}, u32[]{:S(2)}) copy-start(bf16[16,1024]{1,0:T(8,128)(2,1)S(1)} %collective-permute-done.refs_2_) | copy-start | bytes 98308
  48.4 8.8 %collective-permute-start.2 = (bf16[288,512]{1,0:T(8,128)(2,1)}, bf16[288,512]{1,0:T(8,128)(2,1)S(1)}, u32[]{:S(2)}, u32[]{:S(2)}) collective-permute-start(bf16[288,512]{1,0:T(8,128)(2,1)} %get-tuple-element.67.refs_1_), channel_id=1, source_target_pairs={{0,4},{4,0},{8,12},{12,8},{16,20},{20,16},{24,28},{28,24},{1,5},{5... | collective-permute-start | bytes 884744 | tf_op jit(solution)/shard_map/ppermute | solution.py:489
  51.4 5.8 %copy-start.1 = (bf16[288,512]{1,0:T(8,128)(2,1)S(1)}, bf16[288,512]{1,0:T(8,128)(2,1)}, u32[]{:S(2)}) copy-start(bf16[288,512]{1,0:T(8,128)(2,1)} %get-tuple-element.67.refs_1_) | copy-start | bytes 884740
  58.8 12.2 %collective-permute-start.9 = (bf16[768,1024]{1,0:T(8,128)(2,1)}, bf16[768,1024]{1,0:T(8,128)(2,1)}, u32[]{:S(2)}, u32[]{:S(2)}) collective-permute-start(bf16[768,1024]{1,0:T(8,128)(2,1)} %pad_maximum_fusion), channel_id=1, source_target_pairs={{0,4},{4,0},{8,12},{12,8},{16,20},{20,16},{24,28},{28,24},{1,5},{5... | collective-permute-start | bytes 4718600 | tf_op jit(solution)/shard_map/ppermute | solution.py:554
  58.9 11.1 %collective-permute-start.7 = (bf16[144,512]{1,0:T(8,128)(2,1)S(1)}, bf16[144,512]{1,0:T(8,128)(2,1)S(1)}, u32[]{:S(2)}, u32[]{:S(2)}) collective-permute-start(bf16[144,512]{1,0:T(8,128)(2,1)S(1)} %get-tuple-element.121), channel_id=1, source_target_pairs={{0,16},{4,20},{8,24},{12,28},{16,0},{20,4},{24,8},{28,12},{1,17},{... | collective-permute-start | bytes 442376 | tf_op jit(solution)/shard_map/ppermute | solution.py:508
  60.5 9.5 %collective-permute-start.8 = (bf16[144,512]{1,0:T(8,128)(2,1)S(1)}, bf16[144,512]{1,0:T(8,128)(2,1)S(1)}, u32[]{:S(2)}, u32[]{:S(2)}) collective-permute-start(bf16[144,512]{1,0:T(8,128)(2,1)S(1)} %get-tuple-element.121), channel_id=1, source_target_pairs={{0,24},{4,28},{8,16},{12,20},{16,8},{20,12},{24,0},{28,4},{1,25},{... | collective-permute-start | bytes 442376 | tf_op jit(solution)/shard_map/ppermute | solution.py:508
  62.8 7.2 %collective-permute-start.6 = (bf16[144,512]{1,0:T(8,128)(2,1)S(1)}, bf16[144,512]{1,0:T(8,128)(2,1)S(1)}, u32[]{:S(2)}, u32[]{:S(2)}) collective-permute-start(bf16[144,512]{1,0:T(8,128)(2,1)S(1)} %get-tuple-element.122), channel_id=1, source_target_pairs={{0,8},{4,12},{8,0},{12,4},{16,24},{20,28},{24,16},{28,20},{1,9},{5... | collective-permute-start | bytes 442376 | tf_op jit(solution)/shard_map/ppermute | solution.py:508
  78.6 22.7 %collective-permute-start.10 = (bf16[256,512]{1,0:T(8,128)(2,1)}, bf16[256,512]{1,0:T(8,128)(2,1)S(1)}, u32[]{:S(2)}, u32[]{:S(2)}) collective-permute-start(bf16[256,512]{1,0:T(8,128)(2,1)} %get-tuple-element.97), channel_id=1, source_target_pairs={{0,1},{1,2},{2,3},{3,0},{4,5},{5,6},{6,7},{7,4},{8,9},{9,10},{10,1... | collective-permute-start | bytes 786440 | tf_op jit(solution)/shard_map/ppermute | solution.py:520
  79.0 22.3 %collective-permute-start.11 = (bf16[256,512]{1,0:T(8,128)(2,1)}, bf16[256,512]{1,0:T(8,128)(2,1)S(1)}, u32[]{:S(2)}, u32[]{:S(2)}) collective-permute-start(bf16[256,512]{1,0:T(8,128)(2,1)} %get-tuple-element.98), channel_id=1, source_target_pairs={{0,2},{1,3},{2,0},{3,1},{4,6},{5,7},{6,4},{7,5},{8,10},{9,11},{10,... | collective-permute-start | bytes 786440 | tf_op jit(solution)/shard_map/ppermute | solution.py:520
  79.3 22.0 %collective-permute-start.12 = (bf16[256,512]{1,0:T(8,128)(2,1)}, bf16[256,512]{1,0:T(8,128)(2,1)S(1)}, u32[]{:S(2)}, u32[]{:S(2)}) collective-permute-start(bf16[256,512]{1,0:T(8,128)(2,1)} %get-tuple-element.99), channel_id=1, source_target_pairs={{0,3},{1,0},{2,1},{3,2},{4,7},{5,4},{6,5},{7,6},{8,11},{9,8},{10,9... | collective-permute-start | bytes 786440 | tf_op jit(solution)/shard_map/ppermute | solution.py:520
  99.6 1.7 %copy-start.6 = (bf16[256,512]{1,0:T(8,128)(2,1)S(1)}, bf16[256,512]{1,0:T(8,128)(2,1)}, u32[]{:S(2)}) copy-start(bf16[256,512]{1,0:T(8,128)(2,1)} %get-tuple-element.108) | copy-start | bytes 786436
  99.7 5.2 %copy-start.5 = (bf16[256,512]{1,0:T(8,128)(2,1)S(1)}, bf16[256,512]{1,0:T(8,128)(2,1)}, u32[]{:S(2)}) copy-start(bf16[256,512]{1,0:T(8,128)(2,1)} %get-tuple-element.107) | copy-start | bytes 786436
  99.7 7.2 %copy-start.4 = (bf16[256,512]{1,0:T(8,128)(2,1)S(1)}, bf16[256,512]{1,0:T(8,128)(2,1)}, u32[]{:S(2)}) copy-start(bf16[256,512]{1,0:T(8,128)(2,1)} %get-tuple-element.106) | copy-start | bytes 786436
  101.4 10.3 %collective-permute-start.15 = (bf16[256,512]{1,0:T(8,128)(2,1)S(1)}, bf16[256,512]{1,0:T(8,128)(2,1)S(1)}, u32[]{:S(2)}, u32[]{:S(2)}) collective-permute-start(bf16[256,512]{1,0:T(8,128)(2,1)S(1)} %copy-done.6), channel_id=1, source_target_pairs={{0,3},{1,0},{2,1},{3,2},{4,7},{5,4},{6,5},{7,6},{8,11},{9,8},{10,9... | collective-permute-start | bytes 786440 | tf_op jit(solution)/shard_map/ppermute | solution.py:520
  104.8 24.3 %collective-permute-start.14 = (bf16[256,512]{1,0:T(8,128)(2,1)S(1)}, bf16[256,512]{1,0:T(8,128)(2,1)S(1)}, u32[]{:S(2)}, u32[]{:S(2)}) collective-permute-start(bf16[256,512]{1,0:T(8,128)(2,1)S(1)} %copy-done.5), channel_id=1, source_target_pairs={{0,2},{1,3},{2,0},{3,1},{4,6},{5,7},{6,4},{7,5},{8,10},{9,11},{10,... | collective-permute-start | bytes 786440 | tf_op jit(solution)/shard_map/ppermute | solution.py:520
  106.9 22.6 %collective-permute-start.13 = (bf16[256,512]{1,0:T(8,128)(2,1)S(1)}, bf16[256,512]{1,0:T(8,128)(2,1)S(1)}, u32[]{:S(2)}, u32[]{:S(2)}) collective-permute-start(bf16[256,512]{1,0:T(8,128)(2,1)S(1)} %copy-done.4), channel_id=1, source_target_pairs={{0,1},{1,2},{2,3},{3,0},{4,5},{5,6},{6,7},{7,4},{8,9},{9,10},{10,1... | collective-permute-start | bytes 786440 | tf_op jit(solution)/shard_map/ppermute | solution.py:520
  107.4 1.0 copy-start.3
  112.1 17.9 %copy-start.2 = (bf16[256,512]{1,0:T(8,128)(2,1)S(1)}, bf16[256,512]{1,0:T(8,128)(2,1)}, u32[]{:S(2)}) copy-start(bf16[256,512]{1,0:T(8,128)(2,1)} %get-tuple-element.105) | copy-start | bytes 786436
  (1 other events, 0.6 us)

commit v6 on v5

--- a/solution.py
+++ b/solution.py
@@ -536,6 +536,7 @@
     half = w_out.shape[0] // 2
     parity = ctx % 2
     own_half = lax.dynamic_slice_in_dim(w_out, parity * half, half, 0)
+    rim_f, rim_r, own_half = lax.optimization_barrier((rim_f, rim_r, own_half))
     same = [rotated(own_half, d, n_head) for d in range(1, n_head)]
 
     lanes = jnp.pad(jnp.stack([dt_bias, decay_rate, skip_gain]), [(0, 0), (0, 128 - heads)])
@@ -570,8 +571,8 @@
     result = None
     for k in range(pieces):
         total = own_rows[k * size : (k + 1) * size].astype(F32)
-        for block, weights in zip(arrived[k], groups):
-            total = total + jnp.dot(block, weights, preferred_element_type=F32)
+        for d in sorted(range(n_head), key=lambda d: -abs(2 * d - n_head)):
+            total = total + jnp.dot(arrived[k][d], groups[d], preferred_element_type=F32)
         total = total.astype(BF16)
         if result is None:
             result = jnp.pad(total, ((0, share - size), (0, 0)))

time: 133 us -> 131 us (0.985)
  the two profiles are of different devices: /device:TPU:0 before, /device:TPU:10 now
where the time goes in v6:
time: 131 us; the launch traced here: 130 us
  Pallas kernels  70.8 us (54%)
  waiting for transfers between devices  23.4 us (18%)
  starting transfers between devices  22.4 us (17%)
  matrix products  5.8 us (4%)
  other arithmetic  5.27 us (4%)
  local copies, waits for them, and re-layouts  1.79 us (1%)
    pallas_call x5, Pallas kernels, by_destination(): pl.pallas_call(lambda _, *refs: kernel(*refs), grid_spec=pltpu.PrefetchSc...  37.7 us
    pallas_call x1, Pallas kernels, project(): pl.pallas_call(functools.partial(project_kernel, heads, inner), grid=(n,)...  31.9 us
    ppermute x9, waiting for transfers between devices, rotated(): lax.ppermute(block, 'head', [(i, (i + d) % count) for i in range(count)])  23.3 us
    ppermute x9, starting transfers between devices, rotated(): lax.ppermute(block, 'head', [(i, (i + d) % count) for i in range(count)])  12 us
    dot_general x8, matrix products, on_device(): jnp.dot(arrived[k][d], groups[d], preferred_element_type=F32)  5.8 us
    ppermute x2, starting transfers between devices, shifted(): lax.ppermute(block, axis, [(i - distance, i) for i in devices if i - dist...  5.55 us
    ppermute x3, starting transfers between devices, incoming(): lax.ppermute(block, axis, [(i, i ^ d * distance) for i in range(count)])  3.58 us
  transfers between devices with their start and end apart: 16, of which 6 were waited for; matrix products, arithmetic and copies ran while one was open for 6% of the time, Pallas kernels for 49%

profile of v6, /device:TPU:10, one launch (start us, length us, event | category | flops | bytes accessed | tf_op | source)
XLA Modules:
  0.0 129.6 jit_solution(17992120503616819065)
XLA Ops:
  0.9 1.9 %collective-permute-start = (bf16[16,1024]{1,0:T(8,128)(2,1)S(1)}, bf16[16,1024]{1,0:T(8,128)(2,1)S(1)}, u32[]{:S(2)}, u32[]{:S(2)}) collective-permute-start(bf16[16,1024]{1,0:T(8,128)(2,1)S(1)} %get-tuple-element.116), channel_id=1, source_target_pairs={{0,4},{4,8},{8,12},{12,16},{16,20},{20,24},{24,28},{1,5},{5,9},{9,... | collective-permute-start | bytes 98312 | tf_op jit(solution)/shard_map/ppermute | solution.py:516
  2.8 3.6 %collective-permute-start.1 = (bf16[16,1024]{1,0:T(8,128)(2,1)S(1)}, bf16[16,1024]{1,0:T(8,128)(2,1)S(1)}, u32[]{:S(2)}, u32[]{:S(2)}) collective-permute-start(bf16[16,1024]{1,0:T(8,128)(2,1)S(1)} %get-tuple-element.115), channel_id=1, source_target_pairs={{4,0},{8,4},{12,8},{16,12},{20,16},{24,20},{28,24},{5,1},{9,5},{13... | collective-permute-start | bytes 98312 | tf_op jit(solution)/shard_map/ppermute | solution.py:516
  8.6 1.6 %collective-permute-start.3 = (bf16[256,1024]{1,0:T(8,128)(2,1)}, bf16[256,1024]{1,0:T(8,128)(2,1)S(1)}, u32[]{:S(2)}, u32[]{:S(2)}) collective-permute-start(bf16[256,1024]{1,0:T(8,128)(2,1)} %constant_dynamic-slice_fusion.2), channel_id=1, source_target_pairs={{0,1},{1,2},{2,3},{3,0},{4,5},{5,6},{6,7},{7,4},{8,9},{9,10},{10,1... | collective-permute-start | bytes 1572872 | tf_op jit(solution)/shard_map/ppermute | solution.py:520
  11.5 1.8 %collective-permute-start.5 = (bf16[256,1024]{1,0:T(8,128)(2,1)}, bf16[256,1024]{1,0:T(8,128)(2,1)S(1)}, u32[]{:S(2)}, u32[]{:S(2)}) collective-permute-start(bf16[256,1024]{1,0:T(8,128)(2,1)} %constant_dynamic-slice_fusion.2), channel_id=1, source_target_pairs={{0,3},{1,0},{2,1},{3,2},{4,7},{5,4},{6,5},{7,6},{8,11},{9,8},{10,9... | collective-permute-start | bytes 1572872 | tf_op jit(solution)/shard_map/ppermute | solution.py:520
  13.3 31.9 %project.1 = (bf16[2048,768]{1,0:T(8,128)(2,1)}, f32[2048,128]{1,0:T(8,128)}, f32[8,2048]{1,0:T(8,128)}, bf16[16,128,512]{2,1,0:T(8,128)(2,1)}, f32[16,8,512]{2,...) custom-call(bf16[2048,1024]{1,0:T(8,128)(2,1)} %refs_0_.5, ...), custom_call_target="tpu_custom_call" | custom-call | flops 22000001024 | bytes 40000000 | tf_op jit(solution)/shard_map/project/pallas_call | solution.py:223
  46.3 5.8 %gates.2 = (bf16[1024,512]{1,0:T(8,128)(2,1)}, bf16[1024,512]{1,0:T(8,128)(2,1)}) custom-call(s32[1]{0:T(128)} %bitcast._, bf16[2048,1024]{1,0:T(8,128)(2,1)} %refs_0_.5, bf16[1024,512]{1,0:T(8,128)(2,1)} %get-tuple-element.94.refs_1_, bf16[1024,512]{1,0:T(8,128)(2,1)} %get-tuple-element.95.refs_2_), custom_call_target="tpu_custom_call" | custom-call | flops 5000000000 | bytes 1000000 | tf_op jit(solution)/shard_map/gates/pallas_call | solution.py:264
  52.3 3.4 %collective-permute-done.4 = bf16[256,1024]{1,0:T(8,128)(2,1)S(1)} collective-permute-done((bf16[256,1024]{1,0:T(8,128)(2,1)}, bf16[256,1024]{1,0:T(8,128)(2,1)S(1)}, u32[]{:S(2)}, u32[]{:S(2)}) %collective-permute-start.4) | collective-permute-done | bytes 524320 | tf_op jit(solution)/shard_map/ppermute | solution.py:520
  55.7 2.4 %collective-permute-done.5 = bf16[256,1024]{1,0:T(8,128)(2,1)S(1)} collective-permute-done((bf16[256,1024]{1,0:T(8,128)(2,1)}, bf16[256,1024]{1,0:T(8,128)(2,1)S(1)}, u32[]{:S(2)}, u32[]{:S(2)}) %collective-permute-start.5) | collective-permute-done | bytes 524320 | tf_op jit(solution)/shard_map/ppermute | solution.py:520
  59.7 1.6 %collective-permute-start.8 = (bf16[144,512]{1,0:T(8,128)(2,1)S(1)}, bf16[144,512]{1,0:T(8,128)(2,1)S(1)}, u32[]{:S(2)}, u32[]{:S(2)}) collective-permute-start(bf16[144,512]{1,0:T(8,128)(2,1)S(1)} %get-tuple-element.127), channel_id=1, source_target_pairs={{0,24},{4,28},{8,16},{12,20},{16,8},{20,12},{24,0},{28,4},{1,25},{... | collective-permute-start | bytes 442376 | tf_op jit(solution)/shard_map/ppermute | solution.py:508
  61.3 1.9 %collective-permute-start.6 = (bf16[144,512]{1,0:T(8,128)(2,1)S(1)}, bf16[144,512]{1,0:T(8,128)(2,1)S(1)}, u32[]{:S(2)}, u32[]{:S(2)}) collective-permute-start(bf16[144,512]{1,0:T(8,128)(2,1)S(1)} %get-tuple-element.128), channel_id=1, source_target_pairs={{0,8},{4,12},{8,0},{12,4},{16,24},{20,28},{24,16},{28,20},{1,9},{5... | collective-permute-start | bytes 442376 | tf_op jit(solution)/shard_map/ppermute | solution.py:508
  63.2 7.2 %inside.1 = (bf16[1024,512]{1,0:T(8,128)(2,1)}, bf16[1024,512]{1,0:T(8,128)(2,1)}) custom-call(s32[1]{0:T(128)} %bitcast._, bf16[2048,768]{1,0:T(8,128)(2,1)} %get-tuple-element.62.refs_0_, f32[2048,128]{1,0:T(8,128)} %get-tuple-element.63.refs_1_.refs_3_, f32[8,2048]{1,0:T(8,128)} %get-tuple-element.64.refs_2_, ...), custom_call_target="tpu_custom_call" | custom-call | flops 8000000000 | bytes 1000000 | tf_op jit(solution)/shard_map/inside/pallas_call | solution.py:264
  71.4 7.5 %finish.1 = (bf16[256,512]{1,0:T(8,128)(2,1)}, bf16[256,512]{1,0:T(8,128)(2,1)}, bf16[256,512]{1,0:T(8,128)(2,1)}, bf16[256,512]{1,0:T(8,128)(2,1)}) custom-call(s32[1]{0:T(128)} %bitcast._, bf16[2048,768]{1,0:T(8,128)(2,1)} %get-tuple-element.62.refs_0_, bf16[16,128,512]{2,1,0:T(8,128)(2,1)} %get-tuple-element.68.refs_1_.refs_6_, ...), custom_call_target="tpu_custom_call" | custom-call | flops 100000000 | bytes 1000000 | tf_op jit(solution)/shard_map/finish/pallas_call | solution.py:264
  79.0 1.5 %collective-permute-start.11 = (bf16[256,512]{1,0:T(8,128)(2,1)}, bf16[256,512]{1,0:T(8,128)(2,1)S(1)}, u32[]{:S(2)}, u32[]{:S(2)}) collective-permute-start(bf16[256,512]{1,0:T(8,128)(2,1)} %get-tuple-element.104), channel_id=1, source_target_pairs={{0,2},{1,3},{2,0},{3,1},{4,6},{5,7},{6,4},{7,5},{8,10},{9,11},{10,... | collective-permute-start | bytes 786440 | tf_op jit(solution)/shard_map/ppermute | solution.py:520
  80.4 1.9 %collective-permute-start.12 = (bf16[256,512]{1,0:T(8,128)(2,1)}, bf16[256,512]{1,0:T(8,128)(2,1)S(1)}, u32[]{:S(2)}, u32[]{:S(2)}) collective-permute-start(bf16[256,512]{1,0:T(8,128)(2,1)} %get-tuple-element.105), channel_id=1, source_target_pairs={{0,3},{1,0},{2,1},{3,2},{4,7},{5,4},{6,5},{7,6},{8,11},{9,8},{10,9... | collective-permute-start | bytes 786440 | tf_op jit(solution)/shard_map/ppermute | solution.py:520
  82.4 5.8 %gates.3 = (bf16[1024,512]{1,0:T(8,128)(2,1)}, bf16[1024,512]{1,0:T(8,128)(2,1)}) custom-call(s32[1]{0:T(128)} %bitcast._, bf16[2048,1024]{1,0:T(8,128)(2,1)} %refs_0_.5, bf16[1024,512]{1,0:T(8,128)(2,1)} %get-tuple-element.94.refs_1_, bf16[1024,512]{1,0:T(8,128)(2,1)} %get-tuple-element.95.refs_2_), custom_call_target="tpu_custom_call" | custom-call | flops 100000000 | bytes 1000000 | tf_op jit(solution)/shard_map/gates/pallas_call | solution.py:264
  88.2 11.4 %settle.1 = (bf16[256,512]{1,0:T(8,128)(2,1)}, bf16[256,512]{1,0:T(8,128)(2,1)}, bf16[256,512]{1,0:T(8,128)(2,1)}, bf16[256,512]{1,0:T(8,128)(2,1)}) custom-call(s32[1]{0:T(128)} %bitcast._, bf16[2048,768]{1,0:T(8,128)(2,1)} %get-tuple-element.62.refs_0_, f32[2048,128]{1,0:T(8,128)} %get-tuple-element.63.refs_1_.refs_3_, ...), custom_call_target="tpu_custom_call" | custom-call | flops 100000000 | bytes 1000000 | tf_op jit(solution)/shard_map/settle/pallas_call | solution.py:264
  99.6 1.6 %broadcast_select_fusion.5 = (bf16[256,1024]{1,0:T(8,128)(2,1)S(1)}, bf16[256,1024]{1,0:T(8,128)(2,1)S(1)}, bf16[256,1024]{1,0:T(8,128)(2,1)S(1)}, bf16[256,1024...) fusion(bf16[256,1024]{1,0:T(8,128)(2,1)S(1)} %collective-permute-done.3, ...), kind=kLoop, calls=%fused_computation.26 | loop fusion | flops 1572864 | bytes 6291457 | tf_op jit(solution)/shard_map/jit(_where)/select_n | solution.py:570
  101.7 1.4 %collective-permute-done.12 = bf16[256,512]{1,0:T(8,128)(2,1)S(1)} collective-permute-done((bf16[256,512]{1,0:T(8,128)(2,1)}, bf16[256,512]{1,0:T(8,128)(2,1)S(1)}, u32[]{:S(2)}, u32[]{:S(2)}) %collective-permute-start.12) | collective-permute-done | bytes 262176 | tf_op jit(solution)/shard_map/ppermute | solution.py:520
  103.1 1.9 %collective-permute-start.15 = (bf16[256,512]{1,0:T(8,128)(2,1)S(1)}, bf16[256,512]{1,0:T(8,128)(2,1)S(1)}, u32[]{:S(2)}, u32[]{:S(2)}) collective-permute-start(bf16[256,512]{1,0:T(8,128)(2,1)S(1)} %copy-done.6), channel_id=1, source_target_pairs={{0,2},{1,3},{2,0},{3,1},{4,6},{5,7},{6,4},{7,5},{8,10},{9,11},{10,... | collective-permute-start | bytes 786440 | tf_op jit(solution)/shard_map/ppermute | solution.py:520
  105.0 2.0 %collective-permute-start.13 = (bf16[256,512]{1,0:T(8,128)(2,1)S(1)}, bf16[256,512]{1,0:T(8,128)(2,1)S(1)}, u32[]{:S(2)}, u32[]{:S(2)}) collective-permute-start(bf16[256,512]{1,0:T(8,128)(2,1)S(1)} %copy-done.4), channel_id=1, source_target_pairs={{0,1},{1,2},{2,3},{3,0},{4,5},{5,6},{6,7},{7,4},{8,9},{9,10},{10,1... | collective-permute-start | bytes 786440 | tf_op jit(solution)/shard_map/ppermute | solution.py:520
  108.4 1.6 %fusion.6 = bf16[256,1024]{1,0:T(8,128)(2,1)S(1)} fusion(f32[256,1024]{1,0:T(8,128)S(1)} %fusion.9, f32[256,1024]{1,0:T(8,128)S(1)} %fusion.11, f32[256,1024]{1,0:T(8,128)S(1)} %fusion.13, bf16[256,512]{1,0:T(8,128)(2,1)S(1)} %copy-done.3, bf16[512,1024]{1,0:T(8,128)(2,1)S(1)} %copy-done, bf16[2048,1024]{1,0:T(8,128)(2,1)} %refs_0_.5, s32[]{:T(128)S(6)} %select_n.70), kind=kOutput, calls=%fused_computation.9 | convolution fusion | flops 270008320 | bytes 5505028 | tf_op jit(solution)/shard_map/dot_general | solution.py:575
  110.0 10.8 %collective-permute-done.15 = bf16[256,512]{1,0:T(8,128)(2,1)S(1)} collective-permute-done((bf16[256,512]{1,0:T(8,128)(2,1)S(1)}, bf16[256,512]{1,0:T(8,128)(2,1)S(1)}, u32[]{:S(2)}, u32[]{:S(2)}) %collective-permute-start.15) | collective-permute-done | bytes 262176 | tf_op jit(solution)/shard_map/ppermute | solution.py:520
  121.3 4.9 %collective-permute-done.14 = bf16[256,512]{1,0:T(8,128)(2,1)S(1)} collective-permute-done((bf16[256,512]{1,0:T(8,128)(2,1)S(1)}, bf16[256,512]{1,0:T(8,128)(2,1)S(1)}, u32[]{:S(2)}, u32[]{:S(2)}) %collective-permute-start.14) | collective-permute-done | bytes 262176 | tf_op jit(solution)/shard_map/ppermute | solution.py:520
  127.0 1.6 %fusion.7 = bf16[256,1024]{1,0:T(8,128)(2,1)S(1)} fusion(f32[256,1024]{1,0:T(8,128)S(1)} %fusion.8, f32[256,1024]{1,0:T(8,128)S(1)} %fusion.10, f32[256,1024]{1,0:T(8,128)S(1)} %fusion.12, bf16[256,512]{1,0:T(8,128)(2,1)S(1)} %copy-done.2, bf16[512,1024]{1,0:T(8,128)(2,1)S(1)} %copy-done, bf16[2048,1024]{1,0:T(8,128)(2,1)} %refs_0_.5, s32[]{:T(128)S(6)} %add.70), kind=kOutput, calls=%fused_computation.10 | convolution fusion | flops 270008320 | bytes 5505028 | tf_op jit(solution)/shard_map/dot_general | solution.py:575
  (49 shorter events, 12.4 us)
Async XLA Ops:
  0.0 6.5 %copy-start = (bf16[512,1024]{1,0:T(8,128)(2,1)S(1)}, bf16[512,1024]{1,0:T(8,128)(2,1)}, u32[]{:S(2)}) copy-start(bf16[512,1024]{1,0:T(8,128)(2,1)} %param.23) | copy-start | bytes 3145732
  0.9 7.7 %collective-permute-start = (bf16[16,1024]{1,0:T(8,128)(2,1)S(1)}, bf16[16,1024]{1,0:T(8,128)(2,1)S(1)}, u32[]{:S(2)}, u32[]{:S(2)}) collective-permute-start(bf16[16,1024]{1,0:T(8,128)(2,1)S(1)} %get-tuple-element.116), channel_id=1, source_target_pairs={{0,4},{4,8},{8,12},{12,16},{16,20},{20,24},{24,28},{1,5},{5,9},{9,... | collective-permute-start | bytes 98312 | tf_op jit(solution)/shard_map/ppermute | solution.py:516
  2.8 5.8 %collective-permute-start.1 = (bf16[16,1024]{1,0:T(8,128)(2,1)S(1)}, bf16[16,1024]{1,0:T(8,128)(2,1)S(1)}, u32[]{:S(2)}, u32[]{:S(2)}) collective-permute-start(bf16[16,1024]{1,0:T(8,128)(2,1)S(1)} %get-tuple-element.115), channel_id=1, source_target_pairs={{4,0},{8,4},{12,8},{16,12},{20,16},{24,20},{28,24},{5,1},{9,5},{13... | collective-permute-start | bytes 98312 | tf_op jit(solution)/shard_map/ppermute | solution.py:516
  8.6 4.7 %copy-start.7 = (bf16[16,1024]{1,0:T(8,128)(2,1)}, bf16[16,1024]{1,0:T(8,128)(2,1)S(1)}, u32[]{:S(2)}) copy-start(bf16[16,1024]{1,0:T(8,128)(2,1)S(1)} %collective-permute-done.refs_2_) | copy-start | bytes 98308
  8.6 4.7 %copy-start.8 = (bf16[16,1024]{1,0:T(8,128)(2,1)}, bf16[16,1024]{1,0:T(8,128)(2,1)S(1)}, u32[]{:S(2)}) copy-start(bf16[16,1024]{1,0:T(8,128)(2,1)S(1)} %collective-permute-done.1.refs_3_) | copy-start | bytes 98308
  8.6 43.7 %collective-permute-start.3 = (bf16[256,1024]{1,0:T(8,128)(2,1)}, bf16[256,1024]{1,0:T(8,128)(2,1)S(1)}, u32[]{:S(2)}, u32[]{:S(2)}) collective-permute-start(bf16[256,1024]{1,0:T(8,128)(2,1)} %constant_dynamic-slice_fusion.2), channel_id=1, source_target_pairs={{0,1},{1,2},{2,3},{3,0},{4,5},{5,6},{6,7},{7,4},{8,9},{9,10},{10,1... | collective-permute-start | bytes 1572872 | tf_op jit(solution)/shard_map/ppermute | solution.py:520
  10.2 45.5 %collective-permute-start.4 = (bf16[256,1024]{1,0:T(8,128)(2,1)}, bf16[256,1024]{1,0:T(8,128)(2,1)S(1)}, u32[]{:S(2)}, u32[]{:S(2)}) collective-permute-start(bf16[256,1024]{1,0:T(8,128)(2,1)} %constant_dynamic-slice_fusion.2), channel_id=1, source_target_pairs={{0,2},{1,3},{2,0},{3,1},{4,6},{5,7},{6,4},{7,5},{8,10},{9,11},{10,... | collective-permute-start | bytes 1572872 | tf_op jit(solution)/shard_map/ppermute | solution.py:520
  11.5 46.7 %collective-permute-start.5 = (bf16[256,1024]{1,0:T(8,128)(2,1)}, bf16[256,1024]{1,0:T(8,128)(2,1)S(1)}, u32[]{:S(2)}, u32[]{:S(2)}) collective-permute-start(bf16[256,1024]{1,0:T(8,128)(2,1)} %constant_dynamic-slice_fusion.2), channel_id=1, source_target_pairs={{0,3},{1,0},{2,1},{3,2},{4,7},{5,4},{6,5},{7,6},{8,11},{9,8},{10,9... | collective-permute-start | bytes 1572872 | tf_op jit(solution)/shard_map/ppermute | solution.py:520
  45.2 6.9 %collective-permute-start.2 = (bf16[288,512]{1,0:T(8,128)(2,1)}, bf16[288,512]{1,0:T(8,128)(2,1)S(1)}, u32[]{:S(2)}, u32[]{:S(2)}) collective-permute-start(bf16[288,512]{1,0:T(8,128)(2,1)} %get-tuple-element.72.refs_1_), channel_id=1, source_target_pairs={{0,4},{4,0},{8,12},{12,8},{16,20},{20,16},{24,28},{28,24},{1,5},{5... | collective-permute-start | bytes 884744 | tf_op jit(solution)/shard_map/ppermute | solution.py:489
  46.3 5.8 %copy-start.1 = (bf16[288,512]{1,0:T(8,128)(2,1)S(1)}, bf16[288,512]{1,0:T(8,128)(2,1)}, u32[]{:S(2)}) copy-start(bf16[288,512]{1,0:T(8,128)(2,1)} %get-tuple-element.72.refs_1_) | copy-start | bytes 884740
  59.5 11.9 %collective-permute-start.9 = (bf16[768,1024]{1,0:T(8,128)(2,1)}, bf16[768,1024]{1,0:T(8,128)(2,1)}, u32[]{:S(2)}, u32[]{:S(2)}) collective-permute-start(bf16[768,1024]{1,0:T(8,128)(2,1)} %pad_maximum_fusion), channel_id=1, source_target_pairs={{0,4},{4,0},{8,12},{12,8},{16,20},{20,16},{24,28},{28,24},{1,5},{5... | collective-permute-start | bytes 4718600 | tf_op jit(solution)/shard_map/ppermute | solution.py:555
  59.6 10.7 %collective-permute-start.7 = (bf16[144,512]{1,0:T(8,128)(2,1)S(1)}, bf16[144,512]{1,0:T(8,128)(2,1)S(1)}, u32[]{:S(2)}, u32[]{:S(2)}) collective-permute-start(bf16[144,512]{1,0:T(8,128)(2,1)S(1)} %get-tuple-element.127), channel_id=1, source_target_pairs={{0,16},{4,20},{8,24},{12,28},{16,0},{20,4},{24,8},{28,12},{1,17},{... | collective-permute-start | bytes 442376 | tf_op jit(solution)/shard_map/ppermute | solution.py:508
  59.7 10.7 %collective-permute-start.8 = (bf16[144,512]{1,0:T(8,128)(2,1)S(1)}, bf16[144,512]{1,0:T(8,128)(2,1)S(1)}, u32[]{:S(2)}, u32[]{:S(2)}) collective-permute-start(bf16[144,512]{1,0:T(8,128)(2,1)S(1)} %get-tuple-element.127), channel_id=1, source_target_pairs={{0,24},{4,28},{8,16},{12,20},{16,8},{20,12},{24,0},{28,4},{1,25},{... | collective-permute-start | bytes 442376 | tf_op jit(solution)/shard_map/ppermute | solution.py:508
  61.3 9.1 %collective-permute-start.6 = (bf16[144,512]{1,0:T(8,128)(2,1)S(1)}, bf16[144,512]{1,0:T(8,128)(2,1)S(1)}, u32[]{:S(2)}, u32[]{:S(2)}) collective-permute-start(bf16[144,512]{1,0:T(8,128)(2,1)S(1)} %get-tuple-element.128), channel_id=1, source_target_pairs={{0,8},{4,12},{8,0},{12,4},{16,24},{20,28},{24,16},{28,20},{1,9},{5... | collective-permute-start | bytes 442376 | tf_op jit(solution)/shard_map/ppermute | solution.py:508
  78.9 22.3 %collective-permute-start.10 = (bf16[256,512]{1,0:T(8,128)(2,1)}, bf16[256,512]{1,0:T(8,128)(2,1)S(1)}, u32[]{:S(2)}, u32[]{:S(2)}) collective-permute-start(bf16[256,512]{1,0:T(8,128)(2,1)} %get-tuple-element.103), channel_id=1, source_target_pairs={{0,1},{1,2},{2,3},{3,0},{4,5},{5,6},{6,7},{7,4},{8,9},{9,10},{10,1... | collective-permute-start | bytes 786440 | tf_op jit(solution)/shard_map/ppermute | solution.py:520
  79.0 22.7 %collective-permute-start.11 = (bf16[256,512]{1,0:T(8,128)(2,1)}, bf16[256,512]{1,0:T(8,128)(2,1)S(1)}, u32[]{:S(2)}, u32[]{:S(2)}) collective-permute-start(bf16[256,512]{1,0:T(8,128)(2,1)} %get-tuple-element.104), channel_id=1, source_target_pairs={{0,2},{1,3},{2,0},{3,1},{4,6},{5,7},{6,4},{7,5},{8,10},{9,11},{10,... | collective-permute-start | bytes 786440 | tf_op jit(solution)/shard_map/ppermute | solution.py:520
  80.4 22.7 %collective-permute-start.12 = (bf16[256,512]{1,0:T(8,128)(2,1)}, bf16[256,512]{1,0:T(8,128)(2,1)S(1)}, u32[]{:S(2)}, u32[]{:S(2)}) collective-permute-start(bf16[256,512]{1,0:T(8,128)(2,1)} %get-tuple-element.105), channel_id=1, source_target_pairs={{0,3},{1,0},{2,1},{3,2},{4,7},{5,4},{6,5},{7,6},{8,11},{9,8},{10,9... | collective-permute-start | bytes 786440 | tf_op jit(solution)/shard_map/ppermute | solution.py:520
  99.6 3.5 %copy-start.6 = (bf16[256,512]{1,0:T(8,128)(2,1)S(1)}, bf16[256,512]{1,0:T(8,128)(2,1)}, u32[]{:S(2)}) copy-start(bf16[256,512]{1,0:T(8,128)(2,1)} %get-tuple-element.114) | copy-start | bytes 786436
  99.6 5.4 %copy-start.5 = (bf16[256,512]{1,0:T(8,128)(2,1)S(1)}, bf16[256,512]{1,0:T(8,128)(2,1)}, u32[]{:S(2)}) copy-start(bf16[256,512]{1,0:T(8,128)(2,1)} %get-tuple-element.113) | copy-start | bytes 786436
  99.6 5.4 %copy-start.4 = (bf16[256,512]{1,0:T(8,128)(2,1)S(1)}, bf16[256,512]{1,0:T(8,128)(2,1)}, u32[]{:S(2)}) copy-start(bf16[256,512]{1,0:T(8,128)(2,1)} %get-tuple-element.112) | copy-start | bytes 786436
  103.1 17.7 %collective-permute-start.15 = (bf16[256,512]{1,0:T(8,128)(2,1)S(1)}, bf16[256,512]{1,0:T(8,128)(2,1)S(1)}, u32[]{:S(2)}, u32[]{:S(2)}) collective-permute-start(bf16[256,512]{1,0:T(8,128)(2,1)S(1)} %copy-done.6), channel_id=1, source_target_pairs={{0,2},{1,3},{2,0},{3,1},{4,6},{5,7},{6,4},{7,5},{8,10},{9,11},{10,... | collective-permute-start | bytes 786440 | tf_op jit(solution)/shard_map/ppermute | solution.py:520
  105.0 21.1 %collective-permute-start.14 = (bf16[256,512]{1,0:T(8,128)(2,1)S(1)}, bf16[256,512]{1,0:T(8,128)(2,1)S(1)}, u32[]{:S(2)}, u32[]{:S(2)}) collective-permute-start(bf16[256,512]{1,0:T(8,128)(2,1)S(1)} %copy-done.5), channel_id=1, source_target_pairs={{0,3},{1,0},{2,1},{3,2},{4,7},{5,4},{6,5},{7,6},{8,11},{9,8},{10,9... | collective-permute-start | bytes 786440 | tf_op jit(solution)/shard_map/ppermute | solution.py:520
  105.0 21.6 %collective-permute-start.13 = (bf16[256,512]{1,0:T(8,128)(2,1)S(1)}, bf16[256,512]{1,0:T(8,128)(2,1)S(1)}, u32[]{:S(2)}, u32[]{:S(2)}) collective-permute-start(bf16[256,512]{1,0:T(8,128)(2,1)S(1)} %copy-done.4), channel_id=1, source_target_pairs={{0,1},{1,2},{2,3},{3,0},{4,5},{5,6},{6,7},{7,4},{8,9},{9,10},{10,1... | collective-permute-start | bytes 786440 | tf_op jit(solution)/shard_map/ppermute | solution.py:520
  121.2 5.8 %copy-start.2 = (bf16[256,512]{1,0:T(8,128)(2,1)S(1)}, bf16[256,512]{1,0:T(8,128)(2,1)}, u32[]{:S(2)}) copy-start(bf16[256,512]{1,0:T(8,128)(2,1)} %get-tuple-element.111) | copy-start | bytes 786436
  (1 other events, 1.0 us)

commit v7 on v6

--- a/solution.py
+++ b/solution.py
@@ -537,7 +537,9 @@
     parity = ctx % 2
     own_half = lax.dynamic_slice_in_dim(w_out, parity * half, half, 0)
     rim_f, rim_r, own_half = lax.optimization_barrier((rim_f, rim_r, own_half))
-    same = [rotated(own_half, d, n_head) for d in range(1, n_head)]
+    middle = n_head // 2
+    early = [d for d in range(1, n_head) if d != middle]
+    same = [rotated(own_half, d, n_head) for d in early]
 
     lanes = jnp.pad(jnp.stack([dt_bias, decay_rate, skip_gain]), [(0, 0), (0, 128 - heads)])
     copy_first = spread_matrix(0, heads, width)
@@ -551,22 +553,27 @@
     place = lambda k: (k, pieces, tile, rows, head.astype(jnp.int32).reshape(1), n_head)
     strands = ((act_f, small_f, cumt_f), (act_r, small_r, cumt_r))
     ends = ((enter_f, prior_f), (enter_r, prior_r))
+    message, own_half, *same = lax.optimization_barrier((message, own_half, *same))
+    across = rotated(same[early.index(middle - 1)], 1, n_head) if middle > 1 else rotated(own_half, 1, n_head)
     entering, gated, same = incoming(message, "ctx", gates(place(0), hidden, g_f, g_r, 5e9), same)
     other = lax.ppermute(jnp.concatenate(same, axis=0), "ctx", [(i, i ^ 1) for i in range(n_ctx)])
     entering, other = lax.optimization_barrier((entering, other))
     bases = inside(place(0), strands, lanes, copy_first, heads, inner, 8e9)
     parts = finish(place(0), strands, ends, bases, gated, entering, copy_second, heads, inner)
-    (g_f, g_r), parts = lax.optimization_barrier(((g_f, g_r), parts))
+    (g_f, g_r), parts, across = lax.optimization_barrier(((g_f, g_r), parts, across))
+    across_other = lax.ppermute(across, "ctx", [(i, i ^ 1) for i in range(n_ctx)])
     arrived = [[rotated(block, d, n_head) if d else block for d, block in enumerate(parts)]]
     for k in range(1, pieces):
         gated = gates(place(k), hidden, g_f, g_r, 1e8)
         parts = settle(place(k), strands, ends, gated, lanes, copy_first, entering, copy_second, heads, inner)
-        parts, arrived[k - 1] = lax.optimization_barrier((parts, arrived[k - 1]))
+        parts, arrived[k - 1], across_other = lax.optimization_barrier((parts, arrived[k - 1], across_other))
         arrived.append([rotated(block, d, n_head) if d else block for d, block in enumerate(parts)])
     own_rows = lax.dynamic_slice_in_dim(hidden, head * share, share, 0)
+    pairs = {d: (one, other[i * half : (i + 1) * half]) for i, (d, one) in enumerate(zip(early, same))}
+    pairs[middle] = (across, across_other)
     groups = [w_out]
-    for d, one in enumerate(same):
-        two = other[d * half : (d + 1) * half]
+    for d in range(1, n_head):
+        one, two = pairs[d]
         groups.append(jnp.concatenate([jnp.where(parity == 0, one, two), jnp.where(parity == 0, two, one)], axis=0))
     result = None
     for k in range(pieces):

time: 131 us -> 127 us (0.969)
  waiting for transfers between devices: 23.4 us -> 19.9 us
    ppermute x9, waiting for transfers between devices: 23.3 us -> 19.7 us  [rotated(): lax.ppermute(block, 'head', [(i, (i + d) % count) for i in range(count)])]
  transfers between devices with their start and end apart: 16 -> 17, of which waited for: 6 -> 5; matrix products, arithmetic and copies ran while one was open for 6% -> 5% of each run, Pallas kernels for 49% -> 56%
where the time goes in v7:
time: 127 us; the launch traced here: 126 us
  Pallas kernels  70.7 us (56%)
  starting transfers between devices  23.2 us (18%)
  waiting for transfers between devices  19.9 us (16%)
  matrix products  5.78 us (5%)
  other arithmetic  4.85 us (4%)
    pallas_call x5, Pallas kernels, by_destination(): pl.pallas_call(lambda _, *refs: kernel(*refs), grid_spec=pltpu.PrefetchSc...  37.6 us
    pallas_call x1, Pallas kernels, project(): pl.pallas_call(functools.partial(project_kernel, heads, inner), grid=(n,)...  31.9 us
    ppermute x9, waiting for transfers between devices, rotated(): lax.ppermute(block, 'head', [(i, (i + d) % count) for i in range(count)])  19.7 us
    ppermute x9, starting transfers between devices, rotated(): lax.ppermute(block, 'head', [(i, (i + d) % count) for i in range(count)])  12 us
    dot_general x8, matrix products, on_device(): jnp.dot(arrived[k][d], groups[d], preferred_element_type=F32)  5.78 us
    ppermute x2, starting transfers between devices, shifted(): lax.ppermute(block, axis, [(i - distance, i) for i in devices if i - dist...  5.55 us
    ppermute x3, starting transfers between devices, incoming(): lax.ppermute(block, axis, [(i, i ^ d * distance) for i in range(count)])  3.55 us
  transfers between devices with their start and end apart: 17, of which 5 were waited for; matrix products, arithmetic and copies ran while one was open for 5% of the time, Pallas kernels for 56%

profile of v7, /device:TPU:10, one launch (start us, length us, event | category | flops | bytes accessed | tf_op | source)
XLA Modules:
  0.0 125.8 jit_solution(1690619418502563802)
XLA Ops:
  0.9 1.9 %collective-permute-start = (bf16[16,1024]{1,0:T(8,128)(2,1)S(1)}, bf16[16,1024]{1,0:T(8,128)(2,1)S(1)}, u32[]{:S(2)}, u32[]{:S(2)}) collective-permute-start(bf16[16,1024]{1,0:T(8,128)(2,1)S(1)} %get-tuple-element.124), channel_id=1, source_target_pairs={{0,4},{4,8},{8,12},{12,16},{16,20},{20,24},{24,28},{1,5},{5,9},{9,... | collective-permute-start | bytes 98312 | tf_op jit(solution)/shard_map/ppermute | solution.py:516
  2.8 3.6 %collective-permute-start.1 = (bf16[16,1024]{1,0:T(8,128)(2,1)S(1)}, bf16[16,1024]{1,0:T(8,128)(2,1)S(1)}, u32[]{:S(2)}, u32[]{:S(2)}) collective-permute-start(bf16[16,1024]{1,0:T(8,128)(2,1)S(1)} %get-tuple-element.123), channel_id=1, source_target_pairs={{4,0},{8,4},{12,8},{16,12},{20,16},{24,20},{28,24},{5,1},{9,5},{13... | collective-permute-start | bytes 98312 | tf_op jit(solution)/shard_map/ppermute | solution.py:516
  6.5 1.3 %select_maximum_fusion.refs_10_.refs_6_ = f32[3,128]{1,0:T(4,128)} fusion(f32[1,8]{1,0:T(1,128)} %bitcast.18, f32[1,8]{1,0:T(1,128)} %bitcast.19, f32[1,8]{1,0:T(1,128)} %bitcast.20), kind=kLoop, calls=%fused_computation.27 | loop fusion | flops 2304 | bytes 1632 | tf_op jit(solution)/shard_map/stack | solution.py:544
  8.0 1.6 %collective-permute-start.2 = (bf16[256,1024]{1,0:T(8,128)(2,1)S(1)}, bf16[256,1024]{1,0:T(8,128)(2,1)S(1)}, u32[]{:S(2)}, u32[]{:S(2)}) collective-permute-start(bf16[256,1024]{1,0:T(8,128)(2,1)S(1)} %constant_dynamic-slice_fusion.2), channel_id=1, source_target_pairs={{0,1},{1,2},{2,3},{3,0},{4,5},{5,6},{6,7},{7,4},{8,9},{9,10},{10,1... | collective-permute-start | bytes 1572872 | tf_op jit(solution)/shard_map/ppermute | solution.py:520
  10.0 31.9 %project.1 = (bf16[2048,768]{1,0:T(8,128)(2,1)}, f32[2048,128]{1,0:T(8,128)}, f32[8,2048]{1,0:T(8,128)}, bf16[16,128,512]{2,1,0:T(8,128)(2,1)}, f32[16,8,512]{2,...) custom-call(bf16[2048,1024]{1,0:T(8,128)(2,1)} %refs_0_.5, ...), custom_call_target="tpu_custom_call" | custom-call | flops 22000001024 | bytes 40000000 | tf_op jit(solution)/shard_map/project/pallas_call | solution.py:223
  42.0 2.0 %collective-permute-start.4 = (bf16[288,512]{1,0:T(8,128)(2,1)}, bf16[288,512]{1,0:T(8,128)(2,1)S(1)}, u32[]{:S(2)}, u32[]{:S(2)}) collective-permute-start(bf16[288,512]{1,0:T(8,128)(2,1)} %get-tuple-element.78.refs_1_), channel_id=1, source_target_pairs={{0,4},{4,0},{8,12},{12,8},{16,20},{20,16},{24,28},{28,24},{1,5},{5... | collective-permute-start | bytes 884744 | tf_op jit(solution)/shard_map/ppermute | solution.py:489
  44.0 5.8 %gates.2 = (bf16[1024,512]{1,0:T(8,128)(2,1)}, bf16[1024,512]{1,0:T(8,128)(2,1)}) custom-call(s32[1]{0:T(128)} %bitcast._, bf16[2048,1024]{1,0:T(8,128)(2,1)} %refs_0_.5, bf16[1024,512]{1,0:T(8,128)(2,1)} %get-tuple-element.100.refs_1_, bf16[1024,512]{1,0:T(8,128)(2,1)} %get-tuple-element.101.refs_2_), custom_call_target="tpu_custom_call" | custom-call | flops 5000000000 | bytes 1000000 | tf_op jit(solution)/shard_map/gates/pallas_call | solution.py:264
  51.1 1.6 %collective-permute-start.9 = (bf16[256,1024]{1,0:T(8,128)(2,1)S(1)}, bf16[256,1024]{1,0:T(8,128)(2,1)S(1)}, u32[]{:S(2)}, u32[]{:S(2)}) collective-permute-start(bf16[256,1024]{1,0:T(8,128)(2,1)S(1)} %collective-permute-done.2), channel_id=1, source_target_pairs={{0,1},{1,2},{2,3},{3,0},{4,5},{5,6},{6,7},{7,4},{8,9},{9,10},{10,1... | collective-permute-start | bytes 1572872 | tf_op jit(solution)/shard_map/ppermute | solution.py:520
  53.9 2.4 %collective-permute-start.5 = (bf16[144,512]{1,0:T(8,128)(2,1)S(1)}, bf16[144,512]{1,0:T(8,128)(2,1)S(1)}, u32[]{:S(2)}, u32[]{:S(2)}) collective-permute-start(bf16[144,512]{1,0:T(8,128)(2,1)S(1)} %get-tuple-element.134), channel_id=1, source_target_pairs={{0,8},{4,12},{8,0},{12,4},{16,24},{20,28},{24,16},{28,20},{1,9},{5... | collective-permute-start | bytes 442376 | tf_op jit(solution)/shard_map/ppermute | solution.py:508
  56.3 7.2 %inside.1 = (bf16[1024,512]{1,0:T(8,128)(2,1)}, bf16[1024,512]{1,0:T(8,128)(2,1)}) custom-call(s32[1]{0:T(128)} %bitcast._, bf16[2048,768]{1,0:T(8,128)(2,1)} %get-tuple-element.66.refs_0_, f32[2048,128]{1,0:T(8,128)} %get-tuple-element.67.refs_1_.refs_3_, f32[8,2048]{1,0:T(8,128)} %get-tuple-element.68.refs_2_, ...), custom_call_target="tpu_custom_call" | custom-call | flops 8000000000 | bytes 1000000 | tf_op jit(solution)/shard_map/inside/pallas_call | solution.py:264
  64.4 7.5 %finish.1 = (bf16[256,512]{1,0:T(8,128)(2,1)}, bf16[256,512]{1,0:T(8,128)(2,1)}, bf16[256,512]{1,0:T(8,128)(2,1)}, bf16[256,512]{1,0:T(8,128)(2,1)}) custom-call(s32[1]{0:T(128)} %bitcast._, bf16[2048,768]{1,0:T(8,128)(2,1)} %get-tuple-element.66.refs_0_, bf16[16,128,512]{2,1,0:T(8,128)(2,1)} %get-tuple-element.72.refs_1_.refs_6_, ...), custom_call_target="tpu_custom_call" | custom-call | flops 100000000 | bytes 1000000 | tf_op jit(solution)/shard_map/finish/pallas_call | solution.py:264
  72.0 1.6 %collective-permute-start.10 = (bf16[256,512]{1,0:T(8,128)(2,1)}, bf16[256,512]{1,0:T(8,128)(2,1)S(1)}, u32[]{:S(2)}, u32[]{:S(2)}) collective-permute-start(bf16[256,512]{1,0:T(8,128)(2,1)} %get-tuple-element.109), channel_id=1, source_target_pairs={{0,1},{1,2},{2,3},{3,0},{4,5},{5,6},{6,7},{7,4},{8,9},{9,10},{10,1... | collective-permute-start | bytes 786440 | tf_op jit(solution)/shard_map/ppermute | solution.py:520
  73.7 1.6 %collective-permute-start.11 = (bf16[256,512]{1,0:T(8,128)(2,1)}, bf16[256,512]{1,0:T(8,128)(2,1)S(1)}, u32[]{:S(2)}, u32[]{:S(2)}) collective-permute-start(bf16[256,512]{1,0:T(8,128)(2,1)} %get-tuple-element.110), channel_id=1, source_target_pairs={{0,2},{1,3},{2,0},{3,1},{4,6},{5,7},{6,4},{7,5},{8,10},{9,11},{10,... | collective-permute-start | bytes 786440 | tf_op jit(solution)/shard_map/ppermute | solution.py:520
  75.3 1.9 %collective-permute-start.12 = (bf16[256,512]{1,0:T(8,128)(2,1)}, bf16[256,512]{1,0:T(8,128)(2,1)S(1)}, u32[]{:S(2)}, u32[]{:S(2)}) collective-permute-start(bf16[256,512]{1,0:T(8,128)(2,1)} %get-tuple-element.111), channel_id=1, source_target_pairs={{0,3},{1,0},{2,1},{3,2},{4,7},{5,4},{6,5},{7,6},{8,11},{9,8},{10,9... | collective-permute-start | bytes 786440 | tf_op jit(solution)/shard_map/ppermute | solution.py:520
  77.2 5.8 %gates.3 = (bf16[1024,512]{1,0:T(8,128)(2,1)}, bf16[1024,512]{1,0:T(8,128)(2,1)}) custom-call(s32[1]{0:T(128)} %bitcast._, bf16[2048,1024]{1,0:T(8,128)(2,1)} %refs_0_.5, bf16[1024,512]{1,0:T(8,128)(2,1)} %get-tuple-element.100.refs_1_, bf16[1024,512]{1,0:T(8,128)(2,1)} %get-tuple-element.101.refs_2_), custom_call_target="tpu_custom_call" | custom-call | flops 100000000 | bytes 1000000 | tf_op jit(solution)/shard_map/gates/pallas_call | solution.py:264
  83.0 11.4 %settle.1 = (bf16[256,512]{1,0:T(8,128)(2,1)}, bf16[256,512]{1,0:T(8,128)(2,1)}, bf16[256,512]{1,0:T(8,128)(2,1)}, bf16[256,512]{1,0:T(8,128)(2,1)}) custom-call(s32[1]{0:T(128)} %bitcast._, bf16[2048,768]{1,0:T(8,128)(2,1)} %get-tuple-element.66.refs_0_, f32[2048,128]{1,0:T(8,128)} %get-tuple-element.67.refs_1_.refs_3_, ...), custom_call_target="tpu_custom_call" | custom-call | flops 100000000 | bytes 1000000 | tf_op jit(solution)/shard_map/settle/pallas_call | solution.py:264
  94.4 1.4 %broadcast_select_fusion.5 = (bf16[256,1024]{1,0:T(8,128)(2,1)S(1)}, bf16[256,1024]{1,0:T(8,128)(2,1)S(1)}, bf16[256,1024]{1,0:T(8,128)(2,1)S(1)}, bf16[256,1024]{1,0:T(8,128)(2,1)S(1)}) fusion(bf16[256,1024]{1,0:T(8,128)(2,1)S(1)} %collective-permute-done.2, pred[]{:T(512)S(6)} %eq.14, bf16[512,1024]{1,0:T(8,128)(2,1)} %collective-permute-done.8, ...), kind=kLoop, calls=%fused_computation.26 | loop fusion | flops 1048576 | bytes 4194305 | tf_op jit(solution)/shard_map/jit(_where)/select_n | solution.py:577
  95.8 1.2 collective-permute-done.11
  97.0 2.2 %collective-permute-done.12 = bf16[256,512]{1,0:T(8,128)(2,1)S(1)} collective-permute-done((bf16[256,512]{1,0:T(8,128)(2,1)}, bf16[256,512]{1,0:T(8,128)(2,1)S(1)}, u32[]{:S(2)}, u32[]{:S(2)}) %collective-permute-start.12) | collective-permute-done | bytes 262176 | tf_op jit(solution)/shard_map/ppermute | solution.py:520
  100.5 2.0 %collective-permute-start.14 = (bf16[256,512]{1,0:T(8,128)(2,1)S(1)}, bf16[256,512]{1,0:T(8,128)(2,1)S(1)}, u32[]{:S(2)}, u32[]{:S(2)}) collective-permute-start(bf16[256,512]{1,0:T(8,128)(2,1)S(1)} %copy-done.4), channel_id=1, source_target_pairs={{0,1},{1,2},{2,3},{3,0},{4,5},{5,6},{6,7},{7,4},{8,9},{9,10},{10,1... | collective-permute-start | bytes 786440 | tf_op jit(solution)/shard_map/ppermute | solution.py:520
  103.9 1.5 %fusion.6 = bf16[256,1024]{1,0:T(8,128)(2,1)S(1)} fusion(f32[256,1024]{1,0:T(8,128)S(1)} %fusion.9, f32[256,1024]{1,0:T(8,128)S(1)} %fusion.11, f32[256,1024]{1,0:T(8,128)S(1)} %fusion.13, bf16[256,512]{1,0:T(8,128)(2,1)S(1)} %copy-done.2, bf16[512,1024]{1,0:T(8,128)(2,1)S(1)} %copy-done, bf16[2048,1024]{1,0:T(8,128)(2,1)} %refs_0_.5, s32[]{:T(128)S(6)} %select_n.70), kind=kOutput, calls=%fused_computation.8 | convolution fusion | flops 270008320 | bytes 5505028 | tf_op jit(solution)/shard_map/dot_general | solution.py:582
  105.5 11.4 %collective-permute-done.16 = bf16[256,512]{1,0:T(8,128)(2,1)S(1)} collective-permute-done((bf16[256,512]{1,0:T(8,128)(2,1)S(1)}, bf16[256,512]{1,0:T(8,128)(2,1)S(1)}, u32[]{:S(2)}, u32[]{:S(2)}) %collective-permute-start.16) | collective-permute-done | bytes 262176 | tf_op jit(solution)/shard_map/ppermute | solution.py:520
  117.4 4.9 %collective-permute-done.15 = bf16[256,512]{1,0:T(8,128)(2,1)S(1)} collective-permute-done((bf16[256,512]{1,0:T(8,128)(2,1)S(1)}, bf16[256,512]{1,0:T(8,128)(2,1)S(1)}, u32[]{:S(2)}, u32[]{:S(2)}) %collective-permute-start.15) | collective-permute-done | bytes 262176 | tf_op jit(solution)/shard_map/ppermute | solution.py:520
  123.2 1.6 %fusion.7 = bf16[256,1024]{1,0:T(8,128)(2,1)S(1)} fusion(f32[256,1024]{1,0:T(8,128)S(1)} %fusion.8, f32[256,1024]{1,0:T(8,128)S(1)} %fusion.10, f32[256,1024]{1,0:T(8,128)S(1)} %fusion.12, bf16[256,512]{1,0:T(8,128)(2,1)S(1)} %copy-done.3, bf16[512,1024]{1,0:T(8,128)(2,1)S(1)} %copy-done, bf16[2048,1024]{1,0:T(8,128)(2,1)} %refs_0_.5, s32[]{:T(128)S(6)} %add.70), kind=kOutput, calls=%fused_computation.9 | convolution fusion | flops 270008320 | bytes 5505028 | tf_op jit(solution)/shard_map/dot_general | solution.py:582
  (52 shorter events, 10.2 us)
Async XLA Ops:
  0.0 6.5 %copy-start = (bf16[512,1024]{1,0:T(8,128)(2,1)S(1)}, bf16[512,1024]{1,0:T(8,128)(2,1)}, u32[]{:S(2)}) copy-start(bf16[512,1024]{1,0:T(8,128)(2,1)} %param.23) | copy-start | bytes 3145732
  0.9 6.9 %collective-permute-start = (bf16[16,1024]{1,0:T(8,128)(2,1)S(1)}, bf16[16,1024]{1,0:T(8,128)(2,1)S(1)}, u32[]{:S(2)}, u32[]{:S(2)}) collective-permute-start(bf16[16,1024]{1,0:T(8,128)(2,1)S(1)} %get-tuple-element.124), channel_id=1, source_target_pairs={{0,4},{4,8},{8,12},{12,16},{16,20},{20,24},{24,28},{1,5},{5,9},{9,... | collective-permute-start | bytes 98312 | tf_op jit(solution)/shard_map/ppermute | solution.py:516
  2.8 5.2 %collective-permute-start.1 = (bf16[16,1024]{1,0:T(8,128)(2,1)S(1)}, bf16[16,1024]{1,0:T(8,128)(2,1)S(1)}, u32[]{:S(2)}, u32[]{:S(2)}) collective-permute-start(bf16[16,1024]{1,0:T(8,128)(2,1)S(1)} %get-tuple-element.123), channel_id=1, source_target_pairs={{4,0},{8,4},{12,8},{16,12},{20,16},{24,20},{28,24},{5,1},{9,5},{13... | collective-permute-start | bytes 98312 | tf_op jit(solution)/shard_map/ppermute | solution.py:516
  7.8 2.2 %copy-start.7 = (bf16[16,1024]{1,0:T(8,128)(2,1)}, bf16[16,1024]{1,0:T(8,128)(2,1)S(1)}, u32[]{:S(2)}) copy-start(bf16[16,1024]{1,0:T(8,128)(2,1)S(1)} %collective-permute-done.refs_2_) | copy-start | bytes 98308
  8.0 33.9 %collective-permute-start.2 = (bf16[256,1024]{1,0:T(8,128)(2,1)S(1)}, bf16[256,1024]{1,0:T(8,128)(2,1)S(1)}, u32[]{:S(2)}, u32[]{:S(2)}) collective-permute-start(bf16[256,1024]{1,0:T(8,128)(2,1)S(1)} %constant_dynamic-slice_fusion.2), channel_id=1, source_target_pairs={{0,1},{1,2},{2,3},{3,0},{4,5},{5,6},{6,7},{7,4},{8,9},{9,10},{10,1... | collective-permute-start | bytes 1572872 | tf_op jit(solution)/shard_map/ppermute | solution.py:520
  9.6 32.4 %collective-permute-start.3 = (bf16[256,1024]{1,0:T(8,128)(2,1)S(1)}, bf16[256,1024]{1,0:T(8,128)(2,1)S(1)}, u32[]{:S(2)}, u32[]{:S(2)}) collective-permute-start(bf16[256,1024]{1,0:T(8,128)(2,1)S(1)} %constant_dynamic-slice_fusion.2), channel_id=1, source_target_pairs={{0,3},{1,0},{2,1},{3,2},{4,7},{5,4},{6,5},{7,6},{8,11},{9,8},{10,9... | collective-permute-start | bytes 1572872 | tf_op jit(solution)/shard_map/ppermute | solution.py:520
  42.0 7.8 %collective-permute-start.4 = (bf16[288,512]{1,0:T(8,128)(2,1)}, bf16[288,512]{1,0:T(8,128)(2,1)S(1)}, u32[]{:S(2)}, u32[]{:S(2)}) collective-permute-start(bf16[288,512]{1,0:T(8,128)(2,1)} %get-tuple-element.78.refs_1_), channel_id=1, source_target_pairs={{0,4},{4,0},{8,12},{12,8},{16,20},{20,16},{24,28},{28,24},{1,5},{5... | collective-permute-start | bytes 884744 | tf_op jit(solution)/shard_map/ppermute | solution.py:489
  44.0 5.8 %copy-start.1 = (bf16[288,512]{1,0:T(8,128)(2,1)S(1)}, bf16[288,512]{1,0:T(8,128)(2,1)}, u32[]{:S(2)}) copy-start(bf16[288,512]{1,0:T(8,128)(2,1)} %get-tuple-element.78.refs_1_) | copy-start | bytes 884740
  51.1 13.4 %collective-permute-start.8 = (bf16[512,1024]{1,0:T(8,128)(2,1)}, bf16[512,1024]{1,0:T(8,128)(2,1)}, u32[]{:S(2)}, u32[]{:S(2)}) collective-permute-start(bf16[512,1024]{1,0:T(8,128)(2,1)} %pad_maximum_fusion), channel_id=1, source_target_pairs={{0,4},{4,0},{8,12},{12,8},{16,20},{20,16},{24,28},{28,24},{1,5},{5... | collective-permute-start | bytes 3145736 | tf_op jit(solution)/shard_map/ppermute | solution.py:559
  51.1 20.8 %collective-permute-start.9 = (bf16[256,1024]{1,0:T(8,128)(2,1)S(1)}, bf16[256,1024]{1,0:T(8,128)(2,1)S(1)}, u32[]{:S(2)}, u32[]{:S(2)}) collective-permute-start(bf16[256,1024]{1,0:T(8,128)(2,1)S(1)} %collective-permute-done.2), channel_id=1, source_target_pairs={{0,1},{1,2},{2,3},{3,0},{4,5},{5,6},{6,7},{7,4},{8,9},{9,10},{10,1... | collective-permute-start | bytes 1572872 | tf_op jit(solution)/shard_map/ppermute | solution.py:520
  52.7 10.7 %collective-permute-start.6 = (bf16[144,512]{1,0:T(8,128)(2,1)S(1)}, bf16[144,512]{1,0:T(8,128)(2,1)S(1)}, u32[]{:S(2)}, u32[]{:S(2)}) collective-permute-start(bf16[144,512]{1,0:T(8,128)(2,1)S(1)} %get-tuple-element.133), channel_id=1, source_target_pairs={{0,16},{4,20},{8,24},{12,28},{16,0},{20,4},{24,8},{28,12},{1,17},{... | collective-permute-start | bytes 442376 | tf_op jit(solution)/shard_map/ppermute | solution.py:508
  52.8 10.6 %collective-permute-start.7 = (bf16[144,512]{1,0:T(8,128)(2,1)S(1)}, bf16[144,512]{1,0:T(8,128)(2,1)S(1)}, u32[]{:S(2)}, u32[]{:S(2)}) collective-permute-start(bf16[144,512]{1,0:T(8,128)(2,1)S(1)} %get-tuple-element.133), channel_id=1, source_target_pairs={{0,24},{4,28},{8,16},{12,20},{16,8},{20,12},{24,0},{28,4},{1,25},{... | collective-permute-start | bytes 442376 | tf_op jit(solution)/shard_map/ppermute | solution.py:508
  53.9 9.5 %collective-permute-start.5 = (bf16[144,512]{1,0:T(8,128)(2,1)S(1)}, bf16[144,512]{1,0:T(8,128)(2,1)S(1)}, u32[]{:S(2)}, u32[]{:S(2)}) collective-permute-start(bf16[144,512]{1,0:T(8,128)(2,1)S(1)} %get-tuple-element.134), channel_id=1, source_target_pairs={{0,8},{4,12},{8,0},{12,4},{16,24},{20,28},{24,16},{28,20},{1,9},{5... | collective-permute-start | bytes 442376 | tf_op jit(solution)/shard_map/ppermute | solution.py:508
  72.0 27.2 %collective-permute-start.13 = (bf16[256,1024]{1,0:T(8,128)(2,1)S(1)}, bf16[256,1024]{1,0:T(8,128)(2,1)S(1)}, u32[]{:S(2)}, u32[]{:S(2)}) collective-permute-start(bf16[256,1024]{1,0:T(8,128)(2,1)S(1)} %collective-permute-done.9), channel_id=1, source_target_pairs={{0,4},{4,0},{8,12},{12,8},{16,20},{20,16},{24,28},{28,24},{1,5},{5... | collective-permute-start | bytes 1572872 | tf_op jit(solution)/shard_map/ppermute | solution.py:564
  72.0 23.7 %collective-permute-start.10 = (bf16[256,512]{1,0:T(8,128)(2,1)}, bf16[256,512]{1,0:T(8,128)(2,1)S(1)}, u32[]{:S(2)}, u32[]{:S(2)}) collective-permute-start(bf16[256,512]{1,0:T(8,128)(2,1)} %get-tuple-element.109), channel_id=1, source_target_pairs={{0,1},{1,2},{2,3},{3,0},{4,5},{5,6},{6,7},{7,4},{8,9},{9,10},{10,1... | collective-permute-start | bytes 786440 | tf_op jit(solution)/shard_map/ppermute | solution.py:520
  73.7 23.3 %collective-permute-start.11 = (bf16[256,512]{1,0:T(8,128)(2,1)}, bf16[256,512]{1,0:T(8,128)(2,1)S(1)}, u32[]{:S(2)}, u32[]{:S(2)}) collective-permute-start(bf16[256,512]{1,0:T(8,128)(2,1)} %get-tuple-element.110), channel_id=1, source_target_pairs={{0,2},{1,3},{2,0},{3,1},{4,6},{5,7},{6,4},{7,5},{8,10},{9,11},{10,... | collective-permute-start | bytes 786440 | tf_op jit(solution)/shard_map/ppermute | solution.py:520
  75.3 23.9 %collective-permute-start.12 = (bf16[256,512]{1,0:T(8,128)(2,1)}, bf16[256,512]{1,0:T(8,128)(2,1)S(1)}, u32[]{:S(2)}, u32[]{:S(2)}) collective-permute-start(bf16[256,512]{1,0:T(8,128)(2,1)} %get-tuple-element.111), channel_id=1, source_target_pairs={{0,3},{1,0},{2,1},{3,2},{4,7},{5,4},{6,5},{7,6},{8,11},{9,8},{10,9... | collective-permute-start | bytes 786440 | tf_op jit(solution)/shard_map/ppermute | solution.py:520
  94.4 4.8 %copy-start.6 = (bf16[256,512]{1,0:T(8,128)(2,1)S(1)}, bf16[256,512]{1,0:T(8,128)(2,1)}, u32[]{:S(2)}) copy-start(bf16[256,512]{1,0:T(8,128)(2,1)} %get-tuple-element.122) | copy-start | bytes 786436
  95.8 4.7 %copy-start.5 = (bf16[256,512]{1,0:T(8,128)(2,1)S(1)}, bf16[256,512]{1,0:T(8,128)(2,1)}, u32[]{:S(2)}) copy-start(bf16[256,512]{1,0:T(8,128)(2,1)} %get-tuple-element.121) | copy-start | bytes 786436
  95.8 4.8 %copy-start.4 = (bf16[256,512]{1,0:T(8,128)(2,1)S(1)}, bf16[256,512]{1,0:T(8,128)(2,1)}, u32[]{:S(2)}) copy-start(bf16[256,512]{1,0:T(8,128)(2,1)} %get-tuple-element.120) | copy-start | bytes 786436
  99.2 17.7 %collective-permute-start.16 = (bf16[256,512]{1,0:T(8,128)(2,1)S(1)}, bf16[256,512]{1,0:T(8,128)(2,1)S(1)}, u32[]{:S(2)}, u32[]{:S(2)}) collective-permute-start(bf16[256,512]{1,0:T(8,128)(2,1)S(1)} %copy-done.6), channel_id=1, source_target_pairs={{0,2},{1,3},{2,0},{3,1},{4,6},{5,7},{6,4},{7,5},{8,10},{9,11},{10,... | collective-permute-start | bytes 786440 | tf_op jit(solution)/shard_map/ppermute | solution.py:520
  100.5 21.8 %collective-permute-start.15 = (bf16[256,512]{1,0:T(8,128)(2,1)S(1)}, bf16[256,512]{1,0:T(8,128)(2,1)S(1)}, u32[]{:S(2)}, u32[]{:S(2)}) collective-permute-start(bf16[256,512]{1,0:T(8,128)(2,1)S(1)} %copy-done.5), channel_id=1, source_target_pairs={{0,3},{1,0},{2,1},{3,2},{4,7},{5,4},{6,5},{7,6},{8,11},{9,8},{10,9... | collective-permute-start | bytes 786440 | tf_op jit(solution)/shard_map/ppermute | solution.py:520
  100.5 22.2 %collective-permute-start.14 = (bf16[256,512]{1,0:T(8,128)(2,1)S(1)}, bf16[256,512]{1,0:T(8,128)(2,1)S(1)}, u32[]{:S(2)}, u32[]{:S(2)}) collective-permute-start(bf16[256,512]{1,0:T(8,128)(2,1)S(1)} %copy-done.4), channel_id=1, source_target_pairs={{0,1},{1,2},{2,3},{3,0},{4,5},{5,6},{6,7},{7,4},{8,9},{9,10},{10,1... | collective-permute-start | bytes 786440 | tf_op jit(solution)/shard_map/ppermute | solution.py:520
  117.4 5.8 %copy-start.3 = (bf16[256,512]{1,0:T(8,128)(2,1)S(1)}, bf16[256,512]{1,0:T(8,128)(2,1)}, u32[]{:S(2)}) copy-start(bf16[256,512]{1,0:T(8,128)(2,1)} %get-tuple-element.119) | copy-start | bytes 786436
  (2 other events, 3.0 us)

commit v8 on v7

--- a/solution.py
+++ b/solution.py
@@ -562,12 +562,13 @@
     parts = finish(place(0), strands, ends, bases, gated, entering, copy_second, heads, inner)
     (g_f, g_r), parts, across = lax.optimization_barrier(((g_f, g_r), parts, across))
     across_other = lax.ppermute(across, "ctx", [(i, i ^ 1) for i in range(n_ctx)])
-    arrived = [[rotated(block, d, n_head) if d else block for d, block in enumerate(parts)]]
+    middle_first = sorted(range(1, n_head), key=lambda d: abs(2 * d - n_head))
+    arrived = [{0: parts[0], **{d: rotated(parts[d], d, n_head) for d in middle_first}}]
     for k in range(1, pieces):
         gated = gates(place(k), hidden, g_f, g_r, 1e8)
         parts = settle(place(k), strands, ends, gated, lanes, copy_first, entering, copy_second, heads, inner)
         parts, arrived[k - 1], across_other = lax.optimization_barrier((parts, arrived[k - 1], across_other))
-        arrived.append([rotated(block, d, n_head) if d else block for d, block in enumerate(parts)])
+        arrived.append({0: parts[0], **{d: rotated(parts[d], d, n_head) for d in middle_first}})
     own_rows = lax.dynamic_slice_in_dim(hidden, head * share, share, 0)
     pairs = {d: (one, other[i * half : (i + 1) * half]) for i, (d, one) in enumerate(zip(early, same))}
     pairs[middle] = (across, across_other)
@@ -576,11 +577,15 @@
         one, two = pairs[d]
         groups.append(jnp.concatenate([jnp.where(parity == 0, one, two), jnp.where(parity == 0, two, one)], axis=0))
     result = None
+    order = sorted(range(n_head), key=lambda d: (-abs(2 * d - n_head), -d))
+    order = order[:-2] + order[:-3:-1]
     for k in range(pieces):
         total = own_rows[k * size : (k + 1) * size].astype(F32)
-        for d in sorted(range(n_head), key=lambda d: -abs(2 * d - n_head)):
+        for d in order[:-1]:
             total = total + jnp.dot(arrived[k][d], groups[d], preferred_element_type=F32)
-        total = total.astype(BF16)
+        if k == pieces - 1:
+            total = lax.optimization_barrier(total)
+        total = (total + jnp.dot(arrived[k][order[-1]], groups[order[-1]], preferred_element_type=F32)).astype(BF16)
         if result is None:
             result = jnp.pad(total, ((0, share - size), (0, 0)))
         else:

time: 127 us -> 127 us (level)
    dot_general x8 -> x6, matrix products: 5.78 us -> 4.84 us  [on_device(): jnp.dot(arrived[k][d], groups[d], preferred_element_type=F32)]
  transfers between devices with their start and end apart: 17 -> 17, of which waited for: 5 -> 5; matrix products, arithmetic and copies ran while one was open for 5% -> 6% of each run, Pallas kernels for 56% -> 56%
where the time goes in v8:
time: 127 us; the launch traced here: 126 us
  Pallas kernels  70.7 us (56%)
  starting transfers between devices  23.2 us (18%)
  waiting for transfers between devices  19.9 us (16%)
  matrix products  5.74 us (5%)
  other arithmetic  5.05 us (4%)
    pallas_call x5, Pallas kernels, by_destination(): pl.pallas_call(lambda _, *refs: kernel(*refs), grid_spec=pltpu.PrefetchSc...  37.6 us
    pallas_call x1, Pallas kernels, project(): pl.pallas_call(functools.partial(project_kernel, heads, inner), grid=(n,)...  31.9 us
    ppermute x9, waiting for transfers between devices, rotated(): lax.ppermute(block, 'head', [(i, (i + d) % count) for i in range(count)])  19.7 us
    ppermute x9, starting transfers between devices, rotated(): lax.ppermute(block, 'head', [(i, (i + d) % count) for i in range(count)])  12 us
    ppermute x2, starting transfers between devices, shifted(): lax.ppermute(block, axis, [(i - distance, i) for i in devices if i - dist...  5.55 us
    dot_general x6, matrix products, on_device(): jnp.dot(arrived[k][d], groups[d], preferred_element_type=F32)  4.84 us
    ppermute x3, starting transfers between devices, incoming(): lax.ppermute(block, axis, [(i, i ^ d * distance) for i in range(count)])  3.55 us
  transfers between devices with their start and end apart: 17, of which 5 were waited for; matrix products, arithmetic and copies ran while one was open for 6% of the time, Pallas kernels for 56%

profile of v8, /device:TPU:10, one launch (start us, length us, event | category | flops | bytes accessed | tf_op | source)
XLA Modules:
  0.0 125.9 jit_solution(17296491918545362447)
XLA Ops:
  0.9 1.9 %collective-permute-start = (bf16[16,1024]{1,0:T(8,128)(2,1)S(1)}, bf16[16,1024]{1,0:T(8,128)(2,1)S(1)}, u32[]{:S(2)}, u32[]{:S(2)}) collective-permute-start(bf16[16,1024]{1,0:T(8,128)(2,1)S(1)} %get-tuple-element.124), channel_id=1, source_target_pairs={{0,4},{4,8},{8,12},{12,16},{16,20},{20,24},{24,28},{1,5},{5,9},{9,... | collective-permute-start | bytes 98312 | tf_op jit(solution)/shard_map/ppermute | solution.py:516
  2.8 3.6 %collective-permute-start.1 = (bf16[16,1024]{1,0:T(8,128)(2,1)S(1)}, bf16[16,1024]{1,0:T(8,128)(2,1)S(1)}, u32[]{:S(2)}, u32[]{:S(2)}) collective-permute-start(bf16[16,1024]{1,0:T(8,128)(2,1)S(1)} %get-tuple-element.123), channel_id=1, source_target_pairs={{4,0},{8,4},{12,8},{16,12},{20,16},{24,20},{28,24},{5,1},{9,5},{13... | collective-permute-start | bytes 98312 | tf_op jit(solution)/shard_map/ppermute | solution.py:516
  6.5 1.3 %select_maximum_fusion.refs_10_.refs_6_ = f32[3,128]{1,0:T(4,128)} fusion(f32[1,8]{1,0:T(1,128)} %bitcast.18, f32[1,8]{1,0:T(1,128)} %bitcast.19, f32[1,8]{1,0:T(1,128)} %bitcast.20), kind=kLoop, calls=%fused_computation.26 | loop fusion | flops 2304 | bytes 1632 | tf_op jit(solution)/shard_map/stack | solution.py:544
  8.0 1.6 %collective-permute-start.2 = (bf16[256,1024]{1,0:T(8,128)(2,1)S(1)}, bf16[256,1024]{1,0:T(8,128)(2,1)S(1)}, u32[]{:S(2)}, u32[]{:S(2)}) collective-permute-start(bf16[256,1024]{1,0:T(8,128)(2,1)S(1)} %constant_dynamic-slice_fusion.2), channel_id=1, source_target_pairs={{0,1},{1,2},{2,3},{3,0},{4,5},{5,6},{6,7},{7,4},{8,9},{9,10},{10,1... | collective-permute-start | bytes 1572872 | tf_op jit(solution)/shard_map/ppermute | solution.py:520
  10.0 31.9 %project.1 = (bf16[2048,768]{1,0:T(8,128)(2,1)}, f32[2048,128]{1,0:T(8,128)}, f32[8,2048]{1,0:T(8,128)}, bf16[16,128,512]{2,1,0:T(8,128)(2,1)}, f32[16,8,512]{2,...) custom-call(bf16[2048,1024]{1,0:T(8,128)(2,1)} %refs_0_.5, ...), custom_call_target="tpu_custom_call" | custom-call | flops 22000001024 | bytes 40000000 | tf_op jit(solution)/shard_map/project/pallas_call | solution.py:223
  42.0 2.0 %collective-permute-start.4 = (bf16[288,512]{1,0:T(8,128)(2,1)}, bf16[288,512]{1,0:T(8,128)(2,1)S(1)}, u32[]{:S(2)}, u32[]{:S(2)}) collective-permute-start(bf16[288,512]{1,0:T(8,128)(2,1)} %get-tuple-element.78.refs_1_), channel_id=1, source_target_pairs={{0,4},{4,0},{8,12},{12,8},{16,20},{20,16},{24,28},{28,24},{1,5},{5... | collective-permute-start | bytes 884744 | tf_op jit(solution)/shard_map/ppermute | solution.py:489
  44.0 5.8 %gates.2 = (bf16[1024,512]{1,0:T(8,128)(2,1)}, bf16[1024,512]{1,0:T(8,128)(2,1)}) custom-call(s32[1]{0:T(128)} %bitcast._, bf16[2048,1024]{1,0:T(8,128)(2,1)} %refs_0_.5, bf16[1024,512]{1,0:T(8,128)(2,1)} %get-tuple-element.100.refs_1_, bf16[1024,512]{1,0:T(8,128)(2,1)} %get-tuple-element.101.refs_2_), custom_call_target="tpu_custom_call" | custom-call | flops 5000000000 | bytes 1000000 | tf_op jit(solution)/shard_map/gates/pallas_call | solution.py:264
  51.1 1.6 %collective-permute-start.9 = (bf16[256,1024]{1,0:T(8,128)(2,1)S(1)}, bf16[256,1024]{1,0:T(8,128)(2,1)S(1)}, u32[]{:S(2)}, u32[]{:S(2)}) collective-permute-start(bf16[256,1024]{1,0:T(8,128)(2,1)S(1)} %collective-permute-done.2), channel_id=1, source_target_pairs={{0,1},{1,2},{2,3},{3,0},{4,5},{5,6},{6,7},{7,4},{8,9},{9,10},{10,1... | collective-permute-start | bytes 1572872 | tf_op jit(solution)/shard_map/ppermute | solution.py:520
  53.9 2.4 %collective-permute-start.5 = (bf16[144,512]{1,0:T(8,128)(2,1)S(1)}, bf16[144,512]{1,0:T(8,128)(2,1)S(1)}, u32[]{:S(2)}, u32[]{:S(2)}) collective-permute-start(bf16[144,512]{1,0:T(8,128)(2,1)S(1)} %get-tuple-element.134), channel_id=1, source_target_pairs={{0,8},{4,12},{8,0},{12,4},{16,24},{20,28},{24,16},{28,20},{1,9},{5... | collective-permute-start | bytes 442376 | tf_op jit(solution)/shard_map/ppermute | solution.py:508
  56.3 7.2 %inside.1 = (bf16[1024,512]{1,0:T(8,128)(2,1)}, bf16[1024,512]{1,0:T(8,128)(2,1)}) custom-call(s32[1]{0:T(128)} %bitcast._, bf16[2048,768]{1,0:T(8,128)(2,1)} %get-tuple-element.66.refs_0_, f32[2048,128]{1,0:T(8,128)} %get-tuple-element.67.refs_1_.refs_3_, f32[8,2048]{1,0:T(8,128)} %get-tuple-element.68.refs_2_, ...), custom_call_target="tpu_custom_call" | custom-call | flops 8000000000 | bytes 1000000 | tf_op jit(solution)/shard_map/inside/pallas_call | solution.py:264
  64.4 7.5 %finish.1 = (bf16[256,512]{1,0:T(8,128)(2,1)}, bf16[256,512]{1,0:T(8,128)(2,1)}, bf16[256,512]{1,0:T(8,128)(2,1)}, bf16[256,512]{1,0:T(8,128)(2,1)}) custom-call(s32[1]{0:T(128)} %bitcast._, bf16[2048,768]{1,0:T(8,128)(2,1)} %get-tuple-element.66.refs_0_, bf16[16,128,512]{2,1,0:T(8,128)(2,1)} %get-tuple-element.72.refs_1_.refs_6_, ...), custom_call_target="tpu_custom_call" | custom-call | flops 100000000 | bytes 1000000 | tf_op jit(solution)/shard_map/finish/pallas_call | solution.py:264
  72.0 1.6 %collective-permute-start.10 = (bf16[256,512]{1,0:T(8,128)(2,1)}, bf16[256,512]{1,0:T(8,128)(2,1)S(1)}, u32[]{:S(2)}, u32[]{:S(2)}) collective-permute-start(bf16[256,512]{1,0:T(8,128)(2,1)} %get-tuple-element.109), channel_id=1, source_target_pairs={{0,1},{1,2},{2,3},{3,0},{4,5},{5,6},{6,7},{7,4},{8,9},{9,10},{10,1... | collective-permute-start | bytes 786440 | tf_op jit(solution)/shard_map/ppermute | solution.py:520
  73.7 1.6 %collective-permute-start.11 = (bf16[256,512]{1,0:T(8,128)(2,1)}, bf16[256,512]{1,0:T(8,128)(2,1)S(1)}, u32[]{:S(2)}, u32[]{:S(2)}) collective-permute-start(bf16[256,512]{1,0:T(8,128)(2,1)} %get-tuple-element.110), channel_id=1, source_target_pairs={{0,2},{1,3},{2,0},{3,1},{4,6},{5,7},{6,4},{7,5},{8,10},{9,11},{10,... | collective-permute-start | bytes 786440 | tf_op jit(solution)/shard_map/ppermute | solution.py:520
  75.3 1.9 %collective-permute-start.12 = (bf16[256,512]{1,0:T(8,128)(2,1)}, bf16[256,512]{1,0:T(8,128)(2,1)S(1)}, u32[]{:S(2)}, u32[]{:S(2)}) collective-permute-start(bf16[256,512]{1,0:T(8,128)(2,1)} %get-tuple-element.111), channel_id=1, source_target_pairs={{0,3},{1,0},{2,1},{3,2},{4,7},{5,4},{6,5},{7,6},{8,11},{9,8},{10,9... | collective-permute-start | bytes 786440 | tf_op jit(solution)/shard_map/ppermute | solution.py:520
  77.2 5.8 %gates.3 = (bf16[1024,512]{1,0:T(8,128)(2,1)}, bf16[1024,512]{1,0:T(8,128)(2,1)}) custom-call(s32[1]{0:T(128)} %bitcast._, bf16[2048,1024]{1,0:T(8,128)(2,1)} %refs_0_.5, bf16[1024,512]{1,0:T(8,128)(2,1)} %get-tuple-element.100.refs_1_, bf16[1024,512]{1,0:T(8,128)(2,1)} %get-tuple-element.101.refs_2_), custom_call_target="tpu_custom_call" | custom-call | flops 100000000 | bytes 1000000 | tf_op jit(solution)/shard_map/gates/pallas_call | solution.py:264
  83.0 11.4 %settle.1 = (bf16[256,512]{1,0:T(8,128)(2,1)}, bf16[256,512]{1,0:T(8,128)(2,1)}, bf16[256,512]{1,0:T(8,128)(2,1)}, bf16[256,512]{1,0:T(8,128)(2,1)}) custom-call(s32[1]{0:T(128)} %bitcast._, bf16[2048,768]{1,0:T(8,128)(2,1)} %get-tuple-element.66.refs_0_, f32[2048,128]{1,0:T(8,128)} %get-tuple-element.67.refs_1_.refs_3_, ...), custom_call_target="tpu_custom_call" | custom-call | flops 100000000 | bytes 1000000 | tf_op jit(solution)/shard_map/settle/pallas_call | solution.py:264
  94.4 1.4 %broadcast_select_fusion.1 = (bf16[256,1024]{1,0:T(8,128)(2,1)S(1)}, bf16[256,1024]{1,0:T(8,128)(2,1)S(1)}, bf16[256,1024]{1,0:T(8,128)(2,1)S(1)}, bf16[256,1024]{1,0:T(8,128)(2,1)S(1)}) fusion(bf16[256,1024]{1,0:T(8,128)(2,1)S(1)} %collective-permute-done.2, pred[]{:T(512)S(6)} %eq.14, bf16[512,1024]{1,0:T(8,128)(2,1)} %collective-permute-done.8, ...), kind=kLoop, calls=%fused_computation.21 | loop fusion | flops 1048576 | bytes 4194305 | tf_op jit(solution)/shard_map/jit(_where)/select_n | solution.py:578
  95.8 1.2 collective-permute-done.11
  97.0 2.2 %collective-permute-done.12 = bf16[256,512]{1,0:T(8,128)(2,1)S(1)} collective-permute-done((bf16[256,512]{1,0:T(8,128)(2,1)}, bf16[256,512]{1,0:T(8,128)(2,1)S(1)}, u32[]{:S(2)}, u32[]{:S(2)}) %collective-permute-start.12) | collective-permute-done | bytes 262176 | tf_op jit(solution)/shard_map/ppermute | solution.py:520
  100.5 2.0 %collective-permute-start.16 = (bf16[256,512]{1,0:T(8,128)(2,1)S(1)}, bf16[256,512]{1,0:T(8,128)(2,1)S(1)}, u32[]{:S(2)}, u32[]{:S(2)}) collective-permute-start(bf16[256,512]{1,0:T(8,128)(2,1)S(1)} %copy-done.4), channel_id=1, source_target_pairs={{0,1},{1,2},{2,3},{3,0},{4,5},{5,6},{6,7},{7,4},{8,9},{9,10},{10,1... | collective-permute-start | bytes 786440 | tf_op jit(solution)/shard_map/ppermute | solution.py:520
  104.0 1.6 %fusion.5 = bf16[256,1024]{1,0:T(8,128)(2,1)S(1)} fusion(f32[256,1024]{1,0:T(8,128)S(1)} %fusion.7, f32[256,1024]{1,0:T(8,128)S(1)} %fusion.9, f32[256,1024]{1,0:T(8,128)S(1)} %fusion.11, bf16[256,512]{1,0:T(8,128)(2,1)S(1)} %copy-done.2, bf16[512,1024]{1,0:T(8,128)(2,1)S(1)} %copy-done, bf16[2048,1024]{1,0:T(8,128)(2,1)} %refs_0_.5, s32[]{:T(128)S(6)} %select_n.70), kind=kOutput, calls=%fused_computation.7 | convolution fusion | flops 270008320 | bytes 5505028 | tf_op jit(solution)/shard_map/dot_general | solution.py:585
  105.5 11.4 %collective-permute-done.15 = bf16[256,512]{1,0:T(8,128)(2,1)S(1)} collective-permute-done((bf16[256,512]{1,0:T(8,128)(2,1)S(1)}, bf16[256,512]{1,0:T(8,128)(2,1)S(1)}, u32[]{:S(2)}, u32[]{:S(2)}) %collective-permute-start.15) | collective-permute-done | bytes 262176 | tf_op jit(solution)/shard_map/ppermute | solution.py:520
  117.4 4.9 %collective-permute-done.14 = bf16[256,512]{1,0:T(8,128)(2,1)S(1)} collective-permute-done((bf16[256,512]{1,0:T(8,128)(2,1)S(1)}, bf16[256,512]{1,0:T(8,128)(2,1)S(1)}, u32[]{:S(2)}, u32[]{:S(2)}) %collective-permute-start.14) | collective-permute-done | bytes 262176 | tf_op jit(solution)/shard_map/ppermute | solution.py:520
  122.7 1.5 %fusion.1 = f32[256,1024]{1,0:T(8,128)S(1)} fusion(f32[256,1024]{1,0:T(8,128)S(1)} %fusion.8, f32[256,1024]{1,0:T(8,128)S(1)} %fusion.10, bf16[256,512]{1,0:T(8,128)(2,1)S(1)} %copy-done.3, bf16[512,1024]{1,0:T(8,128)(2,1)S(1)} %copy-done, bf16[2048,1024]{1,0:T(8,128)(2,1)} %refs_0_.5, s32[]{:T(128)S(6)} %add.70), kind=kOutput, calls=%fused_computation.2 | convolution fusion | flops 269484032 | bytes 4980740 | tf_op jit(solution)/shard_map/dot_general | solution.py:585
  (53 shorter events, 10.4 us)
Async XLA Ops:
  0.0 6.5 %copy-start = (bf16[512,1024]{1,0:T(8,128)(2,1)S(1)}, bf16[512,1024]{1,0:T(8,128)(2,1)}, u32[]{:S(2)}) copy-start(bf16[512,1024]{1,0:T(8,128)(2,1)} %param.23) | copy-start | bytes 3145732
  0.9 6.9 %collective-permute-start = (bf16[16,1024]{1,0:T(8,128)(2,1)S(1)}, bf16[16,1024]{1,0:T(8,128)(2,1)S(1)}, u32[]{:S(2)}, u32[]{:S(2)}) collective-permute-start(bf16[16,1024]{1,0:T(8,128)(2,1)S(1)} %get-tuple-element.124), channel_id=1, source_target_pairs={{0,4},{4,8},{8,12},{12,16},{16,20},{20,24},{24,28},{1,5},{5,9},{9,... | collective-permute-start | bytes 98312 | tf_op jit(solution)/shard_map/ppermute | solution.py:516
  2.8 5.2 %collective-permute-start.1 = (bf16[16,1024]{1,0:T(8,128)(2,1)S(1)}, bf16[16,1024]{1,0:T(8,128)(2,1)S(1)}, u32[]{:S(2)}, u32[]{:S(2)}) collective-permute-start(bf16[16,1024]{1,0:T(8,128)(2,1)S(1)} %get-tuple-element.123), channel_id=1, source_target_pairs={{4,0},{8,4},{12,8},{16,12},{20,16},{24,20},{28,24},{5,1},{9,5},{13... | collective-permute-start | bytes 98312 | tf_op jit(solution)/shard_map/ppermute | solution.py:516
  7.8 2.2 %copy-start.7 = (bf16[16,1024]{1,0:T(8,128)(2,1)}, bf16[16,1024]{1,0:T(8,128)(2,1)S(1)}, u32[]{:S(2)}) copy-start(bf16[16,1024]{1,0:T(8,128)(2,1)S(1)} %collective-permute-done.refs_2_) | copy-start | bytes 98308
  8.0 33.9 %collective-permute-start.2 = (bf16[256,1024]{1,0:T(8,128)(2,1)S(1)}, bf16[256,1024]{1,0:T(8,128)(2,1)S(1)}, u32[]{:S(2)}, u32[]{:S(2)}) collective-permute-start(bf16[256,1024]{1,0:T(8,128)(2,1)S(1)} %constant_dynamic-slice_fusion.2), channel_id=1, source_target_pairs={{0,1},{1,2},{2,3},{3,0},{4,5},{5,6},{6,7},{7,4},{8,9},{9,10},{10,1... | collective-permute-start | bytes 1572872 | tf_op jit(solution)/shard_map/ppermute | solution.py:520
  9.6 32.4 %collective-permute-start.3 = (bf16[256,1024]{1,0:T(8,128)(2,1)S(1)}, bf16[256,1024]{1,0:T(8,128)(2,1)S(1)}, u32[]{:S(2)}, u32[]{:S(2)}) collective-permute-start(bf16[256,1024]{1,0:T(8,128)(2,1)S(1)} %constant_dynamic-slice_fusion.2), channel_id=1, source_target_pairs={{0,3},{1,0},{2,1},{3,2},{4,7},{5,4},{6,5},{7,6},{8,11},{9,8},{10,9... | collective-permute-start | bytes 1572872 | tf_op jit(solution)/shard_map/ppermute | solution.py:520
  42.0 7.8 %collective-permute-start.4 = (bf16[288,512]{1,0:T(8,128)(2,1)}, bf16[288,512]{1,0:T(8,128)(2,1)S(1)}, u32[]{:S(2)}, u32[]{:S(2)}) collective-permute-start(bf16[288,512]{1,0:T(8,128)(2,1)} %get-tuple-element.78.refs_1_), channel_id=1, source_target_pairs={{0,4},{4,0},{8,12},{12,8},{16,20},{20,16},{24,28},{28,24},{1,5},{5... | collective-permute-start | bytes 884744 | tf_op jit(solution)/shard_map/ppermute | solution.py:489
  44.0 5.8 %copy-start.1 = (bf16[288,512]{1,0:T(8,128)(2,1)S(1)}, bf16[288,512]{1,0:T(8,128)(2,1)}, u32[]{:S(2)}) copy-start(bf16[288,512]{1,0:T(8,128)(2,1)} %get-tuple-element.78.refs_1_) | copy-start | bytes 884740
  51.1 13.4 %collective-permute-start.8 = (bf16[512,1024]{1,0:T(8,128)(2,1)}, bf16[512,1024]{1,0:T(8,128)(2,1)}, u32[]{:S(2)}, u32[]{:S(2)}) collective-permute-start(bf16[512,1024]{1,0:T(8,128)(2,1)} %pad_maximum_fusion), channel_id=1, source_target_pairs={{0,4},{4,0},{8,12},{12,8},{16,20},{20,16},{24,28},{28,24},{1,5},{5... | collective-permute-start | bytes 3145736 | tf_op jit(solution)/shard_map/ppermute | solution.py:559
  51.1 20.8 %collective-permute-start.9 = (bf16[256,1024]{1,0:T(8,128)(2,1)S(1)}, bf16[256,1024]{1,0:T(8,128)(2,1)S(1)}, u32[]{:S(2)}, u32[]{:S(2)}) collective-permute-start(bf16[256,1024]{1,0:T(8,128)(2,1)S(1)} %collective-permute-done.2), channel_id=1, source_target_pairs={{0,1},{1,2},{2,3},{3,0},{4,5},{5,6},{6,7},{7,4},{8,9},{9,10},{10,1... | collective-permute-start | bytes 1572872 | tf_op jit(solution)/shard_map/ppermute | solution.py:520
  52.7 10.7 %collective-permute-start.6 = (bf16[144,512]{1,0:T(8,128)(2,1)S(1)}, bf16[144,512]{1,0:T(8,128)(2,1)S(1)}, u32[]{:S(2)}, u32[]{:S(2)}) collective-permute-start(bf16[144,512]{1,0:T(8,128)(2,1)S(1)} %get-tuple-element.133), channel_id=1, source_target_pairs={{0,16},{4,20},{8,24},{12,28},{16,0},{20,4},{24,8},{28,12},{1,17},{... | collective-permute-start | bytes 442376 | tf_op jit(solution)/shard_map/ppermute | solution.py:508
  52.8 10.6 %collective-permute-start.7 = (bf16[144,512]{1,0:T(8,128)(2,1)S(1)}, bf16[144,512]{1,0:T(8,128)(2,1)S(1)}, u32[]{:S(2)}, u32[]{:S(2)}) collective-permute-start(bf16[144,512]{1,0:T(8,128)(2,1)S(1)} %get-tuple-element.133), channel_id=1, source_target_pairs={{0,24},{4,28},{8,16},{12,20},{16,8},{20,12},{24,0},{28,4},{1,25},{... | collective-permute-start | bytes 442376 | tf_op jit(solution)/shard_map/ppermute | solution.py:508
  53.9 9.5 %collective-permute-start.5 = (bf16[144,512]{1,0:T(8,128)(2,1)S(1)}, bf16[144,512]{1,0:T(8,128)(2,1)S(1)}, u32[]{:S(2)}, u32[]{:S(2)}) collective-permute-start(bf16[144,512]{1,0:T(8,128)(2,1)S(1)} %get-tuple-element.134), channel_id=1, source_target_pairs={{0,8},{4,12},{8,0},{12,4},{16,24},{20,28},{24,16},{28,20},{1,9},{5... | collective-permute-start | bytes 442376 | tf_op jit(solution)/shard_map/ppermute | solution.py:508
  72.0 27.2 %collective-permute-start.13 = (bf16[256,1024]{1,0:T(8,128)(2,1)S(1)}, bf16[256,1024]{1,0:T(8,128)(2,1)S(1)}, u32[]{:S(2)}, u32[]{:S(2)}) collective-permute-start(bf16[256,1024]{1,0:T(8,128)(2,1)S(1)} %collective-permute-done.9), channel_id=1, source_target_pairs={{0,4},{4,0},{8,12},{12,8},{16,20},{20,16},{24,28},{28,24},{1,5},{5... | collective-permute-start | bytes 1572872 | tf_op jit(solution)/shard_map/ppermute | solution.py:564
  72.0 23.7 %collective-permute-start.10 = (bf16[256,512]{1,0:T(8,128)(2,1)}, bf16[256,512]{1,0:T(8,128)(2,1)S(1)}, u32[]{:S(2)}, u32[]{:S(2)}) collective-permute-start(bf16[256,512]{1,0:T(8,128)(2,1)} %get-tuple-element.109), channel_id=1, source_target_pairs={{0,1},{1,2},{2,3},{3,0},{4,5},{5,6},{6,7},{7,4},{8,9},{9,10},{10,1... | collective-permute-start | bytes 786440 | tf_op jit(solution)/shard_map/ppermute | solution.py:520
  73.7 23.3 %collective-permute-start.11 = (bf16[256,512]{1,0:T(8,128)(2,1)}, bf16[256,512]{1,0:T(8,128)(2,1)S(1)}, u32[]{:S(2)}, u32[]{:S(2)}) collective-permute-start(bf16[256,512]{1,0:T(8,128)(2,1)} %get-tuple-element.110), channel_id=1, source_target_pairs={{0,2},{1,3},{2,0},{3,1},{4,6},{5,7},{6,4},{7,5},{8,10},{9,11},{10,... | collective-permute-start | bytes 786440 | tf_op jit(solution)/shard_map/ppermute | solution.py:520
  75.3 23.9 %collective-permute-start.12 = (bf16[256,512]{1,0:T(8,128)(2,1)}, bf16[256,512]{1,0:T(8,128)(2,1)S(1)}, u32[]{:S(2)}, u32[]{:S(2)}) collective-permute-start(bf16[256,512]{1,0:T(8,128)(2,1)} %get-tuple-element.111), channel_id=1, source_target_pairs={{0,3},{1,0},{2,1},{3,2},{4,7},{5,4},{6,5},{7,6},{8,11},{9,8},{10,9... | collective-permute-start | bytes 786440 | tf_op jit(solution)/shard_map/ppermute | solution.py:520
  94.4 4.8 %copy-start.6 = (bf16[256,512]{1,0:T(8,128)(2,1)S(1)}, bf16[256,512]{1,0:T(8,128)(2,1)}, u32[]{:S(2)}) copy-start(bf16[256,512]{1,0:T(8,128)(2,1)} %get-tuple-element.121) | copy-start | bytes 786436
  95.8 4.7 %copy-start.5 = (bf16[256,512]{1,0:T(8,128)(2,1)S(1)}, bf16[256,512]{1,0:T(8,128)(2,1)}, u32[]{:S(2)}) copy-start(bf16[256,512]{1,0:T(8,128)(2,1)} %get-tuple-element.120) | copy-start | bytes 786436
  95.8 4.8 %copy-start.4 = (bf16[256,512]{1,0:T(8,128)(2,1)S(1)}, bf16[256,512]{1,0:T(8,128)(2,1)}, u32[]{:S(2)}) copy-start(bf16[256,512]{1,0:T(8,128)(2,1)} %get-tuple-element.122) | copy-start | bytes 786436
  99.2 17.7 %collective-permute-start.15 = (bf16[256,512]{1,0:T(8,128)(2,1)S(1)}, bf16[256,512]{1,0:T(8,128)(2,1)S(1)}, u32[]{:S(2)}, u32[]{:S(2)}) collective-permute-start(bf16[256,512]{1,0:T(8,128)(2,1)S(1)} %copy-done.6), channel_id=1, source_target_pairs={{0,2},{1,3},{2,0},{3,1},{4,6},{5,7},{6,4},{7,5},{8,10},{9,11},{10,... | collective-permute-start | bytes 786440 | tf_op jit(solution)/shard_map/ppermute | solution.py:520
  100.5 21.8 %collective-permute-start.14 = (bf16[256,512]{1,0:T(8,128)(2,1)S(1)}, bf16[256,512]{1,0:T(8,128)(2,1)S(1)}, u32[]{:S(2)}, u32[]{:S(2)}) collective-permute-start(bf16[256,512]{1,0:T(8,128)(2,1)S(1)} %copy-done.5), channel_id=1, source_target_pairs={{0,3},{1,0},{2,1},{3,2},{4,7},{5,4},{6,5},{7,6},{8,11},{9,8},{10,9... | collective-permute-start | bytes 786440 | tf_op jit(solution)/shard_map/ppermute | solution.py:520
  100.5 23.7 %collective-permute-start.16 = (bf16[256,512]{1,0:T(8,128)(2,1)S(1)}, bf16[256,512]{1,0:T(8,128)(2,1)S(1)}, u32[]{:S(2)}, u32[]{:S(2)}) collective-permute-start(bf16[256,512]{1,0:T(8,128)(2,1)S(1)} %copy-done.4), channel_id=1, source_target_pairs={{0,1},{1,2},{2,3},{3,0},{4,5},{5,6},{6,7},{7,4},{8,9},{9,10},{10,1... | collective-permute-start | bytes 786440 | tf_op jit(solution)/shard_map/ppermute | solution.py:520
  105.5 17.2 %copy-start.3 = (bf16[256,512]{1,0:T(8,128)(2,1)S(1)}, bf16[256,512]{1,0:T(8,128)(2,1)}, u32[]{:S(2)}) copy-start(bf16[256,512]{1,0:T(8,128)(2,1)} %get-tuple-element.119) | copy-start | bytes 786436
  (2 other events, 3.0 us)

commit v9 on v8

--- a/solution.py
+++ b/solution.py
@@ -11,6 +11,7 @@
 STATE = 128
 CHUNK = 128
 TILE = 256
+PROJECT_TILE = 512
 EPS = 1e-05
 RIM = 16
 TAIL = 16
@@ -203,14 +204,14 @@
 def project(hidden, rim_f, rim_r, weights, conv_x, conv_bc, lanes, copy, heads, inner):
     rows, depth = hidden.shape
     stream = inner + 2 * STATE
-    n = rows // TILE
-    per = TILE // CHUNK
+    n = rows // PROJECT_TILE
+    per = PROJECT_TILE // CHUNK
     up, down = (lambda i: i), (lambda i: n - 1 - i)
-    by_rows = lambda width, at: pl.BlockSpec((TILE, width), lambda i: (at(i), 0))
+    by_rows = lambda width, at: pl.BlockSpec((PROJECT_TILE, width), lambda i: (at(i), 0))
     out_specs, out_shape = [], []
     for at in (up, down):
         out_specs += [by_rows(stream, at), by_rows(128, at),
-                      pl.BlockSpec((heads, TILE), lambda i, at=at: (0, at(i))),
+                      pl.BlockSpec((heads, PROJECT_TILE), lambda i, at=at: (0, at(i))),
                       pl.BlockSpec((per, STATE, inner), lambda i, at=at: (at(i), 0, 0)),
                       pl.BlockSpec((per, 8, inner), lambda i, at=at: (at(i), 0, 0))]
         out_shape += [jax.ShapeDtypeStruct((rows, stream), BF16),
@@ -218,7 +219,7 @@
                       jax.ShapeDtypeStruct((n * per, STATE, inner), BF16),
                       jax.ShapeDtypeStruct((n * per, 8, inner), F32)]
     message = (2 * (STATE + TAIL), inner)
-    buf = pltpu.VMEM((stream // 128, TILE + 8, 128), F32)
+    buf = pltpu.VMEM((stream // 128, PROJECT_TILE + 8, 128), F32)
     state, total = pltpu.VMEM((STATE, inner), F32), pltpu.VMEM((8, 128), F32)
     return pl.pallas_call(
         functools.partial(project_kernel, heads, inner),
@@ -567,7 +568,9 @@
     for k in range(1, pieces):
         gated = gates(place(k), hidden, g_f, g_r, 1e8)
         parts = settle(place(k), strands, ends, gated, lanes, copy_first, entering, copy_second, heads, inner)
-        parts, arrived[k - 1], across_other = lax.optimization_barrier((parts, arrived[k - 1], across_other))
+        keys = [*middle_first, 0]
+        parts, blocks, across_other = lax.optimization_barrier((parts, [arrived[k - 1][d] for d in keys], across_other))
+        arrived[k - 1] = dict(zip(keys, blocks))
         arrived.append({0: parts[0], **{d: rotated(parts[d], d, n_head) for d in middle_first}})
     own_rows = lax.dynamic_slice_in_dim(hidden, head * share, share, 0)
     pairs = {d: (one, other[i * half : (i + 1) * half]) for i, (d, one) in enumerate(zip(early, same))}

time: 127 us -> 127 us (level)
  transfers between devices with their start and end apart: 17 -> 17, of which waited for: 5 -> 5; matrix products, arithmetic and copies ran while one was open for 6% -> 6% of each run, Pallas kernels for 56% -> 55%
where the time goes in v9:
time: 127 us; the launch traced here: 126 us
  Pallas kernels  69.7 us (55%)
  starting transfers between devices  23.8 us (19%)
  waiting for transfers between devices  20.9 us (16%)
  matrix products  5.74 us (5%)
  other arithmetic  5.05 us (4%)
    pallas_call x5, Pallas kernels, by_destination(): pl.pallas_call(lambda _, *refs: kernel(*refs), grid_spec=pltpu.PrefetchSc...  37.6 us
    pallas_call x1, Pallas kernels, project(): pl.pallas_call(functools.partial(project_kernel, heads, inner), grid=(n,)...  30.9 us
    ppermute x9, waiting for transfers between devices, rotated(): lax.ppermute(block, 'head', [(i, (i + d) % count) for i in range(count)])  20.6 us
    ppermute x9, starting transfers between devices, rotated(): lax.ppermute(block, 'head', [(i, (i + d) % count) for i in range(count)])  12.6 us
    ppermute x2, starting transfers between devices, shifted(): lax.ppermute(block, axis, [(i - distance, i) for i in devices if i - dist...  5.55 us
    dot_general x6, matrix products, on_device(): jnp.dot(arrived[k][d], groups[d], preferred_element_type=F32)  4.84 us
    ppermute x3, starting transfers between devices, incoming(): lax.ppermute(block, axis, [(i, i ^ d * distance) for i in range(count)])  3.55 us
  transfers between devices with their start and end apart: 17, of which 5 were waited for; matrix products, arithmetic and copies ran while one was open for 6% of the time, Pallas kernels for 55%

profile of v9, /device:TPU:10, one launch (start us, length us, event | category | flops | bytes accessed | tf_op | source)
XLA Modules:
  0.0 126.5 jit_solution(10167384651041949838)
XLA Ops:
  0.9 1.9 %collective-permute-start = (bf16[16,1024]{1,0:T(8,128)(2,1)S(1)}, bf16[16,1024]{1,0:T(8,128)(2,1)S(1)}, u32[]{:S(2)}, u32[]{:S(2)}) collective-permute-start(bf16[16,1024]{1,0:T(8,128)(2,1)S(1)} %get-tuple-element.124), channel_id=1, source_target_pairs={{0,4},{4,8},{8,12},{12,16},{16,20},{20,24},{24,28},{1,5},{5,9},{9,... | collective-permute-start | bytes 98312 | tf_op jit(solution)/shard_map/ppermute | solution.py:517
  2.8 3.6 %collective-permute-start.1 = (bf16[16,1024]{1,0:T(8,128)(2,1)S(1)}, bf16[16,1024]{1,0:T(8,128)(2,1)S(1)}, u32[]{:S(2)}, u32[]{:S(2)}) collective-permute-start(bf16[16,1024]{1,0:T(8,128)(2,1)S(1)} %get-tuple-element.123), channel_id=1, source_target_pairs={{4,0},{8,4},{12,8},{16,12},{20,16},{24,20},{28,24},{5,1},{9,5},{13... | collective-permute-start | bytes 98312 | tf_op jit(solution)/shard_map/ppermute | solution.py:517
  6.5 1.3 %select_maximum_fusion.refs_10_.refs_6_ = f32[3,128]{1,0:T(4,128)} fusion(f32[1,8]{1,0:T(1,128)} %bitcast.18, f32[1,8]{1,0:T(1,128)} %bitcast.19, f32[1,8]{1,0:T(1,128)} %bitcast.20), kind=kLoop, calls=%fused_computation.26 | loop fusion | flops 2304 | bytes 1632 | tf_op jit(solution)/shard_map/stack | solution.py:545
  8.0 1.6 %collective-permute-start.2 = (bf16[256,1024]{1,0:T(8,128)(2,1)S(1)}, bf16[256,1024]{1,0:T(8,128)(2,1)S(1)}, u32[]{:S(2)}, u32[]{:S(2)}) collective-permute-start(bf16[256,1024]{1,0:T(8,128)(2,1)S(1)} %constant_dynamic-slice_fusion.2), channel_id=1, source_target_pairs={{0,1},{1,2},{2,3},{3,0},{4,5},{5,6},{6,7},{7,4},{8,9},{9,10},{10,1... | collective-permute-start | bytes 1572872 | tf_op jit(solution)/shard_map/ppermute | solution.py:521
  10.0 30.9 %project.1 = (bf16[2048,768]{1,0:T(8,128)(2,1)}, f32[2048,128]{1,0:T(8,128)}, f32[8,2048]{1,0:T(8,128)}, bf16[16,128,512]{2,1,0:T(8,128)(2,1)}, f32[16,8,512]{2,...) custom-call(bf16[2048,1024]{1,0:T(8,128)(2,1)} %refs_0_.5, ...), custom_call_target="tpu_custom_call" | custom-call | flops 22000001024 | bytes 40000000 | tf_op jit(solution)/shard_map/project/pallas_call | solution.py:224
  40.9 2.0 %collective-permute-start.4 = (bf16[288,512]{1,0:T(8,128)(2,1)}, bf16[288,512]{1,0:T(8,128)(2,1)S(1)}, u32[]{:S(2)}, u32[]{:S(2)}) collective-permute-start(bf16[288,512]{1,0:T(8,128)(2,1)} %get-tuple-element.78.refs_1_), channel_id=1, source_target_pairs={{0,4},{4,0},{8,12},{12,8},{16,20},{20,16},{24,28},{28,24},{1,5},{5... | collective-permute-start | bytes 884744 | tf_op jit(solution)/shard_map/ppermute | solution.py:490
  43.0 5.8 %gates.2 = (bf16[1024,512]{1,0:T(8,128)(2,1)}, bf16[1024,512]{1,0:T(8,128)(2,1)}) custom-call(s32[1]{0:T(128)} %bitcast._, bf16[2048,1024]{1,0:T(8,128)(2,1)} %refs_0_.5, bf16[1024,512]{1,0:T(8,128)(2,1)} %get-tuple-element.100.refs_1_, bf16[1024,512]{1,0:T(8,128)(2,1)} %get-tuple-element.101.refs_2_), custom_call_target="tpu_custom_call" | custom-call | flops 5000000000 | bytes 1000000 | tf_op jit(solution)/shard_map/gates/pallas_call | solution.py:265
  49.0 1.1 pad_maximum_fusion
  50.1 1.6 %collective-permute-start.9 = (bf16[256,1024]{1,0:T(8,128)(2,1)S(1)}, bf16[256,1024]{1,0:T(8,128)(2,1)S(1)}, u32[]{:S(2)}, u32[]{:S(2)}) collective-permute-start(bf16[256,1024]{1,0:T(8,128)(2,1)S(1)} %collective-permute-done.2), channel_id=1, source_target_pairs={{0,1},{1,2},{2,3},{3,0},{4,5},{5,6},{6,7},{7,4},{8,9},{9,10},{10,1... | collective-permute-start | bytes 1572872 | tf_op jit(solution)/shard_map/ppermute | solution.py:521
  51.8 1.0 collective-permute-start.7
  52.8 2.4 %collective-permute-start.5 = (bf16[144,512]{1,0:T(8,128)(2,1)S(1)}, bf16[144,512]{1,0:T(8,128)(2,1)S(1)}, u32[]{:S(2)}, u32[]{:S(2)}) collective-permute-start(bf16[144,512]{1,0:T(8,128)(2,1)S(1)} %get-tuple-element.134), channel_id=1, source_target_pairs={{0,8},{4,12},{8,0},{12,4},{16,24},{20,28},{24,16},{28,20},{1,9},{5... | collective-permute-start | bytes 442376 | tf_op jit(solution)/shard_map/ppermute | solution.py:509
  55.2 7.2 %inside.1 = (bf16[1024,512]{1,0:T(8,128)(2,1)}, bf16[1024,512]{1,0:T(8,128)(2,1)}) custom-call(s32[1]{0:T(128)} %bitcast._, bf16[2048,768]{1,0:T(8,128)(2,1)} %get-tuple-element.66.refs_0_, f32[2048,128]{1,0:T(8,128)} %get-tuple-element.67.refs_1_.refs_3_, f32[8,2048]{1,0:T(8,128)} %get-tuple-element.68.refs_2_, ...), custom_call_target="tpu_custom_call" | custom-call | flops 8000000000 | bytes 1000000 | tf_op jit(solution)/shard_map/inside/pallas_call | solution.py:265
  63.4 7.5 %finish.1 = (bf16[256,512]{1,0:T(8,128)(2,1)}, bf16[256,512]{1,0:T(8,128)(2,1)}, bf16[256,512]{1,0:T(8,128)(2,1)}, bf16[256,512]{1,0:T(8,128)(2,1)}) custom-call(s32[1]{0:T(128)} %bitcast._, bf16[2048,768]{1,0:T(8,128)(2,1)} %get-tuple-element.66.refs_0_, bf16[16,128,512]{2,1,0:T(8,128)(2,1)} %get-tuple-element.72.refs_1_.refs_6_, ...), custom_call_target="tpu_custom_call" | custom-call | flops 100000000 | bytes 1000000 | tf_op jit(solution)/shard_map/finish/pallas_call | solution.py:265
  71.0 3.2 %collective-permute-start.10 = (bf16[256,512]{1,0:T(8,128)(2,1)}, bf16[256,512]{1,0:T(8,128)(2,1)S(1)}, u32[]{:S(2)}, u32[]{:S(2)}) collective-permute-start(bf16[256,512]{1,0:T(8,128)(2,1)} %get-tuple-element.108), channel_id=1, source_target_pairs={{0,2},{1,3},{2,0},{3,1},{4,6},{5,7},{6,4},{7,5},{8,10},{9,11},{10,... | collective-permute-start | bytes 786440 | tf_op jit(solution)/shard_map/ppermute | solution.py:521
  74.2 2.0 %collective-permute-start.12 = (bf16[256,512]{1,0:T(8,128)(2,1)}, bf16[256,512]{1,0:T(8,128)(2,1)S(1)}, u32[]{:S(2)}, u32[]{:S(2)}) collective-permute-start(bf16[256,512]{1,0:T(8,128)(2,1)} %get-tuple-element.110), channel_id=1, source_target_pairs={{0,3},{1,0},{2,1},{3,2},{4,7},{5,4},{6,5},{7,6},{8,11},{9,8},{10,9... | collective-permute-start | bytes 786440 | tf_op jit(solution)/shard_map/ppermute | solution.py:521
  76.2 5.8 %gates.3 = (bf16[1024,512]{1,0:T(8,128)(2,1)}, bf16[1024,512]{1,0:T(8,128)(2,1)}) custom-call(s32[1]{0:T(128)} %bitcast._, bf16[2048,1024]{1,0:T(8,128)(2,1)} %refs_0_.5, bf16[1024,512]{1,0:T(8,128)(2,1)} %get-tuple-element.100.refs_1_, bf16[1024,512]{1,0:T(8,128)(2,1)} %get-tuple-element.101.refs_2_), custom_call_target="tpu_custom_call" | custom-call | flops 100000000 | bytes 1000000 | tf_op jit(solution)/shard_map/gates/pallas_call | solution.py:265
  82.0 11.4 %settle.1 = (bf16[256,512]{1,0:T(8,128)(2,1)}, bf16[256,512]{1,0:T(8,128)(2,1)}, bf16[256,512]{1,0:T(8,128)(2,1)}, bf16[256,512]{1,0:T(8,128)(2,1)}) custom-call(s32[1]{0:T(128)} %bitcast._, bf16[2048,768]{1,0:T(8,128)(2,1)} %get-tuple-element.66.refs_0_, f32[2048,128]{1,0:T(8,128)} %get-tuple-element.67.refs_1_.refs_3_, ...), custom_call_target="tpu_custom_call" | custom-call | flops 100000000 | bytes 1000000 | tf_op jit(solution)/shard_map/settle/pallas_call | solution.py:265
  93.4 1.4 %broadcast_select_fusion.1 = (bf16[256,1024]{1,0:T(8,128)(2,1)S(1)}, bf16[256,1024]{1,0:T(8,128)(2,1)S(1)}, bf16[256,1024]{1,0:T(8,128)(2,1)S(1)}, bf16[256,1024]{1,0:T(8,128)(2,1)S(1)}) fusion(bf16[256,1024]{1,0:T(8,128)(2,1)S(1)} %collective-permute-done.2, pred[]{:T(512)S(6)} %eq.14, bf16[512,1024]{1,0:T(8,128)(2,1)} %collective-permute-done.8, ...), kind=kLoop, calls=%fused_computation.21 | loop fusion | flops 1048576 | bytes 4194305 | tf_op jit(solution)/shard_map/jit(_where)/select_n | solution.py:581
  94.8 2.1 %collective-permute-done.11 = bf16[256,512]{1,0:T(8,128)(2,1)S(1)} collective-permute-done((bf16[256,512]{1,0:T(8,128)(2,1)}, bf16[256,512]{1,0:T(8,128)(2,1)S(1)}, u32[]{:S(2)}, u32[]{:S(2)}) %collective-permute-start.11) | collective-permute-done | bytes 262176 | tf_op jit(solution)/shard_map/ppermute | solution.py:521
  97.1 3.8 %collective-permute-start.14 = (bf16[256,512]{1,0:T(8,128)(2,1)S(1)}, bf16[256,512]{1,0:T(8,128)(2,1)S(1)}, u32[]{:S(2)}, u32[]{:S(2)}) collective-permute-start(bf16[256,512]{1,0:T(8,128)(2,1)S(1)} %copy-done.5), channel_id=1, source_target_pairs={{0,3},{1,0},{2,1},{3,2},{4,7},{5,4},{6,5},{7,6},{8,11},{9,8},{10,9... | collective-permute-start | bytes 786440 | tf_op jit(solution)/shard_map/ppermute | solution.py:521
  102.4 1.6 %fusion.5 = bf16[256,1024]{1,0:T(8,128)(2,1)S(1)} fusion(f32[256,1024]{1,0:T(8,128)S(1)} %fusion.7, f32[256,1024]{1,0:T(8,128)S(1)} %fusion.9, f32[256,1024]{1,0:T(8,128)S(1)} %fusion.11, bf16[256,512]{1,0:T(8,128)(2,1)S(1)} %copy-done.2, bf16[512,1024]{1,0:T(8,128)(2,1)S(1)} %copy-done, bf16[2048,1024]{1,0:T(8,128)(2,1)} %refs_0_.5, s32[]{:T(128)S(6)} %select_n.70), kind=kOutput, calls=%fused_computation.7 | convolution fusion | flops 270008320 | bytes 5505028 | tf_op jit(solution)/shard_map/dot_general | solution.py:588
  103.9 11.0 %collective-permute-done.15 = bf16[256,512]{1,0:T(8,128)(2,1)S(1)} collective-permute-done((bf16[256,512]{1,0:T(8,128)(2,1)S(1)}, bf16[256,512]{1,0:T(8,128)(2,1)S(1)}, u32[]{:S(2)}, u32[]{:S(2)}) %collective-permute-start.15) | collective-permute-done | bytes 262176 | tf_op jit(solution)/shard_map/ppermute | solution.py:521
  115.3 7.4 %collective-permute-done.14 = bf16[256,512]{1,0:T(8,128)(2,1)S(1)} collective-permute-done((bf16[256,512]{1,0:T(8,128)(2,1)S(1)}, bf16[256,512]{1,0:T(8,128)(2,1)S(1)}, u32[]{:S(2)}, u32[]{:S(2)}) %collective-permute-start.14) | collective-permute-done | bytes 262176 | tf_op jit(solution)/shard_map/ppermute | solution.py:521
  123.3 1.5 %fusion.1 = f32[256,1024]{1,0:T(8,128)S(1)} fusion(f32[256,1024]{1,0:T(8,128)S(1)} %fusion.8, f32[256,1024]{1,0:T(8,128)S(1)} %fusion.10, bf16[256,512]{1,0:T(8,128)(2,1)S(1)} %copy-done.3, bf16[512,1024]{1,0:T(8,128)(2,1)S(1)} %copy-done, bf16[2048,1024]{1,0:T(8,128)(2,1)} %refs_0_.5, s32[]{:T(128)S(6)} %add.70), kind=kOutput, calls=%fused_computation.2 | convolution fusion | flops 269484032 | bytes 4980740 | tf_op jit(solution)/shard_map/dot_general | solution.py:588
  (53 shorter events, 7.2 us)
Async XLA Ops:
  0.0 6.5 %copy-start = (bf16[512,1024]{1,0:T(8,128)(2,1)S(1)}, bf16[512,1024]{1,0:T(8,128)(2,1)}, u32[]{:S(2)}) copy-start(bf16[512,1024]{1,0:T(8,128)(2,1)} %param.23) | copy-start | bytes 3145732
  0.9 6.9 %collective-permute-start = (bf16[16,1024]{1,0:T(8,128)(2,1)S(1)}, bf16[16,1024]{1,0:T(8,128)(2,1)S(1)}, u32[]{:S(2)}, u32[]{:S(2)}) collective-permute-start(bf16[16,1024]{1,0:T(8,128)(2,1)S(1)} %get-tuple-element.124), channel_id=1, source_target_pairs={{0,4},{4,8},{8,12},{12,16},{16,20},{20,24},{24,28},{1,5},{5,9},{9,... | collective-permute-start | bytes 98312 | tf_op jit(solution)/shard_map/ppermute | solution.py:517
  2.8 5.2 %collective-permute-start.1 = (bf16[16,1024]{1,0:T(8,128)(2,1)S(1)}, bf16[16,1024]{1,0:T(8,128)(2,1)S(1)}, u32[]{:S(2)}, u32[]{:S(2)}) collective-permute-start(bf16[16,1024]{1,0:T(8,128)(2,1)S(1)} %get-tuple-element.123), channel_id=1, source_target_pairs={{4,0},{8,4},{12,8},{16,12},{20,16},{24,20},{28,24},{5,1},{9,5},{13... | collective-permute-start | bytes 98312 | tf_op jit(solution)/shard_map/ppermute | solution.py:517
  7.8 2.2 %copy-start.7 = (bf16[16,1024]{1,0:T(8,128)(2,1)}, bf16[16,1024]{1,0:T(8,128)(2,1)S(1)}, u32[]{:S(2)}) copy-start(bf16[16,1024]{1,0:T(8,128)(2,1)S(1)} %collective-permute-done.refs_2_) | copy-start | bytes 98308
  8.0 32.9 %collective-permute-start.2 = (bf16[256,1024]{1,0:T(8,128)(2,1)S(1)}, bf16[256,1024]{1,0:T(8,128)(2,1)S(1)}, u32[]{:S(2)}, u32[]{:S(2)}) collective-permute-start(bf16[256,1024]{1,0:T(8,128)(2,1)S(1)} %constant_dynamic-slice_fusion.2), channel_id=1, source_target_pairs={{0,1},{1,2},{2,3},{3,0},{4,5},{5,6},{6,7},{7,4},{8,9},{9,10},{10,1... | collective-permute-start | bytes 1572872 | tf_op jit(solution)/shard_map/ppermute | solution.py:521
  9.6 31.3 %collective-permute-start.3 = (bf16[256,1024]{1,0:T(8,128)(2,1)S(1)}, bf16[256,1024]{1,0:T(8,128)(2,1)S(1)}, u32[]{:S(2)}, u32[]{:S(2)}) collective-permute-start(bf16[256,1024]{1,0:T(8,128)(2,1)S(1)} %constant_dynamic-slice_fusion.2), channel_id=1, source_target_pairs={{0,3},{1,0},{2,1},{3,2},{4,7},{5,4},{6,5},{7,6},{8,11},{9,8},{10,9... | collective-permute-start | bytes 1572872 | tf_op jit(solution)/shard_map/ppermute | solution.py:521
  40.9 7.8 %collective-permute-start.4 = (bf16[288,512]{1,0:T(8,128)(2,1)}, bf16[288,512]{1,0:T(8,128)(2,1)S(1)}, u32[]{:S(2)}, u32[]{:S(2)}) collective-permute-start(bf16[288,512]{1,0:T(8,128)(2,1)} %get-tuple-element.78.refs_1_), channel_id=1, source_target_pairs={{0,4},{4,0},{8,12},{12,8},{16,20},{20,16},{24,28},{28,24},{1,5},{5... | collective-permute-start | bytes 884744 | tf_op jit(solution)/shard_map/ppermute | solution.py:490
  43.0 5.8 %copy-start.1 = (bf16[288,512]{1,0:T(8,128)(2,1)S(1)}, bf16[288,512]{1,0:T(8,128)(2,1)}, u32[]{:S(2)}) copy-start(bf16[288,512]{1,0:T(8,128)(2,1)} %get-tuple-element.78.refs_1_) | copy-start | bytes 884740
  50.1 13.4 %collective-permute-start.8 = (bf16[512,1024]{1,0:T(8,128)(2,1)}, bf16[512,1024]{1,0:T(8,128)(2,1)}, u32[]{:S(2)}, u32[]{:S(2)}) collective-permute-start(bf16[512,1024]{1,0:T(8,128)(2,1)} %pad_maximum_fusion), channel_id=1, source_target_pairs={{0,4},{4,0},{8,12},{12,8},{16,20},{20,16},{24,28},{28,24},{1,5},{5... | collective-permute-start | bytes 3145736 | tf_op jit(solution)/shard_map/ppermute | solution.py:560
  50.1 20.8 %collective-permute-start.9 = (bf16[256,1024]{1,0:T(8,128)(2,1)S(1)}, bf16[256,1024]{1,0:T(8,128)(2,1)S(1)}, u32[]{:S(2)}, u32[]{:S(2)}) collective-permute-start(bf16[256,1024]{1,0:T(8,128)(2,1)S(1)} %collective-permute-done.2), channel_id=1, source_target_pairs={{0,1},{1,2},{2,3},{3,0},{4,5},{5,6},{6,7},{7,4},{8,9},{9,10},{10,1... | collective-permute-start | bytes 1572872 | tf_op jit(solution)/shard_map/ppermute | solution.py:521
  51.7 10.7 %collective-permute-start.6 = (bf16[144,512]{1,0:T(8,128)(2,1)S(1)}, bf16[144,512]{1,0:T(8,128)(2,1)S(1)}, u32[]{:S(2)}, u32[]{:S(2)}) collective-permute-start(bf16[144,512]{1,0:T(8,128)(2,1)S(1)} %get-tuple-element.133), channel_id=1, source_target_pairs={{0,16},{4,20},{8,24},{12,28},{16,0},{20,4},{24,8},{28,12},{1,17},{... | collective-permute-start | bytes 442376 | tf_op jit(solution)/shard_map/ppermute | solution.py:509
  51.8 10.6 %collective-permute-start.7 = (bf16[144,512]{1,0:T(8,128)(2,1)S(1)}, bf16[144,512]{1,0:T(8,128)(2,1)S(1)}, u32[]{:S(2)}, u32[]{:S(2)}) collective-permute-start(bf16[144,512]{1,0:T(8,128)(2,1)S(1)} %get-tuple-element.133), channel_id=1, source_target_pairs={{0,24},{4,28},{8,16},{12,20},{16,8},{20,12},{24,0},{28,4},{1,25},{... | collective-permute-start | bytes 442376 | tf_op jit(solution)/shard_map/ppermute | solution.py:509
  52.8 9.5 %collective-permute-start.5 = (bf16[144,512]{1,0:T(8,128)(2,1)S(1)}, bf16[144,512]{1,0:T(8,128)(2,1)S(1)}, u32[]{:S(2)}, u32[]{:S(2)}) collective-permute-start(bf16[144,512]{1,0:T(8,128)(2,1)S(1)} %get-tuple-element.134), channel_id=1, source_target_pairs={{0,8},{4,12},{8,0},{12,4},{16,24},{20,28},{24,16},{28,20},{1,9},{5... | collective-permute-start | bytes 442376 | tf_op jit(solution)/shard_map/ppermute | solution.py:509
  70.9 26.1 %collective-permute-start.13 = (bf16[256,1024]{1,0:T(8,128)(2,1)S(1)}, bf16[256,1024]{1,0:T(8,128)(2,1)S(1)}, u32[]{:S(2)}, u32[]{:S(2)}) collective-permute-start(bf16[256,1024]{1,0:T(8,128)(2,1)S(1)} %collective-permute-done.9), channel_id=1, source_target_pairs={{0,4},{4,0},{8,12},{12,8},{16,20},{20,16},{24,28},{28,24},{1,5},{5... | collective-permute-start | bytes 1572872 | tf_op jit(solution)/shard_map/ppermute | solution.py:565
  71.0 23.8 %collective-permute-start.10 = (bf16[256,512]{1,0:T(8,128)(2,1)}, bf16[256,512]{1,0:T(8,128)(2,1)S(1)}, u32[]{:S(2)}, u32[]{:S(2)}) collective-permute-start(bf16[256,512]{1,0:T(8,128)(2,1)} %get-tuple-element.108), channel_id=1, source_target_pairs={{0,2},{1,3},{2,0},{3,1},{4,6},{5,7},{6,4},{7,5},{8,10},{9,11},{10,... | collective-permute-start | bytes 786440 | tf_op jit(solution)/shard_map/ppermute | solution.py:521
  74.2 22.7 %collective-permute-start.11 = (bf16[256,512]{1,0:T(8,128)(2,1)}, bf16[256,512]{1,0:T(8,128)(2,1)S(1)}, u32[]{:S(2)}, u32[]{:S(2)}) collective-permute-start(bf16[256,512]{1,0:T(8,128)(2,1)} %get-tuple-element.109), channel_id=1, source_target_pairs={{0,1},{1,2},{2,3},{3,0},{4,5},{5,6},{6,7},{7,4},{8,9},{9,10},{10,1... | collective-permute-start | bytes 786440 | tf_op jit(solution)/shard_map/ppermute | solution.py:521
  74.2 22.8 %collective-permute-start.12 = (bf16[256,512]{1,0:T(8,128)(2,1)}, bf16[256,512]{1,0:T(8,128)(2,1)S(1)}, u32[]{:S(2)}, u32[]{:S(2)}) collective-permute-start(bf16[256,512]{1,0:T(8,128)(2,1)} %get-tuple-element.110), channel_id=1, source_target_pairs={{0,3},{1,0},{2,1},{3,2},{4,7},{5,4},{6,5},{7,6},{8,11},{9,8},{10,9... | collective-permute-start | bytes 786440 | tf_op jit(solution)/shard_map/ppermute | solution.py:521
  93.4 3.7 %copy-start.6 = (bf16[256,512]{1,0:T(8,128)(2,1)S(1)}, bf16[256,512]{1,0:T(8,128)(2,1)}, u32[]{:S(2)}) copy-start(bf16[256,512]{1,0:T(8,128)(2,1)} %get-tuple-element.121) | copy-start | bytes 786436
  94.8 2.4 %copy-start.5 = (bf16[256,512]{1,0:T(8,128)(2,1)S(1)}, bf16[256,512]{1,0:T(8,128)(2,1)}, u32[]{:S(2)}) copy-start(bf16[256,512]{1,0:T(8,128)(2,1)} %get-tuple-element.120) | copy-start | bytes 786436
  94.8 6.2 %copy-start.4 = (bf16[256,512]{1,0:T(8,128)(2,1)S(1)}, bf16[256,512]{1,0:T(8,128)(2,1)}, u32[]{:S(2)}) copy-start(bf16[256,512]{1,0:T(8,128)(2,1)} %get-tuple-element.122) | copy-start | bytes 786436
  97.0 17.9 %collective-permute-start.15 = (bf16[256,512]{1,0:T(8,128)(2,1)S(1)}, bf16[256,512]{1,0:T(8,128)(2,1)S(1)}, u32[]{:S(2)}, u32[]{:S(2)}) collective-permute-start(bf16[256,512]{1,0:T(8,128)(2,1)S(1)} %copy-done.6), channel_id=1, source_target_pairs={{0,2},{1,3},{2,0},{3,1},{4,6},{5,7},{6,4},{7,5},{8,10},{9,11},{10,... | collective-permute-start | bytes 786440 | tf_op jit(solution)/shard_map/ppermute | solution.py:521
  97.1 25.7 %collective-permute-start.14 = (bf16[256,512]{1,0:T(8,128)(2,1)S(1)}, bf16[256,512]{1,0:T(8,128)(2,1)S(1)}, u32[]{:S(2)}, u32[]{:S(2)}) collective-permute-start(bf16[256,512]{1,0:T(8,128)(2,1)S(1)} %copy-done.5), channel_id=1, source_target_pairs={{0,3},{1,0},{2,1},{3,2},{4,7},{5,4},{6,5},{7,6},{8,11},{9,8},{10,9... | collective-permute-start | bytes 786440 | tf_op jit(solution)/shard_map/ppermute | solution.py:521
  101.0 23.8 %collective-permute-start.16 = (bf16[256,512]{1,0:T(8,128)(2,1)S(1)}, bf16[256,512]{1,0:T(8,128)(2,1)S(1)}, u32[]{:S(2)}, u32[]{:S(2)}) collective-permute-start(bf16[256,512]{1,0:T(8,128)(2,1)S(1)} %copy-done.4), channel_id=1, source_target_pairs={{0,1},{1,2},{2,3},{3,0},{4,5},{5,6},{6,7},{7,4},{8,9},{9,10},{10,1... | collective-permute-start | bytes 786440 | tf_op jit(solution)/shard_map/ppermute | solution.py:521
  103.9 19.3 %copy-start.3 = (bf16[256,512]{1,0:T(8,128)(2,1)S(1)}, bf16[256,512]{1,0:T(8,128)(2,1)}, u32[]{:S(2)}) copy-start(bf16[256,512]{1,0:T(8,128)(2,1)} %get-tuple-element.119) | copy-start | bytes 786436
  (2 other events, 3.0 us)

commit v10 on v9

--- a/solution.py
+++ b/solution.py
@@ -568,9 +568,8 @@
     for k in range(1, pieces):
         gated = gates(place(k), hidden, g_f, g_r, 1e8)
         parts = settle(place(k), strands, ends, gated, lanes, copy_first, entering, copy_second, heads, inner)
-        keys = [*middle_first, 0]
-        parts, blocks, across_other = lax.optimization_barrier((parts, [arrived[k - 1][d] for d in keys], across_other))
-        arrived[k - 1] = dict(zip(keys, blocks))
+        parts, arrived[k - 1], across_other, other, same = lax.optimization_barrier(
+            (parts, arrived[k - 1], across_other, other, same))
         arrived.append({0: parts[0], **{d: rotated(parts[d], d, n_head) for d in middle_first}})
     own_rows = lax.dynamic_slice_in_dim(hidden, head * share, share, 0)
     pairs = {d: (one, other[i * half : (i + 1) * half]) for i, (d, one) in enumerate(zip(early, same))}

time: 127 us -> 126 us (level)
  waiting for transfers between devices: 20.9 us -> 18.4 us
  matrix products: 5.74 us -> 7.7 us
    ppermute x9, waiting for transfers between devices: 20.6 us -> 18.2 us  [rotated(): lax.ppermute(block, 'head', [(i, (i + d) % count) for i in range(count)])]
    dot_general x6, matrix products: 4.84 us -> 6.81 us  [on_device(): jnp.dot(arrived[k][d], groups[d], preferred_element_type=F32)]
  transfers between devices with their start and end apart: 17 -> 17, of which waited for: 5 -> 5; matrix products, arithmetic and copies ran while one was open for 6% -> 8% of each run, Pallas kernels for 55% -> 56%
where the time goes in v10:
time: 126 us; the launch traced here: 125 us
  Pallas kernels  69.7 us (55%)
  starting transfers between devices  23.1 us (18%)
  waiting for transfers between devices  18.4 us (15%)
  matrix products  7.7 us (6%)
  other arithmetic  5 us (4%)
    pallas_call x5, Pallas kernels, by_destination(): pl.pallas_call(lambda _, *refs: kernel(*refs), grid_spec=pltpu.PrefetchSc...  37.6 us
    pallas_call x1, Pallas kernels, project(): pl.pallas_call(functools.partial(project_kernel, heads, inner), grid=(n,)...  30.9 us
    ppermute x9, waiting for transfers between devices, rotated(): lax.ppermute(block, 'head', [(i, (i + d) % count) for i in range(count)])  18.2 us
    ppermute x9, starting transfers between devices, rotated(): lax.ppermute(block, 'head', [(i, (i + d) % count) for i in range(count)])  11.9 us
    dot_general x6, matrix products, on_device(): jnp.dot(arrived[k][d], groups[d], preferred_element_type=F32)  6.81 us
    ppermute x2, starting transfers between devices, shifted(): lax.ppermute(block, axis, [(i - distance, i) for i in devices if i - dist...  5.55 us
    ppermute x3, starting transfers between devices, incoming(): lax.ppermute(block, axis, [(i, i ^ d * distance) for i in range(count)])  3.55 us
  transfers between devices with their start and end apart: 17, of which 5 were waited for; matrix products, arithmetic and copies ran while one was open for 8% of the time, Pallas kernels for 56%

profile of v10, /device:TPU:10, one launch (start us, length us, event | category | flops | bytes accessed | tf_op | source)
XLA Modules:
  0.0 125.2 jit_solution(16785431073656608491)
XLA Ops:
  0.9 1.9 %collective-permute-start = (bf16[16,1024]{1,0:T(8,128)(2,1)S(1)}, bf16[16,1024]{1,0:T(8,128)(2,1)S(1)}, u32[]{:S(2)}, u32[]{:S(2)}) collective-permute-start(bf16[16,1024]{1,0:T(8,128)(2,1)S(1)} %get-tuple-element.130), channel_id=1, source_target_pairs={{0,4},{4,8},{8,12},{12,16},{16,20},{20,24},{24,28},{1,5},{5,9},{9,... | collective-permute-start | bytes 98312 | tf_op jit(solution)/shard_map/ppermute | solution.py:517
  2.8 3.6 %collective-permute-start.1 = (bf16[16,1024]{1,0:T(8,128)(2,1)S(1)}, bf16[16,1024]{1,0:T(8,128)(2,1)S(1)}, u32[]{:S(2)}, u32[]{:S(2)}) collective-permute-start(bf16[16,1024]{1,0:T(8,128)(2,1)S(1)} %get-tuple-element.129), channel_id=1, source_target_pairs={{4,0},{8,4},{12,8},{16,12},{20,16},{24,20},{28,24},{5,1},{9,5},{13... | collective-permute-start | bytes 98312 | tf_op jit(solution)/shard_map/ppermute | solution.py:517
  8.0 1.6 %collective-permute-start.2 = (bf16[256,1024]{1,0:T(8,128)(2,1)S(1)}, bf16[256,1024]{1,0:T(8,128)(2,1)S(1)}, u32[]{:S(2)}, u32[]{:S(2)}) collective-permute-start(bf16[256,1024]{1,0:T(8,128)(2,1)S(1)} %constant_dynamic-slice_fusion.2), channel_id=1, source_target_pairs={{0,1},{1,2},{2,3},{3,0},{4,5},{5,6},{6,7},{7,4},{8,9},{9,10},{10,1... | collective-permute-start | bytes 1572872 | tf_op jit(solution)/shard_map/ppermute | solution.py:521
  10.0 30.9 %project.1 = (bf16[2048,768]{1,0:T(8,128)(2,1)}, f32[2048,128]{1,0:T(8,128)}, f32[8,2048]{1,0:T(8,128)}, bf16[16,128,512]{2,1,0:T(8,128)(2,1)}, f32[16,8,512]{2,...) custom-call(bf16[2048,1024]{1,0:T(8,128)(2,1)} %refs_0_.5, ...), custom_call_target="tpu_custom_call" | custom-call | flops 22000001024 | bytes 40000000 | tf_op jit(solution)/shard_map/project/pallas_call | solution.py:224
  41.0 2.0 %collective-permute-start.4 = (bf16[288,512]{1,0:T(8,128)(2,1)}, bf16[288,512]{1,0:T(8,128)(2,1)S(1)}, u32[]{:S(2)}, u32[]{:S(2)}) collective-permute-start(bf16[288,512]{1,0:T(8,128)(2,1)} %get-tuple-element.81.refs_1_), channel_id=1, source_target_pairs={{0,4},{4,0},{8,12},{12,8},{16,20},{20,16},{24,28},{28,24},{1,5},{5... | collective-permute-start | bytes 884744 | tf_op jit(solution)/shard_map/ppermute | solution.py:490
  43.0 5.8 %gates.2 = (bf16[1024,512]{1,0:T(8,128)(2,1)}, bf16[1024,512]{1,0:T(8,128)(2,1)}) custom-call(s32[1]{0:T(128)} %bitcast._, bf16[2048,1024]{1,0:T(8,128)(2,1)} %refs_0_.5, bf16[1024,512]{1,0:T(8,128)(2,1)} %get-tuple-element.103.refs_1_, bf16[1024,512]{1,0:T(8,128)(2,1)} %get-tuple-element.104.refs_2_), custom_call_target="tpu_custom_call" | custom-call | flops 5000000000 | bytes 1000000 | tf_op jit(solution)/shard_map/gates/pallas_call | solution.py:265
  50.1 1.6 %collective-permute-start.9 = (bf16[256,1024]{1,0:T(8,128)(2,1)S(1)}, bf16[256,1024]{1,0:T(8,128)(2,1)S(1)}, u32[]{:S(2)}, u32[]{:S(2)}) collective-permute-start(bf16[256,1024]{1,0:T(8,128)(2,1)S(1)} %collective-permute-done.2), channel_id=1, source_target_pairs={{0,1},{1,2},{2,3},{3,0},{4,5},{5,6},{6,7},{7,4},{8,9},{9,10},{10,1... | collective-permute-start | bytes 1572872 | tf_op jit(solution)/shard_map/ppermute | solution.py:521
  52.8 2.4 %collective-permute-start.5 = (bf16[144,512]{1,0:T(8,128)(2,1)S(1)}, bf16[144,512]{1,0:T(8,128)(2,1)S(1)}, u32[]{:S(2)}, u32[]{:S(2)}) collective-permute-start(bf16[144,512]{1,0:T(8,128)(2,1)S(1)} %get-tuple-element.140), channel_id=1, source_target_pairs={{0,8},{4,12},{8,0},{12,4},{16,24},{20,28},{24,16},{28,20},{1,9},{5... | collective-permute-start | bytes 442376 | tf_op jit(solution)/shard_map/ppermute | solution.py:509
  55.2 7.2 %inside.1 = (bf16[1024,512]{1,0:T(8,128)(2,1)}, bf16[1024,512]{1,0:T(8,128)(2,1)}) custom-call(s32[1]{0:T(128)} %bitcast._, bf16[2048,768]{1,0:T(8,128)(2,1)} %get-tuple-element.69.refs_0_, f32[2048,128]{1,0:T(8,128)} %get-tuple-element.70.refs_1_.refs_3_, f32[8,2048]{1,0:T(8,128)} %get-tuple-element.71.refs_2_, ...), custom_call_target="tpu_custom_call" | custom-call | flops 8000000000 | bytes 1000000 | tf_op jit(solution)/shard_map/inside/pallas_call | solution.py:265
  63.4 7.5 %finish.1 = (bf16[256,512]{1,0:T(8,128)(2,1)}, bf16[256,512]{1,0:T(8,128)(2,1)}, bf16[256,512]{1,0:T(8,128)(2,1)}, bf16[256,512]{1,0:T(8,128)(2,1)}) custom-call(s32[1]{0:T(128)} %bitcast._, bf16[2048,768]{1,0:T(8,128)(2,1)} %get-tuple-element.69.refs_0_, bf16[16,128,512]{2,1,0:T(8,128)(2,1)} %get-tuple-element.75.refs_1_.refs_6_, ...), custom_call_target="tpu_custom_call" | custom-call | flops 100000000 | bytes 1000000 | tf_op jit(solution)/shard_map/finish/pallas_call | solution.py:265
  71.0 1.6 %collective-permute-start.10 = (bf16[256,512]{1,0:T(8,128)(2,1)}, bf16[256,512]{1,0:T(8,128)(2,1)S(1)}, u32[]{:S(2)}, u32[]{:S(2)}) collective-permute-start(bf16[256,512]{1,0:T(8,128)(2,1)} %get-tuple-element.112), channel_id=1, source_target_pairs={{0,1},{1,2},{2,3},{3,0},{4,5},{5,6},{6,7},{7,4},{8,9},{9,10},{10,1... | collective-permute-start | bytes 786440 | tf_op jit(solution)/shard_map/ppermute | solution.py:521
  72.7 1.6 %collective-permute-start.11 = (bf16[256,512]{1,0:T(8,128)(2,1)}, bf16[256,512]{1,0:T(8,128)(2,1)}, u32[]{:S(2)}, u32[]{:S(2)}) collective-permute-start(bf16[256,512]{1,0:T(8,128)(2,1)} %get-tuple-element.113), channel_id=1, source_target_pairs={{0,2},{1,3},{2,0},{3,1},{4,6},{5,7},{6,4},{7,5},{8,10},{9,11},{10,... | collective-permute-start | bytes 786440 | tf_op jit(solution)/shard_map/ppermute | solution.py:521
  74.3 1.9 %collective-permute-start.12 = (bf16[256,512]{1,0:T(8,128)(2,1)}, bf16[256,512]{1,0:T(8,128)(2,1)}, u32[]{:S(2)}, u32[]{:S(2)}) collective-permute-start(bf16[256,512]{1,0:T(8,128)(2,1)} %get-tuple-element.114), channel_id=1, source_target_pairs={{0,3},{1,0},{2,1},{3,2},{4,7},{5,4},{6,5},{7,6},{8,11},{9,8},{10,9... | collective-permute-start | bytes 786440 | tf_op jit(solution)/shard_map/ppermute | solution.py:521
  76.2 5.8 %gates.3 = (bf16[1024,512]{1,0:T(8,128)(2,1)}, bf16[1024,512]{1,0:T(8,128)(2,1)}) custom-call(s32[1]{0:T(128)} %bitcast._, bf16[2048,1024]{1,0:T(8,128)(2,1)} %refs_0_.5, bf16[1024,512]{1,0:T(8,128)(2,1)} %get-tuple-element.103.refs_1_, bf16[1024,512]{1,0:T(8,128)(2,1)} %get-tuple-element.104.refs_2_), custom_call_target="tpu_custom_call" | custom-call | flops 100000000 | bytes 1000000 | tf_op jit(solution)/shard_map/gates/pallas_call | solution.py:265
  82.0 11.4 %settle.1 = (bf16[256,512]{1,0:T(8,128)(2,1)}, bf16[256,512]{1,0:T(8,128)(2,1)}, bf16[256,512]{1,0:T(8,128)(2,1)}, bf16[256,512]{1,0:T(8,128)(2,1)}) custom-call(s32[1]{0:T(128)} %bitcast._, bf16[2048,768]{1,0:T(8,128)(2,1)} %get-tuple-element.69.refs_0_, f32[2048,128]{1,0:T(8,128)} %get-tuple-element.70.refs_1_.refs_3_, ...), custom_call_target="tpu_custom_call" | custom-call | flops 100000000 | bytes 1000000 | tf_op jit(solution)/shard_map/settle/pallas_call | solution.py:265
  93.4 2.6 %collective-permute-done.11 = bf16[256,512]{1,0:T(8,128)(2,1)} collective-permute-done((bf16[256,512]{1,0:T(8,128)(2,1)}, bf16[256,512]{1,0:T(8,128)(2,1)}, u32[]{:S(2)}, u32[]{:S(2)}) %collective-permute-start.11) | collective-permute-done | bytes 262176 | tf_op jit(solution)/shard_map/ppermute | solution.py:521
  96.0 2.3 %collective-permute-done.12 = bf16[256,512]{1,0:T(8,128)(2,1)} collective-permute-done((bf16[256,512]{1,0:T(8,128)(2,1)}, bf16[256,512]{1,0:T(8,128)(2,1)}, u32[]{:S(2)}, u32[]{:S(2)}) %collective-permute-start.12) | collective-permute-done | bytes 262176 | tf_op jit(solution)/shard_map/ppermute | solution.py:521
  99.4 2.0 %collective-permute-start.16 = (bf16[256,512]{1,0:T(8,128)(2,1)}, bf16[256,512]{1,0:T(8,128)(2,1)S(1)}, u32[]{:S(2)}, u32[]{:S(2)}) collective-permute-start(bf16[256,512]{1,0:T(8,128)(2,1)} %get-tuple-element.128), channel_id=1, source_target_pairs={{0,1},{1,2},{2,3},{3,0},{4,5},{5,6},{6,7},{7,4},{8,9},{9,10},{10,1... | collective-permute-start | bytes 786440 | tf_op jit(solution)/shard_map/ppermute | solution.py:521
  103.3 1.4 %fusion.9 = f32[256,1024]{1,0:T(8,128)S(1)} fusion(bf16[256,512]{1,0:T(8,128)(2,1)} %collective-permute-done.11, bf16[256,1024]{1,0:T(8,128)(2,1)S(1)} %get-tuple-element.138, bf16[256,1024]{1,0:T(8,128)(2,1)S(1)} %get-tuple-element.137), kind=kOutput, calls=%fused_computation.17 | convolution fusion | flops 270532608 | bytes 2359296 | tf_op jit(solution)/shard_map/dot_general | solution.py:587
  104.8 1.4 %fusion.11 = f32[256,1024]{1,0:T(8,128)S(1)} fusion(bf16[256,512]{1,0:T(8,128)(2,1)} %collective-permute-done.12, bf16[256,1024]{1,0:T(8,128)(2,1)S(1)} %get-tuple-element.135, bf16[256,1024]{1,0:T(8,128)(2,1)S(1)} %get-tuple-element.136), kind=kOutput, calls=%fused_computation.19 | convolution fusion | flops 270532608 | bytes 2359296 | tf_op jit(solution)/shard_map/dot_general | solution.py:587
  106.2 1.6 %fusion.5 = bf16[256,1024]{1,0:T(8,128)(2,1)S(1)} fusion(f32[256,1024]{1,0:T(8,128)S(1)} %fusion.7, f32[256,1024]{1,0:T(8,128)S(1)} %fusion.9, f32[256,1024]{1,0:T(8,128)S(1)} %fusion.11, bf16[256,512]{1,0:T(8,128)(2,1)S(1)} %copy-done.2, bf16[512,1024]{1,0:T(8,128)(2,1)S(1)} %copy-done, bf16[2048,1024]{1,0:T(8,128)(2,1)} %refs_0_.5, s32[]{:T(128)S(6)} %select_n.70), kind=kOutput, calls=%fused_computation.7 | convolution fusion | flops 270008320 | bytes 5505028 | tf_op jit(solution)/shard_map/dot_general | solution.py:587
  107.8 8.5 %collective-permute-done.15 = bf16[256,512]{1,0:T(8,128)(2,1)S(1)} collective-permute-done((bf16[256,512]{1,0:T(8,128)(2,1)}, bf16[256,512]{1,0:T(8,128)(2,1)S(1)}, u32[]{:S(2)}, u32[]{:S(2)}) %collective-permute-start.15) | collective-permute-done | bytes 262176 | tf_op jit(solution)/shard_map/ppermute | solution.py:521
  116.7 4.8 %collective-permute-done.14 = bf16[256,512]{1,0:T(8,128)(2,1)S(1)} collective-permute-done((bf16[256,512]{1,0:T(8,128)(2,1)}, bf16[256,512]{1,0:T(8,128)(2,1)S(1)}, u32[]{:S(2)}, u32[]{:S(2)}) %collective-permute-start.14) | collective-permute-done | bytes 262176 | tf_op jit(solution)/shard_map/ppermute | solution.py:521
  121.9 1.5 %fusion.1 = f32[256,1024]{1,0:T(8,128)S(1)} fusion(f32[256,1024]{1,0:T(8,128)S(1)} %fusion.8, f32[256,1024]{1,0:T(8,128)S(1)} %fusion.10, bf16[256,512]{1,0:T(8,128)(2,1)S(1)} %copy-done.3, bf16[512,1024]{1,0:T(8,128)(2,1)S(1)} %copy-done, bf16[2048,1024]{1,0:T(8,128)(2,1)} %refs_0_.5, s32[]{:T(128)S(6)} %add.70), kind=kOutput, calls=%fused_computation.2 | convolution fusion | flops 269484032 | bytes 4980740 | tf_op jit(solution)/shard_map/dot_general | solution.py:587
  (47 shorter events, 12.0 us)
Async XLA Ops:
  0.0 6.5 %copy-start = (bf16[512,1024]{1,0:T(8,128)(2,1)S(1)}, bf16[512,1024]{1,0:T(8,128)(2,1)}, u32[]{:S(2)}) copy-start(bf16[512,1024]{1,0:T(8,128)(2,1)} %param.23) | copy-start | bytes 3145732
  0.9 6.9 %collective-permute-start = (bf16[16,1024]{1,0:T(8,128)(2,1)S(1)}, bf16[16,1024]{1,0:T(8,128)(2,1)S(1)}, u32[]{:S(2)}, u32[]{:S(2)}) collective-permute-start(bf16[16,1024]{1,0:T(8,128)(2,1)S(1)} %get-tuple-element.130), channel_id=1, source_target_pairs={{0,4},{4,8},{8,12},{12,16},{16,20},{20,24},{24,28},{1,5},{5,9},{9,... | collective-permute-start | bytes 98312 | tf_op jit(solution)/shard_map/ppermute | solution.py:517
  2.8 5.2 %collective-permute-start.1 = (bf16[16,1024]{1,0:T(8,128)(2,1)S(1)}, bf16[16,1024]{1,0:T(8,128)(2,1)S(1)}, u32[]{:S(2)}, u32[]{:S(2)}) collective-permute-start(bf16[16,1024]{1,0:T(8,128)(2,1)S(1)} %get-tuple-element.129), channel_id=1, source_target_pairs={{4,0},{8,4},{12,8},{16,12},{20,16},{24,20},{28,24},{5,1},{9,5},{13... | collective-permute-start | bytes 98312 | tf_op jit(solution)/shard_map/ppermute | solution.py:517
  7.8 2.2 %copy-start.4 = (bf16[16,1024]{1,0:T(8,128)(2,1)}, bf16[16,1024]{1,0:T(8,128)(2,1)S(1)}, u32[]{:S(2)}) copy-start(bf16[16,1024]{1,0:T(8,128)(2,1)S(1)} %collective-permute-done.refs_2_) | copy-start | bytes 98308
  8.0 2.0 %copy-start.5 = (bf16[16,1024]{1,0:T(8,128)(2,1)}, bf16[16,1024]{1,0:T(8,128)(2,1)S(1)}, u32[]{:S(2)}) copy-start(bf16[16,1024]{1,0:T(8,128)(2,1)S(1)} %collective-permute-done.1.refs_3_) | copy-start | bytes 98308
  8.0 32.9 %collective-permute-start.2 = (bf16[256,1024]{1,0:T(8,128)(2,1)S(1)}, bf16[256,1024]{1,0:T(8,128)(2,1)S(1)}, u32[]{:S(2)}, u32[]{:S(2)}) collective-permute-start(bf16[256,1024]{1,0:T(8,128)(2,1)S(1)} %constant_dynamic-slice_fusion.2), channel_id=1, source_target_pairs={{0,1},{1,2},{2,3},{3,0},{4,5},{5,6},{6,7},{7,4},{8,9},{9,10},{10,1... | collective-permute-start | bytes 1572872 | tf_op jit(solution)/shard_map/ppermute | solution.py:521
  9.6 31.4 %collective-permute-start.3 = (bf16[256,1024]{1,0:T(8,128)(2,1)S(1)}, bf16[256,1024]{1,0:T(8,128)(2,1)S(1)}, u32[]{:S(2)}, u32[]{:S(2)}) collective-permute-start(bf16[256,1024]{1,0:T(8,128)(2,1)S(1)} %constant_dynamic-slice_fusion.2), channel_id=1, source_target_pairs={{0,3},{1,0},{2,1},{3,2},{4,7},{5,4},{6,5},{7,6},{8,11},{9,8},{10,9... | collective-permute-start | bytes 1572872 | tf_op jit(solution)/shard_map/ppermute | solution.py:521
  41.0 7.8 %collective-permute-start.4 = (bf16[288,512]{1,0:T(8,128)(2,1)}, bf16[288,512]{1,0:T(8,128)(2,1)S(1)}, u32[]{:S(2)}, u32[]{:S(2)}) collective-permute-start(bf16[288,512]{1,0:T(8,128)(2,1)} %get-tuple-element.81.refs_1_), channel_id=1, source_target_pairs={{0,4},{4,0},{8,12},{12,8},{16,20},{20,16},{24,28},{28,24},{1,5},{5... | collective-permute-start | bytes 884744 | tf_op jit(solution)/shard_map/ppermute | solution.py:490
  43.0 5.8 %copy-start.1 = (bf16[288,512]{1,0:T(8,128)(2,1)S(1)}, bf16[288,512]{1,0:T(8,128)(2,1)}, u32[]{:S(2)}) copy-start(bf16[288,512]{1,0:T(8,128)(2,1)} %get-tuple-element.81.refs_1_) | copy-start | bytes 884740
  50.1 13.4 %collective-permute-start.8 = (bf16[512,1024]{1,0:T(8,128)(2,1)}, bf16[512,1024]{1,0:T(8,128)(2,1)}, u32[]{:S(2)}, u32[]{:S(2)}) collective-permute-start(bf16[512,1024]{1,0:T(8,128)(2,1)} %pad_maximum_fusion), channel_id=1, source_target_pairs={{0,4},{4,0},{8,12},{12,8},{16,20},{20,16},{24,28},{28,24},{1,5},{5... | collective-permute-start | bytes 3145736 | tf_op jit(solution)/shard_map/ppermute | solution.py:560
  50.1 20.8 %collective-permute-start.9 = (bf16[256,1024]{1,0:T(8,128)(2,1)S(1)}, bf16[256,1024]{1,0:T(8,128)(2,1)S(1)}, u32[]{:S(2)}, u32[]{:S(2)}) collective-permute-start(bf16[256,1024]{1,0:T(8,128)(2,1)S(1)} %collective-permute-done.2), channel_id=1, source_target_pairs={{0,1},{1,2},{2,3},{3,0},{4,5},{5,6},{6,7},{7,4},{8,9},{9,10},{10,1... | collective-permute-start | bytes 1572872 | tf_op jit(solution)/shard_map/ppermute | solution.py:521
  51.7 10.7 %collective-permute-start.6 = (bf16[144,512]{1,0:T(8,128)(2,1)S(1)}, bf16[144,512]{1,0:T(8,128)(2,1)S(1)}, u32[]{:S(2)}, u32[]{:S(2)}) collective-permute-start(bf16[144,512]{1,0:T(8,128)(2,1)S(1)} %get-tuple-element.139), channel_id=1, source_target_pairs={{0,16},{4,20},{8,24},{12,28},{16,0},{20,4},{24,8},{28,12},{1,17},{... | collective-permute-start | bytes 442376 | tf_op jit(solution)/shard_map/ppermute | solution.py:509
  51.8 10.6 %collective-permute-start.7 = (bf16[144,512]{1,0:T(8,128)(2,1)S(1)}, bf16[144,512]{1,0:T(8,128)(2,1)S(1)}, u32[]{:S(2)}, u32[]{:S(2)}) collective-permute-start(bf16[144,512]{1,0:T(8,128)(2,1)S(1)} %get-tuple-element.139), channel_id=1, source_target_pairs={{0,24},{4,28},{8,16},{12,20},{16,8},{20,12},{24,0},{28,4},{1,25},{... | collective-permute-start | bytes 442376 | tf_op jit(solution)/shard_map/ppermute | solution.py:509
  52.8 9.5 %collective-permute-start.5 = (bf16[144,512]{1,0:T(8,128)(2,1)S(1)}, bf16[144,512]{1,0:T(8,128)(2,1)S(1)}, u32[]{:S(2)}, u32[]{:S(2)}) collective-permute-start(bf16[144,512]{1,0:T(8,128)(2,1)S(1)} %get-tuple-element.140), channel_id=1, source_target_pairs={{0,8},{4,12},{8,0},{12,4},{16,24},{20,28},{24,16},{28,20},{1,9},{5... | collective-permute-start | bytes 442376 | tf_op jit(solution)/shard_map/ppermute | solution.py:509
  70.9 27.4 %collective-permute-start.13 = (bf16[256,1024]{1,0:T(8,128)(2,1)S(1)}, bf16[256,1024]{1,0:T(8,128)(2,1)S(1)}, u32[]{:S(2)}, u32[]{:S(2)}) collective-permute-start(bf16[256,1024]{1,0:T(8,128)(2,1)S(1)} %collective-permute-done.9), channel_id=1, source_target_pairs={{0,4},{4,0},{8,12},{12,8},{16,20},{20,16},{24,28},{28,24},{1,5},{5... | collective-permute-start | bytes 1572872 | tf_op jit(solution)/shard_map/ppermute | solution.py:565
  71.0 22.3 %collective-permute-start.10 = (bf16[256,512]{1,0:T(8,128)(2,1)}, bf16[256,512]{1,0:T(8,128)(2,1)S(1)}, u32[]{:S(2)}, u32[]{:S(2)}) collective-permute-start(bf16[256,512]{1,0:T(8,128)(2,1)} %get-tuple-element.112), channel_id=1, source_target_pairs={{0,1},{1,2},{2,3},{3,0},{4,5},{5,6},{6,7},{7,4},{8,9},{9,10},{10,1... | collective-permute-start | bytes 786440 | tf_op jit(solution)/shard_map/ppermute | solution.py:521
  72.7 23.3 %collective-permute-start.11 = (bf16[256,512]{1,0:T(8,128)(2,1)}, bf16[256,512]{1,0:T(8,128)(2,1)}, u32[]{:S(2)}, u32[]{:S(2)}) collective-permute-start(bf16[256,512]{1,0:T(8,128)(2,1)} %get-tuple-element.113), channel_id=1, source_target_pairs={{0,2},{1,3},{2,0},{3,1},{4,6},{5,7},{6,4},{7,5},{8,10},{9,11},{10,... | collective-permute-start | bytes 786440 | tf_op jit(solution)/shard_map/ppermute | solution.py:521
  74.3 24.0 %collective-permute-start.12 = (bf16[256,512]{1,0:T(8,128)(2,1)}, bf16[256,512]{1,0:T(8,128)(2,1)}, u32[]{:S(2)}, u32[]{:S(2)}) collective-permute-start(bf16[256,512]{1,0:T(8,128)(2,1)} %get-tuple-element.114), channel_id=1, source_target_pairs={{0,3},{1,0},{2,1},{3,2},{4,7},{5,4},{6,5},{7,6},{8,11},{9,8},{10,9... | collective-permute-start | bytes 786440 | tf_op jit(solution)/shard_map/ppermute | solution.py:521
  98.3 17.9 %collective-permute-start.15 = (bf16[256,512]{1,0:T(8,128)(2,1)}, bf16[256,512]{1,0:T(8,128)(2,1)S(1)}, u32[]{:S(2)}, u32[]{:S(2)}) collective-permute-start(bf16[256,512]{1,0:T(8,128)(2,1)} %get-tuple-element.127), channel_id=1, source_target_pairs={{0,2},{1,3},{2,0},{3,1},{4,6},{5,7},{6,4},{7,5},{8,10},{9,11},{10,... | collective-permute-start | bytes 786440 | tf_op jit(solution)/shard_map/ppermute | solution.py:521
  99.4 22.1 %collective-permute-start.14 = (bf16[256,512]{1,0:T(8,128)(2,1)}, bf16[256,512]{1,0:T(8,128)(2,1)S(1)}, u32[]{:S(2)}, u32[]{:S(2)}) collective-permute-start(bf16[256,512]{1,0:T(8,128)(2,1)} %get-tuple-element.126), channel_id=1, source_target_pairs={{0,3},{1,0},{2,1},{3,2},{4,7},{5,4},{6,5},{7,6},{8,11},{9,8},{10,9... | collective-permute-start | bytes 786440 | tf_op jit(solution)/shard_map/ppermute | solution.py:521
  99.4 24.1 %collective-permute-start.16 = (bf16[256,512]{1,0:T(8,128)(2,1)}, bf16[256,512]{1,0:T(8,128)(2,1)S(1)}, u32[]{:S(2)}, u32[]{:S(2)}) collective-permute-start(bf16[256,512]{1,0:T(8,128)(2,1)} %get-tuple-element.128), channel_id=1, source_target_pairs={{0,1},{1,2},{2,3},{3,0},{4,5},{5,6},{6,7},{7,4},{8,9},{9,10},{10,1... | collective-permute-start | bytes 786440 | tf_op jit(solution)/shard_map/ppermute | solution.py:521
  103.3 2.9 %copy-start.2 = (bf16[256,512]{1,0:T(8,128)(2,1)S(1)}, bf16[256,512]{1,0:T(8,128)(2,1)}, u32[]{:S(2)}) copy-start(bf16[256,512]{1,0:T(8,128)(2,1)} %get-tuple-element.117) | copy-start | bytes 786436
  107.8 14.1 %copy-start.3 = (bf16[256,512]{1,0:T(8,128)(2,1)S(1)}, bf16[256,512]{1,0:T(8,128)(2,1)}, u32[]{:S(2)}) copy-start(bf16[256,512]{1,0:T(8,128)(2,1)} %get-tuple-element.125) | copy-start | bytes 786436

commit v11 on v10

--- a/solution.py
+++ b/solution.py
@@ -568,8 +568,16 @@
     for k in range(1, pieces):
         gated = gates(place(k), hidden, g_f, g_r, 1e8)
         parts = settle(place(k), strands, ends, gated, lanes, copy_first, entering, copy_second, heads, inner)
-        parts, arrived[k - 1], across_other, other, same = lax.optimization_barrier(
-            (parts, arrived[k - 1], across_other, other, same))
+        parts = list(parts)
+        before = arrived[k - 1]
+        middle = middle_first[0]
+        parts[middle], before[1] = lax.optimization_barrier((parts[middle], before[1]))
+        rest = [d for d in range(n_head) if d != middle]
+        moved, before, across_other, other, same = lax.optimization_barrier(
+            ([parts[d] for d in rest], before, across_other, other, same))
+        arrived[k - 1] = before
+        for d, block in zip(rest, moved):
+            parts[d] = block
         arrived.append({0: parts[0], **{d: rotated(parts[d], d, n_head) for d in middle_first}})
     own_rows = lax.dynamic_slice_in_dim(hidden, head * share, share, 0)
     pairs = {d: (one, other[i * half : (i + 1) * half]) for i, (d, one) in enumerate(zip(early, same))}

time: 126 us -> 127 us (level); the launches traced: 125 us -> 124 us
  no operation moved by 1% of the time
where the time goes in v11:
time: 127 us; the launch traced here: 124 us
  Pallas kernels  69.7 us (55%)
  starting transfers between devices  22.1 us (17%)
  waiting for transfers between devices  18.7 us (15%)
  matrix products  7.71 us (6%)
  other arithmetic  5 us (4%)
    pallas_call x5, Pallas kernels, by_destination(): pl.pallas_call(lambda _, *refs: kernel(*refs), grid_spec=pltpu.PrefetchSc...  37.6 us
    pallas_call x1, Pallas kernels, project(): pl.pallas_call(functools.partial(project_kernel, heads, inner), grid=(n,)...  30.9 us
    ppermute x9, waiting for transfers between devices, rotated(): lax.ppermute(block, 'head', [(i, (i + d) % count) for i in range(count)])  18.5 us
    ppermute x9, starting transfers between devices, rotated(): lax.ppermute(block, 'head', [(i, (i + d) % count) for i in range(count)])  10.9 us
    dot_general x6, matrix products, on_device(): jnp.dot(arrived[k][d], groups[d], preferred_element_type=F32)  6.81 us
    ppermute x2, starting transfers between devices, shifted(): lax.ppermute(block, axis, [(i - distance, i) for i in devices if i - dist...  5.55 us
    ppermute x3, starting transfers between devices, incoming(): lax.ppermute(block, axis, [(i, i ^ d * distance) for i in range(count)])  3.55 us
  transfers between devices with their start and end apart: 17, of which 5 were waited for; matrix products, arithmetic and copies ran while one was open for 8% of the time, Pallas kernels for 56%

profile of v11, /device:TPU:10, one launch (start us, length us, event | category | flops | bytes accessed | tf_op | source)
XLA Modules:
  0.0 124.4 jit_solution(13692908761943833441)
XLA Ops:
  0.9 1.9 %collective-permute-start = (bf16[16,1024]{1,0:T(8,128)(2,1)S(1)}, bf16[16,1024]{1,0:T(8,128)(2,1)S(1)}, u32[]{:S(2)}, u32[]{:S(2)}) collective-permute-start(bf16[16,1024]{1,0:T(8,128)(2,1)S(1)} %get-tuple-element.132), channel_id=1, source_target_pairs={{0,4},{4,8},{8,12},{12,16},{16,20},{20,24},{24,28},{1,5},{5,9},{9,... | collective-permute-start | bytes 98312 | tf_op jit(solution)/shard_map/ppermute | solution.py:517
  2.8 3.6 %collective-permute-start.1 = (bf16[16,1024]{1,0:T(8,128)(2,1)S(1)}, bf16[16,1024]{1,0:T(8,128)(2,1)S(1)}, u32[]{:S(2)}, u32[]{:S(2)}) collective-permute-start(bf16[16,1024]{1,0:T(8,128)(2,1)S(1)} %get-tuple-element.131), channel_id=1, source_target_pairs={{4,0},{8,4},{12,8},{16,12},{20,16},{24,20},{28,24},{5,1},{9,5},{13... | collective-permute-start | bytes 98312 | tf_op jit(solution)/shard_map/ppermute | solution.py:517
  8.0 1.6 %collective-permute-start.2 = (bf16[256,1024]{1,0:T(8,128)(2,1)S(1)}, bf16[256,1024]{1,0:T(8,128)(2,1)S(1)}, u32[]{:S(2)}, u32[]{:S(2)}) collective-permute-start(bf16[256,1024]{1,0:T(8,128)(2,1)S(1)} %constant_dynamic-slice_fusion.2), channel_id=1, source_target_pairs={{0,1},{1,2},{2,3},{3,0},{4,5},{5,6},{6,7},{7,4},{8,9},{9,10},{10,1... | collective-permute-start | bytes 1572872 | tf_op jit(solution)/shard_map/ppermute | solution.py:521
  10.0 30.9 %project.1 = (bf16[2048,768]{1,0:T(8,128)(2,1)}, f32[2048,128]{1,0:T(8,128)}, f32[8,2048]{1,0:T(8,128)}, bf16[16,128,512]{2,1,0:T(8,128)(2,1)}, f32[16,8,512]{2,...) custom-call(bf16[2048,1024]{1,0:T(8,128)(2,1)} %refs_0_.5, ...), custom_call_target="tpu_custom_call" | custom-call | flops 22000001024 | bytes 40000000 | tf_op jit(solution)/shard_map/project/pallas_call | solution.py:224
  41.0 2.0 %collective-permute-start.4 = (bf16[288,512]{1,0:T(8,128)(2,1)}, bf16[288,512]{1,0:T(8,128)(2,1)S(1)}, u32[]{:S(2)}, u32[]{:S(2)}) collective-permute-start(bf16[288,512]{1,0:T(8,128)(2,1)} %get-tuple-element.82.refs_1_), channel_id=1, source_target_pairs={{0,4},{4,0},{8,12},{12,8},{16,20},{20,16},{24,28},{28,24},{1,5},{5... | collective-permute-start | bytes 884744 | tf_op jit(solution)/shard_map/ppermute | solution.py:490
  43.0 5.8 %gates.2 = (bf16[1024,512]{1,0:T(8,128)(2,1)}, bf16[1024,512]{1,0:T(8,128)(2,1)}) custom-call(s32[1]{0:T(128)} %bitcast._, bf16[2048,1024]{1,0:T(8,128)(2,1)} %refs_0_.5, bf16[1024,512]{1,0:T(8,128)(2,1)} %get-tuple-element.104.refs_1_, bf16[1024,512]{1,0:T(8,128)(2,1)} %get-tuple-element.105.refs_2_), custom_call_target="tpu_custom_call" | custom-call | flops 5000000000 | bytes 1000000 | tf_op jit(solution)/shard_map/gates/pallas_call | solution.py:265
  50.1 1.6 %collective-permute-start.9 = (bf16[256,1024]{1,0:T(8,128)(2,1)S(1)}, bf16[256,1024]{1,0:T(8,128)(2,1)S(1)}, u32[]{:S(2)}, u32[]{:S(2)}) collective-permute-start(bf16[256,1024]{1,0:T(8,128)(2,1)S(1)} %collective-permute-done.2), channel_id=1, source_target_pairs={{0,1},{1,2},{2,3},{3,0},{4,5},{5,6},{6,7},{7,4},{8,9},{9,10},{10,1... | collective-permute-start | bytes 1572872 | tf_op jit(solution)/shard_map/ppermute | solution.py:521
  52.8 2.4 %collective-permute-start.5 = (bf16[144,512]{1,0:T(8,128)(2,1)S(1)}, bf16[144,512]{1,0:T(8,128)(2,1)S(1)}, u32[]{:S(2)}, u32[]{:S(2)}) collective-permute-start(bf16[144,512]{1,0:T(8,128)(2,1)S(1)} %get-tuple-element.142), channel_id=1, source_target_pairs={{0,8},{4,12},{8,0},{12,4},{16,24},{20,28},{24,16},{28,20},{1,9},{5... | collective-permute-start | bytes 442376 | tf_op jit(solution)/shard_map/ppermute | solution.py:509
  55.2 7.2 %inside.1 = (bf16[1024,512]{1,0:T(8,128)(2,1)}, bf16[1024,512]{1,0:T(8,128)(2,1)}) custom-call(s32[1]{0:T(128)} %bitcast._, bf16[2048,768]{1,0:T(8,128)(2,1)} %get-tuple-element.70.refs_0_, f32[2048,128]{1,0:T(8,128)} %get-tuple-element.71.refs_1_.refs_3_, f32[8,2048]{1,0:T(8,128)} %get-tuple-element.72.refs_2_, ...), custom_call_target="tpu_custom_call" | custom-call | flops 8000000000 | bytes 1000000 | tf_op jit(solution)/shard_map/inside/pallas_call | solution.py:265
  63.4 7.5 %finish.1 = (bf16[256,512]{1,0:T(8,128)(2,1)}, bf16[256,512]{1,0:T(8,128)(2,1)}, bf16[256,512]{1,0:T(8,128)(2,1)}, bf16[256,512]{1,0:T(8,128)(2,1)}) custom-call(s32[1]{0:T(128)} %bitcast._, bf16[2048,768]{1,0:T(8,128)(2,1)} %get-tuple-element.70.refs_0_, bf16[16,128,512]{2,1,0:T(8,128)(2,1)} %get-tuple-element.76.refs_1_.refs_6_, ...), custom_call_target="tpu_custom_call" | custom-call | flops 100000000 | bytes 1000000 | tf_op jit(solution)/shard_map/finish/pallas_call | solution.py:265
  71.0 1.6 %collective-permute-start.10 = (bf16[256,512]{1,0:T(8,128)(2,1)}, bf16[256,512]{1,0:T(8,128)(2,1)S(1)}, u32[]{:S(2)}, u32[]{:S(2)}) collective-permute-start(bf16[256,512]{1,0:T(8,128)(2,1)} %get-tuple-element.113), channel_id=1, source_target_pairs={{0,1},{1,2},{2,3},{3,0},{4,5},{5,6},{6,7},{7,4},{8,9},{9,10},{10,1... | collective-permute-start | bytes 786440 | tf_op jit(solution)/shard_map/ppermute | solution.py:521
  72.7 1.6 %collective-permute-start.11 = (bf16[256,512]{1,0:T(8,128)(2,1)}, bf16[256,512]{1,0:T(8,128)(2,1)}, u32[]{:S(2)}, u32[]{:S(2)}) collective-permute-start(bf16[256,512]{1,0:T(8,128)(2,1)} %get-tuple-element.115), channel_id=1, source_target_pairs={{0,2},{1,3},{2,0},{3,1},{4,6},{5,7},{6,4},{7,5},{8,10},{9,11},{10,... | collective-permute-start | bytes 786440 | tf_op jit(solution)/shard_map/ppermute | solution.py:521
  74.3 1.9 %collective-permute-start.12 = (bf16[256,512]{1,0:T(8,128)(2,1)}, bf16[256,512]{1,0:T(8,128)(2,1)}, u32[]{:S(2)}, u32[]{:S(2)}) collective-permute-start(bf16[256,512]{1,0:T(8,128)(2,1)} %get-tuple-element.116), channel_id=1, source_target_pairs={{0,3},{1,0},{2,1},{3,2},{4,7},{5,4},{6,5},{7,6},{8,11},{9,8},{10,9... | collective-permute-start | bytes 786440 | tf_op jit(solution)/shard_map/ppermute | solution.py:521
  76.2 5.8 %gates.3 = (bf16[1024,512]{1,0:T(8,128)(2,1)}, bf16[1024,512]{1,0:T(8,128)(2,1)}) custom-call(s32[1]{0:T(128)} %bitcast._, bf16[2048,1024]{1,0:T(8,128)(2,1)} %refs_0_.5, bf16[1024,512]{1,0:T(8,128)(2,1)} %get-tuple-element.104.refs_1_, bf16[1024,512]{1,0:T(8,128)(2,1)} %get-tuple-element.105.refs_2_), custom_call_target="tpu_custom_call" | custom-call | flops 100000000 | bytes 1000000 | tf_op jit(solution)/shard_map/gates/pallas_call | solution.py:265
  82.0 11.4 %settle.1 = (bf16[256,512]{1,0:T(8,128)(2,1)}, bf16[256,512]{1,0:T(8,128)(2,1)}, bf16[256,512]{1,0:T(8,128)(2,1)}, bf16[256,512]{1,0:T(8,128)(2,1)}) custom-call(s32[1]{0:T(128)} %bitcast._, bf16[2048,768]{1,0:T(8,128)(2,1)} %get-tuple-element.70.refs_0_, f32[2048,128]{1,0:T(8,128)} %get-tuple-element.71.refs_1_.refs_3_, ...), custom_call_target="tpu_custom_call" | custom-call | flops 100000000 | bytes 1000000 | tf_op jit(solution)/shard_map/settle/pallas_call | solution.py:265
  93.5 8.6 %collective-permute-done.11 = bf16[256,512]{1,0:T(8,128)(2,1)} collective-permute-done((bf16[256,512]{1,0:T(8,128)(2,1)}, bf16[256,512]{1,0:T(8,128)(2,1)}, u32[]{:S(2)}, u32[]{:S(2)}) %collective-permute-start.11) | collective-permute-done | bytes 262176 | tf_op jit(solution)/shard_map/ppermute | solution.py:521
  102.1 1.9 %collective-permute-done.12 = bf16[256,512]{1,0:T(8,128)(2,1)} collective-permute-done((bf16[256,512]{1,0:T(8,128)(2,1)}, bf16[256,512]{1,0:T(8,128)(2,1)}, u32[]{:S(2)}, u32[]{:S(2)}) %collective-permute-start.12) | collective-permute-done | bytes 262176 | tf_op jit(solution)/shard_map/ppermute | solution.py:521
  104.0 2.0 %collective-permute-start.16 = (bf16[256,512]{1,0:T(8,128)(2,1)}, bf16[256,512]{1,0:T(8,128)(2,1)S(1)}, u32[]{:S(2)}, u32[]{:S(2)}) collective-permute-start(bf16[256,512]{1,0:T(8,128)(2,1)} %get-tuple-element.130), channel_id=1, source_target_pairs={{0,1},{1,2},{2,3},{3,0},{4,5},{5,6},{6,7},{7,4},{8,9},{9,10},{10,1... | collective-permute-start | bytes 786440 | tf_op jit(solution)/shard_map/ppermute | solution.py:521
  106.1 1.3 %broadcast_select_fusion.1 = (bf16[256,1024]{1,0:T(8,128)(2,1)S(1)}, bf16[256,1024]{1,0:T(8,128)(2,1)S(1)}, bf16[256,1024]{1,0:T(8,128)(2,1)S(1)}, bf16[256,1024]{1,0:T(8,128)(2,1)S(1)}) fusion(bf16[256,1024]{1,0:T(8,128)(2,1)S(1)} %collective-permute-done.2, pred[]{:T(512)S(6)} %eq.14, bf16[512,1024]{1,0:T(8,128)(2,1)} %collective-permute-done.8, ...), kind=kLoop, calls=%fused_computation.21 | loop fusion | flops 1048576 | bytes 4194305 | tf_op jit(solution)/shard_map/jit(_where)/select_n | solution.py:588
  107.9 1.4 %fusion.9 = f32[256,1024]{1,0:T(8,128)S(1)} fusion(bf16[256,512]{1,0:T(8,128)(2,1)} %collective-permute-done.11, bf16[256,1024]{1,0:T(8,128)(2,1)S(1)} %get-tuple-element.140, bf16[256,1024]{1,0:T(8,128)(2,1)S(1)} %get-tuple-element.139), kind=kOutput, calls=%fused_computation.17 | convolution fusion | flops 270532608 | bytes 2359296 | tf_op jit(solution)/shard_map/dot_general | solution.py:595
  109.3 1.4 %fusion.11 = f32[256,1024]{1,0:T(8,128)S(1)} fusion(bf16[256,512]{1,0:T(8,128)(2,1)} %collective-permute-done.12, bf16[256,1024]{1,0:T(8,128)(2,1)S(1)} %get-tuple-element.137, bf16[256,1024]{1,0:T(8,128)(2,1)S(1)} %get-tuple-element.138), kind=kOutput, calls=%fused_computation.19 | convolution fusion | flops 270532608 | bytes 2359296 | tf_op jit(solution)/shard_map/dot_general | solution.py:595
  110.8 1.6 %fusion.5 = bf16[256,1024]{1,0:T(8,128)(2,1)S(1)} fusion(f32[256,1024]{1,0:T(8,128)S(1)} %fusion.7, f32[256,1024]{1,0:T(8,128)S(1)} %fusion.9, f32[256,1024]{1,0:T(8,128)S(1)} %fusion.11, bf16[256,512]{1,0:T(8,128)(2,1)S(1)} %copy-done.2, bf16[512,1024]{1,0:T(8,128)(2,1)S(1)} %copy-done, bf16[2048,1024]{1,0:T(8,128)(2,1)} %refs_0_.5, s32[]{:T(128)S(6)} %select_n.70), kind=kOutput, calls=%fused_computation.7 | convolution fusion | flops 270008320 | bytes 5505028 | tf_op jit(solution)/shard_map/dot_general | solution.py:595
  113.2 7.5 %collective-permute-done.14 = bf16[256,512]{1,0:T(8,128)(2,1)S(1)} collective-permute-done((bf16[256,512]{1,0:T(8,128)(2,1)}, bf16[256,512]{1,0:T(8,128)(2,1)S(1)}, u32[]{:S(2)}, u32[]{:S(2)}) %collective-permute-start.14) | collective-permute-done | bytes 262176 | tf_op jit(solution)/shard_map/ppermute | solution.py:521
  121.2 1.5 %fusion.1 = f32[256,1024]{1,0:T(8,128)S(1)} fusion(f32[256,1024]{1,0:T(8,128)S(1)} %fusion.8, f32[256,1024]{1,0:T(8,128)S(1)} %fusion.10, bf16[256,512]{1,0:T(8,128)(2,1)S(1)} %copy-done.3, bf16[512,1024]{1,0:T(8,128)(2,1)S(1)} %copy-done, bf16[2048,1024]{1,0:T(8,128)(2,1)} %refs_0_.5, s32[]{:T(128)S(6)} %add.70), kind=kOutput, calls=%fused_computation.2 | convolution fusion | flops 269484032 | bytes 4980740 | tf_op jit(solution)/shard_map/dot_general | solution.py:595
  (47 shorter events, 10.0 us)
Async XLA Ops:
  0.0 6.5 %copy-start = (bf16[512,1024]{1,0:T(8,128)(2,1)S(1)}, bf16[512,1024]{1,0:T(8,128)(2,1)}, u32[]{:S(2)}) copy-start(bf16[512,1024]{1,0:T(8,128)(2,1)} %param.23) | copy-start | bytes 3145732
  0.9 6.9 %collective-permute-start = (bf16[16,1024]{1,0:T(8,128)(2,1)S(1)}, bf16[16,1024]{1,0:T(8,128)(2,1)S(1)}, u32[]{:S(2)}, u32[]{:S(2)}) collective-permute-start(bf16[16,1024]{1,0:T(8,128)(2,1)S(1)} %get-tuple-element.132), channel_id=1, source_target_pairs={{0,4},{4,8},{8,12},{12,16},{16,20},{20,24},{24,28},{1,5},{5,9},{9,... | collective-permute-start | bytes 98312 | tf_op jit(solution)/shard_map/ppermute | solution.py:517
  2.8 5.2 %collective-permute-start.1 = (bf16[16,1024]{1,0:T(8,128)(2,1)S(1)}, bf16[16,1024]{1,0:T(8,128)(2,1)S(1)}, u32[]{:S(2)}, u32[]{:S(2)}) collective-permute-start(bf16[16,1024]{1,0:T(8,128)(2,1)S(1)} %get-tuple-element.131), channel_id=1, source_target_pairs={{4,0},{8,4},{12,8},{16,12},{20,16},{24,20},{28,24},{5,1},{9,5},{13... | collective-permute-start | bytes 98312 | tf_op jit(solution)/shard_map/ppermute | solution.py:517
  7.8 2.2 %copy-start.4 = (bf16[16,1024]{1,0:T(8,128)(2,1)}, bf16[16,1024]{1,0:T(8,128)(2,1)S(1)}, u32[]{:S(2)}) copy-start(bf16[16,1024]{1,0:T(8,128)(2,1)S(1)} %collective-permute-done.refs_2_) | copy-start | bytes 98308
  8.0 2.0 %copy-start.5 = (bf16[16,1024]{1,0:T(8,128)(2,1)}, bf16[16,1024]{1,0:T(8,128)(2,1)S(1)}, u32[]{:S(2)}) copy-start(bf16[16,1024]{1,0:T(8,128)(2,1)S(1)} %collective-permute-done.1.refs_3_) | copy-start | bytes 98308
  8.0 32.9 %collective-permute-start.2 = (bf16[256,1024]{1,0:T(8,128)(2,1)S(1)}, bf16[256,1024]{1,0:T(8,128)(2,1)S(1)}, u32[]{:S(2)}, u32[]{:S(2)}) collective-permute-start(bf16[256,1024]{1,0:T(8,128)(2,1)S(1)} %constant_dynamic-slice_fusion.2), channel_id=1, source_target_pairs={{0,1},{1,2},{2,3},{3,0},{4,5},{5,6},{6,7},{7,4},{8,9},{9,10},{10,1... | collective-permute-start | bytes 1572872 | tf_op jit(solution)/shard_map/ppermute | solution.py:521
  9.6 31.4 %collective-permute-start.3 = (bf16[256,1024]{1,0:T(8,128)(2,1)S(1)}, bf16[256,1024]{1,0:T(8,128)(2,1)S(1)}, u32[]{:S(2)}, u32[]{:S(2)}) collective-permute-start(bf16[256,1024]{1,0:T(8,128)(2,1)S(1)} %constant_dynamic-slice_fusion.2), channel_id=1, source_target_pairs={{0,3},{1,0},{2,1},{3,2},{4,7},{5,4},{6,5},{7,6},{8,11},{9,8},{10,9... | collective-permute-start | bytes 1572872 | tf_op jit(solution)/shard_map/ppermute | solution.py:521
  41.0 7.8 %collective-permute-start.4 = (bf16[288,512]{1,0:T(8,128)(2,1)}, bf16[288,512]{1,0:T(8,128)(2,1)S(1)}, u32[]{:S(2)}, u32[]{:S(2)}) collective-permute-start(bf16[288,512]{1,0:T(8,128)(2,1)} %get-tuple-element.82.refs_1_), channel_id=1, source_target_pairs={{0,4},{4,0},{8,12},{12,8},{16,20},{20,16},{24,28},{28,24},{1,5},{5... | collective-permute-start | bytes 884744 | tf_op jit(solution)/shard_map/ppermute | solution.py:490
  43.0 5.8 %copy-start.1 = (bf16[288,512]{1,0:T(8,128)(2,1)S(1)}, bf16[288,512]{1,0:T(8,128)(2,1)}, u32[]{:S(2)}) copy-start(bf16[288,512]{1,0:T(8,128)(2,1)} %get-tuple-element.82.refs_1_) | copy-start | bytes 884740
  50.1 13.4 %collective-permute-start.8 = (bf16[512,1024]{1,0:T(8,128)(2,1)}, bf16[512,1024]{1,0:T(8,128)(2,1)}, u32[]{:S(2)}, u32[]{:S(2)}) collective-permute-start(bf16[512,1024]{1,0:T(8,128)(2,1)} %pad_maximum_fusion), channel_id=1, source_target_pairs={{0,4},{4,0},{8,12},{12,8},{16,20},{20,16},{24,28},{28,24},{1,5},{5... | collective-permute-start | bytes 3145736 | tf_op jit(solution)/shard_map/ppermute | solution.py:560
  50.1 20.8 %collective-permute-start.9 = (bf16[256,1024]{1,0:T(8,128)(2,1)S(1)}, bf16[256,1024]{1,0:T(8,128)(2,1)S(1)}, u32[]{:S(2)}, u32[]{:S(2)}) collective-permute-start(bf16[256,1024]{1,0:T(8,128)(2,1)S(1)} %collective-permute-done.2), channel_id=1, source_target_pairs={{0,1},{1,2},{2,3},{3,0},{4,5},{5,6},{6,7},{7,4},{8,9},{9,10},{10,1... | collective-permute-start | bytes 1572872 | tf_op jit(solution)/shard_map/ppermute | solution.py:521
  51.7 10.7 %collective-permute-start.6 = (bf16[144,512]{1,0:T(8,128)(2,1)S(1)}, bf16[144,512]{1,0:T(8,128)(2,1)S(1)}, u32[]{:S(2)}, u32[]{:S(2)}) collective-permute-start(bf16[144,512]{1,0:T(8,128)(2,1)S(1)} %get-tuple-element.141), channel_id=1, source_target_pairs={{0,16},{4,20},{8,24},{12,28},{16,0},{20,4},{24,8},{28,12},{1,17},{... | collective-permute-start | bytes 442376 | tf_op jit(solution)/shard_map/ppermute | solution.py:509
  51.8 10.6 %collective-permute-start.7 = (bf16[144,512]{1,0:T(8,128)(2,1)S(1)}, bf16[144,512]{1,0:T(8,128)(2,1)S(1)}, u32[]{:S(2)}, u32[]{:S(2)}) collective-permute-start(bf16[144,512]{1,0:T(8,128)(2,1)S(1)} %get-tuple-element.141), channel_id=1, source_target_pairs={{0,24},{4,28},{8,16},{12,20},{16,8},{20,12},{24,0},{28,4},{1,25},{... | collective-permute-start | bytes 442376 | tf_op jit(solution)/shard_map/ppermute | solution.py:509
  52.8 9.5 %collective-permute-start.5 = (bf16[144,512]{1,0:T(8,128)(2,1)S(1)}, bf16[144,512]{1,0:T(8,128)(2,1)S(1)}, u32[]{:S(2)}, u32[]{:S(2)}) collective-permute-start(bf16[144,512]{1,0:T(8,128)(2,1)S(1)} %get-tuple-element.142), channel_id=1, source_target_pairs={{0,8},{4,12},{8,0},{12,4},{16,24},{20,28},{24,16},{28,20},{1,9},{5... | collective-permute-start | bytes 442376 | tf_op jit(solution)/shard_map/ppermute | solution.py:509
  70.9 33.0 %collective-permute-start.13 = (bf16[256,1024]{1,0:T(8,128)(2,1)S(1)}, bf16[256,1024]{1,0:T(8,128)(2,1)S(1)}, u32[]{:S(2)}, u32[]{:S(2)}) collective-permute-start(bf16[256,1024]{1,0:T(8,128)(2,1)S(1)} %collective-permute-done.9), channel_id=1, source_target_pairs={{0,4},{4,0},{8,12},{12,8},{16,20},{20,16},{24,28},{28,24},{1,5},{5... | collective-permute-start | bytes 1572872 | tf_op jit(solution)/shard_map/ppermute | solution.py:565
  71.0 22.3 %collective-permute-start.10 = (bf16[256,512]{1,0:T(8,128)(2,1)}, bf16[256,512]{1,0:T(8,128)(2,1)S(1)}, u32[]{:S(2)}, u32[]{:S(2)}) collective-permute-start(bf16[256,512]{1,0:T(8,128)(2,1)} %get-tuple-element.113), channel_id=1, source_target_pairs={{0,1},{1,2},{2,3},{3,0},{4,5},{5,6},{6,7},{7,4},{8,9},{9,10},{10,1... | collective-permute-start | bytes 786440 | tf_op jit(solution)/shard_map/ppermute | solution.py:521
  72.7 29.4 %collective-permute-start.11 = (bf16[256,512]{1,0:T(8,128)(2,1)}, bf16[256,512]{1,0:T(8,128)(2,1)}, u32[]{:S(2)}, u32[]{:S(2)}) collective-permute-start(bf16[256,512]{1,0:T(8,128)(2,1)} %get-tuple-element.115), channel_id=1, source_target_pairs={{0,2},{1,3},{2,0},{3,1},{4,6},{5,7},{6,4},{7,5},{8,10},{9,11},{10,... | collective-permute-start | bytes 786440 | tf_op jit(solution)/shard_map/ppermute | solution.py:521
  74.3 29.7 %collective-permute-start.12 = (bf16[256,512]{1,0:T(8,128)(2,1)}, bf16[256,512]{1,0:T(8,128)(2,1)}, u32[]{:S(2)}, u32[]{:S(2)}) collective-permute-start(bf16[256,512]{1,0:T(8,128)(2,1)} %get-tuple-element.116), channel_id=1, source_target_pairs={{0,3},{1,0},{2,1},{3,2},{4,7},{5,4},{6,5},{7,6},{8,11},{9,8},{10,9... | collective-permute-start | bytes 786440 | tf_op jit(solution)/shard_map/ppermute | solution.py:521
  93.4 19.4 %collective-permute-start.15 = (bf16[256,512]{1,0:T(8,128)(2,1)}, bf16[256,512]{1,0:T(8,128)(2,1)S(1)}, u32[]{:S(2)}, u32[]{:S(2)}) collective-permute-start(bf16[256,512]{1,0:T(8,128)(2,1)} %get-tuple-element.129), channel_id=1, source_target_pairs={{0,2},{1,3},{2,0},{3,1},{4,6},{5,7},{6,4},{7,5},{8,10},{9,11},{10,... | collective-permute-start | bytes 786440 | tf_op jit(solution)/shard_map/ppermute | solution.py:521
  104.0 16.7 %collective-permute-start.14 = (bf16[256,512]{1,0:T(8,128)(2,1)}, bf16[256,512]{1,0:T(8,128)(2,1)S(1)}, u32[]{:S(2)}, u32[]{:S(2)}) collective-permute-start(bf16[256,512]{1,0:T(8,128)(2,1)} %get-tuple-element.128), channel_id=1, source_target_pairs={{0,3},{1,0},{2,1},{3,2},{4,7},{5,4},{6,5},{7,6},{8,11},{9,8},{10,9... | collective-permute-start | bytes 786440 | tf_op jit(solution)/shard_map/ppermute | solution.py:521
  104.0 18.7 %collective-permute-start.16 = (bf16[256,512]{1,0:T(8,128)(2,1)}, bf16[256,512]{1,0:T(8,128)(2,1)S(1)}, u32[]{:S(2)}, u32[]{:S(2)}) collective-permute-start(bf16[256,512]{1,0:T(8,128)(2,1)} %get-tuple-element.130), channel_id=1, source_target_pairs={{0,1},{1,2},{2,3},{3,0},{4,5},{5,6},{6,7},{7,4},{8,9},{9,10},{10,1... | collective-permute-start | bytes 786440 | tf_op jit(solution)/shard_map/ppermute | solution.py:521
  107.9 2.9 %copy-start.2 = (bf16[256,512]{1,0:T(8,128)(2,1)S(1)}, bf16[256,512]{1,0:T(8,128)(2,1)}, u32[]{:S(2)}) copy-start(bf16[256,512]{1,0:T(8,128)(2,1)} %get-tuple-element.119) | copy-start | bytes 786436
  112.3 8.8 %copy-start.3 = (bf16[256,512]{1,0:T(8,128)(2,1)S(1)}, bf16[256,512]{1,0:T(8,128)(2,1)}, u32[]{:S(2)}) copy-start(bf16[256,512]{1,0:T(8,128)(2,1)} %get-tuple-element.127) | copy-start | bytes 786436

commit v12 on v10

--- a/solution.py
+++ b/solution.py
@@ -589,7 +589,7 @@
             total = lax.optimization_barrier(total)
         total = (total + jnp.dot(arrived[k][order[-1]], groups[order[-1]], preferred_element_type=F32)).astype(BF16)
         if result is None:
-            result = jnp.pad(total, ((0, share - size), (0, 0)))
+            result = lax.optimization_barrier(jnp.pad(total, ((0, share - size), (0, 0))))
         else:
             result = lax.dynamic_update_slice(result, total, (k * size, 0))
     return result

time: 126 us -> 125 us (level)
  transfers between devices with their start and end apart: 17 -> 17, of which waited for: 5 -> 5; matrix products, arithmetic and copies ran while one was open for 8% -> 9% of each run, Pallas kernels for 56% -> 56%
where the time goes in v12:
time: 125 us
  Pallas kernels  69.7 us (56%)
  starting transfers between devices  23.1 us (18%)
  waiting for transfers between devices  17.3 us (14%)
  matrix products  7.69 us (6%)
  other arithmetic  4.71 us (4%)
  local copies, waits for them, and re-layouts  2.06 us (2%)
    pallas_call x5, Pallas kernels, by_destination(): pl.pallas_call(lambda _, *refs: kernel(*refs), grid_spec=pltpu.PrefetchSc...  37.7 us
    pallas_call x1, Pallas kernels, project(): pl.pallas_call(functools.partial(project_kernel, heads, inner), grid=(n,)...  30.9 us
    ppermute x9, waiting for transfers between devices, rotated(): lax.ppermute(block, 'head', [(i, (i + d) % count) for i in range(count)])  17 us
    ppermute x9, starting transfers between devices, rotated(): lax.ppermute(block, 'head', [(i, (i + d) % count) for i in range(count)])  11.9 us
    dot_general x6, matrix products, on_device(): jnp.dot(arrived[k][d], groups[d], preferred_element_type=F32)  6.8 us
    ppermute x2, starting transfers between devices, shifted(): lax.ppermute(block, axis, [(i - distance, i) for i in devices if i - dist...  5.55 us
    ppermute x3, starting transfers between devices, incoming(): lax.ppermute(block, axis, [(i, i ^ d * distance) for i in range(count)])  3.55 us
  transfers between devices with their start and end apart: 17, of which 5 were waited for; matrix products, arithmetic and copies ran while one was open for 9% of the time, Pallas kernels for 56%

profile of v12, /device:TPU:10, one launch (start us, length us, event | category | flops | bytes accessed | tf_op | source)
XLA Modules:
  0.0 124.9 jit_solution(5312708804269082003)
XLA Ops:
  0.9 1.9 %collective-permute-start = (bf16[16,1024]{1,0:T(8,128)(2,1)S(1)}, bf16[16,1024]{1,0:T(8,128)(2,1)S(1)}, u32[]{:S(2)}, u32[]{:S(2)}) collective-permute-start(bf16[16,1024]{1,0:T(8,128)(2,1)S(1)} %get-tuple-element.130), channel_id=1, source_target_pairs={{0,4},{4,8},{8,12},{12,16},{16,20},{20,24},{24,28},{1,5},{5,9},{9,... | collective-permute-start | bytes 98312 | tf_op jit(solution)/shard_map/ppermute | solution.py:517
  2.8 3.6 %collective-permute-start.1 = (bf16[16,1024]{1,0:T(8,128)(2,1)S(1)}, bf16[16,1024]{1,0:T(8,128)(2,1)S(1)}, u32[]{:S(2)}, u32[]{:S(2)}) collective-permute-start(bf16[16,1024]{1,0:T(8,128)(2,1)S(1)} %get-tuple-element.129), channel_id=1, source_target_pairs={{4,0},{8,4},{12,8},{16,12},{20,16},{24,20},{28,24},{5,1},{9,5},{13... | collective-permute-start | bytes 98312 | tf_op jit(solution)/shard_map/ppermute | solution.py:517
  8.0 1.6 %collective-permute-start.2 = (bf16[256,1024]{1,0:T(8,128)(2,1)S(1)}, bf16[256,1024]{1,0:T(8,128)(2,1)S(1)}, u32[]{:S(2)}, u32[]{:S(2)}) collective-permute-start(bf16[256,1024]{1,0:T(8,128)(2,1)S(1)} %constant_dynamic-slice_fusion.2), channel_id=1, source_target_pairs={{0,1},{1,2},{2,3},{3,0},{4,5},{5,6},{6,7},{7,4},{8,9},{9,10},{10,1... | collective-permute-start | bytes 1572872 | tf_op jit(solution)/shard_map/ppermute | solution.py:521
  10.0 30.9 %project.1 = (bf16[2048,768]{1,0:T(8,128)(2,1)}, f32[2048,128]{1,0:T(8,128)}, f32[8,2048]{1,0:T(8,128)}, bf16[16,128,512]{2,1,0:T(8,128)(2,1)}, f32[16,8,512]{2,...) custom-call(bf16[2048,1024]{1,0:T(8,128)(2,1)} %refs_0_.5, ...), custom_call_target="tpu_custom_call" | custom-call | flops 22000001024 | bytes 40000000 | tf_op jit(solution)/shard_map/project/pallas_call | solution.py:224
  41.0 2.0 %collective-permute-start.4 = (bf16[288,512]{1,0:T(8,128)(2,1)}, bf16[288,512]{1,0:T(8,128)(2,1)S(1)}, u32[]{:S(2)}, u32[]{:S(2)}) collective-permute-start(bf16[288,512]{1,0:T(8,128)(2,1)} %get-tuple-element.81.refs_1_), channel_id=1, source_target_pairs={{0,4},{4,0},{8,12},{12,8},{16,20},{20,16},{24,28},{28,24},{1,5},{5... | collective-permute-start | bytes 884744 | tf_op jit(solution)/shard_map/ppermute | solution.py:490
  43.0 5.8 %gates.2 = (bf16[1024,512]{1,0:T(8,128)(2,1)}, bf16[1024,512]{1,0:T(8,128)(2,1)}) custom-call(s32[1]{0:T(128)} %bitcast._, bf16[2048,1024]{1,0:T(8,128)(2,1)} %refs_0_.5, bf16[1024,512]{1,0:T(8,128)(2,1)} %get-tuple-element.103.refs_1_, bf16[1024,512]{1,0:T(8,128)(2,1)} %get-tuple-element.104.refs_2_), custom_call_target="tpu_custom_call" | custom-call | flops 5000000000 | bytes 1000000 | tf_op jit(solution)/shard_map/gates/pallas_call | solution.py:265
  50.1 1.6 %collective-permute-start.9 = (bf16[256,1024]{1,0:T(8,128)(2,1)S(1)}, bf16[256,1024]{1,0:T(8,128)(2,1)S(1)}, u32[]{:S(2)}, u32[]{:S(2)}) collective-permute-start(bf16[256,1024]{1,0:T(8,128)(2,1)S(1)} %collective-permute-done.2), channel_id=1, source_target_pairs={{0,1},{1,2},{2,3},{3,0},{4,5},{5,6},{6,7},{7,4},{8,9},{9,10},{10,1... | collective-permute-start | bytes 1572872 | tf_op jit(solution)/shard_map/ppermute | solution.py:521
  52.9 2.4 %collective-permute-start.5 = (bf16[144,512]{1,0:T(8,128)(2,1)S(1)}, bf16[144,512]{1,0:T(8,128)(2,1)S(1)}, u32[]{:S(2)}, u32[]{:S(2)}) collective-permute-start(bf16[144,512]{1,0:T(8,128)(2,1)S(1)} %get-tuple-element.140), channel_id=1, source_target_pairs={{0,8},{4,12},{8,0},{12,4},{16,24},{20,28},{24,16},{28,20},{1,9},{5... | collective-permute-start | bytes 442376 | tf_op jit(solution)/shard_map/ppermute | solution.py:509
  55.3 7.2 %inside.1 = (bf16[1024,512]{1,0:T(8,128)(2,1)}, bf16[1024,512]{1,0:T(8,128)(2,1)}) custom-call(s32[1]{0:T(128)} %bitcast._, bf16[2048,768]{1,0:T(8,128)(2,1)} %get-tuple-element.69.refs_0_, f32[2048,128]{1,0:T(8,128)} %get-tuple-element.70.refs_1_.refs_3_, f32[8,2048]{1,0:T(8,128)} %get-tuple-element.71.refs_2_, ...), custom_call_target="tpu_custom_call" | custom-call | flops 8000000000 | bytes 1000000 | tf_op jit(solution)/shard_map/inside/pallas_call | solution.py:265
  63.5 7.5 %finish.1 = (bf16[256,512]{1,0:T(8,128)(2,1)}, bf16[256,512]{1,0:T(8,128)(2,1)}, bf16[256,512]{1,0:T(8,128)(2,1)}, bf16[256,512]{1,0:T(8,128)(2,1)}) custom-call(s32[1]{0:T(128)} %bitcast._, bf16[2048,768]{1,0:T(8,128)(2,1)} %get-tuple-element.69.refs_0_, bf16[16,128,512]{2,1,0:T(8,128)(2,1)} %get-tuple-element.75.refs_1_.refs_6_, ...), custom_call_target="tpu_custom_call" | custom-call | flops 100000000 | bytes 1000000 | tf_op jit(solution)/shard_map/finish/pallas_call | solution.py:265
  71.1 1.6 %collective-permute-start.10 = (bf16[256,512]{1,0:T(8,128)(2,1)}, bf16[256,512]{1,0:T(8,128)(2,1)S(1)}, u32[]{:S(2)}, u32[]{:S(2)}) collective-permute-start(bf16[256,512]{1,0:T(8,128)(2,1)} %get-tuple-element.112), channel_id=1, source_target_pairs={{0,1},{1,2},{2,3},{3,0},{4,5},{5,6},{6,7},{7,4},{8,9},{9,10},{10,1... | collective-permute-start | bytes 786440 | tf_op jit(solution)/shard_map/ppermute | solution.py:521
  72.7 1.6 %collective-permute-start.11 = (bf16[256,512]{1,0:T(8,128)(2,1)}, bf16[256,512]{1,0:T(8,128)(2,1)}, u32[]{:S(2)}, u32[]{:S(2)}) collective-permute-start(bf16[256,512]{1,0:T(8,128)(2,1)} %get-tuple-element.113), channel_id=1, source_target_pairs={{0,2},{1,3},{2,0},{3,1},{4,6},{5,7},{6,4},{7,5},{8,10},{9,11},{10,... | collective-permute-start | bytes 786440 | tf_op jit(solution)/shard_map/ppermute | solution.py:521
  74.3 1.9 %collective-permute-start.12 = (bf16[256,512]{1,0:T(8,128)(2,1)}, bf16[256,512]{1,0:T(8,128)(2,1)}, u32[]{:S(2)}, u32[]{:S(2)}) collective-permute-start(bf16[256,512]{1,0:T(8,128)(2,1)} %get-tuple-element.114), channel_id=1, source_target_pairs={{0,3},{1,0},{2,1},{3,2},{4,7},{5,4},{6,5},{7,6},{8,11},{9,8},{10,9... | collective-permute-start | bytes 786440 | tf_op jit(solution)/shard_map/ppermute | solution.py:521
  76.2 5.8 %gates.3 = (bf16[1024,512]{1,0:T(8,128)(2,1)}, bf16[1024,512]{1,0:T(8,128)(2,1)}) custom-call(s32[1]{0:T(128)} %bitcast._, bf16[2048,1024]{1,0:T(8,128)(2,1)} %refs_0_.5, bf16[1024,512]{1,0:T(8,128)(2,1)} %get-tuple-element.103.refs_1_, bf16[1024,512]{1,0:T(8,128)(2,1)} %get-tuple-element.104.refs_2_), custom_call_target="tpu_custom_call" | custom-call | flops 100000000 | bytes 1000000 | tf_op jit(solution)/shard_map/gates/pallas_call | solution.py:265
  82.0 11.4 %settle.1 = (bf16[256,512]{1,0:T(8,128)(2,1)}, bf16[256,512]{1,0:T(8,128)(2,1)}, bf16[256,512]{1,0:T(8,128)(2,1)}, bf16[256,512]{1,0:T(8,128)(2,1)}) custom-call(s32[1]{0:T(128)} %bitcast._, bf16[2048,768]{1,0:T(8,128)(2,1)} %get-tuple-element.69.refs_0_, f32[2048,128]{1,0:T(8,128)} %get-tuple-element.70.refs_1_.refs_3_, ...), custom_call_target="tpu_custom_call" | custom-call | flops 100000000 | bytes 1000000 | tf_op jit(solution)/shard_map/settle/pallas_call | solution.py:265
  93.4 2.6 %collective-permute-done.11 = bf16[256,512]{1,0:T(8,128)(2,1)} collective-permute-done((bf16[256,512]{1,0:T(8,128)(2,1)}, bf16[256,512]{1,0:T(8,128)(2,1)}, u32[]{:S(2)}, u32[]{:S(2)}) %collective-permute-start.11) | collective-permute-done | bytes 262176 | tf_op jit(solution)/shard_map/ppermute | solution.py:521
  96.1 2.3 %collective-permute-done.12 = bf16[256,512]{1,0:T(8,128)(2,1)} collective-permute-done((bf16[256,512]{1,0:T(8,128)(2,1)}, bf16[256,512]{1,0:T(8,128)(2,1)}, u32[]{:S(2)}, u32[]{:S(2)}) %collective-permute-start.12) | collective-permute-done | bytes 262176 | tf_op jit(solution)/shard_map/ppermute | solution.py:521
  101.3 1.4 %fusion.9 = f32[256,1024]{1,0:T(8,128)S(1)} fusion(bf16[256,512]{1,0:T(8,128)(2,1)} %collective-permute-done.11, bf16[256,1024]{1,0:T(8,128)(2,1)S(1)} %get-tuple-element.138, bf16[256,1024]{1,0:T(8,128)(2,1)S(1)} %get-tuple-element.137), kind=kOutput, calls=%fused_computation.16 | convolution fusion | flops 270532608 | bytes 2359296 | tf_op jit(solution)/shard_map/dot_general | solution.py:587
  102.8 1.4 %fusion.11 = f32[256,1024]{1,0:T(8,128)S(1)} fusion(bf16[256,512]{1,0:T(8,128)(2,1)} %collective-permute-done.12, bf16[256,1024]{1,0:T(8,128)(2,1)S(1)} %get-tuple-element.132, bf16[256,1024]{1,0:T(8,128)(2,1)S(1)} %get-tuple-element.131), kind=kOutput, calls=%fused_computation.18 | convolution fusion | flops 270532608 | bytes 2359296 | tf_op jit(solution)/shard_map/dot_general | solution.py:587
  104.2 1.6 %fusion.5 = bf16[256,1024]{1,0:T(8,128)(2,1)S(1)} fusion(f32[256,1024]{1,0:T(8,128)S(1)} %fusion.7, f32[256,1024]{1,0:T(8,128)S(1)} %fusion.9, f32[256,1024]{1,0:T(8,128)S(1)} %fusion.11, bf16[256,512]{1,0:T(8,128)(2,1)S(1)} %copy-done.2, bf16[512,1024]{1,0:T(8,128)(2,1)S(1)} %copy-done, bf16[2048,1024]{1,0:T(8,128)(2,1)} %refs_0_.5, s32[]{:T(128)S(6)} %select_n.70), kind=kOutput, calls=%fused_computation.7 | convolution fusion | flops 270008320 | bytes 5505028 | tf_op jit(solution)/shard_map/dot_general | solution.py:587
  106.9 2.0 %collective-permute-start.16 = (bf16[256,512]{1,0:T(8,128)(2,1)S(1)}, bf16[256,512]{1,0:T(8,128)(2,1)S(1)}, u32[]{:S(2)}, u32[]{:S(2)}) collective-permute-start(bf16[256,512]{1,0:T(8,128)(2,1)S(1)} %copy-done.4), channel_id=1, source_target_pairs={{0,1},{1,2},{2,3},{3,0},{4,5},{5,6},{6,7},{7,4},{8,9},{9,10},{10,1... | collective-permute-start | bytes 786440 | tf_op jit(solution)/shard_map/ppermute | solution.py:521
  108.9 7.3 %collective-permute-done.15 = bf16[256,512]{1,0:T(8,128)(2,1)S(1)} collective-permute-done((bf16[256,512]{1,0:T(8,128)(2,1)}, bf16[256,512]{1,0:T(8,128)(2,1)S(1)}, u32[]{:S(2)}, u32[]{:S(2)}) %collective-permute-start.15) | collective-permute-done | bytes 262176 | tf_op jit(solution)/shard_map/ppermute | solution.py:521
  116.7 4.8 %collective-permute-done.14 = bf16[256,512]{1,0:T(8,128)(2,1)S(1)} collective-permute-done((bf16[256,512]{1,0:T(8,128)(2,1)}, bf16[256,512]{1,0:T(8,128)(2,1)S(1)}, u32[]{:S(2)}, u32[]{:S(2)}) %collective-permute-start.14) | collective-permute-done | bytes 262176 | tf_op jit(solution)/shard_map/ppermute | solution.py:521
  122.0 1.5 %fusion.1 = f32[256,1024]{1,0:T(8,128)S(1)} fusion(f32[256,1024]{1,0:T(8,128)S(1)} %fusion.8, f32[256,1024]{1,0:T(8,128)S(1)} %fusion.10, bf16[256,512]{1,0:T(8,128)(2,1)S(1)} %copy-done.3, bf16[512,1024]{1,0:T(8,128)(2,1)S(1)} %copy-done, bf16[2048,1024]{1,0:T(8,128)(2,1)} %refs_0_.5, s32[]{:T(128)S(6)} %add.72), kind=kOutput, calls=%fused_computation.2 | convolution fusion | flops 269484032 | bytes 4980740 | tf_op jit(solution)/shard_map/dot_general | solution.py:587
  (49 shorter events, 12.8 us)
Async XLA Ops:
  0.0 6.5 %copy-start = (bf16[512,1024]{1,0:T(8,128)(2,1)S(1)}, bf16[512,1024]{1,0:T(8,128)(2,1)}, u32[]{:S(2)}) copy-start(bf16[512,1024]{1,0:T(8,128)(2,1)} %param.23) | copy-start | bytes 3145732
  0.9 6.9 %collective-permute-start = (bf16[16,1024]{1,0:T(8,128)(2,1)S(1)}, bf16[16,1024]{1,0:T(8,128)(2,1)S(1)}, u32[]{:S(2)}, u32[]{:S(2)}) collective-permute-start(bf16[16,1024]{1,0:T(8,128)(2,1)S(1)} %get-tuple-element.130), channel_id=1, source_target_pairs={{0,4},{4,8},{8,12},{12,16},{16,20},{20,24},{24,28},{1,5},{5,9},{9,... | collective-permute-start | bytes 98312 | tf_op jit(solution)/shard_map/ppermute | solution.py:517
  2.8 5.2 %collective-permute-start.1 = (bf16[16,1024]{1,0:T(8,128)(2,1)S(1)}, bf16[16,1024]{1,0:T(8,128)(2,1)S(1)}, u32[]{:S(2)}, u32[]{:S(2)}) collective-permute-start(bf16[16,1024]{1,0:T(8,128)(2,1)S(1)} %get-tuple-element.129), channel_id=1, source_target_pairs={{4,0},{8,4},{12,8},{16,12},{20,16},{24,20},{28,24},{5,1},{9,5},{13... | collective-permute-start | bytes 98312 | tf_op jit(solution)/shard_map/ppermute | solution.py:517
  7.8 2.2 %copy-start.5 = (bf16[16,1024]{1,0:T(8,128)(2,1)}, bf16[16,1024]{1,0:T(8,128)(2,1)S(1)}, u32[]{:S(2)}) copy-start(bf16[16,1024]{1,0:T(8,128)(2,1)S(1)} %collective-permute-done.refs_2_) | copy-start | bytes 98308
  8.0 2.0 %copy-start.6 = (bf16[16,1024]{1,0:T(8,128)(2,1)}, bf16[16,1024]{1,0:T(8,128)(2,1)S(1)}, u32[]{:S(2)}) copy-start(bf16[16,1024]{1,0:T(8,128)(2,1)S(1)} %collective-permute-done.1.refs_3_) | copy-start | bytes 98308
  8.0 32.9 %collective-permute-start.2 = (bf16[256,1024]{1,0:T(8,128)(2,1)S(1)}, bf16[256,1024]{1,0:T(8,128)(2,1)S(1)}, u32[]{:S(2)}, u32[]{:S(2)}) collective-permute-start(bf16[256,1024]{1,0:T(8,128)(2,1)S(1)} %constant_dynamic-slice_fusion.2), channel_id=1, source_target_pairs={{0,1},{1,2},{2,3},{3,0},{4,5},{5,6},{6,7},{7,4},{8,9},{9,10},{10,1... | collective-permute-start | bytes 1572872 | tf_op jit(solution)/shard_map/ppermute | solution.py:521
  9.6 31.4 %collective-permute-start.3 = (bf16[256,1024]{1,0:T(8,128)(2,1)S(1)}, bf16[256,1024]{1,0:T(8,128)(2,1)S(1)}, u32[]{:S(2)}, u32[]{:S(2)}) collective-permute-start(bf16[256,1024]{1,0:T(8,128)(2,1)S(1)} %constant_dynamic-slice_fusion.2), channel_id=1, source_target_pairs={{0,3},{1,0},{2,1},{3,2},{4,7},{5,4},{6,5},{7,6},{8,11},{9,8},{10,9... | collective-permute-start | bytes 1572872 | tf_op jit(solution)/shard_map/ppermute | solution.py:521
  41.0 7.8 %collective-permute-start.4 = (bf16[288,512]{1,0:T(8,128)(2,1)}, bf16[288,512]{1,0:T(8,128)(2,1)S(1)}, u32[]{:S(2)}, u32[]{:S(2)}) collective-permute-start(bf16[288,512]{1,0:T(8,128)(2,1)} %get-tuple-element.81.refs_1_), channel_id=1, source_target_pairs={{0,4},{4,0},{8,12},{12,8},{16,20},{20,16},{24,28},{28,24},{1,5},{5... | collective-permute-start | bytes 884744 | tf_op jit(solution)/shard_map/ppermute | solution.py:490
  43.0 5.8 %copy-start.1 = (bf16[288,512]{1,0:T(8,128)(2,1)S(1)}, bf16[288,512]{1,0:T(8,128)(2,1)}, u32[]{:S(2)}) copy-start(bf16[288,512]{1,0:T(8,128)(2,1)} %get-tuple-element.81.refs_1_) | copy-start | bytes 884740
  50.1 13.4 %collective-permute-start.8 = (bf16[512,1024]{1,0:T(8,128)(2,1)}, bf16[512,1024]{1,0:T(8,128)(2,1)}, u32[]{:S(2)}, u32[]{:S(2)}) collective-permute-start(bf16[512,1024]{1,0:T(8,128)(2,1)} %pad_maximum_fusion), channel_id=1, source_target_pairs={{0,4},{4,0},{8,12},{12,8},{16,20},{20,16},{24,28},{28,24},{1,5},{5... | collective-permute-start | bytes 3145736 | tf_op jit(solution)/shard_map/ppermute | solution.py:560
  50.1 20.9 %collective-permute-start.9 = (bf16[256,1024]{1,0:T(8,128)(2,1)S(1)}, bf16[256,1024]{1,0:T(8,128)(2,1)S(1)}, u32[]{:S(2)}, u32[]{:S(2)}) collective-permute-start(bf16[256,1024]{1,0:T(8,128)(2,1)S(1)} %collective-permute-done.2), channel_id=1, source_target_pairs={{0,1},{1,2},{2,3},{3,0},{4,5},{5,6},{6,7},{7,4},{8,9},{9,10},{10,1... | collective-permute-start | bytes 1572872 | tf_op jit(solution)/shard_map/ppermute | solution.py:521
  51.7 10.7 %collective-permute-start.6 = (bf16[144,512]{1,0:T(8,128)(2,1)S(1)}, bf16[144,512]{1,0:T(8,128)(2,1)S(1)}, u32[]{:S(2)}, u32[]{:S(2)}) collective-permute-start(bf16[144,512]{1,0:T(8,128)(2,1)S(1)} %get-tuple-element.139), channel_id=1, source_target_pairs={{0,16},{4,20},{8,24},{12,28},{16,0},{20,4},{24,8},{28,12},{1,17},{... | collective-permute-start | bytes 442376 | tf_op jit(solution)/shard_map/ppermute | solution.py:509
  51.8 10.6 %collective-permute-start.7 = (bf16[144,512]{1,0:T(8,128)(2,1)S(1)}, bf16[144,512]{1,0:T(8,128)(2,1)S(1)}, u32[]{:S(2)}, u32[]{:S(2)}) collective-permute-start(bf16[144,512]{1,0:T(8,128)(2,1)S(1)} %get-tuple-element.139), channel_id=1, source_target_pairs={{0,24},{4,28},{8,16},{12,20},{16,8},{20,12},{24,0},{28,4},{1,25},{... | collective-permute-start | bytes 442376 | tf_op jit(solution)/shard_map/ppermute | solution.py:509
  52.9 9.6 %collective-permute-start.5 = (bf16[144,512]{1,0:T(8,128)(2,1)S(1)}, bf16[144,512]{1,0:T(8,128)(2,1)S(1)}, u32[]{:S(2)}, u32[]{:S(2)}) collective-permute-start(bf16[144,512]{1,0:T(8,128)(2,1)S(1)} %get-tuple-element.140), channel_id=1, source_target_pairs={{0,8},{4,12},{8,0},{12,4},{16,24},{20,28},{24,16},{28,20},{1,9},{5... | collective-permute-start | bytes 442376 | tf_op jit(solution)/shard_map/ppermute | solution.py:509
  71.0 27.4 %collective-permute-start.13 = (bf16[256,1024]{1,0:T(8,128)(2,1)S(1)}, bf16[256,1024]{1,0:T(8,128)(2,1)S(1)}, u32[]{:S(2)}, u32[]{:S(2)}) collective-permute-start(bf16[256,1024]{1,0:T(8,128)(2,1)S(1)} %collective-permute-done.9), channel_id=1, source_target_pairs={{0,4},{4,0},{8,12},{12,8},{16,20},{20,16},{24,28},{28,24},{1,5},{5... | collective-permute-start | bytes 1572872 | tf_op jit(solution)/shard_map/ppermute | solution.py:565
  71.1 22.4 %collective-permute-start.10 = (bf16[256,512]{1,0:T(8,128)(2,1)}, bf16[256,512]{1,0:T(8,128)(2,1)S(1)}, u32[]{:S(2)}, u32[]{:S(2)}) collective-permute-start(bf16[256,512]{1,0:T(8,128)(2,1)} %get-tuple-element.112), channel_id=1, source_target_pairs={{0,1},{1,2},{2,3},{3,0},{4,5},{5,6},{6,7},{7,4},{8,9},{9,10},{10,1... | collective-permute-start | bytes 786440 | tf_op jit(solution)/shard_map/ppermute | solution.py:521
  72.7 23.3 %collective-permute-start.11 = (bf16[256,512]{1,0:T(8,128)(2,1)}, bf16[256,512]{1,0:T(8,128)(2,1)}, u32[]{:S(2)}, u32[]{:S(2)}) collective-permute-start(bf16[256,512]{1,0:T(8,128)(2,1)} %get-tuple-element.113), channel_id=1, source_target_pairs={{0,2},{1,3},{2,0},{3,1},{4,6},{5,7},{6,4},{7,5},{8,10},{9,11},{10,... | collective-permute-start | bytes 786440 | tf_op jit(solution)/shard_map/ppermute | solution.py:521
  74.3 24.0 %collective-permute-start.12 = (bf16[256,512]{1,0:T(8,128)(2,1)}, bf16[256,512]{1,0:T(8,128)(2,1)}, u32[]{:S(2)}, u32[]{:S(2)}) collective-permute-start(bf16[256,512]{1,0:T(8,128)(2,1)} %get-tuple-element.114), channel_id=1, source_target_pairs={{0,3},{1,0},{2,1},{3,2},{4,7},{5,4},{6,5},{7,6},{8,11},{9,8},{10,9... | collective-permute-start | bytes 786440 | tf_op jit(solution)/shard_map/ppermute | solution.py:521
  98.3 17.9 %collective-permute-start.15 = (bf16[256,512]{1,0:T(8,128)(2,1)}, bf16[256,512]{1,0:T(8,128)(2,1)S(1)}, u32[]{:S(2)}, u32[]{:S(2)}) collective-permute-start(bf16[256,512]{1,0:T(8,128)(2,1)} %get-tuple-element.127), channel_id=1, source_target_pairs={{0,2},{1,3},{2,0},{3,1},{4,6},{5,7},{6,4},{7,5},{8,10},{9,11},{10,... | collective-permute-start | bytes 786440 | tf_op jit(solution)/shard_map/ppermute | solution.py:521
  99.4 22.1 %collective-permute-start.14 = (bf16[256,512]{1,0:T(8,128)(2,1)}, bf16[256,512]{1,0:T(8,128)(2,1)S(1)}, u32[]{:S(2)}, u32[]{:S(2)}) collective-permute-start(bf16[256,512]{1,0:T(8,128)(2,1)} %get-tuple-element.126), channel_id=1, source_target_pairs={{0,3},{1,0},{2,1},{3,2},{4,7},{5,4},{6,5},{7,6},{8,11},{9,8},{10,9... | collective-permute-start | bytes 786440 | tf_op jit(solution)/shard_map/ppermute | solution.py:521
  101.3 2.9 %copy-start.2 = (bf16[256,512]{1,0:T(8,128)(2,1)S(1)}, bf16[256,512]{1,0:T(8,128)(2,1)}, u32[]{:S(2)}) copy-start(bf16[256,512]{1,0:T(8,128)(2,1)} %get-tuple-element.117) | copy-start | bytes 786436
  104.2 2.7 %copy-start.4 = (bf16[256,512]{1,0:T(8,128)(2,1)S(1)}, bf16[256,512]{1,0:T(8,128)(2,1)}, u32[]{:S(2)}) copy-start(bf16[256,512]{1,0:T(8,128)(2,1)} %get-tuple-element.128) | copy-start | bytes 786436
  106.9 15.0 %copy-start.3 = (bf16[256,512]{1,0:T(8,128)(2,1)S(1)}, bf16[256,512]{1,0:T(8,128)(2,1)}, u32[]{:S(2)}) copy-start(bf16[256,512]{1,0:T(8,128)(2,1)} %get-tuple-element.125) | copy-start | bytes 786436
  106.9 16.5 %collective-permute-start.16 = (bf16[256,512]{1,0:T(8,128)(2,1)S(1)}, bf16[256,512]{1,0:T(8,128)(2,1)S(1)}, u32[]{:S(2)}, u32[]{:S(2)}) collective-permute-start(bf16[256,512]{1,0:T(8,128)(2,1)S(1)} %copy-done.4), channel_id=1, source_target_pairs={{0,1},{1,2},{2,3},{3,0},{4,5},{5,6},{6,7},{7,4},{8,9},{9,10},{10,1... | collective-permute-start | bytes 786440 | tf_op jit(solution)/shard_map/ppermute | solution.py:521

commit v13 on v10

--- a/solution.py
+++ b/solution.py
@@ -11,7 +11,7 @@
 STATE = 128
 CHUNK = 128
 TILE = 256
-PROJECT_TILE = 512
+PROJECT_TILE = 1024
 EPS = 1e-05
 RIM = 16
 TAIL = 16

time: 126 us -> 125 us (level)
  transfers between devices with their start and end apart: 17 -> 17, of which waited for: 5 -> 5; matrix products, arithmetic and copies ran while one was open for 8% -> 8% of each run, Pallas kernels for 56% -> 55%
where the time goes in v13:
time: 125 us
  Pallas kernels  69.2 us (55%)
  starting transfers between devices  23.3 us (19%)
  waiting for transfers between devices  18.4 us (15%)
  matrix products  7.7 us (6%)
  other arithmetic  5 us (4%)
    pallas_call x5, Pallas kernels, by_destination(): pl.pallas_call(lambda _, *refs: kernel(*refs), grid_spec=pltpu.PrefetchSc...  37.6 us
    pallas_call x1, Pallas kernels, project(): pl.pallas_call(functools.partial(project_kernel, heads, inner), grid=(n,)...  30.4 us
    ppermute x9, waiting for transfers between devices, rotated(): lax.ppermute(block, 'head', [(i, (i + d) % count) for i in range(count)])  18.2 us
    ppermute x9, starting transfers between devices, rotated(): lax.ppermute(block, 'head', [(i, (i + d) % count) for i in range(count)])  11.9 us
    dot_general x6, matrix products, on_device(): jnp.dot(arrived[k][d], groups[d], preferred_element_type=F32)  6.81 us
    ppermute x2, starting transfers between devices, shifted(): lax.ppermute(block, axis, [(i - distance, i) for i in devices if i - dist...  5.55 us
    ppermute x3, starting transfers between devices, incoming(): lax.ppermute(block, axis, [(i, i ^ d * distance) for i in range(count)])  3.55 us
  transfers between devices with their start and end apart: 17, of which 5 were waited for; matrix products, arithmetic and copies ran while one was open for 8% of the time, Pallas kernels for 55%

profile of v13, /device:TPU:10, one launch (start us, length us, event | category | flops | bytes accessed | tf_op | source)
XLA Modules:
  0.0 124.8 jit_solution(6638258995876915331)
XLA Ops:
  0.9 1.9 %collective-permute-start = (bf16[16,1024]{1,0:T(8,128)(2,1)S(1)}, bf16[16,1024]{1,0:T(8,128)(2,1)S(1)}, u32[]{:S(2)}, u32[]{:S(2)}) collective-permute-start(bf16[16,1024]{1,0:T(8,128)(2,1)S(1)} %get-tuple-element.130), channel_id=1, source_target_pairs={{0,4},{4,8},{8,12},{12,16},{16,20},{20,24},{24,28},{1,5},{5,9},{9,... | collective-permute-start | bytes 98312 | tf_op jit(solution)/shard_map/ppermute | solution.py:517
  2.8 3.6 %collective-permute-start.1 = (bf16[16,1024]{1,0:T(8,128)(2,1)S(1)}, bf16[16,1024]{1,0:T(8,128)(2,1)S(1)}, u32[]{:S(2)}, u32[]{:S(2)}) collective-permute-start(bf16[16,1024]{1,0:T(8,128)(2,1)S(1)} %get-tuple-element.129), channel_id=1, source_target_pairs={{4,0},{8,4},{12,8},{16,12},{20,16},{24,20},{28,24},{5,1},{9,5},{13... | collective-permute-start | bytes 98312 | tf_op jit(solution)/shard_map/ppermute | solution.py:517
  8.0 1.6 %collective-permute-start.2 = (bf16[256,1024]{1,0:T(8,128)(2,1)S(1)}, bf16[256,1024]{1,0:T(8,128)(2,1)S(1)}, u32[]{:S(2)}, u32[]{:S(2)}) collective-permute-start(bf16[256,1024]{1,0:T(8,128)(2,1)S(1)} %constant_dynamic-slice_fusion.2), channel_id=1, source_target_pairs={{0,1},{1,2},{2,3},{3,0},{4,5},{5,6},{6,7},{7,4},{8,9},{9,10},{10,1... | collective-permute-start | bytes 1572872 | tf_op jit(solution)/shard_map/ppermute | solution.py:521
  10.0 30.4 %project.1 = (bf16[2048,768]{1,0:T(8,128)(2,1)}, f32[2048,128]{1,0:T(8,128)}, f32[8,2048]{1,0:T(8,128)}, bf16[16,128,512]{2,1,0:T(8,128)(2,1)}, f32[16,8,512]{2,...) custom-call(bf16[2048,1024]{1,0:T(8,128)(2,1)} %refs_0_.5, ...), custom_call_target="tpu_custom_call" | custom-call | flops 22000001024 | bytes 40000000 | tf_op jit(solution)/shard_map/project/pallas_call | solution.py:224
  40.5 2.0 %collective-permute-start.4 = (bf16[288,512]{1,0:T(8,128)(2,1)}, bf16[288,512]{1,0:T(8,128)(2,1)S(1)}, u32[]{:S(2)}, u32[]{:S(2)}) collective-permute-start(bf16[288,512]{1,0:T(8,128)(2,1)} %get-tuple-element.81.refs_1_), channel_id=1, source_target_pairs={{0,4},{4,0},{8,12},{12,8},{16,20},{20,16},{24,28},{28,24},{1,5},{5... | collective-permute-start | bytes 884744 | tf_op jit(solution)/shard_map/ppermute | solution.py:490
  42.5 5.8 %gates.2 = (bf16[1024,512]{1,0:T(8,128)(2,1)}, bf16[1024,512]{1,0:T(8,128)(2,1)}) custom-call(s32[1]{0:T(128)} %bitcast._, bf16[2048,1024]{1,0:T(8,128)(2,1)} %refs_0_.5, bf16[1024,512]{1,0:T(8,128)(2,1)} %get-tuple-element.103.refs_1_, bf16[1024,512]{1,0:T(8,128)(2,1)} %get-tuple-element.104.refs_2_), custom_call_target="tpu_custom_call" | custom-call | flops 5000000000 | bytes 1000000 | tf_op jit(solution)/shard_map/gates/pallas_call | solution.py:265
  49.8 1.6 %collective-permute-start.9 = (bf16[256,1024]{1,0:T(8,128)(2,1)S(1)}, bf16[256,1024]{1,0:T(8,128)(2,1)S(1)}, u32[]{:S(2)}, u32[]{:S(2)}) collective-permute-start(bf16[256,1024]{1,0:T(8,128)(2,1)S(1)} %collective-permute-done.2), channel_id=1, source_target_pairs={{0,1},{1,2},{2,3},{3,0},{4,5},{5,6},{6,7},{7,4},{8,9},{9,10},{10,1... | collective-permute-start | bytes 1572872 | tf_op jit(solution)/shard_map/ppermute | solution.py:521
  52.5 2.4 %collective-permute-start.5 = (bf16[144,512]{1,0:T(8,128)(2,1)S(1)}, bf16[144,512]{1,0:T(8,128)(2,1)S(1)}, u32[]{:S(2)}, u32[]{:S(2)}) collective-permute-start(bf16[144,512]{1,0:T(8,128)(2,1)S(1)} %get-tuple-element.140), channel_id=1, source_target_pairs={{0,8},{4,12},{8,0},{12,4},{16,24},{20,28},{24,16},{28,20},{1,9},{5... | collective-permute-start | bytes 442376 | tf_op jit(solution)/shard_map/ppermute | solution.py:509
  54.9 7.2 %inside.1 = (bf16[1024,512]{1,0:T(8,128)(2,1)}, bf16[1024,512]{1,0:T(8,128)(2,1)}) custom-call(s32[1]{0:T(128)} %bitcast._, bf16[2048,768]{1,0:T(8,128)(2,1)} %get-tuple-element.69.refs_0_, f32[2048,128]{1,0:T(8,128)} %get-tuple-element.70.refs_1_.refs_3_, f32[8,2048]{1,0:T(8,128)} %get-tuple-element.71.refs_2_, ...), custom_call_target="tpu_custom_call" | custom-call | flops 8000000000 | bytes 1000000 | tf_op jit(solution)/shard_map/inside/pallas_call | solution.py:265
  63.1 7.5 %finish.1 = (bf16[256,512]{1,0:T(8,128)(2,1)}, bf16[256,512]{1,0:T(8,128)(2,1)}, bf16[256,512]{1,0:T(8,128)(2,1)}, bf16[256,512]{1,0:T(8,128)(2,1)}) custom-call(s32[1]{0:T(128)} %bitcast._, bf16[2048,768]{1,0:T(8,128)(2,1)} %get-tuple-element.69.refs_0_, bf16[16,128,512]{2,1,0:T(8,128)(2,1)} %get-tuple-element.75.refs_1_.refs_6_, ...), custom_call_target="tpu_custom_call" | custom-call | flops 100000000 | bytes 1000000 | tf_op jit(solution)/shard_map/finish/pallas_call | solution.py:265
  70.7 1.6 %collective-permute-start.10 = (bf16[256,512]{1,0:T(8,128)(2,1)}, bf16[256,512]{1,0:T(8,128)(2,1)S(1)}, u32[]{:S(2)}, u32[]{:S(2)}) collective-permute-start(bf16[256,512]{1,0:T(8,128)(2,1)} %get-tuple-element.112), channel_id=1, source_target_pairs={{0,1},{1,2},{2,3},{3,0},{4,5},{5,6},{6,7},{7,4},{8,9},{9,10},{10,1... | collective-permute-start | bytes 786440 | tf_op jit(solution)/shard_map/ppermute | solution.py:521
  72.3 1.6 %collective-permute-start.11 = (bf16[256,512]{1,0:T(8,128)(2,1)}, bf16[256,512]{1,0:T(8,128)(2,1)}, u32[]{:S(2)}, u32[]{:S(2)}) collective-permute-start(bf16[256,512]{1,0:T(8,128)(2,1)} %get-tuple-element.113), channel_id=1, source_target_pairs={{0,2},{1,3},{2,0},{3,1},{4,6},{5,7},{6,4},{7,5},{8,10},{9,11},{10,... | collective-permute-start | bytes 786440 | tf_op jit(solution)/shard_map/ppermute | solution.py:521
  73.9 1.9 %collective-permute-start.12 = (bf16[256,512]{1,0:T(8,128)(2,1)}, bf16[256,512]{1,0:T(8,128)(2,1)}, u32[]{:S(2)}, u32[]{:S(2)}) collective-permute-start(bf16[256,512]{1,0:T(8,128)(2,1)} %get-tuple-element.114), channel_id=1, source_target_pairs={{0,3},{1,0},{2,1},{3,2},{4,7},{5,4},{6,5},{7,6},{8,11},{9,8},{10,9... | collective-permute-start | bytes 786440 | tf_op jit(solution)/shard_map/ppermute | solution.py:521
  75.9 5.8 %gates.3 = (bf16[1024,512]{1,0:T(8,128)(2,1)}, bf16[1024,512]{1,0:T(8,128)(2,1)}) custom-call(s32[1]{0:T(128)} %bitcast._, bf16[2048,1024]{1,0:T(8,128)(2,1)} %refs_0_.5, bf16[1024,512]{1,0:T(8,128)(2,1)} %get-tuple-element.103.refs_1_, bf16[1024,512]{1,0:T(8,128)(2,1)} %get-tuple-element.104.refs_2_), custom_call_target="tpu_custom_call" | custom-call | flops 100000000 | bytes 1000000 | tf_op jit(solution)/shard_map/gates/pallas_call | solution.py:265
  81.7 11.4 %settle.1 = (bf16[256,512]{1,0:T(8,128)(2,1)}, bf16[256,512]{1,0:T(8,128)(2,1)}, bf16[256,512]{1,0:T(8,128)(2,1)}, bf16[256,512]{1,0:T(8,128)(2,1)}) custom-call(s32[1]{0:T(128)} %bitcast._, bf16[2048,768]{1,0:T(8,128)(2,1)} %get-tuple-element.69.refs_0_, f32[2048,128]{1,0:T(8,128)} %get-tuple-element.70.refs_1_.refs_3_, ...), custom_call_target="tpu_custom_call" | custom-call | flops 100000000 | bytes 1000000 | tf_op jit(solution)/shard_map/settle/pallas_call | solution.py:265
  93.1 2.6 %collective-permute-done.11 = bf16[256,512]{1,0:T(8,128)(2,1)} collective-permute-done((bf16[256,512]{1,0:T(8,128)(2,1)}, bf16[256,512]{1,0:T(8,128)(2,1)}, u32[]{:S(2)}, u32[]{:S(2)}) %collective-permute-start.11) | collective-permute-done | bytes 262176 | tf_op jit(solution)/shard_map/ppermute | solution.py:521
  95.7 2.3 %collective-permute-done.12 = bf16[256,512]{1,0:T(8,128)(2,1)} collective-permute-done((bf16[256,512]{1,0:T(8,128)(2,1)}, bf16[256,512]{1,0:T(8,128)(2,1)}, u32[]{:S(2)}, u32[]{:S(2)}) %collective-permute-start.12) | collective-permute-done | bytes 262176 | tf_op jit(solution)/shard_map/ppermute | solution.py:521
  99.1 2.0 %collective-permute-start.16 = (bf16[256,512]{1,0:T(8,128)(2,1)}, bf16[256,512]{1,0:T(8,128)(2,1)S(1)}, u32[]{:S(2)}, u32[]{:S(2)}) collective-permute-start(bf16[256,512]{1,0:T(8,128)(2,1)} %get-tuple-element.128), channel_id=1, source_target_pairs={{0,1},{1,2},{2,3},{3,0},{4,5},{5,6},{6,7},{7,4},{8,9},{9,10},{10,1... | collective-permute-start | bytes 786440 | tf_op jit(solution)/shard_map/ppermute | solution.py:521
  103.0 1.4 %fusion.9 = f32[256,1024]{1,0:T(8,128)S(1)} fusion(bf16[256,512]{1,0:T(8,128)(2,1)} %collective-permute-done.11, bf16[256,1024]{1,0:T(8,128)(2,1)S(1)} %get-tuple-element.138, bf16[256,1024]{1,0:T(8,128)(2,1)S(1)} %get-tuple-element.137), kind=kOutput, calls=%fused_computation.17 | convolution fusion | flops 270532608 | bytes 2359296 | tf_op jit(solution)/shard_map/dot_general | solution.py:587
  104.4 1.4 %fusion.11 = f32[256,1024]{1,0:T(8,128)S(1)} fusion(bf16[256,512]{1,0:T(8,128)(2,1)} %collective-permute-done.12, bf16[256,1024]{1,0:T(8,128)(2,1)S(1)} %get-tuple-element.135, bf16[256,1024]{1,0:T(8,128)(2,1)S(1)} %get-tuple-element.136), kind=kOutput, calls=%fused_computation.19 | convolution fusion | flops 270532608 | bytes 2359296 | tf_op jit(solution)/shard_map/dot_general | solution.py:587
  105.9 1.6 %fusion.5 = bf16[256,1024]{1,0:T(8,128)(2,1)S(1)} fusion(f32[256,1024]{1,0:T(8,128)S(1)} %fusion.7, f32[256,1024]{1,0:T(8,128)S(1)} %fusion.9, f32[256,1024]{1,0:T(8,128)S(1)} %fusion.11, bf16[256,512]{1,0:T(8,128)(2,1)S(1)} %copy-done.2, bf16[512,1024]{1,0:T(8,128)(2,1)S(1)} %copy-done, bf16[2048,1024]{1,0:T(8,128)(2,1)} %refs_0_.5, s32[]{:T(128)S(6)} %select_n.70), kind=kOutput, calls=%fused_computation.7 | convolution fusion | flops 270008320 | bytes 5505028 | tf_op jit(solution)/shard_map/dot_general | solution.py:587
  107.4 8.5 %collective-permute-done.15 = bf16[256,512]{1,0:T(8,128)(2,1)S(1)} collective-permute-done((bf16[256,512]{1,0:T(8,128)(2,1)}, bf16[256,512]{1,0:T(8,128)(2,1)S(1)}, u32[]{:S(2)}, u32[]{:S(2)}) %collective-permute-start.15) | collective-permute-done | bytes 262176 | tf_op jit(solution)/shard_map/ppermute | solution.py:521
  116.4 4.8 %collective-permute-done.14 = bf16[256,512]{1,0:T(8,128)(2,1)S(1)} collective-permute-done((bf16[256,512]{1,0:T(8,128)(2,1)}, bf16[256,512]{1,0:T(8,128)(2,1)S(1)}, u32[]{:S(2)}, u32[]{:S(2)}) %collective-permute-start.14) | collective-permute-done | bytes 262176 | tf_op jit(solution)/shard_map/ppermute | solution.py:521
  121.6 1.5 %fusion.1 = f32[256,1024]{1,0:T(8,128)S(1)} fusion(f32[256,1024]{1,0:T(8,128)S(1)} %fusion.8, f32[256,1024]{1,0:T(8,128)S(1)} %fusion.10, bf16[256,512]{1,0:T(8,128)(2,1)S(1)} %copy-done.3, bf16[512,1024]{1,0:T(8,128)(2,1)S(1)} %copy-done, bf16[2048,1024]{1,0:T(8,128)(2,1)} %refs_0_.5, s32[]{:T(128)S(6)} %add.70), kind=kOutput, calls=%fused_computation.2 | convolution fusion | flops 269484032 | bytes 4980740 | tf_op jit(solution)/shard_map/dot_general | solution.py:587
  (47 shorter events, 12.1 us)
Async XLA Ops:
  0.0 6.5 %copy-start = (bf16[512,1024]{1,0:T(8,128)(2,1)S(1)}, bf16[512,1024]{1,0:T(8,128)(2,1)}, u32[]{:S(2)}) copy-start(bf16[512,1024]{1,0:T(8,128)(2,1)} %param.23) | copy-start | bytes 3145732
  0.9 6.9 %collective-permute-start = (bf16[16,1024]{1,0:T(8,128)(2,1)S(1)}, bf16[16,1024]{1,0:T(8,128)(2,1)S(1)}, u32[]{:S(2)}, u32[]{:S(2)}) collective-permute-start(bf16[16,1024]{1,0:T(8,128)(2,1)S(1)} %get-tuple-element.130), channel_id=1, source_target_pairs={{0,4},{4,8},{8,12},{12,16},{16,20},{20,24},{24,28},{1,5},{5,9},{9,... | collective-permute-start | bytes 98312 | tf_op jit(solution)/shard_map/ppermute | solution.py:517
  2.8 5.2 %collective-permute-start.1 = (bf16[16,1024]{1,0:T(8,128)(2,1)S(1)}, bf16[16,1024]{1,0:T(8,128)(2,1)S(1)}, u32[]{:S(2)}, u32[]{:S(2)}) collective-permute-start(bf16[16,1024]{1,0:T(8,128)(2,1)S(1)} %get-tuple-element.129), channel_id=1, source_target_pairs={{4,0},{8,4},{12,8},{16,12},{20,16},{24,20},{28,24},{5,1},{9,5},{13... | collective-permute-start | bytes 98312 | tf_op jit(solution)/shard_map/ppermute | solution.py:517
  7.8 2.2 %copy-start.4 = (bf16[16,1024]{1,0:T(8,128)(2,1)}, bf16[16,1024]{1,0:T(8,128)(2,1)S(1)}, u32[]{:S(2)}) copy-start(bf16[16,1024]{1,0:T(8,128)(2,1)S(1)} %collective-permute-done.refs_2_) | copy-start | bytes 98308
  8.0 2.0 %copy-start.5 = (bf16[16,1024]{1,0:T(8,128)(2,1)}, bf16[16,1024]{1,0:T(8,128)(2,1)S(1)}, u32[]{:S(2)}) copy-start(bf16[16,1024]{1,0:T(8,128)(2,1)S(1)} %collective-permute-done.1.refs_3_) | copy-start | bytes 98308
  8.0 32.5 %collective-permute-start.2 = (bf16[256,1024]{1,0:T(8,128)(2,1)S(1)}, bf16[256,1024]{1,0:T(8,128)(2,1)S(1)}, u32[]{:S(2)}, u32[]{:S(2)}) collective-permute-start(bf16[256,1024]{1,0:T(8,128)(2,1)S(1)} %constant_dynamic-slice_fusion.2), channel_id=1, source_target_pairs={{0,1},{1,2},{2,3},{3,0},{4,5},{5,6},{6,7},{7,4},{8,9},{9,10},{10,1... | collective-permute-start | bytes 1572872 | tf_op jit(solution)/shard_map/ppermute | solution.py:521
  9.6 30.9 %collective-permute-start.3 = (bf16[256,1024]{1,0:T(8,128)(2,1)S(1)}, bf16[256,1024]{1,0:T(8,128)(2,1)S(1)}, u32[]{:S(2)}, u32[]{:S(2)}) collective-permute-start(bf16[256,1024]{1,0:T(8,128)(2,1)S(1)} %constant_dynamic-slice_fusion.2), channel_id=1, source_target_pairs={{0,3},{1,0},{2,1},{3,2},{4,7},{5,4},{6,5},{7,6},{8,11},{9,8},{10,9... | collective-permute-start | bytes 1572872 | tf_op jit(solution)/shard_map/ppermute | solution.py:521
  40.5 7.8 %collective-permute-start.4 = (bf16[288,512]{1,0:T(8,128)(2,1)}, bf16[288,512]{1,0:T(8,128)(2,1)S(1)}, u32[]{:S(2)}, u32[]{:S(2)}) collective-permute-start(bf16[288,512]{1,0:T(8,128)(2,1)} %get-tuple-element.81.refs_1_), channel_id=1, source_target_pairs={{0,4},{4,0},{8,12},{12,8},{16,20},{20,16},{24,28},{28,24},{1,5},{5... | collective-permute-start | bytes 884744 | tf_op jit(solution)/shard_map/ppermute | solution.py:490
  42.5 5.8 %copy-start.1 = (bf16[288,512]{1,0:T(8,128)(2,1)S(1)}, bf16[288,512]{1,0:T(8,128)(2,1)}, u32[]{:S(2)}) copy-start(bf16[288,512]{1,0:T(8,128)(2,1)} %get-tuple-element.81.refs_1_) | copy-start | bytes 884740
  49.6 13.5 %collective-permute-start.8 = (bf16[512,1024]{1,0:T(8,128)(2,1)}, bf16[512,1024]{1,0:T(8,128)(2,1)}, u32[]{:S(2)}, u32[]{:S(2)}) collective-permute-start(bf16[512,1024]{1,0:T(8,128)(2,1)} %pad_maximum_fusion), channel_id=1, source_target_pairs={{0,4},{4,0},{8,12},{12,8},{16,20},{20,16},{24,28},{28,24},{1,5},{5... | collective-permute-start | bytes 3145736 | tf_op jit(solution)/shard_map/ppermute | solution.py:560
  49.8 20.9 %collective-permute-start.9 = (bf16[256,1024]{1,0:T(8,128)(2,1)S(1)}, bf16[256,1024]{1,0:T(8,128)(2,1)S(1)}, u32[]{:S(2)}, u32[]{:S(2)}) collective-permute-start(bf16[256,1024]{1,0:T(8,128)(2,1)S(1)} %collective-permute-done.2), channel_id=1, source_target_pairs={{0,1},{1,2},{2,3},{3,0},{4,5},{5,6},{6,7},{7,4},{8,9},{9,10},{10,1... | collective-permute-start | bytes 1572872 | tf_op jit(solution)/shard_map/ppermute | solution.py:521
  51.4 10.7 %collective-permute-start.6 = (bf16[144,512]{1,0:T(8,128)(2,1)S(1)}, bf16[144,512]{1,0:T(8,128)(2,1)S(1)}, u32[]{:S(2)}, u32[]{:S(2)}) collective-permute-start(bf16[144,512]{1,0:T(8,128)(2,1)S(1)} %get-tuple-element.139), channel_id=1, source_target_pairs={{0,16},{4,20},{8,24},{12,28},{16,0},{20,4},{24,8},{28,12},{1,17},{... | collective-permute-start | bytes 442376 | tf_op jit(solution)/shard_map/ppermute | solution.py:509
  51.4 10.7 %collective-permute-start.7 = (bf16[144,512]{1,0:T(8,128)(2,1)S(1)}, bf16[144,512]{1,0:T(8,128)(2,1)S(1)}, u32[]{:S(2)}, u32[]{:S(2)}) collective-permute-start(bf16[144,512]{1,0:T(8,128)(2,1)S(1)} %get-tuple-element.139), channel_id=1, source_target_pairs={{0,24},{4,28},{8,16},{12,20},{16,8},{20,12},{24,0},{28,4},{1,25},{... | collective-permute-start | bytes 442376 | tf_op jit(solution)/shard_map/ppermute | solution.py:509
  52.5 9.6 %collective-permute-start.5 = (bf16[144,512]{1,0:T(8,128)(2,1)S(1)}, bf16[144,512]{1,0:T(8,128)(2,1)S(1)}, u32[]{:S(2)}, u32[]{:S(2)}) collective-permute-start(bf16[144,512]{1,0:T(8,128)(2,1)S(1)} %get-tuple-element.140), channel_id=1, source_target_pairs={{0,8},{4,12},{8,0},{12,4},{16,24},{20,28},{24,16},{28,20},{1,9},{5... | collective-permute-start | bytes 442376 | tf_op jit(solution)/shard_map/ppermute | solution.py:509
  70.6 27.3 %collective-permute-start.13 = (bf16[256,1024]{1,0:T(8,128)(2,1)S(1)}, bf16[256,1024]{1,0:T(8,128)(2,1)S(1)}, u32[]{:S(2)}, u32[]{:S(2)}) collective-permute-start(bf16[256,1024]{1,0:T(8,128)(2,1)S(1)} %collective-permute-done.9), channel_id=1, source_target_pairs={{0,4},{4,0},{8,12},{12,8},{16,20},{20,16},{24,28},{28,24},{1,5},{5... | collective-permute-start | bytes 1572872 | tf_op jit(solution)/shard_map/ppermute | solution.py:565
  70.7 22.3 %collective-permute-start.10 = (bf16[256,512]{1,0:T(8,128)(2,1)}, bf16[256,512]{1,0:T(8,128)(2,1)S(1)}, u32[]{:S(2)}, u32[]{:S(2)}) collective-permute-start(bf16[256,512]{1,0:T(8,128)(2,1)} %get-tuple-element.112), channel_id=1, source_target_pairs={{0,1},{1,2},{2,3},{3,0},{4,5},{5,6},{6,7},{7,4},{8,9},{9,10},{10,1... | collective-permute-start | bytes 786440 | tf_op jit(solution)/shard_map/ppermute | solution.py:521
  72.3 23.3 %collective-permute-start.11 = (bf16[256,512]{1,0:T(8,128)(2,1)}, bf16[256,512]{1,0:T(8,128)(2,1)}, u32[]{:S(2)}, u32[]{:S(2)}) collective-permute-start(bf16[256,512]{1,0:T(8,128)(2,1)} %get-tuple-element.113), channel_id=1, source_target_pairs={{0,2},{1,3},{2,0},{3,1},{4,6},{5,7},{6,4},{7,5},{8,10},{9,11},{10,... | collective-permute-start | bytes 786440 | tf_op jit(solution)/shard_map/ppermute | solution.py:521
  73.9 24.0 %collective-permute-start.12 = (bf16[256,512]{1,0:T(8,128)(2,1)}, bf16[256,512]{1,0:T(8,128)(2,1)}, u32[]{:S(2)}, u32[]{:S(2)}) collective-permute-start(bf16[256,512]{1,0:T(8,128)(2,1)} %get-tuple-element.114), channel_id=1, source_target_pairs={{0,3},{1,0},{2,1},{3,2},{4,7},{5,4},{6,5},{7,6},{8,11},{9,8},{10,9... | collective-permute-start | bytes 786440 | tf_op jit(solution)/shard_map/ppermute | solution.py:521
  98.0 17.9 %collective-permute-start.15 = (bf16[256,512]{1,0:T(8,128)(2,1)}, bf16[256,512]{1,0:T(8,128)(2,1)S(1)}, u32[]{:S(2)}, u32[]{:S(2)}) collective-permute-start(bf16[256,512]{1,0:T(8,128)(2,1)} %get-tuple-element.127), channel_id=1, source_target_pairs={{0,2},{1,3},{2,0},{3,1},{4,6},{5,7},{6,4},{7,5},{8,10},{9,11},{10,... | collective-permute-start | bytes 786440 | tf_op jit(solution)/shard_map/ppermute | solution.py:521
  99.1 22.1 %collective-permute-start.14 = (bf16[256,512]{1,0:T(8,128)(2,1)}, bf16[256,512]{1,0:T(8,128)(2,1)S(1)}, u32[]{:S(2)}, u32[]{:S(2)}) collective-permute-start(bf16[256,512]{1,0:T(8,128)(2,1)} %get-tuple-element.126), channel_id=1, source_target_pairs={{0,3},{1,0},{2,1},{3,2},{4,7},{5,4},{6,5},{7,6},{8,11},{9,8},{10,9... | collective-permute-start | bytes 786440 | tf_op jit(solution)/shard_map/ppermute | solution.py:521
  99.1 24.1 %collective-permute-start.16 = (bf16[256,512]{1,0:T(8,128)(2,1)}, bf16[256,512]{1,0:T(8,128)(2,1)S(1)}, u32[]{:S(2)}, u32[]{:S(2)}) collective-permute-start(bf16[256,512]{1,0:T(8,128)(2,1)} %get-tuple-element.128), channel_id=1, source_target_pairs={{0,1},{1,2},{2,3},{3,0},{4,5},{5,6},{6,7},{7,4},{8,9},{9,10},{10,1... | collective-permute-start | bytes 786440 | tf_op jit(solution)/shard_map/ppermute | solution.py:521
  103.0 2.9 %copy-start.2 = (bf16[256,512]{1,0:T(8,128)(2,1)S(1)}, bf16[256,512]{1,0:T(8,128)(2,1)}, u32[]{:S(2)}) copy-start(bf16[256,512]{1,0:T(8,128)(2,1)} %get-tuple-element.117) | copy-start | bytes 786436
  107.4 14.2 %copy-start.3 = (bf16[256,512]{1,0:T(8,128)(2,1)S(1)}, bf16[256,512]{1,0:T(8,128)(2,1)}, u32[]{:S(2)}) copy-start(bf16[256,512]{1,0:T(8,128)(2,1)} %get-tuple-element.125) | copy-start | bytes 786436
